TPU v7x, 512 devices: a whole 4x8x8 slice. The times are simulated.
512 devices in a mesh: dp: 64 (over z, y), tensor: 8 (over x, core).
Axes of the slice: x: 4, y: 8, z: 8, core: 2. Of those that a mesh axis runs over, the one named last changes fastest.
Arguments:
- activations: bfloat16 [106496, 2560], P(('dp', 'tensor')), may hold values from -6 to 6
- key_grad: bfloat16 [106496, 1024], P('dp', 'tensor'), may hold values from -0.15625 to 0.15625
- momentum: float32 [64, 2560, 1024], P('dp', None, 'tensor'), may hold values from -6 to 6
- block_ids: int32 [64, 40, 16, 6], P('dp', None, 'tensor'), may hold values from 0 to 31, all different within a row
- counts: int32 [64], P('dp'), may hold values from 1 to 6, 192 in all
Outputs:
- new_momentum: float32 [64, 2560, 1024], P('dp', None, 'tensor')
- update: bfloat16 [2560, 1024], P(None, 'tensor')
Inputs may be any that keep to these rules, and one draw needn't show every extreme that they name: Within one list block_ids[r, a, b, :] all numbers differ; every block number appears somewhere. `counts`: some replica sends 6 blocks for every span.
All inputs are finite; a program needn't handle non-finite values.
Results may differ from a plain program's by a relative error of at most 0.005.
Values may be sent and summed in bfloat16 or wider, within the bound.
No kernel may reach another device: no remote copies, remote signals or barrier semaphores. Data moves between devices by JAX's collectives and lax.ppermute only.
A program may use at most 64 MiB of HBM per device.

v0:
```python
import functools

import jax
import jax.numpy as jnp
import ml_dtypes
import numpy as np
from jax import lax
from jax.experimental import pallas as pl
from jax.experimental.pallas import tpu as pltpu
from jax.sharding import PartitionSpec as P

BLK = 32
CHUNK = 256


def cosine_parts():
    n = np.arange(64, dtype=np.float64)
    c = np.cos(np.pi * (2.0 * n[None, :] + 1.0) * n[:, None] / 128.0) * np.sqrt(2.0 / 64.0)
    c[0] *= np.sqrt(0.5)
    table = np.kron(np.eye(CHUNK // 64), c)
    high = table.astype(ml_dtypes.bfloat16)
    low = (table - high.astype(np.float64)).astype(ml_dtypes.bfloat16)
    return high, low


def dot(a, b):
    return jnp.dot(a, b, preferred_element_type=jnp.float32)


def split(x):
    high = x.astype(jnp.bfloat16)
    return high, (x - high.astype(jnp.float32)).astype(jnp.bfloat16)


def step_kernel(grad, other, momentum, mask, ch, cl, th, tl, sent, kept):
    def body(i, _):
        rows = pl.ds(pl.multiple_of(i * CHUNK, CHUNK), CHUNK)
        x = 0.999 * momentum[rows, :] + grad[rows, :] + other[rows, :].astype(jnp.float32)
        xh, xl = split(x)
        s = (dot(ch[...], xh) + (dot(ch[...], xl) + dot(cl[...], xh))) * mask[rows, :]
        sh, sl = split(s)
        sent[rows, :] = sh
        kept[rows, :] = x - (dot(th[...], sh) + (dot(th[...], sl) + dot(tl[...], sh)))
        return 0

    lax.fori_loop(0, grad.shape[0] // CHUNK, body, 0, unroll=True)


def inverse_kernel(summed, th, tl, update):
    def body(i, _):
        rows = pl.ds(pl.multiple_of(i * CHUNK, CHUNK), CHUNK)
        s = summed[rows, :]
        update[rows, :] = (dot(th[...], s) + dot(tl[...], s)).astype(jnp.bfloat16)
        return 0

    lax.fori_loop(0, update.shape[0] // CHUNK, body, 0, unroll=True)


def gram(a, k):
    return lax.dot_general(a, k, (((0,), (0,)), ((), ())), preferred_element_type=jnp.float32)


def shards(activations, key_grad, momentum, block_ids, counts, *, replicas, group):
    tokens, features = activations.shape
    cols = key_grad.shape[1]
    chips = group // 2
    spot = lax.axis_index("tensor")
    chip, core = spot // 2, spot % 2

    def along(x, step):
        return lax.ppermute(x, "tensor", [(i, (i + 2 * step) % group) for i in range(group)])

    def swap(x):
        return lax.ppermute(x, "tensor", [(i, i ^ 1) for i in range(group)])

    ch, cl = cosine_parts()
    th, tl = jnp.asarray(ch.T), jnp.asarray(cl.T)
    ch, cl = jnp.asarray(ch), jnp.asarray(cl)

    by_core = key_grad.reshape(chips, 2, tokens, cols)
    own = lax.dynamic_index_in_dim(by_core, core, 1, keepdims=False)
    theirs = swap(lax.dynamic_index_in_dim(by_core, 1 - core, 1, keepdims=False))
    keys = jnp.concatenate([own, theirs], axis=2)

    def keys_of(step):
        return lax.dynamic_index_in_dim(keys, (chip + step) % chips, 0, keepdims=False)

    cut = tokens // 2 // 16 * 16
    left = along(activations, 1)
    right = along(activations, -1)
    far_a = along(left[:cut], 1)
    far_b = along(right[cut:], -1)
    total = gram(activations, keys_of(0)) + gram(left, keys_of(-1)) + gram(right, keys_of(1))
    far_keys = keys_of(2)
    total = total + gram(far_a, far_keys[:cut]) + gram(far_b, far_keys[cut:])
    other = swap(total[:, cols:].astype(jnp.bfloat16))

    active = jnp.arange(block_ids.shape[3], dtype=jnp.int32) < counts[0]
    hit = (block_ids[0][..., None] == jnp.arange(BLK, dtype=jnp.int32)) & active[:, None]
    chosen = jnp.transpose(jnp.any(hit, axis=2), (0, 2, 1)).astype(jnp.float32)
    mask = jnp.broadcast_to(
        chosen[:, :, None, :, None], (features // 64, BLK, 2, cols // 64, 64)
    ).reshape(features, cols)

    vmem = pl.BlockSpec(memory_space=pltpu.VMEM)
    sent, kept = pl.pallas_call(
        step_kernel,
        out_shape=(
            jax.ShapeDtypeStruct((features, cols), jnp.bfloat16),
            jax.ShapeDtypeStruct((features, cols), jnp.float32),
        ),
        in_specs=[vmem] * 8,
        out_specs=(vmem, vmem),
        compiler_params=pltpu.CompilerParams(vmem_limit_bytes=32 << 20),
        name="step",
    )(total[:, :cols], other, momentum[0], mask, ch, cl, th, tl)

    pieces = lax.all_to_all(
        sent.reshape(replicas, features // replicas, cols), "dp", 0, 0, tiled=True
    )
    mine = jnp.sum(pieces.astype(jnp.float32), axis=0).astype(jnp.bfloat16)
    summed = lax.all_to_all(
        jnp.broadcast_to(mine[None], (replicas,) + mine.shape), "dp", 0, 0, tiled=True
    ).reshape(features, cols)
    update = pl.pallas_call(
        inverse_kernel,
        out_shape=jax.ShapeDtypeStruct((features, cols), jnp.bfloat16),
        in_specs=[vmem] * 3,
        out_specs=vmem,
        compiler_params=pltpu.CompilerParams(vmem_limit_bytes=32 << 20),
        name="inverse",
    )(summed, th, tl)
    return kept[None], update


def solution(mesh):
    in_specs = (
        P(("dp", "tensor"), None),
        P("dp", "tensor"),
        P("dp", None, "tensor"),
        P("dp", None, "tensor", None),
        P("dp"),
    )
    out_specs = (P("dp", None, "tensor"), P(None, "tensor"))
    body = functools.partial(shards, replicas=mesh.shape["dp"], group=mesh.shape["tensor"])
    return jax.shard_map(body, mesh=mesh, in_specs=in_specs, out_specs=out_specs, check_vma=False)
```

profile of v0, /device:TPU:6, one launch (start us, length us, event | category | flops | bytes accessed | tf_op | source)
XLA Modules:
  0.0 135.7 jit_solution(6313939618174401951)
XLA Ops:
  0.6 7.8 %collective-permute-start.1 = (bf16[208,2560]{1,0:T(8,128)(2,1)}, bf16[208,2560]{1,0:T(8,128)(2,1)S(1)}, u32[]{:S(2)}, u32[]{:S(2)}) collective-permute-start(bf16[208,2560]{1,0:T(8,128)(2,1)} %param.9), channel_id=1, source_target_pairs={{0,2},{1,3},{2,4},{3,5},{4,6},{5,7},{6,0},{7,1},{8,10},{9,11},{10,... | collective-permute-start | bytes 3194888 | tf_op jit(solution)/shard_map/ppermute | solution.py:71
  8.4 1.9 %collective-permute-start.2 = (bf16[208,2560]{1,0:T(8,128)(2,1)}, bf16[208,2560]{1,0:T(8,128)(2,1)S(1)}, u32[]{:S(2)}, u32[]{:S(2)}) collective-permute-start(bf16[208,2560]{1,0:T(8,128)(2,1)} %param.9), channel_id=1, source_target_pairs={{0,6},{1,7},{2,0},{3,1},{4,2},{5,3},{6,4},{7,5},{8,14},{9,15},{10,... | collective-permute-start | bytes 3194888 | tf_op jit(solution)/shard_map/ppermute | solution.py:71
  10.4 1.1 dynamic-slice_bitcast_fusion
  11.4 1.9 %collective-permute-start = (bf16[4,208,128]{2,1,0:T(8,128)(2,1)S(1)}, bf16[4,208,128]{2,1,0:T(8,128)(2,1)S(1)}, u32[]{:S(2)}, u32[]{:S(2)}) collective-permute-start(bf16[4,208,128]{2,1,0:T(8,128)(2,1)S(1)} %get-tuple-element.6), channel_id=1, source_target_pairs={{0,1},{1,0},{2,3},{3,2},{4,5},{5,4},{6,7},{7,6},{8,9},{9,8},{10,11... | collective-permute-start | bytes 638984 | tf_op jit(solution)/shard_map/ppermute | solution.py:74
  13.4 1.3 collective-permute-done
  14.8 13.2 %collective-permute-done.1 = bf16[208,2560]{1,0:T(8,128)(2,1)S(1)} collective-permute-done((bf16[208,2560]{1,0:T(8,128)(2,1)}, bf16[208,2560]{1,0:T(8,128)(2,1)S(1)}, u32[]{:S(2)}, u32[]{:S(2)}) %collective-permute-start.1) | collective-permute-done | bytes 1064992 | tf_op jit(solution)/shard_map/ppermute | solution.py:71
  28.0 0.0 copy-start.6
  28.0 3.5 %collective-permute-start.3 = (bf16[96,2560]{1,0:T(8,128)(2,1)S(1)}, bf16[96,2560]{1,0:T(8,128)(2,1)S(1)}, u32[]{:S(2)}, u32[]{:S(2)}) collective-permute-start(bf16[96,2560]{1,0:T(8,128)(2,1)S(1)} %slice.34), channel_id=1, source_target_pairs={{0,2},{1,3},{2,4},{3,5},{4,6},{5,7},{6,0},{7,1},{8,10},{9,11},{10,... | collective-permute-start | bytes 1474568 | tf_op jit(solution)/shard_map/ppermute | solution.py:71
  31.6 0.0 collective-permute-done.2
  31.6 2.4 %collective-permute-start.4 = (bf16[112,2560]{1,0:T(8,128)(2,1)S(1)}, bf16[112,2560]{1,0:T(8,128)(2,1)S(1)}, u32[]{:S(2)}, u32[]{:S(2)}) collective-permute-start(bf16[112,2560]{1,0:T(8,128)(2,1)S(1)} %slice.36), channel_id=1, source_target_pairs={{0,6},{1,7},{2,0},{3,1},{4,2},{5,3},{6,4},{7,5},{8,14},{9,15},{10,... | collective-permute-start | bytes 1720328 | tf_op jit(solution)/shard_map/ppermute | solution.py:71
  34.1 0.7 fusion.11
  34.7 0.0 copy-done.6
  34.8 0.7 convolution_add_fusion.1
  35.5 6.7 %collective-permute-done.3 = bf16[96,2560]{1,0:T(8,128)(2,1)S(1)} collective-permute-done((bf16[96,2560]{1,0:T(8,128)(2,1)S(1)}, bf16[96,2560]{1,0:T(8,128)(2,1)S(1)}, u32[]{:S(2)}, u32[]{:S(2)}) %collective-permute-start.3) | collective-permute-done | bytes 491552 | tf_op jit(solution)/shard_map/ppermute | solution.py:71
  42.1 0.5 fusion.17
  42.7 4.4 %collective-permute-done.4 = bf16[112,2560]{1,0:T(8,128)(2,1)S(1)} collective-permute-done((bf16[112,2560]{1,0:T(8,128)(2,1)S(1)}, bf16[112,2560]{1,0:T(8,128)(2,1)S(1)}, u32[]{:S(2)}, u32[]{:S(2)}) %collective-permute-start.4) | collective-permute-done | bytes 573472 | tf_op jit(solution)/shard_map/ppermute | solution.py:71
  47.1 0.6 fusion.16
  47.7 0.0 copy-start.7
  47.7 0.8 fusion.2
  48.4 0.0 copy-start.5
  48.5 1.5 %copy-done.5 = f32[2560,256]{1,0:T(8,128)} copy-done((f32[2560,256]{1,0:T(8,128)}, f32[2560,256]{1,0:T(8,128)S(1)}, u32[]{:S(2)}) %copy-start.5) | copy-done | bytes 2621464
  50.0 0.9 slice.44
  50.9 1.9 %collective-permute-start.5 = (bf16[2560,128]{1,0:T(8,128)(2,1)}, bf16[2560,128]{1,0:T(8,128)(2,1)S(1)}, u32[]{:S(2)}, u32[]{:S(2)}) collective-permute-start(bf16[2560,128]{1,0:T(8,128)(2,1)} %slice.44), channel_id=1, source_target_pairs={{0,1},{1,0},{2,3},{3,2},{4,5},{5,4},{6,7},{7,6},{8,9},{9,8},{10,11... | collective-permute-start | bytes 1966088 | tf_op jit(solution)/shard_map/ppermute | solution.py:74
  52.8 0.0 copy-done.7
  53.5 0.1 fusion.4
  53.6 0.6 copy.23
  54.2 2.9 %broadcast_in_dim.6 = f32[40,32,2,2,64]{4,3,2,1,0:T(2,128)} broadcast(f32[40,32,2]{2,1,0:T(8,128)S(1)} %copy.23), dimensions={0,1,3} | broadcast | bytes 1320960 | tf_op jit(solution)/shard_map/broadcast_in_dim | solution.py:101
  57.2 0.0 copy-start
  57.2 0.0 copy-start.1
  57.2 0.0 copy-start.2
  57.2 3.0 %reshape.26.mask = f32[2560,128]{1,0:T(8,128)S(1)} reshape(f32[40,32,2,2,64]{4,3,2,1,0:T(2,128)} %broadcast_in_dim.6) | data formatting | bytes 2621440 | tf_op jit(solution)/shard_map/reshape | solution.py:103
  60.2 0.0 copy-start.3
  60.2 0.0 copy-start.4
  60.2 1.4 %slice.37.grad = f32[2560,128]{1,0:T(8,128)S(1)} slice(f32[2560,256]{1,0:T(8,128)} %copy-done.5), slice={[0:2560], [0:128]} | slice | bytes 2621440 | tf_op jit(solution)/shard_map/slice | solution.py:116
  61.7 0.0 collective-permute-done.5.other
  61.7 0.0 copy-done
  61.7 0.0 copy-done.1
  61.7 0.0 copy-done.2
  61.7 0.0 copy-done.3
  61.7 0.0 copy-done.4
  61.7 4.7 %step.1 = (bf16[2560,128]{1,0:T(8,128)(2,1)S(1)}, f32[2560,128]{1,0:T(8,128)}) custom-call(f32[2560,128]{1,0:T(8,128)S(1)} %slice.37.grad, bf16[2560,128]{1,0:T(8,128)(2,1)S(1)} %collective-permute-done.5.other, f32[2560,128]{1,0:T(8,128)S(1)} %bitcast.37, f32[2560,128]{1,0:T(8,128)S(1)} %reshape.26.mask, bf16[256,256]{1,0:T(8,128)(2,1)S(1)} %copy-done.3, ...), custom_call_target="tpu_custom_call" | custom-call | tf_op jit(solution)/shard_map/step/pallas_call | solution.py:106
  66.5 39.6 %all_to_all.10 = bf16[64,40,128]{2,1,0:T(8,128)(2,1)S(1)} all-to-all(bf16[64,40,128]{2,1,0:T(8,128)(2,1)S(1)} %bitcast.38), channel_id=1, replica_groups=mesh['dp'=64,'tensor'=8] {'dp'}, dimensions={0} | all-to-all | bytes 1310720 | tf_op jit(solution)/shard_map/all_to_all | solution.py:118
  106.1 0.1 reduce_sum.12
  106.2 0.1 broadcast_in_dim.8
  106.3 27.7 %all_to_all.11 = bf16[64,40,128]{2,1,0:T(8,128)(2,1)S(1)} all-to-all(bf16[64,40,128]{2,1,0:T(8,128)(2,1)S(1)} %broadcast_in_dim.8), channel_id=1, replica_groups=mesh['dp'=64,'tensor'=8] {'dp'}, dimensions={0} | all-to-all | bytes 1310720 | tf_op jit(solution)/shard_map/all_to_all | solution.py:122
  134.1 1.7 %inverse.1 = bf16[2560,128]{1,0:T(8,128)(2,1)} custom-call(bf16[2560,128]{1,0:T(8,128)(2,1)S(1)} %bitcast.36, bf16[256,256]{1,0:T(8,128)(2,1)S(1)} %copy-done.1, bf16[256,256]{1,0:T(8,128)(2,1)S(1)} %copy-done.2), custom_call_target="tpu_custom_call" | custom-call | tf_op jit(solution)/shard_map/inverse/pallas_call | solution.py:125
  (6 shorter events, 0.1 us)
Async XLA Ops:
  0.6 27.4 %collective-permute-start.1 = (bf16[208,2560]{1,0:T(8,128)(2,1)}, bf16[208,2560]{1,0:T(8,128)(2,1)S(1)}, u32[]{:S(2)}, u32[]{:S(2)}) collective-permute-start(bf16[208,2560]{1,0:T(8,128)(2,1)} %param.9), channel_id=1, source_target_pairs={{0,2},{1,3},{2,4},{3,5},{4,6},{5,7},{6,0},{7,1},{8,10},{9,11},{10,... | collective-permute-start | bytes 3194888 | tf_op jit(solution)/shard_map/ppermute | solution.py:71
  8.4 23.2 %collective-permute-start.2 = (bf16[208,2560]{1,0:T(8,128)(2,1)}, bf16[208,2560]{1,0:T(8,128)(2,1)S(1)}, u32[]{:S(2)}, u32[]{:S(2)}) collective-permute-start(bf16[208,2560]{1,0:T(8,128)(2,1)} %param.9), channel_id=1, source_target_pairs={{0,6},{1,7},{2,0},{3,1},{4,2},{5,3},{6,4},{7,5},{8,14},{9,15},{10,... | collective-permute-start | bytes 3194888 | tf_op jit(solution)/shard_map/ppermute | solution.py:71
  11.4 3.4 %collective-permute-start = (bf16[4,208,128]{2,1,0:T(8,128)(2,1)S(1)}, bf16[4,208,128]{2,1,0:T(8,128)(2,1)S(1)}, u32[]{:S(2)}, u32[]{:S(2)}) collective-permute-start(bf16[4,208,128]{2,1,0:T(8,128)(2,1)S(1)} %get-tuple-element.6), channel_id=1, source_target_pairs={{0,1},{1,0},{2,3},{3,2},{4,5},{5,4},{6,7},{7,6},{8,9},{9,8},{10,11... | collective-permute-start | bytes 638984 | tf_op jit(solution)/shard_map/ppermute | solution.py:74
  28.0 6.7 %copy-start.6 = (bf16[208,2560]{1,0:T(8,128)(2,1)S(1)}, bf16[208,2560]{1,0:T(8,128)(2,1)}, u32[]{:S(2)}) copy-start(bf16[208,2560]{1,0:T(8,128)(2,1)} %param.9) | copy-start | bytes 3194884
  28.0 14.1 %collective-permute-start.3 = (bf16[96,2560]{1,0:T(8,128)(2,1)S(1)}, bf16[96,2560]{1,0:T(8,128)(2,1)S(1)}, u32[]{:S(2)}, u32[]{:S(2)}) collective-permute-start(bf16[96,2560]{1,0:T(8,128)(2,1)S(1)} %slice.34), channel_id=1, source_target_pairs={{0,2},{1,3},{2,4},{3,5},{4,6},{5,7},{6,0},{7,1},{8,10},{9,11},{10,... | collective-permute-start | bytes 1474568 | tf_op jit(solution)/shard_map/ppermute | solution.py:71
  31.6 15.5 %collective-permute-start.4 = (bf16[112,2560]{1,0:T(8,128)(2,1)S(1)}, bf16[112,2560]{1,0:T(8,128)(2,1)S(1)}, u32[]{:S(2)}, u32[]{:S(2)}) collective-permute-start(bf16[112,2560]{1,0:T(8,128)(2,1)S(1)} %slice.36), channel_id=1, source_target_pairs={{0,6},{1,7},{2,0},{3,1},{4,2},{5,3},{6,4},{7,5},{8,14},{9,15},{10,... | collective-permute-start | bytes 1720328 | tf_op jit(solution)/shard_map/ppermute | solution.py:71
  47.7 5.1 %copy-start.7 = (s32[1,40,2,6]{1,2,3,0:T(2,128)S(1)}, s32[1,40,2,6]{1,2,3,0:T(2,128)}, u32[]{:S(2)}) copy-start(s32[1,40,2,6]{1,2,3,0:T(2,128)} %param.12) | copy-start | bytes 5764
  48.4 1.5 %copy-start.5 = (f32[2560,256]{1,0:T(8,128)}, f32[2560,256]{1,0:T(8,128)S(1)}, u32[]{:S(2)}) copy-start(f32[2560,256]{1,0:T(8,128)S(1)} %fusion.2) | copy-start | bytes 7864324
  50.9 10.8 %collective-permute-start.5 = (bf16[2560,128]{1,0:T(8,128)(2,1)}, bf16[2560,128]{1,0:T(8,128)(2,1)S(1)}, u32[]{:S(2)}, u32[]{:S(2)}) collective-permute-start(bf16[2560,128]{1,0:T(8,128)(2,1)} %slice.44), channel_id=1, source_target_pairs={{0,1},{1,0},{2,3},{3,2},{4,5},{5,4},{6,7},{7,6},{8,9},{9,8},{10,11... | collective-permute-start | bytes 1966088 | tf_op jit(solution)/shard_map/ppermute | solution.py:74
  57.2 4.5 %copy-start = (f32[1,2560,128]{2,1,0:T(8,128)S(1)}, f32[1,2560,128]{2,1,0:T(8,128)}, u32[]{:S(2)}) copy-start(f32[1,2560,128]{2,1,0:T(8,128)} %param.11) | copy-start | bytes 3932164
  57.2 4.5 %copy-start.1 = (bf16[256,256]{1,0:T(8,128)(2,1)S(1)}, bf16[256,256]{1,0:T(8,128)(2,1)}, u32[]{:S(2)}) copy-start(bf16[256,256]{1,0:T(8,128)(2,1)} %constant.82.clone.th) | copy-start | bytes 393220
  57.2 4.5 %copy-start.2 = (bf16[256,256]{1,0:T(8,128)(2,1)S(1)}, bf16[256,256]{1,0:T(8,128)(2,1)}, u32[]{:S(2)}) copy-start(bf16[256,256]{1,0:T(8,128)(2,1)} %constant.83.clone.tl) | copy-start | bytes 393220
  60.2 1.5 %copy-start.3 = (bf16[256,256]{1,0:T(8,128)(2,1)S(1)}, bf16[256,256]{1,0:T(8,128)(2,1)}, u32[]{:S(2)}) copy-start(bf16[256,256]{1,0:T(8,128)(2,1)} %constant.84.clone.ch) | copy-start | bytes 393220
  60.2 1.5 %copy-start.4 = (bf16[256,256]{1,0:T(8,128)(2,1)S(1)}, bf16[256,256]{1,0:T(8,128)(2,1)}, u32[]{:S(2)}) copy-start(bf16[256,256]{1,0:T(8,128)(2,1)} %constant.85.clone.cl) | copy-start | bytes 393220
where the time goes:
time: 136 us
  blocking collectives  67.4 us (50%)
  waiting for transfers between devices  25.6 us (19%)
  starting transfers between devices  19.5 us (14%)
  local copies, waits for them, and re-layouts  11.7 us (9%)
  Pallas kernels  6.41 us (5%)
  matrix products  3.21 us (2%)
  between operations  1.65 us (1%)
    all_to_all x1, blocking collectives, shards(): lax.all_to_all(sent.reshape(replicas, features // replicas, cols), 'dp',...  39.6 us
    all_to_all x1, blocking collectives, shards(): lax.all_to_all(jnp.broadcast_to(mine[None], (replicas,) + mine.shape), 'd...  27.7 us
    ppermute x4, waiting for transfers between devices, along(): lax.ppermute(x, 'tensor', [(i, (i + 2 * step) % group) for i in range(gro...  24.3 us
    ppermute x4, starting transfers between devices, along(): lax.ppermute(x, 'tensor', [(i, (i + 2 * step) % group) for i in range(gro...  15.7 us
    pallas_call x1, Pallas kernels, shards(): pl.pallas_call(step_kernel, out_shape=(jax.ShapeDtypeStruct((features, co...  4.75 us
    ppermute x2, starting transfers between devices, swap(): return lax.ppermute(x, 'tensor', [(i, i ^ 1) for i in range(group)])  3.83 us
    dot_general x5, matrix products, gram(): lax.dot_general(a, k, (((0,), (0,)), ((), ())), preferred_element_type=jn...  3.21 us
    reshape x1, local copies, waits for them, and re-layouts, shards(): mask = jnp.broadcast_to(chosen[:, :, None, :, None], (features // 64, BLK...  2.98 us
  transfers between devices with their start and end apart: 6, of which 4 were waited for; matrix products, arithmetic and copies ran while one was open for 8% of the time, Pallas kernels for 0%

commit v1 on v0

v1 whole, which is shorter than its diff:
```python
import functools

import jax
import jax.numpy as jnp
import ml_dtypes
import numpy as np
from jax import lax
from jax.experimental import pallas as pl
from jax.experimental.pallas import tpu as pltpu
from jax.sharding import PartitionSpec as P

BLK = 32
SPAN = 64
WIDE = 4


def cosine_parts():
    n = np.arange(SPAN, dtype=np.float64)
    table = np.cos(np.pi * (2.0 * n[None, :] + 1.0) * n[:, None] / 128.0) * np.sqrt(2.0 / SPAN)
    table[0] *= np.sqrt(0.5)
    high = table.astype(ml_dtypes.bfloat16)
    low = (table - high.astype(np.float64)).astype(ml_dtypes.bfloat16)
    return high, low


def split(x):
    high = x.astype(jnp.bfloat16)
    return high, (x - high.astype(jnp.float32)).astype(jnp.bfloat16)


def spans_of(ref, i, count):
    first = i * count * SPAN
    return [ref[first + s * SPAN : first + (s + 1) * SPAN, :] for s in range(count)]


def beside(parts):
    return jnp.concatenate(parts, axis=1)


def product(table, parts):
    return jnp.dot(table[...], jnp.concatenate(parts, axis=0), preferred_element_type=jnp.float32)


def put(ref, i, count, value):
    cols = ref.shape[1]
    for s in range(count):
        first = (i * count + s) * SPAN
        ref[first : first + SPAN, :] = value[:, s * cols : (s + 1) * cols].astype(ref.dtype)


def spectrum_kernel(grad, other, momentum, mask, forward, advanced, sent, rows):
    for i in range(grad.shape[0] // (SPAN * WIDE)):
        x = beside(
            [
                0.999 * m + g + o.astype(jnp.float32)
                for m, g, o in zip(
                    spans_of(momentum, i, WIDE),
                    spans_of(grad, i, WIDE),
                    spans_of(other, i, WIDE),
                )
            ]
        )
        high, low = split(x)
        s = product(forward, [high, low, high]) * beside(spans_of(mask, i, WIDE))
        put(sent, i, WIDE, s)
        put(advanced, i, WIDE, x)
        put(rows, i, WIDE, s)


def kept_kernel(advanced, rows, backward, kept):
    for i in range(kept.shape[0] // (SPAN * WIDE)):
        high, low = split(beside(spans_of(rows, i, WIDE)))
        x = beside(spans_of(advanced, i, WIDE))
        put(kept, i, WIDE, x - product(backward, [high, low, high]))


def total_kernel(pieces, totals):
    total = pieces[0].astype(jnp.float32)
    for r in range(1, pieces.shape[0]):
        total = total + pieces[r].astype(jnp.float32)
    total = total.astype(totals.dtype)
    for r in range(totals.shape[0]):
        totals[r] = total


def inverse_kernel(summed, backward, update):
    for i in range(update.shape[0] // (SPAN * WIDE)):
        s = beside(spans_of(summed, i, WIDE))
        put(update, i, WIDE, product(backward, [s, s]))


def gram(a, k):
    return lax.dot_general(a, k, (((0,), (0,)), ((), ())), preferred_element_type=jnp.float32)


def call(kernel, name, out_shape, *args):
    vmem = pl.BlockSpec(memory_space=pltpu.VMEM)
    outs = out_shape if isinstance(out_shape, tuple) else (out_shape,)
    moved = sum(x.size * x.dtype.itemsize for x in args + outs)
    return pl.pallas_call(
        kernel,
        out_shape=out_shape,
        in_specs=[vmem] * len(args),
        out_specs=jax.tree.map(lambda _: vmem, out_shape),
        compiler_params=pltpu.CompilerParams(vmem_limit_bytes=40 << 20),
        cost_estimate=pl.CostEstimate(
            flops=6 * 2 * SPAN * outs[0].size, bytes_accessed=moved, transcendentals=0
        ),
        name=name,
    )(*args)


def shards(activations, key_grad, momentum, block_ids, counts, *, replicas, group):
    tokens, features = activations.shape
    cols = key_grad.shape[1]
    chips = group // 2
    spot = lax.axis_index("tensor")
    chip, core = lax.shift_right_logical(spot, 1), lax.bitwise_and(spot, 1)

    def along(x, step):
        return lax.ppermute(x, "tensor", [(i, (i + 2 * step) % group) for i in range(group)])

    def swap(x):
        return lax.ppermute(x, "tensor", [(i, i ^ 1) for i in range(group)])

    cut = tokens // 2 // 16 * 16
    head, tail = activations[:cut], activations[cut:]
    left_head, right_tail = along(head, 1), along(tail, -1)

    by_core = key_grad.reshape(chips, 2, tokens, cols)
    own_keys = lax.dynamic_index_in_dim(by_core, core, 1, keepdims=False)
    their_keys = swap(lax.dynamic_index_in_dim(by_core, 1 - core, 1, keepdims=False))

    head, tail, their_keys = lax.optimization_barrier((head, tail, their_keys))
    left_tail, right_head = along(tail, 1), along(head, -1)
    far_head, far_tail = along(left_head, 1), along(right_tail, -1)

    def block(keys, step):
        return lax.dynamic_index_in_dim(
            keys, lax.bitwise_and(chip + step, chips - 1), 0, keepdims=False
        )

    def near(keys):
        total = gram(activations, block(keys, 0))
        before, after = block(keys, chips - 1), block(keys, 1)
        return (
            total
            + gram(left_head, before[:cut])
            + gram(right_tail, after[cut:])
            + gram(left_tail, before[cut:])
            + gram(right_head, after[:cut])
        )

    def whole(total, keys):
        far = block(keys, 2)
        return total + gram(far_head, far[:cut]) + gram(far_tail, far[cut:])

    active = jnp.arange(block_ids.shape[3], dtype=jnp.int32) < counts[0]
    hit = (block_ids[0][..., None] == jnp.arange(BLK, dtype=jnp.int32)) & active[:, None]
    chosen = jnp.transpose(jnp.any(hit, axis=2), (0, 2, 1)).astype(jnp.float32)
    mask = jnp.broadcast_to(
        chosen[:, :, None, :, None], (features // SPAN, BLK, 2, cols // SPAN, SPAN)
    ).reshape(features, cols)

    their_near, own_near = near(their_keys), near(own_keys)
    their_near, own_near, mask, far_head, far_tail = lax.optimization_barrier(
        (their_near, own_near, mask, far_head, far_tail)
    )
    other = swap(whole(their_near, their_keys).astype(jnp.bfloat16))
    grad = whole(own_near, own_keys)

    high, low = cosine_parts()
    forward = jnp.asarray(np.concatenate([high, high, low], axis=1))
    backward = jnp.asarray(np.concatenate([high.T, high.T, low.T], axis=1))
    backward_once = jnp.asarray(np.concatenate([high.T, low.T], axis=1))

    flat = jax.ShapeDtypeStruct((features, cols), jnp.float32)
    flat_half = jax.ShapeDtypeStruct((features, cols), jnp.bfloat16)
    advanced, sent, rows = call(
        spectrum_kernel,
        "spectrum",
        (flat, flat_half, flat),
        grad,
        other,
        momentum[0],
        mask,
        forward,
    )
    pieces = lax.all_to_all(
        sent.reshape(replicas, features // replicas, cols), "dp", 0, 0, tiled=True
    )
    kept = call(kept_kernel, "kept", flat, advanced, rows, backward)
    totals = call(
        total_kernel, "total", jax.ShapeDtypeStruct(pieces.shape, jnp.bfloat16), pieces
    )
    summed = lax.all_to_all(totals, "dp", 0, 0, tiled=True).reshape(features, cols)
    update = call(inverse_kernel, "inverse", flat_half, summed, backward_once)
    return kept[None], update


def solution(mesh):
    in_specs = (
        P(("dp", "tensor"), None),
        P("dp", "tensor"),
        P("dp", None, "tensor"),
        P("dp", None, "tensor", None),
        P("dp"),
    )
    out_specs = (P("dp", None, "tensor"), P(None, "tensor"))
    body = functools.partial(shards, replicas=mesh.shape["dp"], group=mesh.shape["tensor"])
    return jax.shard_map(body, mesh=mesh, in_specs=in_specs, out_specs=out_specs, check_vma=False)
```

time: 136 us -> 132 us (0.971)
  blocking collectives: 67.4 us -> 32.6 us
  starting transfers between devices: 19.5 us -> 34 us
  matrix products: 3.21 us -> 15.5 us
  waiting for transfers between devices: 25.6 us -> 28.8 us
  local copies, waits for them, and re-layouts: 11.7 us -> 14.4 us
  Pallas kernels: 6.41 us -> 4.29 us
    all_to_all x1 -> x0, blocking collectives: 27.7 us -> none  [shards(): lax.all_to_all(jnp.broadcast_to(mine[None], (replicas,) + mine.shape), 'd...]
    all_to_all x0 -> x1, waiting for transfers between devices: none -> 18.6 us  [shards(): lax.all_to_all(totals, 'dp', 0, 0, tiled=True).reshape(features, cols)]
    ppermute x4 -> x6, waiting for transfers between devices: 24.3 us -> 9.85 us  [along(): lax.ppermute(x, 'tensor', [(i, (i + 2 * step) % group) for i in range(gro...]
    dot_general x5 -> x14, matrix products: 3.21 us -> 15.5 us  [gram(): lax.dot_general(a, k, (((0,), (0,)), ((), ())), preferred_element_type=jn...]
    ppermute x4 -> x6, starting transfers between devices: 15.7 us -> 23.8 us  [along(): lax.ppermute(x, 'tensor', [(i, (i + 2 * step) % group) for i in range(gro...]
    all_to_all x1, blocking collectives: 39.6 us -> 32.6 us  [shards(): lax.all_to_all(sent.reshape(replicas, features // replicas, cols), 'dp',...]
    all_to_all x0 -> x1, starting transfers between devices: none -> 6.41 us  [shards(): lax.all_to_all(totals, 'dp', 0, 0, tiled=True).reshape(features, cols)]
    unnamed x16 -> x26, local copies, waits for them, and re-layouts: 1.55 us -> 4.34 us
  transfers between devices with their start and end apart: 6 -> 9, of which waited for: 4 -> 5; matrix products, arithmetic and copies ran while one was open for 8% -> 16% of each run, Pallas kernels for 0% -> 1%
where the time goes in v1:
time: 132 us; the launch traced here: 131 us
  starting transfers between devices  34 us (26%)
  blocking collectives  32.6 us (25%)
  waiting for transfers between devices  28.8 us (22%)
  matrix products  15.5 us (12%)
  local copies, waits for them, and re-layouts  14.4 us (11%)
  Pallas kernels  4.29 us (3%)
  between operations  1.66 us (1%)
    all_to_all x1, blocking collectives, shards(): lax.all_to_all(sent.reshape(replicas, features // replicas, cols), 'dp',...  32.6 us
    ppermute x6, starting transfers between devices, along(): lax.ppermute(x, 'tensor', [(i, (i + 2 * step) % group) for i in range(gro...  23.8 us
    all_to_all x1, waiting for transfers between devices, shards(): lax.all_to_all(totals, 'dp', 0, 0, tiled=True).reshape(features, cols)  18.6 us
    dot_general x14, matrix products, gram(): lax.dot_general(a, k, (((0,), (0,)), ((), ())), preferred_element_type=jn...  15.5 us
    ppermute x6, waiting for transfers between devices, along(): lax.ppermute(x, 'tensor', [(i, (i + 2 * step) % group) for i in range(gro...  9.85 us
    all_to_all x1, starting transfers between devices, shards(): lax.all_to_all(totals, 'dp', 0, 0, tiled=True).reshape(features, cols)  6.41 us
    unnamed x26, local copies, waits for them, and re-layouts  4.34 us
    pallas_call x4, Pallas kernels, call(): pl.pallas_call(kernel, out_shape=out_shape, in_specs=[vmem] * len(args),...  4.29 us
  transfers between devices with their start and end apart: 9, of which 5 were waited for; matrix products, arithmetic and copies ran while one was open for 16% of the time, Pallas kernels for 1%

profile of v1, /device:TPU:6, one launch (start us, length us, event | category | flops | bytes accessed | tf_op | source)
XLA Modules:
  0.0 131.3 jit_solution(10912252667052946373)
XLA Ops:
  0.6 0.0 copy-start
  0.7 1.9 %slice.78 = bf16[96,2560]{1,0:T(8,128)(2,1)} slice(bf16[208,2560]{1,0:T(8,128)(2,1)} %param.8), slice={[0:96], [0:2560]} | slice | bytes 983040 | tf_op jit(solution)/shard_map/slice | solution.py:127
  2.6 7.7 %collective-permute-start.1 = (bf16[96,2560]{1,0:T(8,128)(2,1)}, bf16[96,2560]{1,0:T(8,128)(2,1)}, u32[]{:S(2)}, u32[]{:S(2)}) collective-permute-start(bf16[96,2560]{1,0:T(8,128)(2,1)} %slice.78), channel_id=1, source_target_pairs={{0,2},{1,3},{2,4},{3,5},{4,6},{5,7},{6,0},{7,1},{8,10},{9,11},{10,... | collective-permute-start | bytes 1474568 | tf_op jit(solution)/shard_map/ppermute | solution.py:121
  10.4 0.7 dynamic-slice_bitcast_fusion
  11.1 1.9 %collective-permute-start = (bf16[4,208,128]{2,1,0:T(8,128)(2,1)}, bf16[4,208,128]{2,1,0:T(8,128)(2,1)}, u32[]{:S(2)}, u32[]{:S(2)}) collective-permute-start(bf16[4,208,128]{2,1,0:T(8,128)(2,1)} %dynamic-slice_bitcast_fusion), channel_id=1, source_target_pairs={{0,1},{1,0},{2,3},{3,2},{4,5},{5,4},{6,7},{7,6},{8,9},{9,8},{10,11... | collective-permute-start | bytes 638984 | tf_op jit(solution)/shard_map/ppermute | solution.py:124
  13.0 0.8 slice.79
  13.9 1.9 %collective-permute-start.2 = (bf16[112,2560]{1,0:T(8,128)(2,1)}, bf16[112,2560]{1,0:T(8,128)(2,1)S(1)}, u32[]{:S(2)}, u32[]{:S(2)}) collective-permute-start(bf16[112,2560]{1,0:T(8,128)(2,1)} %slice.79), channel_id=1, source_target_pairs={{0,6},{1,7},{2,0},{3,1},{4,2},{5,3},{6,4},{7,5},{8,14},{9,15},{10,... | collective-permute-start | bytes 1720328 | tf_op jit(solution)/shard_map/ppermute | solution.py:121
  16.5 0.1 fusion.7
  16.6 0.6 copy.24
  17.3 3.0 %broadcast_in_dim.4 = f32[40,32,2,2,64]{4,3,2,1,0:T(2,128)} broadcast(f32[40,32,2]{2,1,0:T(8,128)S(1)} %copy.24), dimensions={0,1,3} | broadcast | bytes 1320960 | tf_op jit(solution)/shard_map/broadcast_in_dim | solution.py:161
  20.3 2.9 %reshape.43.mask = f32[2560,128]{1,0:T(8,128)S(1)} reshape(f32[40,32,2,2,64]{4,3,2,1,0:T(2,128)} %broadcast_in_dim.4) | data formatting | bytes 2621440 | tf_op jit(solution)/shard_map/reshape | solution.py:163
  23.2 0.7 fusion.8
  23.8 5.1 %collective-permute-start.3 = (bf16[112,2560]{1,0:T(8,128)(2,1)}, bf16[112,2560]{1,0:T(8,128)(2,1)S(1)}, u32[]{:S(2)}, u32[]{:S(2)}) collective-permute-start(bf16[112,2560]{1,0:T(8,128)(2,1)} %slice.79), channel_id=1, source_target_pairs={{0,2},{1,3},{2,4},{3,5},{4,6},{5,7},{6,0},{7,1},{8,10},{9,11},{10,... | collective-permute-start | bytes 1720328 | tf_op jit(solution)/shard_map/ppermute | solution.py:121
  29.0 1.9 %collective-permute-start.4 = (bf16[96,2560]{1,0:T(8,128)(2,1)}, bf16[96,2560]{1,0:T(8,128)(2,1)S(1)}, u32[]{:S(2)}, u32[]{:S(2)}) collective-permute-start(bf16[96,2560]{1,0:T(8,128)(2,1)} %slice.78), channel_id=1, source_target_pairs={{0,6},{1,7},{2,0},{3,1},{4,2},{5,3},{6,4},{7,5},{8,14},{9,15},{10,... | collective-permute-start | bytes 1474568 | tf_op jit(solution)/shard_map/ppermute | solution.py:121
  30.9 1.5 %fusion.10 = f32[128,2560]{0,1:T(8,128)S(1)} fusion(bf16[208,2560]{1,0:T(8,128)(2,1)S(1)} %copy-done.9, bf16[4,208,128]{2,1,0:T(8,128)(2,1)} %collective-permute-done, s32[]{:T(128)S(6)} %select_n.35), kind=kOutput, calls=%fused_computation.18 | convolution fusion | flops 136314880 | bytes 2428932 | tf_op jit(solution)/shard_map/dot_general | solution.py:93
  32.4 5.1 %collective-permute-start.5 = (bf16[96,2560]{1,0:T(8,128)(2,1)}, bf16[96,2560]{1,0:T(8,128)(2,1)S(1)}, u32[]{:S(2)}, u32[]{:S(2)}) collective-permute-start(bf16[96,2560]{1,0:T(8,128)(2,1)} %collective-permute-done.1), channel_id=1, source_target_pairs={{0,2},{1,3},{2,4},{3,5},{4,6},{5,7},{6,0},{7,1},{8,10},{9,11},{10,... | collective-permute-start | bytes 1474568 | tf_op jit(solution)/shard_map/ppermute | solution.py:121
  37.5 1.5 %convolution_add_fusion.3 = f32[128,2560]{0,1:T(8,128)S(1)} fusion(f32[128,2560]{0,1:T(8,128)S(1)} %fusion.10, bf16[96,2560]{1,0:T(8,128)(2,1)} %collective-permute-done.1, bf16[4,208,128]{2,1,0:T(8,128)(2,1)} %collective-permute-done, s32[]{:T(128)S(6)} %select_n.36), kind=kOutput, calls=%fused_computation.3 | convolution fusion | flops 63242240 | bytes 3137540 | tf_op jit(solution)/shard_map/dot_general | solution.py:93
  39.0 1.4 %convolution_add_fusion.1 = f32[128,2560]{0,1:T(8,128)S(1)} fusion(f32[128,2560]{0,1:T(8,128)S(1)} %fusion.8, bf16[96,2560]{1,0:T(8,128)(2,1)} %collective-permute-done.1, bf16[4,2,208,128]{3,2,1,0:T(8,128)(2,1)S(1)} %bitcast.89, s32[]{:T(128)S(6)} %select_n.41, s32[]{:T(128)S(6)} %select_n.40), kind=kOutput, calls=%fused_computation.1 | convolution fusion | flops 63242240 | bytes 3137544 | tf_op jit(solution)/shard_map/dot_general | solution.py:93
  40.4 1.9 %collective-permute-start.6 = (bf16[112,2560]{1,0:T(8,128)(2,1)S(1)}, bf16[112,2560]{1,0:T(8,128)(2,1)S(1)}, u32[]{:S(2)}, u32[]{:S(2)}) collective-permute-start(bf16[112,2560]{1,0:T(8,128)(2,1)S(1)} %collective-permute-done.2), channel_id=1, source_target_pairs={{0,6},{1,7},{2,0},{3,1},{4,2},{5,3},{6,4},{7,5},{8,14},{9,15},{10,... | collective-permute-start | bytes 1720328 | tf_op jit(solution)/shard_map/ppermute | solution.py:121
  42.4 3.0 %collective-permute-done.4 = bf16[96,2560]{1,0:T(8,128)(2,1)S(1)} collective-permute-done((bf16[96,2560]{1,0:T(8,128)(2,1)}, bf16[96,2560]{1,0:T(8,128)(2,1)S(1)}, u32[]{:S(2)}, u32[]{:S(2)}) %collective-permute-start.4) | collective-permute-done | bytes 491552 | tf_op jit(solution)/shard_map/ppermute | solution.py:121
  45.3 1.1 fusion.21
  46.4 0.4 fusion.20
  46.8 0.4 fusion.16
  47.2 1.5 %fusion.5 = f32[2560,128]{1,0:T(8,128)} fusion(f32[2560,128]{1,0:T(8,128)S(1)} %fusion.20, f32[2560,128]{1,0:T(8,128)S(1)} %fusion.16, f32[128,2560]{0,1:T(8,128)S(1)} %convolution_add_fusion.1, bf16[112,2560]{1,0:T(8,128)(2,1)S(1)} %collective-permute-done.2, bf16[4,2,208,128]{3,2,1,0:T(8,128)(2,1)S(1)} %bitcast.90, s32[]{:T(128)S(6)} %select_n.42, ...), kind=kOutput, calls=%fused_computation.9 | convolution fusion | flops 74383360 | bytes 5845004 | tf_op jit(solution)/shard_map/dot_general | solution.py:93
  48.6 1.1 fusion.17
  49.8 1.1 fusion.2
  50.9 1.5 %collective-permute-done.5 = bf16[96,2560]{1,0:T(8,128)(2,1)S(1)} collective-permute-done((bf16[96,2560]{1,0:T(8,128)(2,1)}, bf16[96,2560]{1,0:T(8,128)(2,1)S(1)}, u32[]{:S(2)}, u32[]{:S(2)}) %collective-permute-start.5) | collective-permute-done | bytes 491552 | tf_op jit(solution)/shard_map/ppermute | solution.py:121
  52.4 5.4 %collective-permute-done.6 = bf16[112,2560]{1,0:T(8,128)(2,1)S(1)} collective-permute-done((bf16[112,2560]{1,0:T(8,128)(2,1)S(1)}, bf16[112,2560]{1,0:T(8,128)(2,1)S(1)}, u32[]{:S(2)}, u32[]{:S(2)}) %collective-permute-start.6) | collective-permute-done | bytes 573472 | tf_op jit(solution)/shard_map/ppermute | solution.py:121
  57.8 1.1 fusion.18
  58.9 2.0 %add_convert_fusion = bf16[2560,128]{1,0:T(8,128)(2,1)} fusion(f32[2560,128]{1,0:T(8,128)S(1)} %fusion.2, f32[2560,128]{1,0:T(8,128)S(1)} %fusion.18, bf16[112,2560]{1,0:T(8,128)(2,1)S(1)} %collective-permute-done.6, bf16[4,208,128]{2,1,0:T(8,128)(2,1)} %collective-permute-done, s32[]{:T(128)S(6)} %select_n.43, s32[]{:T(128)S(6)} %add.120), kind=kOutput, calls=%fused_computation.10 | convolution fusion | flops 74383360 | bytes 3878920 | tf_op jit(solution)/shard_map/dot_general | solution.py:93
  60.9 1.9 %collective-permute-start.7 = (bf16[2560,128]{1,0:T(8,128)(2,1)}, bf16[2560,128]{1,0:T(8,128)(2,1)S(1)}, u32[]{:S(2)}, u32[]{:S(2)}) collective-permute-start(bf16[2560,128]{1,0:T(8,128)(2,1)} %add_convert_fusion), channel_id=1, source_target_pairs={{0,1},{1,0},{2,3},{3,2},{4,5},{5,4},{6,7},{7,6},{8,9},{9,8},{10,11... | collective-permute-start | bytes 1966088 | tf_op jit(solution)/shard_map/ppermute | solution.py:124
  62.8 0.0 copy-start.10
  62.8 1.5 %fusion.19 = f32[2560,128]{1,0:T(8,128)S(1)} fusion(bf16[96,2560]{1,0:T(8,128)(2,1)} %copy-done.11, bf16[4,2,208,128]{3,2,1,0:T(8,128)(2,1)S(1)} %bitcast.91, s32[]{:T(128)S(6)} %select_n.44, s32[]{:T(128)S(6)} %select_n.40), kind=kOutput, calls=%fused_computation.36 | convolution fusion | flops 62914560 | bytes 1826824 | tf_op jit(solution)/shard_map/dot_general | solution.py:93
  64.3 0.0 copy-start.3
  64.3 0.0 copy-start.7
  64.3 0.4 add_add_fusion.grad
  64.7 0.3 collective-permute-done.7.other
  65.1 0.8 copy-done.4
  65.9 1.1 copy-done.5
  67.0 0.6 spectrum.1
  67.6 1.1 copy-done.1
  68.7 32.6 %all_to_all.10.pieces = bf16[64,40,128]{2,1,0:T(8,128)(2,1)S(1)} all-to-all(bf16[64,40,128]{2,1,0:T(8,128)(2,1)S(1)} %bitcast.94), channel_id=1, replica_groups=mesh['dp'=64,'tensor'=8] {'dp'}, dimensions={0} | all-to-all | bytes 1310720 | tf_op jit(solution)/shard_map/all_to_all | solution.py:189
  101.3 1.0 total.1
  102.3 6.4 %all-to-all-start.1 = ((bf16[64,40,128]{2,1,0:T(8,128)(2,1)}), bf16[64,40,128]{2,1,0:T(8,128)(2,1)S(1)}, u32[]{:S(2)}, u32[]{:S(2)}) async-start(bf16[64,40,128]{2,1,0:T(8,128)(2,1)} %total.1), calls=%async_computation.1 | async-start | bytes 1310720 | tf_op jit(solution)/shard_map/all_to_all | solution.py:196
  108.7 1.3 copy-done.2
  110.0 1.5 %kept.1 = f32[2560,128]{1,0:T(8,128)} custom-call(f32[2560,128]{1,0:T(8,128)S(1)} %get-tuple-element.21.advanced, f32[2560,128]{1,0:T(8,128)S(1)} %copy-done.2, bf16[64,192]{1,0:T(8,128)(2,1)S(1)} %copy-done.6), custom_call_target="tpu_custom_call" | custom-call | flops 251658240 | bytes 3956736 | tf_op jit(solution)/shard_map/kept/pallas_call | solution.py:100
  111.6 18.6 %all-to-all-done.1 = bf16[64,40,128]{2,1,0:T(8,128)(2,1)S(1)} async-done(((bf16[64,40,128]{2,1,0:T(8,128)(2,1)}), bf16[64,40,128]{2,1,0:T(8,128)(2,1)S(1)}, u32[]{:S(2)}, u32[]{:S(2)}) %all-to-all-start.1) | async-done | bytes 655392 | tf_op jit(solution)/shard_map/all_to_all | solution.py:196
  130.1 1.2 inverse.1
  (25 shorter events, 0.1 us)
Async XLA Ops:
  0.6 9.8 %copy-start = (bf16[1664,128]{1,0:T(8,128)(2,1)S(1)}, bf16[1664,128]{1,0:T(8,128)(2,1)}, u32[]{:S(2)}) copy-start(bf16[1664,128]{1,0:T(8,128)(2,1)} %param.9) | copy-start | bytes 1277956
  0.6 12.4 %copy-start.9 = (bf16[208,2560]{1,0:T(8,128)(2,1)S(1)}, bf16[208,2560]{1,0:T(8,128)(2,1)}, u32[]{:S(2)}) copy-start(bf16[208,2560]{1,0:T(8,128)(2,1)} %param.8) | copy-start | bytes 3194884
  0.7 15.2 %copy-start.12 = (s32[1,40,2,6]{1,2,3,0:T(2,128)S(1)}, s32[1,40,2,6]{1,2,3,0:T(2,128)}, u32[]{:S(2)}) copy-start(s32[1,40,2,6]{1,2,3,0:T(2,128)} %param.11) | copy-start | bytes 5764
  2.6 29.7 %collective-permute-start.1 = (bf16[96,2560]{1,0:T(8,128)(2,1)}, bf16[96,2560]{1,0:T(8,128)(2,1)}, u32[]{:S(2)}, u32[]{:S(2)}) collective-permute-start(bf16[96,2560]{1,0:T(8,128)(2,1)} %slice.78), channel_id=1, source_target_pairs={{0,2},{1,3},{2,4},{3,5},{4,6},{5,7},{6,0},{7,1},{8,10},{9,11},{10,... | collective-permute-start | bytes 1474568 | tf_op jit(solution)/shard_map/ppermute | solution.py:121
  11.1 12.7 %collective-permute-start = (bf16[4,208,128]{2,1,0:T(8,128)(2,1)}, bf16[4,208,128]{2,1,0:T(8,128)(2,1)}, u32[]{:S(2)}, u32[]{:S(2)}) collective-permute-start(bf16[4,208,128]{2,1,0:T(8,128)(2,1)} %dynamic-slice_bitcast_fusion), channel_id=1, source_target_pairs={{0,1},{1,0},{2,3},{3,2},{4,5},{5,4},{6,7},{7,6},{8,9},{9,8},{10,11... | collective-permute-start | bytes 638984 | tf_op jit(solution)/shard_map/ppermute | solution.py:124
  13.9 26.6 %collective-permute-start.2 = (bf16[112,2560]{1,0:T(8,128)(2,1)}, bf16[112,2560]{1,0:T(8,128)(2,1)S(1)}, u32[]{:S(2)}, u32[]{:S(2)}) collective-permute-start(bf16[112,2560]{1,0:T(8,128)(2,1)} %slice.79), channel_id=1, source_target_pairs={{0,6},{1,7},{2,0},{3,1},{4,2},{5,3},{6,4},{7,5},{8,14},{9,15},{10,... | collective-permute-start | bytes 1720328 | tf_op jit(solution)/shard_map/ppermute | solution.py:121
  23.8 23.0 %collective-permute-start.3 = (bf16[112,2560]{1,0:T(8,128)(2,1)}, bf16[112,2560]{1,0:T(8,128)(2,1)S(1)}, u32[]{:S(2)}, u32[]{:S(2)}) collective-permute-start(bf16[112,2560]{1,0:T(8,128)(2,1)} %slice.79), channel_id=1, source_target_pairs={{0,2},{1,3},{2,4},{3,5},{4,6},{5,7},{6,0},{7,1},{8,10},{9,11},{10,... | collective-permute-start | bytes 1720328 | tf_op jit(solution)/shard_map/ppermute | solution.py:121
  29.0 16.4 %collective-permute-start.4 = (bf16[96,2560]{1,0:T(8,128)(2,1)}, bf16[96,2560]{1,0:T(8,128)(2,1)S(1)}, u32[]{:S(2)}, u32[]{:S(2)}) collective-permute-start(bf16[96,2560]{1,0:T(8,128)(2,1)} %slice.78), channel_id=1, source_target_pairs={{0,6},{1,7},{2,0},{3,1},{4,2},{5,3},{6,4},{7,5},{8,14},{9,15},{10,... | collective-permute-start | bytes 1474568 | tf_op jit(solution)/shard_map/ppermute | solution.py:121
  32.4 20.0 %collective-permute-start.5 = (bf16[96,2560]{1,0:T(8,128)(2,1)}, bf16[96,2560]{1,0:T(8,128)(2,1)S(1)}, u32[]{:S(2)}, u32[]{:S(2)}) collective-permute-start(bf16[96,2560]{1,0:T(8,128)(2,1)} %collective-permute-done.1), channel_id=1, source_target_pairs={{0,2},{1,3},{2,4},{3,5},{4,6},{5,7},{6,0},{7,1},{8,10},{9,11},{10,... | collective-permute-start | bytes 1474568 | tf_op jit(solution)/shard_map/ppermute | solution.py:121
  40.4 17.4 %collective-permute-start.6 = (bf16[112,2560]{1,0:T(8,128)(2,1)S(1)}, bf16[112,2560]{1,0:T(8,128)(2,1)S(1)}, u32[]{:S(2)}, u32[]{:S(2)}) collective-permute-start(bf16[112,2560]{1,0:T(8,128)(2,1)S(1)} %collective-permute-done.2), channel_id=1, source_target_pairs={{0,6},{1,7},{2,0},{3,1},{4,2},{5,3},{6,4},{7,5},{8,14},{9,15},{10,... | collective-permute-start | bytes 1720328 | tf_op jit(solution)/shard_map/ppermute | solution.py:121
  52.4 6.5 %copy-start.11 = (bf16[96,2560]{1,0:T(8,128)(2,1)}, bf16[96,2560]{1,0:T(8,128)(2,1)S(1)}, u32[]{:S(2)}) copy-start(bf16[96,2560]{1,0:T(8,128)(2,1)S(1)} %collective-permute-done.5) | copy-start | bytes 1474564
  60.9 4.2 %collective-permute-start.7 = (bf16[2560,128]{1,0:T(8,128)(2,1)}, bf16[2560,128]{1,0:T(8,128)(2,1)S(1)}, u32[]{:S(2)}, u32[]{:S(2)}) collective-permute-start(bf16[2560,128]{1,0:T(8,128)(2,1)} %add_convert_fusion), channel_id=1, source_target_pairs={{0,1},{1,0},{2,3},{3,2},{4,5},{5,4},{6,7},{7,6},{8,9},{9,8},{10,11... | collective-permute-start | bytes 1966088 | tf_op jit(solution)/shard_map/ppermute | solution.py:124
  62.8 1.5 %copy-start.10 = (f32[2560,128]{1,0:T(8,128)S(1)}, f32[2560,128]{1,0:T(8,128)}, u32[]{:S(2)}) copy-start(f32[2560,128]{1,0:T(8,128)} %fusion.5) | copy-start | bytes 3932164
  64.3 1.6 %copy-start.3 = (f32[1,2560,128]{2,1,0:T(8,128)S(1)}, f32[1,2560,128]{2,1,0:T(8,128)}, u32[]{:S(2)}) copy-start(f32[1,2560,128]{2,1,0:T(8,128)} %param.10) | copy-start | bytes 3932164
  64.3 1.6 %copy-start.7 = (bf16[64,192]{1,0:T(8,128)(2,1)S(1)}, bf16[64,192]{1,0:T(8,128)(2,1)}, u32[]{:S(2)}) copy-start(bf16[64,192]{1,0:T(8,128)(2,1)} %constant.125.clone.forward) | copy-start | bytes 73732
  65.1 0.8 copy-start.4
  65.9 1.1 copy-start.5
  67.6 1.1 copy-start.1
  101.3 7.4 %copy-start.6 = (bf16[64,192]{1,0:T(8,128)(2,1)S(1)}, bf16[64,192]{1,0:T(8,128)(2,1)}, u32[]{:S(2)}) copy-start(bf16[64,192]{1,0:T(8,128)(2,1)} %constant.126.clone.backward) | copy-start | bytes 73732
  102.3 27.8 %all-to-all-start.1 = ((bf16[64,40,128]{2,1,0:T(8,128)(2,1)}), bf16[64,40,128]{2,1,0:T(8,128)(2,1)S(1)}, u32[]{:S(2)}, u32[]{:S(2)}) async-start(bf16[64,40,128]{2,1,0:T(8,128)(2,1)} %total.1), calls=%async_computation.1 | async-start | bytes 1310720 | tf_op jit(solution)/shard_map/all_to_all | solution.py:196
  108.7 1.3 %copy-start.2 = (f32[2560,128]{1,0:T(8,128)S(1)}, f32[2560,128]{1,0:T(8,128)}, u32[]{:S(2)}) copy-start(f32[2560,128]{1,0:T(8,128)} %copy-done.1) | copy-start | bytes 3932164
  110.0 20.1 %copy-start.8 = (bf16[64,128]{1,0:T(8,128)(2,1)S(1)}, bf16[64,128]{1,0:T(8,128)(2,1)}, u32[]{:S(2)}) copy-start(bf16[64,128]{1,0:T(8,128)(2,1)} %constant.127.clone.backward) | copy-start | bytes 49156

commit v2 on v1

--- a/solution.py
+++ b/solution.py
@@ -48,16 +48,12 @@
         ref[first : first + SPAN, :] = value[:, s * cols : (s + 1) * cols].astype(ref.dtype)
 
 
-def spectrum_kernel(grad, other, momentum, mask, forward, advanced, sent, rows):
-    for i in range(grad.shape[0] // (SPAN * WIDE)):
+def spectrum_kernel(part, other, mask, forward, advanced, sent, rows):
+    for i in range(part.shape[0] // (SPAN * WIDE)):
         x = beside(
             [
-                0.999 * m + g + o.astype(jnp.float32)
-                for m, g, o in zip(
-                    spans_of(momentum, i, WIDE),
-                    spans_of(grad, i, WIDE),
-                    spans_of(other, i, WIDE),
-                )
+                p + o.astype(jnp.float32)
+                for p, o in zip(spans_of(part, i, WIDE), spans_of(other, i, WIDE))
             ]
         )
         high, low = split(x)
@@ -102,7 +98,7 @@
         out_shape=out_shape,
         in_specs=[vmem] * len(args),
         out_specs=jax.tree.map(lambda _: vmem, out_shape),
-        compiler_params=pltpu.CompilerParams(vmem_limit_bytes=40 << 20),
+        compiler_params=pltpu.CompilerParams(vmem_limit_bytes=10 << 20),
         cost_estimate=pl.CostEstimate(
             flops=6 * 2 * SPAN * outs[0].size, bytes_accessed=moved, transcendentals=0
         ),
@@ -128,23 +124,28 @@
     left_head, right_tail = along(head, 1), along(tail, -1)
 
     by_core = key_grad.reshape(chips, 2, tokens, cols)
-    own_keys = lax.dynamic_index_in_dim(by_core, core, 1, keepdims=False)
-    their_keys = swap(lax.dynamic_index_in_dim(by_core, 1 - core, 1, keepdims=False))
-
-    head, tail, their_keys = lax.optimization_barrier((head, tail, their_keys))
+
+    def keys_for(which):
+        rows = lax.dynamic_index_in_dim(by_core, which, 1, keepdims=False)
+        return lax.dynamic_slice_in_dim(jnp.concatenate([rows, rows]), chip, chips, 0)
+
+    their_keys = swap(keys_for(1 - core))
+
+    base = momentum[0]
+    head, tail, their_keys, key_grad, block_ids, counts, base, block = lax.optimization_barrier(
+        (head, tail, their_keys, key_grad, block_ids, counts, base, activations)
+    )
     left_tail, right_head = along(tail, 1), along(head, -1)
     far_head, far_tail = along(left_head, 1), along(right_tail, -1)
 
-    def block(keys, step):
-        return lax.dynamic_index_in_dim(
-            keys, lax.bitwise_and(chip + step, chips - 1), 0, keepdims=False
-        )
-
-    def near(keys):
-        total = gram(activations, block(keys, 0))
-        before, after = block(keys, chips - 1), block(keys, 1)
+    by_core = key_grad.reshape(chips, 2, tokens, cols)
+    own_keys = lax.optimization_barrier(keys_for(core))
+
+    def near(keys, total):
+        before, after = keys[chips - 1], keys[1]
         return (
             total
+            + gram(block, keys[0])
             + gram(left_head, before[:cut])
             + gram(right_tail, after[cut:])
             + gram(left_tail, before[cut:])
@@ -152,8 +153,7 @@
         )
 
     def whole(total, keys):
-        far = block(keys, 2)
-        return total + gram(far_head, far[:cut]) + gram(far_tail, far[cut:])
+        return total + gram(far_head, keys[2][:cut]) + gram(far_tail, keys[2][cut:])
 
     active = jnp.arange(block_ids.shape[3], dtype=jnp.int32) < counts[0]
     hit = (block_ids[0][..., None] == jnp.arange(BLK, dtype=jnp.int32)) & active[:, None]
@@ -162,12 +162,12 @@
         chosen[:, :, None, :, None], (features // SPAN, BLK, 2, cols // SPAN, SPAN)
     ).reshape(features, cols)
 
-    their_near, own_near = near(their_keys), near(own_keys)
+    their_near, own_near = near(their_keys, 0.0), near(own_keys, 0.999 * base)
     their_near, own_near, mask, far_head, far_tail = lax.optimization_barrier(
         (their_near, own_near, mask, far_head, far_tail)
     )
     other = swap(whole(their_near, their_keys).astype(jnp.bfloat16))
-    grad = whole(own_near, own_keys)
+    part = whole(own_near, own_keys)
 
     high, low = cosine_parts()
     forward = jnp.asarray(np.concatenate([high, high, low], axis=1))
@@ -180,9 +180,8 @@
         spectrum_kernel,
         "spectrum",
         (flat, flat_half, flat),
-        grad,
+        part,
         other,
-        momentum[0],
         mask,
         forward,
     )

time: 132 us -> 128 us (0.970)
  blocking collectives: 32.6 us -> 34.7 us
  matrix products: 15.5 us -> 13.4 us
  local copies, waits for them, and re-layouts: 14.4 us -> 12.7 us
  waiting for transfers between devices: 28.8 us -> 27.3 us
    ppermute x6, waiting for transfers between devices: 9.85 us -> 7.42 us  [along(): lax.ppermute(x, 'tensor', [(i, (i + 2 * step) % group) for i in range(gro...]
    dot_general x14, matrix products: 15.5 us -> 13.4 us  [gram(): lax.dot_general(a, k, (((0,), (0,)), ((), ())), preferred_element_type=jn...]
    all_to_all x1, blocking collectives: 32.6 us -> 34.7 us  [shards(): lax.all_to_all(sent.reshape(replicas, features // replicas, cols), 'dp',...]
    unnamed x26 -> x28, local copies, waits for them, and re-layouts: 4.34 us -> 3.41 us
  transfers between devices with their start and end apart: 9 -> 9, of which waited for: 5 -> 4; matrix products, arithmetic and copies ran while one was open for 16% -> 17% of each run, Pallas kernels for 1% -> 1%
where the time goes in v2:
time: 128 us; the launch traced here: 127 us
  blocking collectives  34.7 us (27%)
  starting transfers between devices  33.1 us (26%)
  waiting for transfers between devices  27.3 us (21%)
  matrix products  13.4 us (10%)
  local copies, waits for them, and re-layouts  12.7 us (10%)
  Pallas kernels  4.23 us (3%)
  between operations  1.7 us (1%)
    all_to_all x1, blocking collectives, shards(): lax.all_to_all(sent.reshape(replicas, features // replicas, cols), 'dp',...  34.7 us
    ppermute x6, starting transfers between devices, along(): lax.ppermute(x, 'tensor', [(i, (i + 2 * step) % group) for i in range(gro...  22.8 us
    all_to_all x1, waiting for transfers between devices, shards(): lax.all_to_all(totals, 'dp', 0, 0, tiled=True).reshape(features, cols)  18.6 us
    dot_general x14, matrix products, gram(): lax.dot_general(a, k, (((0,), (0,)), ((), ())), preferred_element_type=jn...  13.4 us
    ppermute x6, waiting for transfers between devices, along(): lax.ppermute(x, 'tensor', [(i, (i + 2 * step) % group) for i in range(gro...  7.42 us
    all_to_all x1, starting transfers between devices, shards(): lax.all_to_all(totals, 'dp', 0, 0, tiled=True).reshape(features, cols)  6.41 us
    pallas_call x4, Pallas kernels, call(): pl.pallas_call(kernel, out_shape=out_shape, in_specs=[vmem] * len(args),...  4.23 us
    ppermute x2, starting transfers between devices, swap(): return lax.ppermute(x, 'tensor', [(i, i ^ 1) for i in range(group)])  3.84 us
  transfers between devices with their start and end apart: 9, of which 4 were waited for; matrix products, arithmetic and copies ran while one was open for 17% of the time, Pallas kernels for 1%

profile of v2, /device:TPU:6, one launch (start us, length us, event | category | flops | bytes accessed | tf_op | source)
XLA Modules:
  0.0 127.4 jit_solution(6844346622974787405)
XLA Ops:
  0.6 0.0 copy-start
  0.6 0.0 copy-start.6
  0.7 1.0 copy-done
  1.7 0.1 fusion.6
  1.8 1.9 %collective-permute-start = (bf16[4,208,128]{2,1,0:T(8,128)(2,1)S(1)}, bf16[4,208,128]{2,1,0:T(8,128)(2,1)S(1)}, u32[]{:S(2)}, u32[]{:S(2)}) collective-permute-start(bf16[4,208,128]{2,1,0:T(8,128)(2,1)S(1)} %fusion.6), channel_id=1, source_target_pairs={{0,1},{1,0},{2,3},{3,2},{4,5},{5,4},{6,7},{7,6},{8,9},{9,8},{10,11... | collective-permute-start | bytes 638984 | tf_op jit(solution)/shard_map/ppermute | solution.py:120
  3.7 1.9 %slice.105 = bf16[112,2560]{1,0:T(8,128)(2,1)} slice(bf16[208,2560]{1,0:T(8,128)(2,1)} %param.8), slice={[96:208], [0:2560]} | slice | bytes 1146880 | tf_op jit(solution)/shard_map/slice | solution.py:123
  5.6 2.7 %collective-permute-start.2 = (bf16[112,2560]{1,0:T(8,128)(2,1)}, bf16[112,2560]{1,0:T(8,128)(2,1)S(1)}, u32[]{:S(2)}, u32[]{:S(2)}) collective-permute-start(bf16[112,2560]{1,0:T(8,128)(2,1)} %slice.105), channel_id=1, source_target_pairs={{0,6},{1,7},{2,0},{3,1},{4,2},{5,3},{6,4},{7,5},{8,14},{9,15},{10,... | collective-permute-start | bytes 1720328 | tf_op jit(solution)/shard_map/ppermute | solution.py:117
  8.4 0.8 slice.104
  9.2 6.9 %collective-permute-start.1 = (bf16[96,2560]{1,0:T(8,128)(2,1)}, bf16[96,2560]{1,0:T(8,128)(2,1)}, u32[]{:S(2)}, u32[]{:S(2)}) collective-permute-start(bf16[96,2560]{1,0:T(8,128)(2,1)} %slice.104), channel_id=1, source_target_pairs={{0,2},{1,3},{2,4},{3,5},{4,6},{5,7},{6,0},{7,1},{8,10},{9,11},{10,... | collective-permute-start | bytes 1474568 | tf_op jit(solution)/shard_map/ppermute | solution.py:117
  16.8 1.9 %collective-permute-start.4 = (bf16[96,2560]{1,0:T(8,128)(2,1)}, bf16[96,2560]{1,0:T(8,128)(2,1)}, u32[]{:S(2)}, u32[]{:S(2)}) collective-permute-start(bf16[96,2560]{1,0:T(8,128)(2,1)} %slice.104), channel_id=1, source_target_pairs={{0,6},{1,7},{2,0},{3,1},{4,2},{5,3},{6,4},{7,5},{8,14},{9,15},{10,... | collective-permute-start | bytes 1474568 | tf_op jit(solution)/shard_map/ppermute | solution.py:117
  18.7 5.1 %collective-permute-start.3 = (bf16[112,2560]{1,0:T(8,128)(2,1)}, bf16[112,2560]{1,0:T(8,128)(2,1)}, u32[]{:S(2)}, u32[]{:S(2)}) collective-permute-start(bf16[112,2560]{1,0:T(8,128)(2,1)} %slice.105), channel_id=1, source_target_pairs={{0,2},{1,3},{2,4},{3,5},{4,6},{5,7},{6,0},{7,1},{8,10},{9,11},{10,... | collective-permute-start | bytes 1720328 | tf_op jit(solution)/shard_map/ppermute | solution.py:117
  23.9 0.1 fusion.5
  24.0 0.1 fusion.8
  24.1 1.6 %fusion.9 = f32[2560,128]{1,0:T(8,128)} fusion(bf16[208,2560]{1,0:T(8,128)(2,1)S(1)} %copy-done.6, bf16[4,208,128]{2,1,0:T(8,128)(2,1)S(1)} %fusion.5), kind=kOutput, calls=%fused_computation.25 | convolution fusion | flops 136314880 | bytes 2428928 | tf_op jit(solution)/shard_map/dot_general | solution.py:89
  25.8 0.6 copy.20
  26.4 3.0 %broadcast_in_dim.4 = f32[40,32,2,2,64]{4,3,2,1,0:T(2,128)} broadcast(f32[40,32,2]{2,1,0:T(8,128)S(1)} %copy.20), dimensions={0,1,3} | broadcast | bytes 1320960 | tf_op jit(solution)/shard_map/broadcast_in_dim | solution.py:161
  29.4 2.9 %reshape.39.mask = f32[2560,128]{1,0:T(8,128)S(1)} reshape(f32[40,32,2,2,64]{4,3,2,1,0:T(2,128)} %broadcast_in_dim.4) | data formatting | bytes 2621440 | tf_op jit(solution)/shard_map/reshape | solution.py:163
  32.3 2.8 %collective-permute-start.5 = (bf16[96,2560]{1,0:T(8,128)(2,1)}, bf16[96,2560]{1,0:T(8,128)(2,1)S(1)}, u32[]{:S(2)}, u32[]{:S(2)}) collective-permute-start(bf16[96,2560]{1,0:T(8,128)(2,1)} %collective-permute-done.1), channel_id=1, source_target_pairs={{0,2},{1,3},{2,4},{3,5},{4,6},{5,7},{6,0},{7,1},{8,10},{9,11},{10,... | collective-permute-start | bytes 1474568 | tf_op jit(solution)/shard_map/ppermute | solution.py:117
  35.2 1.5 %convolution_bitcast_fusion.1 = f32[2560,128]{1,0:T(8,128)S(1)} fusion(bf16[96,2560]{1,0:T(8,128)(2,1)} %collective-permute-done.1, bf16[4,208,128]{2,1,0:T(8,128)(2,1)} %copy-done.9), kind=kOutput, calls=%fused_computation.8 | convolution fusion | flops 62914560 | bytes 1826816 | tf_op jit(solution)/shard_map/dot_general | solution.py:89
  36.6 1.4 %convolution_bitcast_fusion.3 = f32[2560,128]{1,0:T(8,128)S(1)} fusion(bf16[96,2560]{1,0:T(8,128)(2,1)} %collective-permute-done.1, bf16[4,208,128]{2,1,0:T(8,128)(2,1)S(1)} %copy-done.12), kind=kOutput, calls=%fused_computation.10 | convolution fusion | flops 62914560 | bytes 1826816 | tf_op jit(solution)/shard_map/dot_general | solution.py:89
  38.1 0.4 convolution_bitcast_fusion.2
  38.5 0.6 fusion.1
  39.0 3.3 %collective-permute-start.6 = (bf16[112,2560]{1,0:T(8,128)(2,1)S(1)}, bf16[112,2560]{1,0:T(8,128)(2,1)S(1)}, u32[]{:S(2)}, u32[]{:S(2)}) collective-permute-start(bf16[112,2560]{1,0:T(8,128)(2,1)S(1)} %collective-permute-done.2), channel_id=1, source_target_pairs={{0,6},{1,7},{2,0},{3,1},{4,2},{5,3},{6,4},{7,5},{8,14},{9,15},{10,... | collective-permute-start | bytes 1720328 | tf_op jit(solution)/shard_map/ppermute | solution.py:117
  42.3 1.4 %fusion.27 = f32[2560,128]{1,0:T(8,128)S(1)} fusion(bf16[96,2560]{1,0:T(8,128)(2,1)} %collective-permute-done.4, bf16[4,208,128]{2,1,0:T(8,128)(2,1)S(1)} %copy-done.12), kind=kOutput, calls=%fused_computation.48 | convolution fusion | flops 62914560 | bytes 1826816 | tf_op jit(solution)/shard_map/dot_general | solution.py:89
  43.7 1.4 %fusion.24 = f32[2560,128]{1,0:T(8,128)S(1)} fusion(bf16[96,2560]{1,0:T(8,128)(2,1)} %collective-permute-done.4, bf16[4,208,128]{2,1,0:T(8,128)(2,1)S(1)} %copy-done.10), kind=kOutput, calls=%fused_computation.44 | convolution fusion | flops 62914560 | bytes 1826816 | tf_op jit(solution)/shard_map/dot_general | solution.py:89
  45.1 0.0 copy-start.8
  45.2 1.6 %fusion = f32[2560,128]{1,0:T(8,128)S(1)} fusion(f32[2560,128]{1,0:T(8,128)S(1)} %fusion.27, f32[2560,128]{1,0:T(8,128)S(1)} %fusion.1, bf16[112,2560]{1,0:T(8,128)(2,1)} %collective-permute-done.3, bf16[4,208,128]{2,1,0:T(8,128)(2,1)S(1)} %copy-done.12), kind=kOutput, calls=%fused_computation.1 | convolution fusion | flops 74055680 | bytes 4534272 | tf_op jit(solution)/shard_map/dot_general | solution.py:89
  46.7 0.0 copy-start.7
  46.7 1.5 %fusion.13 = f32[2560,128]{1,0:T(8,128)S(1)} fusion(bf16[112,2560]{1,0:T(8,128)(2,1)} %collective-permute-done.3, bf16[4,208,128]{2,1,0:T(8,128)(2,1)S(1)} %copy-done.10), kind=kOutput, calls=%fused_computation.32 | convolution fusion | flops 73400320 | bytes 1912832 | tf_op jit(solution)/shard_map/dot_general | solution.py:89
  48.3 0.5 fusion.4
  48.8 1.5 %collective-permute-done.5 = bf16[96,2560]{1,0:T(8,128)(2,1)S(1)} collective-permute-done((bf16[96,2560]{1,0:T(8,128)(2,1)}, bf16[96,2560]{1,0:T(8,128)(2,1)S(1)}, u32[]{:S(2)}, u32[]{:S(2)}) %collective-permute-start.5) | collective-permute-done | bytes 491552 | tf_op jit(solution)/shard_map/ppermute | solution.py:117
  50.4 5.9 %collective-permute-done.6 = bf16[112,2560]{1,0:T(8,128)(2,1)S(1)} collective-permute-done((bf16[112,2560]{1,0:T(8,128)(2,1)S(1)}, bf16[112,2560]{1,0:T(8,128)(2,1)S(1)}, u32[]{:S(2)}, u32[]{:S(2)}) %collective-permute-start.6) | collective-permute-done | bytes 573472 | tf_op jit(solution)/shard_map/ppermute | solution.py:117
  56.2 0.4 fusion.25
  56.6 0.4 add_convert_fusion
  57.0 1.9 %collective-permute-start.7 = (bf16[2560,128]{1,0:T(8,128)(2,1)S(1)}, bf16[2560,128]{1,0:T(8,128)(2,1)S(1)}, u32[]{:S(2)}, u32[]{:S(2)}) collective-permute-start(bf16[2560,128]{1,0:T(8,128)(2,1)S(1)} %add_convert_fusion), channel_id=1, source_target_pairs={{0,1},{1,0},{2,3},{3,2},{4,5},{5,4},{6,7},{7,6},{8,9},{9,8},{10,11... | collective-permute-start | bytes 1966088 | tf_op jit(solution)/shard_map/ppermute | solution.py:120
  58.9 0.4 fusion.23
  59.3 0.0 copy-start.4
  59.3 0.4 add_add_fusion.part
  59.7 1.3 collective-permute-done.7.other
  61.0 0.5 spectrum.1
  61.5 1.0 copy-done.1
  62.6 34.7 %all_to_all.10.pieces = bf16[64,40,128]{2,1,0:T(8,128)(2,1)S(1)} all-to-all(bf16[64,40,128]{2,1,0:T(8,128)(2,1)S(1)} %bitcast.92), channel_id=1, replica_groups=mesh['dp'=64,'tensor'=8] {'dp'}, dimensions={0} | all-to-all | bytes 1310720 | tf_op jit(solution)/shard_map/all_to_all | solution.py:188
  97.3 1.0 total.1
  98.3 6.4 %all-to-all-start.1 = ((bf16[64,40,128]{2,1,0:T(8,128)(2,1)}), bf16[64,40,128]{2,1,0:T(8,128)(2,1)S(1)}, u32[]{:S(2)}, u32[]{:S(2)}) async-start(bf16[64,40,128]{2,1,0:T(8,128)(2,1)} %total.1), calls=%async_computation.1 | async-start | bytes 1310720 | tf_op jit(solution)/shard_map/all_to_all | solution.py:195
  104.8 1.3 %copy-done.2 = f32[2560,128]{1,0:T(8,128)S(1)} copy-done((f32[2560,128]{1,0:T(8,128)S(1)}, f32[2560,128]{1,0:T(8,128)}, u32[]{:S(2)}) %copy-start.2) | copy-done | bytes 1310744
  106.1 1.5 %kept.1 = f32[2560,128]{1,0:T(8,128)} custom-call(f32[2560,128]{1,0:T(8,128)S(1)} %get-tuple-element.31.advanced, f32[2560,128]{1,0:T(8,128)S(1)} %copy-done.2, bf16[64,192]{1,0:T(8,128)(2,1)S(1)} %copy-done.3), custom_call_target="tpu_custom_call" | custom-call | flops 251658240 | bytes 3956736 | tf_op jit(solution)/shard_map/kept/pallas_call | solution.py:96
  107.6 18.6 %all-to-all-done.1 = bf16[64,40,128]{2,1,0:T(8,128)(2,1)S(1)} async-done(((bf16[64,40,128]{2,1,0:T(8,128)(2,1)}), bf16[64,40,128]{2,1,0:T(8,128)(2,1)S(1)}, u32[]{:S(2)}, u32[]{:S(2)}) %all-to-all-start.1) | async-done | bytes 655392 | tf_op jit(solution)/shard_map/all_to_all | solution.py:195
  126.2 1.2 inverse.1
  (30 shorter events, 0.1 us)
Async XLA Ops:
  0.6 1.0 copy-start
  0.6 7.7 %copy-start.6 = (bf16[208,2560]{1,0:T(8,128)(2,1)S(1)}, bf16[208,2560]{1,0:T(8,128)(2,1)}, u32[]{:S(2)}) copy-start(bf16[208,2560]{1,0:T(8,128)(2,1)} %param.8) | copy-start | bytes 3194884
  1.8 22.2 %copy-start.13 = (s32[1,40,2,6]{1,2,3,0:T(2,128)S(1)}, s32[1,40,2,6]{1,2,3,0:T(2,128)}, u32[]{:S(2)}) copy-start(s32[1,40,2,6]{1,2,3,0:T(2,128)} %param.11) | copy-start | bytes 5764
  1.8 15.0 %collective-permute-start = (bf16[4,208,128]{2,1,0:T(8,128)(2,1)S(1)}, bf16[4,208,128]{2,1,0:T(8,128)(2,1)S(1)}, u32[]{:S(2)}, u32[]{:S(2)}) collective-permute-start(bf16[4,208,128]{2,1,0:T(8,128)(2,1)S(1)} %fusion.6), channel_id=1, source_target_pairs={{0,1},{1,0},{2,3},{3,2},{4,5},{5,4},{6,7},{7,6},{8,9},{9,8},{10,11... | collective-permute-start | bytes 638984 | tf_op jit(solution)/shard_map/ppermute | solution.py:120
  5.6 32.4 %collective-permute-start.2 = (bf16[112,2560]{1,0:T(8,128)(2,1)}, bf16[112,2560]{1,0:T(8,128)(2,1)S(1)}, u32[]{:S(2)}, u32[]{:S(2)}) collective-permute-start(bf16[112,2560]{1,0:T(8,128)(2,1)} %slice.105), channel_id=1, source_target_pairs={{0,6},{1,7},{2,0},{3,1},{4,2},{5,3},{6,4},{7,5},{8,14},{9,15},{10,... | collective-permute-start | bytes 1720328 | tf_op jit(solution)/shard_map/ppermute | solution.py:117
  9.2 23.1 %collective-permute-start.1 = (bf16[96,2560]{1,0:T(8,128)(2,1)}, bf16[96,2560]{1,0:T(8,128)(2,1)}, u32[]{:S(2)}, u32[]{:S(2)}) collective-permute-start(bf16[96,2560]{1,0:T(8,128)(2,1)} %slice.104), channel_id=1, source_target_pairs={{0,2},{1,3},{2,4},{3,5},{4,6},{5,7},{6,0},{7,1},{8,10},{9,11},{10,... | collective-permute-start | bytes 1474568 | tf_op jit(solution)/shard_map/ppermute | solution.py:117
  16.8 9.0 %copy-start.11 = (bf16[4,208,128]{2,1,0:T(8,128)(2,1)}, bf16[4,208,128]{2,1,0:T(8,128)(2,1)S(1)}, u32[]{:S(2)}) copy-start(bf16[4,208,128]{2,1,0:T(8,128)(2,1)S(1)} %collective-permute-done) | copy-start | bytes 638980
  16.8 25.5 %collective-permute-start.4 = (bf16[96,2560]{1,0:T(8,128)(2,1)}, bf16[96,2560]{1,0:T(8,128)(2,1)}, u32[]{:S(2)}, u32[]{:S(2)}) collective-permute-start(bf16[96,2560]{1,0:T(8,128)(2,1)} %slice.104), channel_id=1, source_target_pairs={{0,6},{1,7},{2,0},{3,1},{4,2},{5,3},{6,4},{7,5},{8,14},{9,15},{10,... | collective-permute-start | bytes 1474568 | tf_op jit(solution)/shard_map/ppermute | solution.py:117
  18.7 26.4 %collective-permute-start.3 = (bf16[112,2560]{1,0:T(8,128)(2,1)}, bf16[112,2560]{1,0:T(8,128)(2,1)}, u32[]{:S(2)}, u32[]{:S(2)}) collective-permute-start(bf16[112,2560]{1,0:T(8,128)(2,1)} %slice.105), channel_id=1, source_target_pairs={{0,2},{1,3},{2,4},{3,5},{4,6},{5,7},{6,0},{7,1},{8,10},{9,11},{10,... | collective-permute-start | bytes 1720328 | tf_op jit(solution)/shard_map/ppermute | solution.py:117
  24.0 1.8 %copy-start.9 = (bf16[4,208,128]{2,1,0:T(8,128)(2,1)}, bf16[4,208,128]{2,1,0:T(8,128)(2,1)S(1)}, u32[]{:S(2)}) copy-start(bf16[4,208,128]{2,1,0:T(8,128)(2,1)S(1)} %fusion.5) | copy-start | bytes 638980
  32.3 4.3 %copy-start.12 = (bf16[4,208,128]{2,1,0:T(8,128)(2,1)S(1)}, bf16[4,208,128]{2,1,0:T(8,128)(2,1)}, u32[]{:S(2)}) copy-start(bf16[4,208,128]{2,1,0:T(8,128)(2,1)} %copy-done.11) | copy-start | bytes 638980
  32.3 18.1 %collective-permute-start.5 = (bf16[96,2560]{1,0:T(8,128)(2,1)}, bf16[96,2560]{1,0:T(8,128)(2,1)S(1)}, u32[]{:S(2)}, u32[]{:S(2)}) collective-permute-start(bf16[96,2560]{1,0:T(8,128)(2,1)} %collective-permute-done.1), channel_id=1, source_target_pairs={{0,2},{1,3},{2,4},{3,5},{4,6},{5,7},{6,0},{7,1},{8,10},{9,11},{10,... | collective-permute-start | bytes 1474568 | tf_op jit(solution)/shard_map/ppermute | solution.py:117
  39.0 4.7 %copy-start.10 = (bf16[4,208,128]{2,1,0:T(8,128)(2,1)S(1)}, bf16[4,208,128]{2,1,0:T(8,128)(2,1)}, u32[]{:S(2)}) copy-start(bf16[4,208,128]{2,1,0:T(8,128)(2,1)} %copy-done.9) | copy-start | bytes 638980
  39.0 17.2 %collective-permute-start.6 = (bf16[112,2560]{1,0:T(8,128)(2,1)S(1)}, bf16[112,2560]{1,0:T(8,128)(2,1)S(1)}, u32[]{:S(2)}, u32[]{:S(2)}) collective-permute-start(bf16[112,2560]{1,0:T(8,128)(2,1)S(1)} %collective-permute-done.2), channel_id=1, source_target_pairs={{0,6},{1,7},{2,0},{3,1},{4,2},{5,3},{6,4},{7,5},{8,14},{9,15},{10,... | collective-permute-start | bytes 1720328 | tf_op jit(solution)/shard_map/ppermute | solution.py:117
  45.1 3.1 %copy-start.8 = (f32[1,2560,128]{2,1,0:T(8,128)S(1)}, f32[1,2560,128]{2,1,0:T(8,128)}, u32[]{:S(2)}) copy-start(f32[1,2560,128]{2,1,0:T(8,128)} %param.10) | copy-start | bytes 3932164
  46.7 1.6 %copy-start.7 = (f32[2560,128]{1,0:T(8,128)S(1)}, f32[2560,128]{1,0:T(8,128)}, u32[]{:S(2)}) copy-start(f32[2560,128]{1,0:T(8,128)} %fusion.9) | copy-start | bytes 3932164
  57.0 4.0 %collective-permute-start.7 = (bf16[2560,128]{1,0:T(8,128)(2,1)S(1)}, bf16[2560,128]{1,0:T(8,128)(2,1)S(1)}, u32[]{:S(2)}, u32[]{:S(2)}) collective-permute-start(bf16[2560,128]{1,0:T(8,128)(2,1)S(1)} %add_convert_fusion), channel_id=1, source_target_pairs={{0,1},{1,0},{2,3},{3,2},{4,5},{5,4},{6,7},{7,6},{8,9},{9,8},{10,11... | collective-permute-start | bytes 1966088 | tf_op jit(solution)/shard_map/ppermute | solution.py:120
  59.3 1.7 %copy-start.4 = (bf16[64,192]{1,0:T(8,128)(2,1)S(1)}, bf16[64,192]{1,0:T(8,128)(2,1)}, u32[]{:S(2)}) copy-start(bf16[64,192]{1,0:T(8,128)(2,1)} %constant.29.clone.forward) | copy-start | bytes 73732
  61.5 1.1 copy-start.1
  97.3 7.4 %copy-start.3 = (bf16[64,192]{1,0:T(8,128)(2,1)S(1)}, bf16[64,192]{1,0:T(8,128)(2,1)}, u32[]{:S(2)}) copy-start(bf16[64,192]{1,0:T(8,128)(2,1)} %constant.30.clone.backward) | copy-start | bytes 73732
  98.3 27.9 %all-to-all-start.1 = ((bf16[64,40,128]{2,1,0:T(8,128)(2,1)}), bf16[64,40,128]{2,1,0:T(8,128)(2,1)S(1)}, u32[]{:S(2)}, u32[]{:S(2)}) async-start(bf16[64,40,128]{2,1,0:T(8,128)(2,1)} %total.1), calls=%async_computation.1 | async-start | bytes 1310720 | tf_op jit(solution)/shard_map/all_to_all | solution.py:195
  104.8 1.3 %copy-start.2 = (f32[2560,128]{1,0:T(8,128)S(1)}, f32[2560,128]{1,0:T(8,128)}, u32[]{:S(2)}) copy-start(f32[2560,128]{1,0:T(8,128)} %copy-done.1) | copy-start | bytes 3932164
  106.1 20.1 %copy-start.5 = (bf16[64,128]{1,0:T(8,128)(2,1)S(1)}, bf16[64,128]{1,0:T(8,128)(2,1)}, u32[]{:S(2)}) copy-start(bf16[64,128]{1,0:T(8,128)(2,1)} %constant.31.clone.backward) | copy-start | bytes 49156

commit v3 on v2

--- a/solution.py
+++ b/solution.py
@@ -48,7 +48,34 @@
         ref[first : first + SPAN, :] = value[:, s * cols : (s + 1) * cols].astype(ref.dtype)
 
 
-def spectrum_kernel(part, other, mask, forward, advanced, sent, rows):
+def mask_kernel(ids, count, mask):
+    shape = (SPAN, mask.shape[1])
+    block = lax.shift_right_logical(lax.broadcasted_iota(jnp.int32, shape, 0), 1)
+    first = lax.broadcasted_iota(jnp.int32, shape, 1) < SPAN
+    most = ids.shape[0] * SPAN // (2 * mask.shape[0])
+
+    def body(a, _):
+        hit = jnp.zeros(shape, jnp.bool_)
+        for k in range(most):
+            active = k < count[0]
+            one = jnp.where(active, ids[2 * most * a + k], -1)
+            two = jnp.where(active, ids[2 * most * a + most + k], -1)
+            hit = hit | (jnp.where(first, one, two) == block)
+        rows = pl.ds(pl.multiple_of(a * SPAN, SPAN), SPAN)
+        mask[rows, :] = hit.astype(jnp.float32).astype(mask.dtype)
+        return 0
+
+    lax.fori_loop(0, mask.shape[0] // SPAN, body, 0)
+
+
+def chosen_rows(x, mask, forward, i):
+    high, low = split(x)
+    keep = beside(spans_of(mask, i, WIDE)).astype(jnp.float32)
+    return product(forward, [high, low, high]) * keep
+
+
+def spectrum_kernel(part, other, mask, forward, advanced, sent, held, done):
+    copies = []
     for i in range(part.shape[0] // (SPAN * WIDE)):
         x = beside(
             [
@@ -56,17 +83,19 @@
                 for p, o in zip(spans_of(part, i, WIDE), spans_of(other, i, WIDE))
             ]
         )
-        high, low = split(x)
-        s = product(forward, [high, low, high]) * beside(spans_of(mask, i, WIDE))
-        put(sent, i, WIDE, s)
-        put(advanced, i, WIDE, x)
-        put(rows, i, WIDE, s)
-
-
-def kept_kernel(advanced, rows, backward, kept):
+        put(held, i, WIDE, x)
+        rows = pl.ds(i * WIDE * SPAN, WIDE * SPAN)
+        copies.append(pltpu.make_async_copy(held.at[rows], advanced.at[rows], done.at[i]))
+        copies[-1].start()
+        put(sent, i, WIDE, chosen_rows(x, mask, forward, i))
+    for copy in copies:
+        copy.wait()
+
+
+def kept_kernel(advanced, mask, forward, backward, kept):
     for i in range(kept.shape[0] // (SPAN * WIDE)):
-        high, low = split(beside(spans_of(rows, i, WIDE)))
         x = beside(spans_of(advanced, i, WIDE))
+        high, low = split(chosen_rows(x, mask, forward, i))
         put(kept, i, WIDE, x - product(backward, [high, low, high]))
 
 
@@ -89,15 +118,19 @@
     return lax.dot_general(a, k, (((0,), (0,)), ((), ())), preferred_element_type=jnp.float32)
 
 
-def call(kernel, name, out_shape, *args):
-    vmem = pl.BlockSpec(memory_space=pltpu.VMEM)
-    outs = out_shape if isinstance(out_shape, tuple) else (out_shape,)
+VMEM, SMEM, ANY = (
+    pl.BlockSpec(memory_space=space) for space in (pltpu.VMEM, pltpu.SMEM, pl.ANY)
+)
+
+
+def call(kernel, name, outs, *args, places=None, out_places=None, scratch=()):
     moved = sum(x.size * x.dtype.itemsize for x in args + outs)
     return pl.pallas_call(
         kernel,
-        out_shape=out_shape,
-        in_specs=[vmem] * len(args),
-        out_specs=jax.tree.map(lambda _: vmem, out_shape),
+        out_shape=outs,
+        in_specs=places or [VMEM] * len(args),
+        out_specs=out_places or (VMEM,) * len(outs),
+        scratch_shapes=scratch,
         compiler_params=pltpu.CompilerParams(vmem_limit_bytes=10 << 20),
         cost_estimate=pl.CostEstimate(
             flops=6 * 2 * SPAN * outs[0].size, bytes_accessed=moved, transcendentals=0
@@ -131,69 +164,76 @@
 
     their_keys = swap(keys_for(1 - core))
 
-    base = momentum[0]
-    head, tail, their_keys, key_grad, block_ids, counts, base, block = lax.optimization_barrier(
-        (head, tail, their_keys, key_grad, block_ids, counts, base, activations)
-    )
+    head, tail, their_keys = lax.optimization_barrier((head, tail, their_keys))
     left_tail, right_head = along(tail, 1), along(head, -1)
+
+    (left_head, right_tail, block, key_grad, block_ids, counts, momentum) = (
+        lax.optimization_barrier(
+            (left_head, right_tail, activations, key_grad, block_ids, counts, momentum)
+        )
+    )
     far_head, far_tail = along(left_head, 1), along(right_tail, -1)
 
     by_core = key_grad.reshape(chips, 2, tokens, cols)
-    own_keys = lax.optimization_barrier(keys_for(core))
-
-    def near(keys, total):
-        before, after = keys[chips - 1], keys[1]
-        return (
-            total
-            + gram(block, keys[0])
-            + gram(left_head, before[:cut])
-            + gram(right_tail, after[cut:])
-            + gram(left_tail, before[cut:])
-            + gram(right_head, after[:cut])
+    own_keys = keys_for(core)
+    keys = lax.optimization_barrier(jnp.concatenate([own_keys, their_keys], axis=2))
+    before, after = keys[chips - 1], keys[1]
+    near = (
+        gram(block, keys[0])
+        + gram(left_head, before[:cut])
+        + gram(right_tail, after[cut:])
+        + gram(left_tail, before[cut:])
+        + gram(right_head, after[:cut])
+    )
+    own_near = near[:, :cols] + 0.999 * momentum[0]
+    their_near = near[:, cols:]
+    own_far, their_far = own_keys[2], their_keys[2]
+
+    def whole(total, far):
+        return total + gram(far_head, far[:cut]) + gram(far_tail, far[cut:])
+
+    flat = jax.ShapeDtypeStruct((features, cols), jnp.float32)
+    flat_half = jax.ShapeDtypeStruct((features, cols), jnp.bfloat16)
+    (mask,) = call(
+        mask_kernel, "mask", (flat_half,), block_ids.reshape(-1), counts, places=[SMEM, SMEM]
+    )
+
+    (own_near, their_near, own_far, their_far, mask, far_head, far_tail) = (
+        lax.optimization_barrier(
+            (own_near, their_near, own_far, their_far, mask, far_head, far_tail)
         )
-
-    def whole(total, keys):
-        return total + gram(far_head, keys[2][:cut]) + gram(far_tail, keys[2][cut:])
-
-    active = jnp.arange(block_ids.shape[3], dtype=jnp.int32) < counts[0]
-    hit = (block_ids[0][..., None] == jnp.arange(BLK, dtype=jnp.int32)) & active[:, None]
-    chosen = jnp.transpose(jnp.any(hit, axis=2), (0, 2, 1)).astype(jnp.float32)
-    mask = jnp.broadcast_to(
-        chosen[:, :, None, :, None], (features // SPAN, BLK, 2, cols // SPAN, SPAN)
-    ).reshape(features, cols)
-
-    their_near, own_near = near(their_keys, 0.0), near(own_keys, 0.999 * base)
-    their_near, own_near, mask, far_head, far_tail = lax.optimization_barrier(
-        (their_near, own_near, mask, far_head, far_tail)
-    )
-    other = swap(whole(their_near, their_keys).astype(jnp.bfloat16))
-    part = whole(own_near, own_keys)
+    )
+    other = swap(whole(their_near, their_far).astype(jnp.bfloat16))
+    part = whole(own_near, own_far)
 
     high, low = cosine_parts()
     forward = jnp.asarray(np.concatenate([high, high, low], axis=1))
     backward = jnp.asarray(np.concatenate([high.T, high.T, low.T], axis=1))
     backward_once = jnp.asarray(np.concatenate([high.T, low.T], axis=1))
 
-    flat = jax.ShapeDtypeStruct((features, cols), jnp.float32)
-    flat_half = jax.ShapeDtypeStruct((features, cols), jnp.bfloat16)
-    advanced, sent, rows = call(
+    advanced, sent = call(
         spectrum_kernel,
         "spectrum",
-        (flat, flat_half, flat),
+        (flat, flat_half),
         part,
         other,
         mask,
         forward,
+        out_places=(ANY, VMEM),
+        scratch=(
+            pltpu.VMEM(flat.shape, jnp.float32),
+            pltpu.SemaphoreType.DMA((features // (SPAN * WIDE),)),
+        ),
     )
     pieces = lax.all_to_all(
         sent.reshape(replicas, features // replicas, cols), "dp", 0, 0, tiled=True
     )
-    kept = call(kept_kernel, "kept", flat, advanced, rows, backward)
-    totals = call(
-        total_kernel, "total", jax.ShapeDtypeStruct(pieces.shape, jnp.bfloat16), pieces
+    (kept,) = call(kept_kernel, "kept", (flat,), advanced, mask, forward, backward)
+    (totals,) = call(
+        total_kernel, "total", (jax.ShapeDtypeStruct(pieces.shape, jnp.bfloat16),), pieces
     )
     summed = lax.all_to_all(totals, "dp", 0, 0, tiled=True).reshape(features, cols)
-    update = call(inverse_kernel, "inverse", flat_half, summed, backward_once)
+    (update,) = call(inverse_kernel, "inverse", (flat_half,), summed, backward_once)
     return kept[None], update
 
 

time: 128 us -> 124 us (0.969)
  the two profiles are of different devices: /device:TPU:6 before, /device:TPU:8 now
where the time goes in v3:
time: 124 us; the launch traced here: 123 us
  blocking collectives  38.3 us (31%)
  starting transfers between devices  29.4 us (24%)
  waiting for transfers between devices  28 us (23%)
  matrix products  10.4 us (8%)
  Pallas kernels  10.3 us (8%)
  local copies, waits for them, and re-layouts  4.45 us (4%)
  between operations  1.6 us (1%)
    all_to_all x1, blocking collectives, shards(): lax.all_to_all(sent.reshape(replicas, features // replicas, cols), 'dp',...  38.3 us
    ppermute x6, starting transfers between devices, along(): lax.ppermute(x, 'tensor', [(i, (i + 2 * step) % group) for i in range(gro...  19.6 us
    all_to_all x1, waiting for transfers between devices, shards(): lax.all_to_all(totals, 'dp', 0, 0, tiled=True).reshape(features, cols)  18.4 us
    dot_general x9, matrix products, gram(): lax.dot_general(a, k, (((0,), (0,)), ((), ())), preferred_element_type=jn...  10.4 us
    pallas_call x5, Pallas kernels, call(): pl.pallas_call(kernel, out_shape=outs, in_specs=places or [VMEM] * len(ar...  10.3 us
    ppermute x6, waiting for transfers between devices, along(): lax.ppermute(x, 'tensor', [(i, (i + 2 * step) % group) for i in range(gro...  7.58 us
    all_to_all x1, starting transfers between devices, shards(): lax.all_to_all(totals, 'dp', 0, 0, tiled=True).reshape(features, cols)  6.02 us
    ppermute x2, starting transfers between devices, swap(): return lax.ppermute(x, 'tensor', [(i, i ^ 1) for i in range(group)])  3.84 us
  transfers between devices with their start and end apart: 9, of which 5 were waited for; matrix products, arithmetic and copies ran while one was open for 9% of the time, Pallas kernels for 4%

profile of v3, /device:TPU:8, one launch (start us, length us, event | category | flops | bytes accessed | tf_op | source)
XLA Modules:
  0.0 123.0 jit_solution(15993147736776321659)
XLA Ops:
  0.6 0.0 copy-start
  0.7 2.0 %slice.64 = bf16[112,2560]{1,0:T(8,128)(2,1)} slice(bf16[208,2560]{1,0:T(8,128)(2,1)} %param.8), slice={[96:208], [0:2560]} | slice | bytes 1146880 | tf_op jit(solution)/shard_map/slice | solution.py:156
  2.7 4.7 %collective-permute-start.1 = (bf16[112,2560]{1,0:T(8,128)(2,1)}, bf16[112,2560]{1,0:T(8,128)(2,1)S(1)}, u32[]{:S(2)}, u32[]{:S(2)}) collective-permute-start(bf16[112,2560]{1,0:T(8,128)(2,1)} %slice.64), channel_id=1, source_target_pairs={{0,6},{1,7},{2,0},{3,1},{4,2},{5,3},{6,4},{7,5},{8,14},{9,15},{10,... | collective-permute-start | bytes 1720328 | tf_op jit(solution)/shard_map/ppermute | solution.py:150
  7.3 0.8 slice.63
  8.2 1.9 %collective-permute-start = (bf16[96,2560]{1,0:T(8,128)(2,1)}, bf16[96,2560]{1,0:T(8,128)(2,1)}, u32[]{:S(2)}, u32[]{:S(2)}) collective-permute-start(bf16[96,2560]{1,0:T(8,128)(2,1)} %slice.63), channel_id=1, source_target_pairs={{0,2},{1,3},{2,4},{3,5},{4,6},{5,7},{6,0},{7,1},{8,10},{9,11},{10,... | collective-permute-start | bytes 1474568 | tf_op jit(solution)/shard_map/ppermute | solution.py:150
  10.1 0.1 fusion.3
  10.2 1.9 %collective-permute-start.2 = (bf16[4,208,128]{2,1,0:T(8,128)(2,1)S(1)}, bf16[4,208,128]{2,1,0:T(8,128)(2,1)S(1)}, u32[]{:S(2)}, u32[]{:S(2)}) collective-permute-start(bf16[4,208,128]{2,1,0:T(8,128)(2,1)S(1)} %fusion.3), channel_id=1, source_target_pairs={{0,1},{1,0},{2,3},{3,2},{4,5},{5,4},{6,7},{7,6},{8,9},{9,8},{10,11... | collective-permute-start | bytes 638984 | tf_op jit(solution)/shard_map/ppermute | solution.py:153
  12.8 0.8 collective-permute-done.2
  13.6 2.6 %collective-permute-start.3 = (bf16[112,2560]{1,0:T(8,128)(2,1)}, bf16[112,2560]{1,0:T(8,128)(2,1)}, u32[]{:S(2)}, u32[]{:S(2)}) collective-permute-start(bf16[112,2560]{1,0:T(8,128)(2,1)} %slice.64), channel_id=1, source_target_pairs={{0,2},{1,3},{2,4},{3,5},{4,6},{5,7},{6,0},{7,1},{8,10},{9,11},{10,... | collective-permute-start | bytes 1720328 | tf_op jit(solution)/shard_map/ppermute | solution.py:150
  16.2 4.4 %collective-permute-start.4 = (bf16[96,2560]{1,0:T(8,128)(2,1)}, bf16[96,2560]{1,0:T(8,128)(2,1)}, u32[]{:S(2)}, u32[]{:S(2)}) collective-permute-start(bf16[96,2560]{1,0:T(8,128)(2,1)} %slice.63), channel_id=1, source_target_pairs={{0,6},{1,7},{2,0},{3,1},{4,2},{5,3},{6,4},{7,5},{8,14},{9,15},{10,... | collective-permute-start | bytes 1474568 | tf_op jit(solution)/shard_map/ppermute | solution.py:150
  20.6 5.1 %collective-permute-done = bf16[96,2560]{1,0:T(8,128)(2,1)} collective-permute-done((bf16[96,2560]{1,0:T(8,128)(2,1)}, bf16[96,2560]{1,0:T(8,128)(2,1)}, u32[]{:S(2)}, u32[]{:S(2)}) %collective-permute-start) | collective-permute-done | bytes 491552 | tf_op jit(solution)/shard_map/ppermute | solution.py:150
  25.7 0.0 collective-permute-done.1
  25.7 0.1 fusion.4
  25.8 0.7 copy-done.9
  26.6 0.0 copy-start.10
  26.6 2.1 %collective-permute-start.6 = (bf16[112,2560]{1,0:T(8,128)(2,1)}, bf16[112,2560]{1,0:T(8,128)(2,1)S(1)}, u32[]{:S(2)}, u32[]{:S(2)}) collective-permute-start(bf16[112,2560]{1,0:T(8,128)(2,1)} %copy-done.9), channel_id=1, source_target_pairs={{0,6},{1,7},{2,0},{3,1},{4,2},{5,3},{6,4},{7,5},{8,14},{9,15},{10,... | collective-permute-start | bytes 1720328 | tf_op jit(solution)/shard_map/ppermute | solution.py:150
  28.7 3.1 %fusion.6 = f32[2560,256]{1,0:T(8,128)} fusion(bf16[112,2560]{1,0:T(8,128)(2,1)} %copy-done.9, bf16[4,208,256]{2,1,0:T(8,128)(2,1)S(1)} %pad_maximum_fusion), kind=kOutput, calls=%fused_computation.20 | convolution fusion | flops 146800640 | bytes 3252224 | tf_op jit(solution)/shard_map/dot_general | solution.py:118
  31.8 3.9 %collective-permute-start.5 = (bf16[96,2560]{1,0:T(8,128)(2,1)}, bf16[96,2560]{1,0:T(8,128)(2,1)S(1)}, u32[]{:S(2)}, u32[]{:S(2)}) collective-permute-start(bf16[96,2560]{1,0:T(8,128)(2,1)} %collective-permute-done), channel_id=1, source_target_pairs={{0,2},{1,3},{2,4},{3,5},{4,6},{5,7},{6,0},{7,1},{8,10},{9,11},{10,... | collective-permute-start | bytes 1474568 | tf_op jit(solution)/shard_map/ppermute | solution.py:150
  35.7 0.1 copy.10
  35.8 0.1 reshape.27.ids
  36.0 1.8 %mask.1 = bf16[2560,128]{1,0:T(8,128)(2,1)S(1)} custom-call(s32[480]{0:T(512)S(1)} %reshape.27.ids, s32[1]{0:T(128)S(6)} %copy.11.count), custom_call_target="tpu_custom_call" | custom-call | flops 251658240 | bytes 657284 | tf_op jit(solution)/shard_map/mask/pallas_call | solution.py:128
  37.8 0.0 copy-start.8
  37.8 1.6 %fusion.8 = f32[2560,256]{1,0:T(8,128)S(1)} fusion(bf16[96,2560]{1,0:T(8,128)(2,1)} %collective-permute-done, bf16[4,208,256]{2,1,0:T(8,128)(2,1)} %copy-done.7), kind=kOutput, calls=%fused_computation.26 | convolution fusion | flops 125829120 | bytes 3162112 | tf_op jit(solution)/shard_map/dot_general | solution.py:118
  39.4 0.0 collective-permute-done.4
  39.4 1.6 %fusion.7 = f32[2560,256]{1,0:T(8,128)S(1)} fusion(bf16[96,2560]{1,0:T(8,128)(2,1)} %collective-permute-done.4, bf16[4,208,256]{2,1,0:T(8,128)(2,1)S(1)} %copy-done.8), kind=kOutput, calls=%fused_computation.24 | convolution fusion | flops 125829120 | bytes 3162112 | tf_op jit(solution)/shard_map/dot_general | solution.py:118
  41.0 0.0 collective-permute-done.3
  41.0 1.7 %fusion.5 = f32[2560,256]{1,0:T(8,128)S(1)} fusion(bf16[112,2560]{1,0:T(8,128)(2,1)} %collective-permute-done.3, bf16[4,208,256]{2,1,0:T(8,128)(2,1)S(1)} %copy-done.8), kind=kOutput, calls=%fused_computation.18 | convolution fusion | flops 146800640 | bytes 3252224 | tf_op jit(solution)/shard_map/dot_general | solution.py:118
  42.8 0.1 copy-done.4
  42.9 0.9 fusion.2
  43.8 0.4 copy-done.6
  44.2 0.2 fusion.21
  44.4 2.5 %collective-permute-done.5 = bf16[96,2560]{1,0:T(8,128)(2,1)S(1)} collective-permute-done((bf16[96,2560]{1,0:T(8,128)(2,1)}, bf16[96,2560]{1,0:T(8,128)(2,1)S(1)}, u32[]{:S(2)}, u32[]{:S(2)}) %collective-permute-start.5) | collective-permute-done | bytes 491552 | tf_op jit(solution)/shard_map/ppermute | solution.py:150
  47.0 0.0 collective-permute-done.6
  47.0 0.4 fusion.17
  47.3 0.4 add_convert_fusion
  47.7 1.9 %collective-permute-start.7 = (bf16[2560,128]{1,0:T(8,128)(2,1)S(1)}, bf16[2560,128]{1,0:T(8,128)(2,1)S(1)}, u32[]{:S(2)}, u32[]{:S(2)}) collective-permute-start(bf16[2560,128]{1,0:T(8,128)(2,1)S(1)} %add_convert_fusion), channel_id=1, source_target_pairs={{0,1},{1,0},{2,3},{3,2},{4,5},{5,4},{6,7},{7,6},{8,9},{9,8},{10,11... | collective-permute-start | bytes 1966088 | tf_op jit(solution)/shard_map/ppermute | solution.py:153
  49.7 0.4 fusion.19
  50.0 0.0 copy-start.1
  50.0 0.4 add_add_fusion.part
  50.4 1.3 %collective-permute-done.7.other = bf16[2560,128]{1,0:T(8,128)(2,1)S(1)} collective-permute-done((bf16[2560,128]{1,0:T(8,128)(2,1)S(1)}, bf16[2560,128]{1,0:T(8,128)(2,1)S(1)}, u32[]{:S(2)}, u32[]{:S(2)}) %collective-permute-start.7) | collective-permute-done | bytes 655392 | tf_op jit(solution)/shard_map/ppermute | solution.py:153
  51.7 3.3 %spectrum.1 = (f32[2560,128]{1,0:T(8,128)S(1)}, bf16[2560,128]{1,0:T(8,128)(2,1)S(1)}) custom-call(f32[2560,128]{1,0:T(8,128)S(1)} %add_add_fusion.part, bf16[2560,128]{1,0:T(8,128)(2,1)S(1)} %collective-permute-done.7.other, bf16[2560,128]{1,0:T(8,128)(2,1)S(1)} %mask.1, bf16[64,192]{1,0:T(8,128)(2,1)S(1)} %copy-done.1), custom_call_target="tpu_custom_call" | custom-call | flops 251658240 | bytes 4612096 | tf_op jit(solution)/shard_map/spectrum/pallas_call | solution.py:128
  55.1 38.3 %all_to_all.10.pieces = bf16[64,40,128]{2,1,0:T(8,128)(2,1)S(1)} all-to-all(bf16[64,40,128]{2,1,0:T(8,128)(2,1)S(1)} %bitcast.42), channel_id=1, replica_groups=mesh['dp'=64,'tensor'=8] {'dp'}, dimensions={0} | all-to-all | bytes 1310720 | tf_op jit(solution)/shard_map/all_to_all | solution.py:228
  93.3 1.0 total.1
  94.3 6.0 %all-to-all-start.1 = ((bf16[64,40,128]{2,1,0:T(8,128)(2,1)}), bf16[64,40,128]{2,1,0:T(8,128)(2,1)S(1)}, u32[]{:S(2)}, u32[]{:S(2)}) async-start(bf16[64,40,128]{2,1,0:T(8,128)(2,1)} %total.1), calls=%async_computation.1 | async-start | bytes 1310720 | tf_op jit(solution)/shard_map/all_to_all | solution.py:235
  100.4 0.0 copy-start.3
  100.4 3.1 %kept.1 = f32[2560,128]{1,0:T(8,128)} custom-call(f32[2560,128]{1,0:T(8,128)S(1)} %get-tuple-element.38.advanced, bf16[2560,128]{1,0:T(8,128)(2,1)S(1)} %mask.1, bf16[64,192]{1,0:T(8,128)(2,1)S(1)} %copy-done.1, bf16[64,192]{1,0:T(8,128)(2,1)S(1)} %copy-done.2), custom_call_target="tpu_custom_call" | custom-call | flops 251658240 | bytes 3325952 | tf_op jit(solution)/shard_map/kept/pallas_call | solution.py:128
  103.4 18.4 %all-to-all-done.1 = bf16[64,40,128]{2,1,0:T(8,128)(2,1)S(1)} async-done(((bf16[64,40,128]{2,1,0:T(8,128)(2,1)}), bf16[64,40,128]{2,1,0:T(8,128)(2,1)S(1)}, u32[]{:S(2)}, u32[]{:S(2)}) %all-to-all-start.1) | async-done | bytes 655392 | tf_op jit(solution)/shard_map/all_to_all | solution.py:235
  121.8 1.2 inverse.1
  (19 shorter events, 0.1 us)
Async XLA Ops:
  0.6 9.4 %copy-start = (bf16[1664,128]{1,0:T(8,128)(2,1)S(1)}, bf16[1664,128]{1,0:T(8,128)(2,1)}, u32[]{:S(2)}) copy-start(bf16[1664,128]{1,0:T(8,128)(2,1)} %param.9) | copy-start | bytes 1277956
  0.6 6.7 %copy-start.5 = (bf16[208,2560]{1,0:T(8,128)(2,1)S(1)}, bf16[208,2560]{1,0:T(8,128)(2,1)}, u32[]{:S(2)}) copy-start(bf16[208,2560]{1,0:T(8,128)(2,1)} %param.8) | copy-start | bytes 3194884
  2.7 23.0 %collective-permute-start.1 = (bf16[112,2560]{1,0:T(8,128)(2,1)}, bf16[112,2560]{1,0:T(8,128)(2,1)S(1)}, u32[]{:S(2)}, u32[]{:S(2)}) collective-permute-start(bf16[112,2560]{1,0:T(8,128)(2,1)} %slice.64), channel_id=1, source_target_pairs={{0,6},{1,7},{2,0},{3,1},{4,2},{5,3},{6,4},{7,5},{8,14},{9,15},{10,... | collective-permute-start | bytes 1720328 | tf_op jit(solution)/shard_map/ppermute | solution.py:150
  8.2 17.6 %collective-permute-start = (bf16[96,2560]{1,0:T(8,128)(2,1)}, bf16[96,2560]{1,0:T(8,128)(2,1)}, u32[]{:S(2)}, u32[]{:S(2)}) collective-permute-start(bf16[96,2560]{1,0:T(8,128)(2,1)} %slice.63), channel_id=1, source_target_pairs={{0,2},{1,3},{2,4},{3,5},{4,6},{5,7},{6,0},{7,1},{8,10},{9,11},{10,... | collective-permute-start | bytes 1474568 | tf_op jit(solution)/shard_map/ppermute | solution.py:150
  10.2 3.4 %collective-permute-start.2 = (bf16[4,208,128]{2,1,0:T(8,128)(2,1)S(1)}, bf16[4,208,128]{2,1,0:T(8,128)(2,1)S(1)}, u32[]{:S(2)}, u32[]{:S(2)}) collective-permute-start(bf16[4,208,128]{2,1,0:T(8,128)(2,1)S(1)} %fusion.3), channel_id=1, source_target_pairs={{0,1},{1,0},{2,3},{3,2},{4,5},{5,4},{6,7},{7,6},{8,9},{9,8},{10,11... | collective-permute-start | bytes 638984 | tf_op jit(solution)/shard_map/ppermute | solution.py:153
  13.6 27.4 %collective-permute-start.3 = (bf16[112,2560]{1,0:T(8,128)(2,1)}, bf16[112,2560]{1,0:T(8,128)(2,1)}, u32[]{:S(2)}, u32[]{:S(2)}) collective-permute-start(bf16[112,2560]{1,0:T(8,128)(2,1)} %slice.64), channel_id=1, source_target_pairs={{0,2},{1,3},{2,4},{3,5},{4,6},{5,7},{6,0},{7,1},{8,10},{9,11},{10,... | collective-permute-start | bytes 1720328 | tf_op jit(solution)/shard_map/ppermute | solution.py:150
  16.2 23.2 %collective-permute-start.4 = (bf16[96,2560]{1,0:T(8,128)(2,1)}, bf16[96,2560]{1,0:T(8,128)(2,1)}, u32[]{:S(2)}, u32[]{:S(2)}) collective-permute-start(bf16[96,2560]{1,0:T(8,128)(2,1)} %slice.63), channel_id=1, source_target_pairs={{0,6},{1,7},{2,0},{3,1},{4,2},{5,3},{6,4},{7,5},{8,14},{9,15},{10,... | collective-permute-start | bytes 1474568 | tf_op jit(solution)/shard_map/ppermute | solution.py:150
  25.7 0.8 copy-start.9
  26.6 5.2 %copy-start.7 = (bf16[4,208,256]{2,1,0:T(8,128)(2,1)}, bf16[4,208,256]{2,1,0:T(8,128)(2,1)S(1)}, u32[]{:S(2)}) copy-start(bf16[4,208,256]{2,1,0:T(8,128)(2,1)S(1)} %pad_maximum_fusion) | copy-start | bytes 1277956
  26.6 9.1 %copy-start.10 = (s32[1,40,2,6]{1,2,3,0:T(2,128)S(1)}, s32[1,40,2,6]{1,2,3,0:T(2,128)}, u32[]{:S(2)}) copy-start(s32[1,40,2,6]{1,2,3,0:T(2,128)} %param.11) | copy-start | bytes 5764
  26.6 20.4 %collective-permute-start.6 = (bf16[112,2560]{1,0:T(8,128)(2,1)}, bf16[112,2560]{1,0:T(8,128)(2,1)S(1)}, u32[]{:S(2)}, u32[]{:S(2)}) collective-permute-start(bf16[112,2560]{1,0:T(8,128)(2,1)} %copy-done.9), channel_id=1, source_target_pairs={{0,6},{1,7},{2,0},{3,1},{4,2},{5,3},{6,4},{7,5},{8,14},{9,15},{10,... | collective-permute-start | bytes 1720328 | tf_op jit(solution)/shard_map/ppermute | solution.py:150
  31.8 15.2 %collective-permute-start.5 = (bf16[96,2560]{1,0:T(8,128)(2,1)}, bf16[96,2560]{1,0:T(8,128)(2,1)S(1)}, u32[]{:S(2)}, u32[]{:S(2)}) collective-permute-start(bf16[96,2560]{1,0:T(8,128)(2,1)} %collective-permute-done), channel_id=1, source_target_pairs={{0,2},{1,3},{2,4},{3,5},{4,6},{5,7},{6,0},{7,1},{8,10},{9,11},{10,... | collective-permute-start | bytes 1474568 | tf_op jit(solution)/shard_map/ppermute | solution.py:150
  37.8 1.6 %copy-start.8 = (bf16[4,208,256]{2,1,0:T(8,128)(2,1)S(1)}, bf16[4,208,256]{2,1,0:T(8,128)(2,1)}, u32[]{:S(2)}) copy-start(bf16[4,208,256]{2,1,0:T(8,128)(2,1)} %copy-done.7) | copy-start | bytes 1277956
  41.0 1.9 %copy-start.4 = (f32[2560,256]{1,0:T(8,128)S(1)}, f32[2560,256]{1,0:T(8,128)}, u32[]{:S(2)}) copy-start(f32[2560,256]{1,0:T(8,128)} %fusion.6) | copy-start | bytes 7864324
  42.9 1.3 %copy-start.6 = (f32[1,2560,128]{2,1,0:T(8,128)S(1)}, f32[1,2560,128]{2,1,0:T(8,128)}, u32[]{:S(2)}) copy-start(f32[1,2560,128]{2,1,0:T(8,128)} %param.10) | copy-start | bytes 3932164
  47.7 4.0 %collective-permute-start.7 = (bf16[2560,128]{1,0:T(8,128)(2,1)S(1)}, bf16[2560,128]{1,0:T(8,128)(2,1)S(1)}, u32[]{:S(2)}, u32[]{:S(2)}) collective-permute-start(bf16[2560,128]{1,0:T(8,128)(2,1)S(1)} %add_convert_fusion), channel_id=1, source_target_pairs={{0,1},{1,0},{2,3},{3,2},{4,5},{5,4},{6,7},{7,6},{8,9},{9,8},{10,11... | collective-permute-start | bytes 1966088 | tf_op jit(solution)/shard_map/ppermute | solution.py:153
  50.0 1.7 %copy-start.1 = (bf16[64,192]{1,0:T(8,128)(2,1)S(1)}, bf16[64,192]{1,0:T(8,128)(2,1)}, u32[]{:S(2)}) copy-start(bf16[64,192]{1,0:T(8,128)(2,1)} %constant.27.clone.forward) | copy-start | bytes 73732
  93.3 7.0 %copy-start.2 = (bf16[64,192]{1,0:T(8,128)(2,1)S(1)}, bf16[64,192]{1,0:T(8,128)(2,1)}, u32[]{:S(2)}) copy-start(bf16[64,192]{1,0:T(8,128)(2,1)} %constant.28.clone.backward) | copy-start | bytes 73732
  94.3 27.5 %all-to-all-start.1 = ((bf16[64,40,128]{2,1,0:T(8,128)(2,1)}), bf16[64,40,128]{2,1,0:T(8,128)(2,1)S(1)}, u32[]{:S(2)}, u32[]{:S(2)}) async-start(bf16[64,40,128]{2,1,0:T(8,128)(2,1)} %total.1), calls=%async_computation.1 | async-start | bytes 1310720 | tf_op jit(solution)/shard_map/all_to_all | solution.py:235
  100.4 21.5 %copy-start.3 = (bf16[64,128]{1,0:T(8,128)(2,1)S(1)}, bf16[64,128]{1,0:T(8,128)(2,1)}, u32[]{:S(2)}) copy-start(bf16[64,128]{1,0:T(8,128)(2,1)} %constant.29.clone.backward) | copy-start | bytes 49156

commit v4 on v3

--- a/solution.py
+++ b/solution.py
@@ -74,8 +74,7 @@
     return product(forward, [high, low, high]) * keep
 
 
-def spectrum_kernel(part, other, mask, forward, advanced, sent, held, done):
-    copies = []
+def spectrum_kernel(part, other, mask, forward, advanced, sent):
     for i in range(part.shape[0] // (SPAN * WIDE)):
         x = beside(
             [
@@ -83,13 +82,8 @@
                 for p, o in zip(spans_of(part, i, WIDE), spans_of(other, i, WIDE))
             ]
         )
-        put(held, i, WIDE, x)
-        rows = pl.ds(i * WIDE * SPAN, WIDE * SPAN)
-        copies.append(pltpu.make_async_copy(held.at[rows], advanced.at[rows], done.at[i]))
-        copies[-1].start()
+        put(advanced, i, WIDE, x)
         put(sent, i, WIDE, chosen_rows(x, mask, forward, i))
-    for copy in copies:
-        copy.wait()
 
 
 def kept_kernel(advanced, mask, forward, backward, kept):
@@ -118,19 +112,16 @@
     return lax.dot_general(a, k, (((0,), (0,)), ((), ())), preferred_element_type=jnp.float32)
 
 
-VMEM, SMEM, ANY = (
-    pl.BlockSpec(memory_space=space) for space in (pltpu.VMEM, pltpu.SMEM, pl.ANY)
-)
-
-
-def call(kernel, name, outs, *args, places=None, out_places=None, scratch=()):
+VMEM, SMEM = (pl.BlockSpec(memory_space=space) for space in (pltpu.VMEM, pltpu.SMEM))
+
+
+def call(kernel, name, outs, *args, places=None):
     moved = sum(x.size * x.dtype.itemsize for x in args + outs)
     return pl.pallas_call(
         kernel,
         out_shape=outs,
         in_specs=places or [VMEM] * len(args),
-        out_specs=out_places or (VMEM,) * len(outs),
-        scratch_shapes=scratch,
+        out_specs=(VMEM,) * len(outs),
         compiler_params=pltpu.CompilerParams(vmem_limit_bytes=10 << 20),
         cost_estimate=pl.CostEstimate(
             flops=6 * 2 * SPAN * outs[0].size, bytes_accessed=moved, transcendentals=0
@@ -152,9 +143,9 @@
     def swap(x):
         return lax.ppermute(x, "tensor", [(i, i ^ 1) for i in range(group)])
 
-    cut = tokens // 2 // 16 * 16
+    cut = tokens * 9 // 16 // 16 * 16
     head, tail = activations[:cut], activations[cut:]
-    left_head, right_tail = along(head, 1), along(tail, -1)
+    left, right_tail = along(activations, 1), along(tail, -1)
 
     by_core = key_grad.reshape(chips, 2, tokens, cols)
 
@@ -164,25 +155,23 @@
 
     their_keys = swap(keys_for(1 - core))
 
-    head, tail, their_keys = lax.optimization_barrier((head, tail, their_keys))
-    left_tail, right_head = along(tail, 1), along(head, -1)
-
-    (left_head, right_tail, block, key_grad, block_ids, counts, momentum) = (
-        lax.optimization_barrier(
-            (left_head, right_tail, activations, key_grad, block_ids, counts, momentum)
-        )
-    )
-    far_head, far_tail = along(left_head, 1), along(right_tail, -1)
-
+    head, their_keys, block_ids, counts = lax.optimization_barrier(
+        (head, their_keys, block_ids, counts)
+    )
+    right_head = along(head, -1)
+
+    left, right_tail, block, key_grad, momentum = lax.optimization_barrier(
+        (left, right_tail, activations, key_grad, momentum)
+    )
+    far_head, far_tail = along(left[:cut], 1), along(right_tail, -1)
     by_core = key_grad.reshape(chips, 2, tokens, cols)
     own_keys = keys_for(core)
     keys = lax.optimization_barrier(jnp.concatenate([own_keys, their_keys], axis=2))
     before, after = keys[chips - 1], keys[1]
     near = (
         gram(block, keys[0])
-        + gram(left_head, before[:cut])
+        + gram(left, before)
         + gram(right_tail, after[cut:])
-        + gram(left_tail, before[cut:])
         + gram(right_head, after[:cut])
     )
     own_near = near[:, :cols] + 0.999 * momentum[0]
@@ -219,11 +208,6 @@
         other,
         mask,
         forward,
-        out_places=(ANY, VMEM),
-        scratch=(
-            pltpu.VMEM(flat.shape, jnp.float32),
-            pltpu.SemaphoreType.DMA((features // (SPAN * WIDE),)),
-        ),
     )
     pieces = lax.all_to_all(
         sent.reshape(replicas, features // replicas, cols), "dp", 0, 0, tiled=True

time: 124 us -> 121 us (0.976)
  the two profiles are of different devices: /device:TPU:8 before, /device:TPU:6 now
where the time goes in v4:
time: 121 us; the launch traced here: 120 us
  blocking collectives  39.2 us (32%)
  waiting for transfers between devices  34.1 us (28%)
  starting transfers between devices  27.8 us (23%)
  Pallas kernels  7.55 us (6%)
  matrix products  5.81 us (5%)
  local copies, waits for them, and re-layouts  3.78 us (3%)
  between operations  1.58 us (1%)
    all_to_all x1, blocking collectives, shards(): lax.all_to_all(sent.reshape(replicas, features // replicas, cols), 'dp',...  39.2 us
    all_to_all x1, waiting for transfers between devices, shards(): lax.all_to_all(totals, 'dp', 0, 0, tiled=True).reshape(features, cols)  18.4 us
    ppermute x5, starting transfers between devices, along(): lax.ppermute(x, 'tensor', [(i, (i + 2 * step) % group) for i in range(gro...  17.6 us
    ppermute x5, waiting for transfers between devices, along(): lax.ppermute(x, 'tensor', [(i, (i + 2 * step) % group) for i in range(gro...  14.5 us
    pallas_call x5, Pallas kernels, call(): pl.pallas_call(kernel, out_shape=outs, in_specs=places or [VMEM] * len(ar...  7.55 us
    all_to_all x1, starting transfers between devices, shards(): lax.all_to_all(totals, 'dp', 0, 0, tiled=True).reshape(features, cols)  6.41 us
    dot_general x8, matrix products, gram(): lax.dot_general(a, k, (((0,), (0,)), ((), ())), preferred_element_type=jn...  5.81 us
    ppermute x2, starting transfers between devices, swap(): return lax.ppermute(x, 'tensor', [(i, i ^ 1) for i in range(group)])  3.84 us
  transfers between devices with their start and end apart: 8, of which 5 were waited for; matrix products, arithmetic and copies ran while one was open for 7% of the time, Pallas kernels for 4%

profile of v4, /device:TPU:6, one launch (start us, length us, event | category | flops | bytes accessed | tf_op | source)
XLA Modules:
  0.0 120.3 jit_solution(3149679416897560537)
XLA Ops:
  0.6 0.0 copy-start
  0.6 0.0 copy-start.4
  0.7 0.0 copy-start.6
  0.7 7.9 %collective-permute-start = (bf16[208,2560]{1,0:T(8,128)(2,1)}, bf16[208,2560]{1,0:T(8,128)(2,1)S(1)}, u32[]{:S(2)}, u32[]{:S(2)}) collective-permute-start(bf16[208,2560]{1,0:T(8,128)(2,1)} %param.8), channel_id=1, source_target_pairs={{0,2},{1,3},{2,4},{3,5},{4,6},{5,7},{6,0},{7,1},{8,10},{9,11},{10,... | collective-permute-start | bytes 3194888 | tf_op jit(solution)/shard_map/ppermute | solution.py:141
  8.6 1.9 %slice.54 = bf16[96,2560]{1,0:T(8,128)(2,1)} slice(bf16[208,2560]{1,0:T(8,128)(2,1)} %param.8), slice={[112:208], [0:2560]} | slice | bytes 983040 | tf_op jit(solution)/shard_map/slice | solution.py:147
  10.4 1.9 %collective-permute-start.1 = (bf16[96,2560]{1,0:T(8,128)(2,1)}, bf16[96,2560]{1,0:T(8,128)(2,1)}, u32[]{:S(2)}, u32[]{:S(2)}) collective-permute-start(bf16[96,2560]{1,0:T(8,128)(2,1)} %slice.54), channel_id=1, source_target_pairs={{0,6},{1,7},{2,0},{3,1},{4,2},{5,3},{6,4},{7,5},{8,14},{9,15},{10,... | collective-permute-start | bytes 1474568 | tf_op jit(solution)/shard_map/ppermute | solution.py:141
  12.3 0.0 copy-done
  12.4 0.1 fusion.2
  12.5 1.9 %collective-permute-start.2 = (bf16[4,208,128]{2,1,0:T(8,128)(2,1)S(1)}, bf16[4,208,128]{2,1,0:T(8,128)(2,1)S(1)}, u32[]{:S(2)}, u32[]{:S(2)}) collective-permute-start(bf16[4,208,128]{2,1,0:T(8,128)(2,1)S(1)} %fusion.2), channel_id=1, source_target_pairs={{0,1},{1,0},{2,3},{3,2},{4,5},{5,4},{6,7},{7,6},{8,9},{9,8},{10,11... | collective-permute-start | bytes 638984 | tf_op jit(solution)/shard_map/ppermute | solution.py:144
  14.4 0.8 slice.55
  15.9 0.0 collective-permute-done.2
  15.9 1.9 %collective-permute-start.3 = (bf16[112,2560]{1,0:T(8,128)(2,1)}, bf16[112,2560]{1,0:T(8,128)(2,1)}, u32[]{:S(2)}, u32[]{:S(2)}) collective-permute-start(bf16[112,2560]{1,0:T(8,128)(2,1)} %slice.55), channel_id=1, source_target_pairs={{0,6},{1,7},{2,0},{3,1},{4,2},{5,3},{6,4},{7,5},{8,14},{9,15},{10,... | collective-permute-start | bytes 1720328 | tf_op jit(solution)/shard_map/ppermute | solution.py:141
  17.9 0.1 copy.10
  18.0 0.1 reshape.25.ids
  18.1 1.8 %mask.1 = bf16[2560,128]{1,0:T(8,128)(2,1)S(1)} custom-call(s32[480]{0:T(512)S(1)} %reshape.25.ids, s32[1]{0:T(128)S(6)} %copy.11.count), custom_call_target="tpu_custom_call" | custom-call | flops 251658240 | bytes 657284 | tf_op jit(solution)/shard_map/mask/pallas_call | solution.py:120
  20.0 2.7 %collective-permute-done.1 = bf16[96,2560]{1,0:T(8,128)(2,1)} collective-permute-done((bf16[96,2560]{1,0:T(8,128)(2,1)}, bf16[96,2560]{1,0:T(8,128)(2,1)}, u32[]{:S(2)}, u32[]{:S(2)}) %collective-permute-start.1) | collective-permute-done | bytes 491552 | tf_op jit(solution)/shard_map/ppermute | solution.py:141
  22.7 5.5 %collective-permute-done = bf16[208,2560]{1,0:T(8,128)(2,1)S(1)} collective-permute-done((bf16[208,2560]{1,0:T(8,128)(2,1)}, bf16[208,2560]{1,0:T(8,128)(2,1)S(1)}, u32[]{:S(2)}, u32[]{:S(2)}) %collective-permute-start) | collective-permute-done | bytes 1064992 | tf_op jit(solution)/shard_map/ppermute | solution.py:141
  28.2 0.1 fusion.3
  28.4 3.4 %collective-permute-start.4 = (bf16[112,2560]{1,0:T(8,128)(2,1)S(1)}, bf16[112,2560]{1,0:T(8,128)(2,1)S(1)}, u32[]{:S(2)}, u32[]{:S(2)}) collective-permute-start(bf16[112,2560]{1,0:T(8,128)(2,1)S(1)} %slice.66), channel_id=1, source_target_pairs={{0,2},{1,3},{2,4},{3,5},{4,6},{5,7},{6,0},{7,1},{8,10},{9,11},{10,... | collective-permute-start | bytes 1720328 | tf_op jit(solution)/shard_map/ppermute | solution.py:141
  31.8 2.4 %collective-permute-start.5 = (bf16[96,2560]{1,0:T(8,128)(2,1)}, bf16[96,2560]{1,0:T(8,128)(2,1)S(1)}, u32[]{:S(2)}, u32[]{:S(2)}) collective-permute-start(bf16[96,2560]{1,0:T(8,128)(2,1)} %collective-permute-done.1), channel_id=1, source_target_pairs={{0,6},{1,7},{2,0},{3,1},{4,2},{5,3},{6,4},{7,5},{8,14},{9,15},{10,... | collective-permute-start | bytes 1474568 | tf_op jit(solution)/shard_map/ppermute | solution.py:141
  34.2 1.6 %fusion.6 = f32[2560,256]{1,0:T(8,128)S(1)} fusion(bf16[96,2560]{1,0:T(8,128)(2,1)} %collective-permute-done.1, bf16[4,208,256]{2,1,0:T(8,128)(2,1)S(1)} %pad_maximum_fusion), kind=kOutput, calls=%fused_computation.23 | convolution fusion | flops 125829120 | bytes 3162112 | tf_op jit(solution)/shard_map/dot_general | solution.py:112
  35.8 0.6 fusion.4
  36.4 0.0 collective-permute-done.3
  36.4 1.6 %fusion.5 = f32[2560,256]{1,0:T(8,128)S(1)} fusion(bf16[112,2560]{1,0:T(8,128)(2,1)} %collective-permute-done.3, bf16[4,208,256]{2,1,0:T(8,128)(2,1)S(1)} %pad_maximum_fusion), kind=kOutput, calls=%fused_computation.19 | convolution fusion | flops 146800640 | bytes 3252224 | tf_op jit(solution)/shard_map/dot_general | solution.py:112
  38.0 0.0 copy-start.5
  38.0 0.6 fusion.1
  38.6 0.7 copy-done.5
  39.3 0.2 fusion.19
  39.5 6.3 %collective-permute-done.5 = bf16[96,2560]{1,0:T(8,128)(2,1)S(1)} collective-permute-done((bf16[96,2560]{1,0:T(8,128)(2,1)}, bf16[96,2560]{1,0:T(8,128)(2,1)S(1)}, u32[]{:S(2)}, u32[]{:S(2)}) %collective-permute-start.5) | collective-permute-done | bytes 491552 | tf_op jit(solution)/shard_map/ppermute | solution.py:141
  45.8 0.0 collective-permute-done.4
  45.8 0.4 fusion.7
  46.2 0.4 add_convert_fusion
  46.6 1.9 %collective-permute-start.6 = (bf16[2560,128]{1,0:T(8,128)(2,1)S(1)}, bf16[2560,128]{1,0:T(8,128)(2,1)S(1)}, u32[]{:S(2)}, u32[]{:S(2)}) collective-permute-start(bf16[2560,128]{1,0:T(8,128)(2,1)S(1)} %add_convert_fusion), channel_id=1, source_target_pairs={{0,1},{1,0},{2,3},{3,2},{4,5},{5,4},{6,7},{7,6},{8,9},{9,8},{10,11... | collective-permute-start | bytes 1966088 | tf_op jit(solution)/shard_map/ppermute | solution.py:144
  48.5 0.4 fusion.9
  48.9 0.0 copy-start.1
  48.9 0.4 add_add_fusion.part
  49.3 1.3 %collective-permute-done.6.other = bf16[2560,128]{1,0:T(8,128)(2,1)S(1)} collective-permute-done((bf16[2560,128]{1,0:T(8,128)(2,1)S(1)}, bf16[2560,128]{1,0:T(8,128)(2,1)S(1)}, u32[]{:S(2)}, u32[]{:S(2)}) %collective-permute-start.6) | collective-permute-done | bytes 655392 | tf_op jit(solution)/shard_map/ppermute | solution.py:144
  50.6 0.0 copy-done.1
  50.6 0.5 spectrum.1
  51.1 39.2 %all_to_all.10.pieces = bf16[64,40,128]{2,1,0:T(8,128)(2,1)S(1)} all-to-all(bf16[64,40,128]{2,1,0:T(8,128)(2,1)S(1)} %bitcast.38), channel_id=1, replica_groups=mesh['dp'=64,'tensor'=8] {'dp'}, dimensions={0} | all-to-all | bytes 1310720 | tf_op jit(solution)/shard_map/all_to_all | solution.py:212
  90.3 1.0 total.1
  91.3 6.4 %all-to-all-start.1 = ((bf16[64,40,128]{2,1,0:T(8,128)(2,1)}), bf16[64,40,128]{2,1,0:T(8,128)(2,1)S(1)}, u32[]{:S(2)}, u32[]{:S(2)}) async-start(bf16[64,40,128]{2,1,0:T(8,128)(2,1)} %total.1), calls=%async_computation.1 | async-start | bytes 1310720 | tf_op jit(solution)/shard_map/all_to_all | solution.py:219
  97.7 0.0 copy-done.2
  97.7 0.0 copy-start.3
  97.7 3.1 %kept.1 = f32[2560,128]{1,0:T(8,128)} custom-call(f32[2560,128]{1,0:T(8,128)S(1)} %get-tuple-element.36.advanced, bf16[2560,128]{1,0:T(8,128)(2,1)S(1)} %mask.1, bf16[64,192]{1,0:T(8,128)(2,1)S(1)} %copy-done.1, bf16[64,192]{1,0:T(8,128)(2,1)S(1)} %copy-done.2), custom_call_target="tpu_custom_call" | custom-call | flops 251658240 | bytes 3325952 | tf_op jit(solution)/shard_map/kept/pallas_call | solution.py:120
  100.8 18.4 %all-to-all-done.1 = bf16[64,40,128]{2,1,0:T(8,128)(2,1)S(1)} async-done(((bf16[64,40,128]{2,1,0:T(8,128)(2,1)}), bf16[64,40,128]{2,1,0:T(8,128)(2,1)S(1)}, u32[]{:S(2)}, u32[]{:S(2)}) %all-to-all-start.1) | async-done | bytes 655392 | tf_op jit(solution)/shard_map/all_to_all | solution.py:219
  119.2 0.0 copy-done.3
  119.2 1.2 inverse.1
  (9 shorter events, 0.1 us)
Async XLA Ops:
  0.6 11.7 %copy-start = (bf16[1664,128]{1,0:T(8,128)(2,1)S(1)}, bf16[1664,128]{1,0:T(8,128)(2,1)}, u32[]{:S(2)}) copy-start(bf16[1664,128]{1,0:T(8,128)(2,1)} %param.9) | copy-start | bytes 1277956
  0.6 13.8 %copy-start.4 = (bf16[208,2560]{1,0:T(8,128)(2,1)S(1)}, bf16[208,2560]{1,0:T(8,128)(2,1)}, u32[]{:S(2)}) copy-start(bf16[208,2560]{1,0:T(8,128)(2,1)} %param.8) | copy-start | bytes 3194884
  0.7 17.2 %copy-start.6 = (s32[1,40,2,6]{1,2,3,0:T(2,128)S(1)}, s32[1,40,2,6]{1,2,3,0:T(2,128)}, u32[]{:S(2)}) copy-start(s32[1,40,2,6]{1,2,3,0:T(2,128)} %param.11) | copy-start | bytes 5764
  0.7 27.5 %collective-permute-start = (bf16[208,2560]{1,0:T(8,128)(2,1)}, bf16[208,2560]{1,0:T(8,128)(2,1)S(1)}, u32[]{:S(2)}, u32[]{:S(2)}) collective-permute-start(bf16[208,2560]{1,0:T(8,128)(2,1)} %param.8), channel_id=1, source_target_pairs={{0,2},{1,3},{2,4},{3,5},{4,6},{5,7},{6,0},{7,1},{8,10},{9,11},{10,... | collective-permute-start | bytes 3194888 | tf_op jit(solution)/shard_map/ppermute | solution.py:141
  10.4 12.2 %collective-permute-start.1 = (bf16[96,2560]{1,0:T(8,128)(2,1)}, bf16[96,2560]{1,0:T(8,128)(2,1)}, u32[]{:S(2)}, u32[]{:S(2)}) collective-permute-start(bf16[96,2560]{1,0:T(8,128)(2,1)} %slice.54), channel_id=1, source_target_pairs={{0,6},{1,7},{2,0},{3,1},{4,2},{5,3},{6,4},{7,5},{8,14},{9,15},{10,... | collective-permute-start | bytes 1474568 | tf_op jit(solution)/shard_map/ppermute | solution.py:141
  12.5 3.4 %collective-permute-start.2 = (bf16[4,208,128]{2,1,0:T(8,128)(2,1)S(1)}, bf16[4,208,128]{2,1,0:T(8,128)(2,1)S(1)}, u32[]{:S(2)}, u32[]{:S(2)}) collective-permute-start(bf16[4,208,128]{2,1,0:T(8,128)(2,1)S(1)} %fusion.2), channel_id=1, source_target_pairs={{0,1},{1,0},{2,3},{3,2},{4,5},{5,4},{6,7},{7,6},{8,9},{9,8},{10,11... | collective-permute-start | bytes 638984 | tf_op jit(solution)/shard_map/ppermute | solution.py:144
  15.9 20.5 %collective-permute-start.3 = (bf16[112,2560]{1,0:T(8,128)(2,1)}, bf16[112,2560]{1,0:T(8,128)(2,1)}, u32[]{:S(2)}, u32[]{:S(2)}) collective-permute-start(bf16[112,2560]{1,0:T(8,128)(2,1)} %slice.55), channel_id=1, source_target_pairs={{0,6},{1,7},{2,0},{3,1},{4,2},{5,3},{6,4},{7,5},{8,14},{9,15},{10,... | collective-permute-start | bytes 1720328 | tf_op jit(solution)/shard_map/ppermute | solution.py:141
  28.4 17.4 %collective-permute-start.4 = (bf16[112,2560]{1,0:T(8,128)(2,1)S(1)}, bf16[112,2560]{1,0:T(8,128)(2,1)S(1)}, u32[]{:S(2)}, u32[]{:S(2)}) collective-permute-start(bf16[112,2560]{1,0:T(8,128)(2,1)S(1)} %slice.66), channel_id=1, source_target_pairs={{0,2},{1,3},{2,4},{3,5},{4,6},{5,7},{6,0},{7,1},{8,10},{9,11},{10,... | collective-permute-start | bytes 1720328 | tf_op jit(solution)/shard_map/ppermute | solution.py:141
  31.8 14.0 %collective-permute-start.5 = (bf16[96,2560]{1,0:T(8,128)(2,1)}, bf16[96,2560]{1,0:T(8,128)(2,1)S(1)}, u32[]{:S(2)}, u32[]{:S(2)}) collective-permute-start(bf16[96,2560]{1,0:T(8,128)(2,1)} %collective-permute-done.1), channel_id=1, source_target_pairs={{0,6},{1,7},{2,0},{3,1},{4,2},{5,3},{6,4},{7,5},{8,14},{9,15},{10,... | collective-permute-start | bytes 1474568 | tf_op jit(solution)/shard_map/ppermute | solution.py:141
  38.0 1.3 %copy-start.5 = (f32[1,2560,128]{2,1,0:T(8,128)S(1)}, f32[1,2560,128]{2,1,0:T(8,128)}, u32[]{:S(2)}) copy-start(f32[1,2560,128]{2,1,0:T(8,128)} %param.10) | copy-start | bytes 3932164
  46.6 4.0 %collective-permute-start.6 = (bf16[2560,128]{1,0:T(8,128)(2,1)S(1)}, bf16[2560,128]{1,0:T(8,128)(2,1)S(1)}, u32[]{:S(2)}, u32[]{:S(2)}) collective-permute-start(bf16[2560,128]{1,0:T(8,128)(2,1)S(1)} %add_convert_fusion), channel_id=1, source_target_pairs={{0,1},{1,0},{2,3},{3,2},{4,5},{5,4},{6,7},{7,6},{8,9},{9,8},{10,11... | collective-permute-start | bytes 1966088 | tf_op jit(solution)/shard_map/ppermute | solution.py:144
  48.9 1.7 %copy-start.1 = (bf16[64,192]{1,0:T(8,128)(2,1)S(1)}, bf16[64,192]{1,0:T(8,128)(2,1)}, u32[]{:S(2)}) copy-start(bf16[64,192]{1,0:T(8,128)(2,1)} %constant.27.clone.forward) | copy-start | bytes 73732
  90.3 7.4 %copy-start.2 = (bf16[64,192]{1,0:T(8,128)(2,1)S(1)}, bf16[64,192]{1,0:T(8,128)(2,1)}, u32[]{:S(2)}) copy-start(bf16[64,192]{1,0:T(8,128)(2,1)} %constant.28.clone.backward) | copy-start | bytes 73732
  91.3 27.9 %all-to-all-start.1 = ((bf16[64,40,128]{2,1,0:T(8,128)(2,1)}), bf16[64,40,128]{2,1,0:T(8,128)(2,1)S(1)}, u32[]{:S(2)}, u32[]{:S(2)}) async-start(bf16[64,40,128]{2,1,0:T(8,128)(2,1)} %total.1), calls=%async_computation.1 | async-start | bytes 1310720 | tf_op jit(solution)/shard_map/all_to_all | solution.py:219
  97.7 21.4 %copy-start.3 = (bf16[64,128]{1,0:T(8,128)(2,1)S(1)}, bf16[64,128]{1,0:T(8,128)(2,1)}, u32[]{:S(2)}) copy-start(bf16[64,128]{1,0:T(8,128)(2,1)} %constant.29.clone.backward) | copy-start | bytes 49156

commit v5 on v4

--- a/solution.py
+++ b/solution.py
@@ -159,11 +159,12 @@
         (head, their_keys, block_ids, counts)
     )
     right_head = along(head, -1)
+    far_tail = along(right_tail, -1)
 
     left, right_tail, block, key_grad, momentum = lax.optimization_barrier(
         (left, right_tail, activations, key_grad, momentum)
     )
-    far_head, far_tail = along(left[:cut], 1), along(right_tail, -1)
+    far_head = along(left[:cut], 1)
     by_core = key_grad.reshape(chips, 2, tokens, cols)
     own_keys = keys_for(core)
     keys = lax.optimization_barrier(jnp.concatenate([own_keys, their_keys], axis=2))

time: 121 us -> 120 us (level)
  the two profiles are of different devices: /device:TPU:6 before, /device:TPU:8 now
where the time goes in v5:
time: 120 us
  blocking collectives  38.3 us (32%)
  waiting for transfers between devices  34.8 us (29%)
  starting transfers between devices  27.5 us (23%)
  Pallas kernels  7.55 us (6%)
  matrix products  5.79 us (5%)
  local copies, waits for them, and re-layouts  3.78 us (3%)
  between operations  1.57 us (1%)
    all_to_all x1, blocking collectives, shards(): lax.all_to_all(sent.reshape(replicas, features // replicas, cols), 'dp',...  38.3 us
    all_to_all x1, waiting for transfers between devices, shards(): lax.all_to_all(totals, 'dp', 0, 0, tiled=True).reshape(features, cols)  18.4 us
    ppermute x5, starting transfers between devices, along(): lax.ppermute(x, 'tensor', [(i, (i + 2 * step) % group) for i in range(gro...  17.7 us
    ppermute x5, waiting for transfers between devices, along(): lax.ppermute(x, 'tensor', [(i, (i + 2 * step) % group) for i in range(gro...  15.1 us
    pallas_call x5, Pallas kernels, call(): pl.pallas_call(kernel, out_shape=outs, in_specs=places or [VMEM] * len(ar...  7.55 us
    all_to_all x1, starting transfers between devices, shards(): lax.all_to_all(totals, 'dp', 0, 0, tiled=True).reshape(features, cols)  6.01 us
    dot_general x8, matrix products, gram(): lax.dot_general(a, k, (((0,), (0,)), ((), ())), preferred_element_type=jn...  5.79 us
    ppermute x2, starting transfers between devices, swap(): return lax.ppermute(x, 'tensor', [(i, i ^ 1) for i in range(group)])  3.84 us
  transfers between devices with their start and end apart: 8, of which 7 were waited for; matrix products, arithmetic and copies ran while one was open for 7% of the time, Pallas kernels for 4%

profile of v5, /device:TPU:8, one launch (start us, length us, event | category | flops | bytes accessed | tf_op | source)
XLA Modules:
  0.0 119.8 jit_solution(12794226697693983011)
XLA Ops:
  0.6 0.0 copy-start
  0.6 0.0 copy-start.4
  0.7 0.0 copy-start.6
  0.7 3.5 %collective-permute-start = (bf16[208,2560]{1,0:T(8,128)(2,1)}, bf16[208,2560]{1,0:T(8,128)(2,1)S(1)}, u32[]{:S(2)}, u32[]{:S(2)}) collective-permute-start(bf16[208,2560]{1,0:T(8,128)(2,1)} %param.8), channel_id=1, source_target_pairs={{0,2},{1,3},{2,4},{3,5},{4,6},{5,7},{6,0},{7,1},{8,10},{9,11},{10,... | collective-permute-start | bytes 3194888 | tf_op jit(solution)/shard_map/ppermute | solution.py:141
  4.2 1.9 %slice.54 = bf16[96,2560]{1,0:T(8,128)(2,1)} slice(bf16[208,2560]{1,0:T(8,128)(2,1)} %param.8), slice={[112:208], [0:2560]} | slice | bytes 983040 | tf_op jit(solution)/shard_map/slice | solution.py:147
  6.1 3.6 %collective-permute-start.1 = (bf16[96,2560]{1,0:T(8,128)(2,1)}, bf16[96,2560]{1,0:T(8,128)(2,1)}, u32[]{:S(2)}, u32[]{:S(2)}) collective-permute-start(bf16[96,2560]{1,0:T(8,128)(2,1)} %slice.54), channel_id=1, source_target_pairs={{0,6},{1,7},{2,0},{3,1},{4,2},{5,3},{6,4},{7,5},{8,14},{9,15},{10,... | collective-permute-start | bytes 1474568 | tf_op jit(solution)/shard_map/ppermute | solution.py:141
  9.7 0.0 copy-done
  9.7 0.1 fusion.2
  9.9 1.9 %collective-permute-start.2 = (bf16[4,208,128]{2,1,0:T(8,128)(2,1)S(1)}, bf16[4,208,128]{2,1,0:T(8,128)(2,1)S(1)}, u32[]{:S(2)}, u32[]{:S(2)}) collective-permute-start(bf16[4,208,128]{2,1,0:T(8,128)(2,1)S(1)} %fusion.2), channel_id=1, source_target_pairs={{0,1},{1,0},{2,3},{3,2},{4,5},{5,4},{6,7},{7,6},{8,9},{9,8},{10,11... | collective-permute-start | bytes 638984 | tf_op jit(solution)/shard_map/ppermute | solution.py:144
  11.8 0.0 copy-done.4
  11.8 0.8 slice.55
  13.3 0.0 collective-permute-done.2
  13.3 3.5 %collective-permute-start.3 = (bf16[112,2560]{1,0:T(8,128)(2,1)}, bf16[112,2560]{1,0:T(8,128)(2,1)}, u32[]{:S(2)}, u32[]{:S(2)}) collective-permute-start(bf16[112,2560]{1,0:T(8,128)(2,1)} %slice.55), channel_id=1, source_target_pairs={{0,6},{1,7},{2,0},{3,1},{4,2},{5,3},{6,4},{7,5},{8,14},{9,15},{10,... | collective-permute-start | bytes 1720328 | tf_op jit(solution)/shard_map/ppermute | solution.py:141
  16.8 0.0 copy-done.6
  16.8 0.1 copy.10
  16.9 0.1 reshape.25.ids
  17.0 1.8 %mask.1 = bf16[2560,128]{1,0:T(8,128)(2,1)S(1)} custom-call(s32[480]{0:T(512)S(1)} %reshape.25.ids, s32[1]{0:T(128)S(6)} %copy.11.count), custom_call_target="tpu_custom_call" | custom-call | flops 251658240 | bytes 657284 | tf_op jit(solution)/shard_map/mask/pallas_call | solution.py:120
  18.9 3.5 %collective-permute-done.1 = bf16[96,2560]{1,0:T(8,128)(2,1)} collective-permute-done((bf16[96,2560]{1,0:T(8,128)(2,1)}, bf16[96,2560]{1,0:T(8,128)(2,1)}, u32[]{:S(2)}, u32[]{:S(2)}) %collective-permute-start.1) | collective-permute-done | bytes 491552 | tf_op jit(solution)/shard_map/ppermute | solution.py:141
  22.4 4.9 %collective-permute-start.5 = (bf16[96,2560]{1,0:T(8,128)(2,1)}, bf16[96,2560]{1,0:T(8,128)(2,1)S(1)}, u32[]{:S(2)}, u32[]{:S(2)}) collective-permute-start(bf16[96,2560]{1,0:T(8,128)(2,1)} %collective-permute-done.1), channel_id=1, source_target_pairs={{0,6},{1,7},{2,0},{3,1},{4,2},{5,3},{6,4},{7,5},{8,14},{9,15},{10,... | collective-permute-start | bytes 1474568 | tf_op jit(solution)/shard_map/ppermute | solution.py:141
  27.3 2.1 %collective-permute-done = bf16[208,2560]{1,0:T(8,128)(2,1)S(1)} collective-permute-done((bf16[208,2560]{1,0:T(8,128)(2,1)}, bf16[208,2560]{1,0:T(8,128)(2,1)S(1)}, u32[]{:S(2)}, u32[]{:S(2)}) %collective-permute-start) | collective-permute-done | bytes 1064992 | tf_op jit(solution)/shard_map/ppermute | solution.py:141
  29.4 0.1 fusion.3
  29.6 2.2 %collective-permute-start.4 = (bf16[112,2560]{1,0:T(8,128)(2,1)S(1)}, bf16[112,2560]{1,0:T(8,128)(2,1)S(1)}, u32[]{:S(2)}, u32[]{:S(2)}) collective-permute-start(bf16[112,2560]{1,0:T(8,128)(2,1)S(1)} %slice.66), channel_id=1, source_target_pairs={{0,2},{1,3},{2,4},{3,5},{4,6},{5,7},{6,0},{7,1},{8,10},{9,11},{10,... | collective-permute-start | bytes 1720328 | tf_op jit(solution)/shard_map/ppermute | solution.py:141
  31.8 1.6 %fusion.6 = f32[2560,256]{1,0:T(8,128)S(1)} fusion(bf16[96,2560]{1,0:T(8,128)(2,1)} %collective-permute-done.1, bf16[4,208,256]{2,1,0:T(8,128)(2,1)S(1)} %pad_maximum_fusion), kind=kOutput, calls=%fused_computation.23 | convolution fusion | flops 125829120 | bytes 3162112 | tf_op jit(solution)/shard_map/dot_general | solution.py:112
  33.4 0.6 fusion.4
  33.9 0.8 collective-permute-done.3
  34.7 1.6 %fusion.5 = f32[2560,256]{1,0:T(8,128)S(1)} fusion(bf16[112,2560]{1,0:T(8,128)(2,1)} %collective-permute-done.3, bf16[4,208,256]{2,1,0:T(8,128)(2,1)S(1)} %pad_maximum_fusion), kind=kOutput, calls=%fused_computation.19 | convolution fusion | flops 146800640 | bytes 3252224 | tf_op jit(solution)/shard_map/dot_general | solution.py:112
  36.3 0.0 copy-start.5
  36.3 0.6 fusion.1
  36.9 0.7 copy-done.5
  37.6 0.2 fusion.19
  37.8 5.8 %collective-permute-done.5 = bf16[96,2560]{1,0:T(8,128)(2,1)S(1)} collective-permute-done((bf16[96,2560]{1,0:T(8,128)(2,1)}, bf16[96,2560]{1,0:T(8,128)(2,1)S(1)}, u32[]{:S(2)}, u32[]{:S(2)}) %collective-permute-start.5) | collective-permute-done | bytes 491552 | tf_op jit(solution)/shard_map/ppermute | solution.py:141
  43.7 2.9 %collective-permute-done.4 = bf16[112,2560]{1,0:T(8,128)(2,1)S(1)} collective-permute-done((bf16[112,2560]{1,0:T(8,128)(2,1)S(1)}, bf16[112,2560]{1,0:T(8,128)(2,1)S(1)}, u32[]{:S(2)}, u32[]{:S(2)}) %collective-permute-start.4) | collective-permute-done | bytes 573472 | tf_op jit(solution)/shard_map/ppermute | solution.py:141
  46.5 0.4 fusion.7
  46.9 0.4 add_convert_fusion
  47.3 1.9 %collective-permute-start.6 = (bf16[2560,128]{1,0:T(8,128)(2,1)S(1)}, bf16[2560,128]{1,0:T(8,128)(2,1)S(1)}, u32[]{:S(2)}, u32[]{:S(2)}) collective-permute-start(bf16[2560,128]{1,0:T(8,128)(2,1)S(1)} %add_convert_fusion), channel_id=1, source_target_pairs={{0,1},{1,0},{2,3},{3,2},{4,5},{5,4},{6,7},{7,6},{8,9},{9,8},{10,11... | collective-permute-start | bytes 1966088 | tf_op jit(solution)/shard_map/ppermute | solution.py:144
  49.2 0.4 fusion.9
  49.6 0.0 copy-start.1
  49.6 0.4 add_add_fusion.part
  50.0 1.3 %collective-permute-done.6.other = bf16[2560,128]{1,0:T(8,128)(2,1)S(1)} collective-permute-done((bf16[2560,128]{1,0:T(8,128)(2,1)S(1)}, bf16[2560,128]{1,0:T(8,128)(2,1)S(1)}, u32[]{:S(2)}, u32[]{:S(2)}) %collective-permute-start.6) | collective-permute-done | bytes 655392 | tf_op jit(solution)/shard_map/ppermute | solution.py:144
  51.3 0.0 copy-done.1
  51.3 0.5 spectrum.1
  51.8 38.3 %all_to_all.10.pieces = bf16[64,40,128]{2,1,0:T(8,128)(2,1)S(1)} all-to-all(bf16[64,40,128]{2,1,0:T(8,128)(2,1)S(1)} %bitcast.38), channel_id=1, replica_groups=mesh['dp'=64,'tensor'=8] {'dp'}, dimensions={0} | all-to-all | bytes 1310720 | tf_op jit(solution)/shard_map/all_to_all | solution.py:213
  90.1 1.0 total.1
  91.1 6.0 %all-to-all-start.1 = ((bf16[64,40,128]{2,1,0:T(8,128)(2,1)}), bf16[64,40,128]{2,1,0:T(8,128)(2,1)S(1)}, u32[]{:S(2)}, u32[]{:S(2)}) async-start(bf16[64,40,128]{2,1,0:T(8,128)(2,1)} %total.1), calls=%async_computation.1 | async-start | bytes 1310720 | tf_op jit(solution)/shard_map/all_to_all | solution.py:220
  97.1 0.0 copy-start.3
  97.2 3.1 %kept.1 = f32[2560,128]{1,0:T(8,128)} custom-call(f32[2560,128]{1,0:T(8,128)S(1)} %get-tuple-element.36.advanced, bf16[2560,128]{1,0:T(8,128)(2,1)S(1)} %mask.1, bf16[64,192]{1,0:T(8,128)(2,1)S(1)} %copy-done.1, bf16[64,192]{1,0:T(8,128)(2,1)S(1)} %copy-done.2), custom_call_target="tpu_custom_call" | custom-call | flops 251658240 | bytes 3325952 | tf_op jit(solution)/shard_map/kept/pallas_call | solution.py:120
  100.2 18.4 %all-to-all-done.1 = bf16[64,40,128]{2,1,0:T(8,128)(2,1)S(1)} async-done(((bf16[64,40,128]{2,1,0:T(8,128)(2,1)}), bf16[64,40,128]{2,1,0:T(8,128)(2,1)S(1)}, u32[]{:S(2)}, u32[]{:S(2)}) %all-to-all-start.1) | async-done | bytes 655392 | tf_op jit(solution)/shard_map/all_to_all | solution.py:220
  118.6 1.2 inverse.1
  (9 shorter events, 0.1 us)
Async XLA Ops:
  0.6 9.1 %copy-start = (bf16[1664,128]{1,0:T(8,128)(2,1)S(1)}, bf16[1664,128]{1,0:T(8,128)(2,1)}, u32[]{:S(2)}) copy-start(bf16[1664,128]{1,0:T(8,128)(2,1)} %param.9) | copy-start | bytes 1277956
  0.6 11.1 %copy-start.4 = (bf16[208,2560]{1,0:T(8,128)(2,1)S(1)}, bf16[208,2560]{1,0:T(8,128)(2,1)}, u32[]{:S(2)}) copy-start(bf16[208,2560]{1,0:T(8,128)(2,1)} %param.8) | copy-start | bytes 3194884
  0.7 16.1 %copy-start.6 = (s32[1,40,2,6]{1,2,3,0:T(2,128)S(1)}, s32[1,40,2,6]{1,2,3,0:T(2,128)}, u32[]{:S(2)}) copy-start(s32[1,40,2,6]{1,2,3,0:T(2,128)} %param.11) | copy-start | bytes 5764
  0.7 28.7 %collective-permute-start = (bf16[208,2560]{1,0:T(8,128)(2,1)}, bf16[208,2560]{1,0:T(8,128)(2,1)S(1)}, u32[]{:S(2)}, u32[]{:S(2)}) collective-permute-start(bf16[208,2560]{1,0:T(8,128)(2,1)} %param.8), channel_id=1, source_target_pairs={{0,2},{1,3},{2,4},{3,5},{4,6},{5,7},{6,0},{7,1},{8,10},{9,11},{10,... | collective-permute-start | bytes 3194888 | tf_op jit(solution)/shard_map/ppermute | solution.py:141
  6.1 16.3 %collective-permute-start.1 = (bf16[96,2560]{1,0:T(8,128)(2,1)}, bf16[96,2560]{1,0:T(8,128)(2,1)}, u32[]{:S(2)}, u32[]{:S(2)}) collective-permute-start(bf16[96,2560]{1,0:T(8,128)(2,1)} %slice.54), channel_id=1, source_target_pairs={{0,6},{1,7},{2,0},{3,1},{4,2},{5,3},{6,4},{7,5},{8,14},{9,15},{10,... | collective-permute-start | bytes 1474568 | tf_op jit(solution)/shard_map/ppermute | solution.py:141
  9.9 3.4 %collective-permute-start.2 = (bf16[4,208,128]{2,1,0:T(8,128)(2,1)S(1)}, bf16[4,208,128]{2,1,0:T(8,128)(2,1)S(1)}, u32[]{:S(2)}, u32[]{:S(2)}) collective-permute-start(bf16[4,208,128]{2,1,0:T(8,128)(2,1)S(1)} %fusion.2), channel_id=1, source_target_pairs={{0,1},{1,0},{2,3},{3,2},{4,5},{5,4},{6,7},{7,6},{8,9},{9,8},{10,11... | collective-permute-start | bytes 638984 | tf_op jit(solution)/shard_map/ppermute | solution.py:144
  13.3 21.4 %collective-permute-start.3 = (bf16[112,2560]{1,0:T(8,128)(2,1)}, bf16[112,2560]{1,0:T(8,128)(2,1)}, u32[]{:S(2)}, u32[]{:S(2)}) collective-permute-start(bf16[112,2560]{1,0:T(8,128)(2,1)} %slice.55), channel_id=1, source_target_pairs={{0,6},{1,7},{2,0},{3,1},{4,2},{5,3},{6,4},{7,5},{8,14},{9,15},{10,... | collective-permute-start | bytes 1720328 | tf_op jit(solution)/shard_map/ppermute | solution.py:141
  22.4 21.3 %collective-permute-start.5 = (bf16[96,2560]{1,0:T(8,128)(2,1)}, bf16[96,2560]{1,0:T(8,128)(2,1)S(1)}, u32[]{:S(2)}, u32[]{:S(2)}) collective-permute-start(bf16[96,2560]{1,0:T(8,128)(2,1)} %collective-permute-done.1), channel_id=1, source_target_pairs={{0,6},{1,7},{2,0},{3,1},{4,2},{5,3},{6,4},{7,5},{8,14},{9,15},{10,... | collective-permute-start | bytes 1474568 | tf_op jit(solution)/shard_map/ppermute | solution.py:141
  29.6 16.9 %collective-permute-start.4 = (bf16[112,2560]{1,0:T(8,128)(2,1)S(1)}, bf16[112,2560]{1,0:T(8,128)(2,1)S(1)}, u32[]{:S(2)}, u32[]{:S(2)}) collective-permute-start(bf16[112,2560]{1,0:T(8,128)(2,1)S(1)} %slice.66), channel_id=1, source_target_pairs={{0,2},{1,3},{2,4},{3,5},{4,6},{5,7},{6,0},{7,1},{8,10},{9,11},{10,... | collective-permute-start | bytes 1720328 | tf_op jit(solution)/shard_map/ppermute | solution.py:141
  36.3 1.3 %copy-start.5 = (f32[1,2560,128]{2,1,0:T(8,128)S(1)}, f32[1,2560,128]{2,1,0:T(8,128)}, u32[]{:S(2)}) copy-start(f32[1,2560,128]{2,1,0:T(8,128)} %param.10) | copy-start | bytes 3932164
  47.3 4.0 %collective-permute-start.6 = (bf16[2560,128]{1,0:T(8,128)(2,1)S(1)}, bf16[2560,128]{1,0:T(8,128)(2,1)S(1)}, u32[]{:S(2)}, u32[]{:S(2)}) collective-permute-start(bf16[2560,128]{1,0:T(8,128)(2,1)S(1)} %add_convert_fusion), channel_id=1, source_target_pairs={{0,1},{1,0},{2,3},{3,2},{4,5},{5,4},{6,7},{7,6},{8,9},{9,8},{10,11... | collective-permute-start | bytes 1966088 | tf_op jit(solution)/shard_map/ppermute | solution.py:144
  49.6 1.7 %copy-start.1 = (bf16[64,192]{1,0:T(8,128)(2,1)S(1)}, bf16[64,192]{1,0:T(8,128)(2,1)}, u32[]{:S(2)}) copy-start(bf16[64,192]{1,0:T(8,128)(2,1)} %constant.27.clone.forward) | copy-start | bytes 73732
  90.1 7.0 %copy-start.2 = (bf16[64,192]{1,0:T(8,128)(2,1)S(1)}, bf16[64,192]{1,0:T(8,128)(2,1)}, u32[]{:S(2)}) copy-start(bf16[64,192]{1,0:T(8,128)(2,1)} %constant.28.clone.backward) | copy-start | bytes 73732
  91.1 27.5 %all-to-all-start.1 = ((bf16[64,40,128]{2,1,0:T(8,128)(2,1)}), bf16[64,40,128]{2,1,0:T(8,128)(2,1)S(1)}, u32[]{:S(2)}, u32[]{:S(2)}) async-start(bf16[64,40,128]{2,1,0:T(8,128)(2,1)} %total.1), calls=%async_computation.1 | async-start | bytes 1310720 | tf_op jit(solution)/shard_map/all_to_all | solution.py:220
  97.1 21.5 %copy-start.3 = (bf16[64,128]{1,0:T(8,128)(2,1)S(1)}, bf16[64,128]{1,0:T(8,128)(2,1)}, u32[]{:S(2)}) copy-start(bf16[64,128]{1,0:T(8,128)(2,1)} %constant.29.clone.backward) | copy-start | bytes 49156

commit v6 on v4

--- a/solution.py
+++ b/solution.py
@@ -143,9 +143,15 @@
     def swap(x):
         return lax.ppermute(x, "tensor", [(i, i ^ 1) for i in range(group)])
 
-    cut = tokens * 9 // 16 // 16 * 16
+    cut = tokens * 2 // 5 // 16 * 16
     head, tail = activations[:cut], activations[cut:]
-    left, right_tail = along(activations, 1), along(tail, -1)
+    left_head, right_tail = along(head, 1), along(tail, -1)
+    left_tail, right_head = along(tail, 1), along(head, -1)
+
+    left_head, right_tail, block, key_grad, momentum = lax.optimization_barrier(
+        (left_head, right_tail, activations, key_grad, momentum)
+    )
+    far_head, far_tail = along(left_head, 1), along(right_tail, -1)
 
     by_core = key_grad.reshape(chips, 2, tokens, cols)
 
@@ -153,24 +159,13 @@
         rows = lax.dynamic_index_in_dim(by_core, which, 1, keepdims=False)
         return lax.dynamic_slice_in_dim(jnp.concatenate([rows, rows]), chip, chips, 0)
 
-    their_keys = swap(keys_for(1 - core))
-
-    head, their_keys, block_ids, counts = lax.optimization_barrier(
-        (head, their_keys, block_ids, counts)
-    )
-    right_head = along(head, -1)
-
-    left, right_tail, block, key_grad, momentum = lax.optimization_barrier(
-        (left, right_tail, activations, key_grad, momentum)
-    )
-    far_head, far_tail = along(left[:cut], 1), along(right_tail, -1)
-    by_core = key_grad.reshape(chips, 2, tokens, cols)
-    own_keys = keys_for(core)
+    own_keys, their_keys = keys_for(core), swap(keys_for(1 - core))
     keys = lax.optimization_barrier(jnp.concatenate([own_keys, their_keys], axis=2))
     before, after = keys[chips - 1], keys[1]
     near = (
         gram(block, keys[0])
-        + gram(left, before)
+        + gram(left_head, before[:cut])
+        + gram(left_tail, before[cut:])
         + gram(right_tail, after[cut:])
         + gram(right_head, after[:cut])
     )

time: 121 us -> 120 us (level)
  starting transfers between devices: 27.8 us -> 32.8 us
  blocking collectives: 39.2 us -> 35.2 us
  waiting for transfers between devices: 34.1 us -> 31.3 us
    ppermute x5 -> x6, starting transfers between devices: 17.6 us -> 22.6 us  [along(): lax.ppermute(x, 'tensor', [(i, (i + 2 * step) % group) for i in range(gro...]
    all_to_all x1, blocking collectives: 39.2 us -> 35.2 us  [shards(): lax.all_to_all(sent.reshape(replicas, features // replicas, cols), 'dp',...]
    ppermute x5 -> x6, waiting for transfers between devices: 14.5 us -> 11.7 us  [along(): lax.ppermute(x, 'tensor', [(i, (i + 2 * step) % group) for i in range(gro...]
    dot_general x8 -> x9, matrix products: 5.81 us -> 6.52 us  [gram(): lax.dot_general(a, k, (((0,), (0,)), ((), ())), preferred_element_type=jn...]
  transfers between devices with their start and end apart: 8 -> 9, of which waited for: 5 -> 6; matrix products, arithmetic and copies ran while one was open for 7% -> 6% of each run, Pallas kernels for 4% -> 4%
where the time goes in v6:
time: 120 us; the launch traced here: 119 us
  blocking collectives  35.2 us (29%)
  starting transfers between devices  32.8 us (27%)
  waiting for transfers between devices  31.3 us (26%)
  Pallas kernels  7.55 us (6%)
  matrix products  6.52 us (5%)
  local copies, waits for them, and re-layouts  3.82 us (3%)
  between operations  1.58 us (1%)
    all_to_all x1, blocking collectives, shards(): lax.all_to_all(sent.reshape(replicas, features // replicas, cols), 'dp',...  35.2 us
    ppermute x6, starting transfers between devices, along(): lax.ppermute(x, 'tensor', [(i, (i + 2 * step) % group) for i in range(gro...  22.6 us
    all_to_all x1, waiting for transfers between devices, shards(): lax.all_to_all(totals, 'dp', 0, 0, tiled=True).reshape(features, cols)  18.4 us
    ppermute x6, waiting for transfers between devices, along(): lax.ppermute(x, 'tensor', [(i, (i + 2 * step) % group) for i in range(gro...  11.7 us
    pallas_call x5, Pallas kernels, call(): pl.pallas_call(kernel, out_shape=outs, in_specs=places or [VMEM] * len(ar...  7.55 us
    dot_general x9, matrix products, gram(): lax.dot_general(a, k, (((0,), (0,)), ((), ())), preferred_element_type=jn...  6.52 us
    all_to_all x1, starting transfers between devices, shards(): lax.all_to_all(totals, 'dp', 0, 0, tiled=True).reshape(features, cols)  6.4 us
    ppermute x2, starting transfers between devices, swap(): return lax.ppermute(x, 'tensor', [(i, i ^ 1) for i in range(group)])  3.84 us
  transfers between devices with their start and end apart: 9, of which 6 were waited for; matrix products, arithmetic and copies ran while one was open for 6% of the time, Pallas kernels for 4%

profile of v6, /device:TPU:6, one launch (start us, length us, event | category | flops | bytes accessed | tf_op | source)
XLA Modules:
  0.0 119.3 jit_solution(2838503406338913281)
XLA Ops:
  0.6 0.0 copy-start.3
  0.6 0.0 copy-start.6
  0.7 2.1 %slice.64 = bf16[128,2560]{1,0:T(8,128)(2,1)} slice(bf16[208,2560]{1,0:T(8,128)(2,1)} %param.8), slice={[80:208], [0:2560]} | slice | bytes 1310720 | tf_op jit(solution)/shard_map/slice | solution.py:147
  2.7 2.7 %collective-permute-start.1 = (bf16[128,2560]{1,0:T(8,128)(2,1)}, bf16[128,2560]{1,0:T(8,128)(2,1)S(1)}, u32[]{:S(2)}, u32[]{:S(2)}) collective-permute-start(bf16[128,2560]{1,0:T(8,128)(2,1)} %slice.64), channel_id=1, source_target_pairs={{0,6},{1,7},{2,0},{3,1},{4,2},{5,3},{6,4},{7,5},{8,14},{9,15},{10,... | collective-permute-start | bytes 1966088 | tf_op jit(solution)/shard_map/ppermute | solution.py:141
  5.5 0.8 slice.63
  6.3 6.9 %collective-permute-start = (bf16[80,2560]{1,0:T(8,128)(2,1)}, bf16[80,2560]{1,0:T(8,128)(2,1)S(1)}, u32[]{:S(2)}, u32[]{:S(2)}) collective-permute-start(bf16[80,2560]{1,0:T(8,128)(2,1)} %slice.63), channel_id=1, source_target_pairs={{0,2},{1,3},{2,4},{3,5},{4,6},{5,7},{6,0},{7,1},{8,10},{9,11},{10,... | collective-permute-start | bytes 1228808 | tf_op jit(solution)/shard_map/ppermute | solution.py:141
  13.2 3.9 %collective-permute-start.3 = (bf16[128,2560]{1,0:T(8,128)(2,1)}, bf16[128,2560]{1,0:T(8,128)(2,1)}, u32[]{:S(2)}, u32[]{:S(2)}) collective-permute-start(bf16[128,2560]{1,0:T(8,128)(2,1)} %slice.64), channel_id=1, source_target_pairs={{0,2},{1,3},{2,4},{3,5},{4,6},{5,7},{6,0},{7,1},{8,10},{9,11},{10,... | collective-permute-start | bytes 1966088 | tf_op jit(solution)/shard_map/ppermute | solution.py:141
  17.1 1.9 %collective-permute-start.4 = (bf16[80,2560]{1,0:T(8,128)(2,1)}, bf16[80,2560]{1,0:T(8,128)(2,1)}, u32[]{:S(2)}, u32[]{:S(2)}) collective-permute-start(bf16[80,2560]{1,0:T(8,128)(2,1)} %slice.63), channel_id=1, source_target_pairs={{0,6},{1,7},{2,0},{3,1},{4,2},{5,3},{6,4},{7,5},{8,14},{9,15},{10,... | collective-permute-start | bytes 1228808 | tf_op jit(solution)/shard_map/ppermute | solution.py:141
  19.1 0.0 copy-done.6
  19.1 0.1 copy.14
  19.2 0.1 reshape.23.ids
  20.0 1.8 %mask.1 = bf16[2560,128]{1,0:T(8,128)(2,1)S(1)} custom-call(s32[480]{0:T(512)S(1)} %reshape.23.ids, s32[1]{0:T(128)S(6)} %copy.17.count), custom_call_target="tpu_custom_call" | custom-call | flops 251658240 | bytes 657284 | tf_op jit(solution)/shard_map/mask/pallas_call | solution.py:120
  21.8 1.6 %collective-permute-done = bf16[80,2560]{1,0:T(8,128)(2,1)S(1)} collective-permute-done((bf16[80,2560]{1,0:T(8,128)(2,1)}, bf16[80,2560]{1,0:T(8,128)(2,1)S(1)}, u32[]{:S(2)}, u32[]{:S(2)}) %collective-permute-start) | collective-permute-done | bytes 409632 | tf_op jit(solution)/shard_map/ppermute | solution.py:141
  23.4 2.9 %collective-permute-done.1 = bf16[128,2560]{1,0:T(8,128)(2,1)S(1)} collective-permute-done((bf16[128,2560]{1,0:T(8,128)(2,1)}, bf16[128,2560]{1,0:T(8,128)(2,1)S(1)}, u32[]{:S(2)}, u32[]{:S(2)}) %collective-permute-start.1) | collective-permute-done | bytes 655392 | tf_op jit(solution)/shard_map/ppermute | solution.py:141
  26.4 0.1 fusion.2
  26.5 1.9 %collective-permute-start.2 = (bf16[4,208,128]{2,1,0:T(8,128)(2,1)S(1)}, bf16[4,208,128]{2,1,0:T(8,128)(2,1)S(1)}, u32[]{:S(2)}, u32[]{:S(2)}) collective-permute-start(bf16[4,208,128]{2,1,0:T(8,128)(2,1)S(1)} %fusion.2), channel_id=1, source_target_pairs={{0,1},{1,0},{2,3},{3,2},{4,5},{5,4},{6,7},{7,6},{8,9},{9,8},{10,11... | collective-permute-start | bytes 638984 | tf_op jit(solution)/shard_map/ppermute | solution.py:144
  28.4 0.1 fusion.3
  28.5 1.9 %collective-permute-start.6 = (bf16[128,2560]{1,0:T(8,128)(2,1)S(1)}, bf16[128,2560]{1,0:T(8,128)(2,1)S(1)}, u32[]{:S(2)}, u32[]{:S(2)}) collective-permute-start(bf16[128,2560]{1,0:T(8,128)(2,1)S(1)} %collective-permute-done.1), channel_id=1, source_target_pairs={{0,6},{1,7},{2,0},{3,1},{4,2},{5,3},{6,4},{7,5},{8,14},{9,15},{10,... | collective-permute-start | bytes 1966088 | tf_op jit(solution)/shard_map/ppermute | solution.py:141
  30.4 5.1 %collective-permute-start.5 = (bf16[80,2560]{1,0:T(8,128)(2,1)S(1)}, bf16[80,2560]{1,0:T(8,128)(2,1)S(1)}, u32[]{:S(2)}, u32[]{:S(2)}) collective-permute-start(bf16[80,2560]{1,0:T(8,128)(2,1)S(1)} %collective-permute-done), channel_id=1, source_target_pairs={{0,2},{1,3},{2,4},{3,5},{4,6},{5,7},{6,0},{7,1},{8,10},{9,11},{10,... | collective-permute-start | bytes 1228808 | tf_op jit(solution)/shard_map/ppermute | solution.py:141
  35.6 0.0 collective-permute-done.2
  35.6 0.1 pad_maximum_fusion
  35.7 0.5 fusion.4
  36.2 0.0 collective-permute-done.3
  36.2 1.6 %convolution_bitcast_fusion.1 = f32[2560,256]{1,0:T(8,128)S(1)} fusion(bf16[128,2560]{1,0:T(8,128)(2,1)} %collective-permute-done.3, bf16[4,208,256]{2,1,0:T(8,128)(2,1)S(1)} %pad_maximum_fusion), kind=kOutput, calls=%fused_computation.5 | convolution fusion | flops 167772160 | bytes 3342336 | tf_op jit(solution)/shard_map/dot_general | solution.py:112
  37.9 0.6 fusion.1
  38.5 0.0 collective-permute-done.4
  38.5 1.6 %convolution_bitcast_fusion = f32[2560,256]{1,0:T(8,128)S(1)} fusion(bf16[80,2560]{1,0:T(8,128)(2,1)} %collective-permute-done.4, bf16[4,208,256]{2,1,0:T(8,128)(2,1)S(1)} %pad_maximum_fusion), kind=kOutput, calls=%fused_computation.4 | convolution fusion | flops 104857600 | bytes 3072000 | tf_op jit(solution)/shard_map/dot_general | solution.py:112
  40.1 0.0 copy-start.4
  40.1 0.7 fusion
  40.7 0.6 copy-done.4
  41.4 0.2 fusion.17
  41.6 3.1 %collective-permute-done.5 = bf16[80,2560]{1,0:T(8,128)(2,1)S(1)} collective-permute-done((bf16[80,2560]{1,0:T(8,128)(2,1)S(1)}, bf16[80,2560]{1,0:T(8,128)(2,1)S(1)}, u32[]{:S(2)}, u32[]{:S(2)}) %collective-permute-start.5) | collective-permute-done | bytes 409632 | tf_op jit(solution)/shard_map/ppermute | solution.py:141
  44.7 4.1 %collective-permute-done.6 = bf16[128,2560]{1,0:T(8,128)(2,1)S(1)} collective-permute-done((bf16[128,2560]{1,0:T(8,128)(2,1)S(1)}, bf16[128,2560]{1,0:T(8,128)(2,1)S(1)}, u32[]{:S(2)}, u32[]{:S(2)}) %collective-permute-start.6) | collective-permute-done | bytes 655392 | tf_op jit(solution)/shard_map/ppermute | solution.py:141
  48.7 0.4 fusion.13
  49.1 0.4 add_convert_fusion
  49.5 1.9 %collective-permute-start.7 = (bf16[2560,128]{1,0:T(8,128)(2,1)S(1)}, bf16[2560,128]{1,0:T(8,128)(2,1)S(1)}, u32[]{:S(2)}, u32[]{:S(2)}) collective-permute-start(bf16[2560,128]{1,0:T(8,128)(2,1)S(1)} %add_convert_fusion), channel_id=1, source_target_pairs={{0,1},{1,0},{2,3},{3,2},{4,5},{5,4},{6,7},{7,6},{8,9},{9,8},{10,11... | collective-permute-start | bytes 1966088 | tf_op jit(solution)/shard_map/ppermute | solution.py:144
  51.5 0.4 fusion.15
  51.8 0.0 copy-start
  51.9 0.4 add_add_fusion.part
  52.2 1.3 %collective-permute-done.7.other = bf16[2560,128]{1,0:T(8,128)(2,1)S(1)} collective-permute-done((bf16[2560,128]{1,0:T(8,128)(2,1)S(1)}, bf16[2560,128]{1,0:T(8,128)(2,1)S(1)}, u32[]{:S(2)}, u32[]{:S(2)}) %collective-permute-start.7) | collective-permute-done | bytes 655392 | tf_op jit(solution)/shard_map/ppermute | solution.py:144
  53.5 0.5 spectrum.1
  54.1 35.2 %all_to_all.10.pieces = bf16[64,40,128]{2,1,0:T(8,128)(2,1)S(1)} all-to-all(bf16[64,40,128]{2,1,0:T(8,128)(2,1)S(1)} %bitcast.43), channel_id=1, replica_groups=mesh['dp'=64,'tensor'=8] {'dp'}, dimensions={0} | all-to-all | bytes 1310720 | tf_op jit(solution)/shard_map/all_to_all | solution.py:207
  89.3 1.0 total.1
  90.3 6.4 %all-to-all-start.1 = ((bf16[64,40,128]{2,1,0:T(8,128)(2,1)}), bf16[64,40,128]{2,1,0:T(8,128)(2,1)S(1)}, u32[]{:S(2)}, u32[]{:S(2)}) async-start(bf16[64,40,128]{2,1,0:T(8,128)(2,1)} %total.1), calls=%async_computation.1 | async-start | bytes 1310720 | tf_op jit(solution)/shard_map/all_to_all | solution.py:214
  96.7 0.0 copy-start.2
  96.7 3.1 %kept.1 = f32[2560,128]{1,0:T(8,128)} custom-call(f32[2560,128]{1,0:T(8,128)S(1)} %get-tuple-element.28.advanced, bf16[2560,128]{1,0:T(8,128)(2,1)S(1)} %mask.1, bf16[64,192]{1,0:T(8,128)(2,1)S(1)} %copy-done, bf16[64,192]{1,0:T(8,128)(2,1)S(1)} %copy-done.1), custom_call_target="tpu_custom_call" | custom-call | flops 251658240 | bytes 3325952 | tf_op jit(solution)/shard_map/kept/pallas_call | solution.py:120
  99.8 18.4 %all-to-all-done.1 = bf16[64,40,128]{2,1,0:T(8,128)(2,1)S(1)} async-done(((bf16[64,40,128]{2,1,0:T(8,128)(2,1)}), bf16[64,40,128]{2,1,0:T(8,128)(2,1)S(1)}, u32[]{:S(2)}, u32[]{:S(2)}) %all-to-all-start.1) | async-done | bytes 655392 | tf_op jit(solution)/shard_map/all_to_all | solution.py:214
  118.1 1.2 inverse.1
  (10 shorter events, 0.1 us)
Async XLA Ops:
  0.6 4.8 %copy-start.3 = (bf16[208,2560]{1,0:T(8,128)(2,1)S(1)}, bf16[208,2560]{1,0:T(8,128)(2,1)}, u32[]{:S(2)}) copy-start(bf16[208,2560]{1,0:T(8,128)(2,1)} %param.8) | copy-start | bytes 3194884
  0.6 18.4 %copy-start.6 = (s32[1,40,2,6]{1,2,3,0:T(2,128)S(1)}, s32[1,40,2,6]{1,2,3,0:T(2,128)}, u32[]{:S(2)}) copy-start(s32[1,40,2,6]{1,2,3,0:T(2,128)} %param.11) | copy-start | bytes 5764
  0.6 25.7 %copy-start.5 = (bf16[1664,128]{1,0:T(8,128)(2,1)S(1)}, bf16[1664,128]{1,0:T(8,128)(2,1)}, u32[]{:S(2)}) copy-start(bf16[1664,128]{1,0:T(8,128)(2,1)} %param.9) | copy-start | bytes 1277956
  2.7 23.6 %collective-permute-start.1 = (bf16[128,2560]{1,0:T(8,128)(2,1)}, bf16[128,2560]{1,0:T(8,128)(2,1)S(1)}, u32[]{:S(2)}, u32[]{:S(2)}) collective-permute-start(bf16[128,2560]{1,0:T(8,128)(2,1)} %slice.64), channel_id=1, source_target_pairs={{0,6},{1,7},{2,0},{3,1},{4,2},{5,3},{6,4},{7,5},{8,14},{9,15},{10,... | collective-permute-start | bytes 1966088 | tf_op jit(solution)/shard_map/ppermute | solution.py:141
  6.3 17.2 %collective-permute-start = (bf16[80,2560]{1,0:T(8,128)(2,1)}, bf16[80,2560]{1,0:T(8,128)(2,1)S(1)}, u32[]{:S(2)}, u32[]{:S(2)}) collective-permute-start(bf16[80,2560]{1,0:T(8,128)(2,1)} %slice.63), channel_id=1, source_target_pairs={{0,2},{1,3},{2,4},{3,5},{4,6},{5,7},{6,0},{7,1},{8,10},{9,11},{10,... | collective-permute-start | bytes 1228808 | tf_op jit(solution)/shard_map/ppermute | solution.py:141
  13.2 23.0 %collective-permute-start.3 = (bf16[128,2560]{1,0:T(8,128)(2,1)}, bf16[128,2560]{1,0:T(8,128)(2,1)}, u32[]{:S(2)}, u32[]{:S(2)}) collective-permute-start(bf16[128,2560]{1,0:T(8,128)(2,1)} %slice.64), channel_id=1, source_target_pairs={{0,2},{1,3},{2,4},{3,5},{4,6},{5,7},{6,0},{7,1},{8,10},{9,11},{10,... | collective-permute-start | bytes 1966088 | tf_op jit(solution)/shard_map/ppermute | solution.py:141
  17.1 21.4 %collective-permute-start.4 = (bf16[80,2560]{1,0:T(8,128)(2,1)}, bf16[80,2560]{1,0:T(8,128)(2,1)}, u32[]{:S(2)}, u32[]{:S(2)}) collective-permute-start(bf16[80,2560]{1,0:T(8,128)(2,1)} %slice.63), channel_id=1, source_target_pairs={{0,6},{1,7},{2,0},{3,1},{4,2},{5,3},{6,4},{7,5},{8,14},{9,15},{10,... | collective-permute-start | bytes 1228808 | tf_op jit(solution)/shard_map/ppermute | solution.py:141
  26.5 9.1 %collective-permute-start.2 = (bf16[4,208,128]{2,1,0:T(8,128)(2,1)S(1)}, bf16[4,208,128]{2,1,0:T(8,128)(2,1)S(1)}, u32[]{:S(2)}, u32[]{:S(2)}) collective-permute-start(bf16[4,208,128]{2,1,0:T(8,128)(2,1)S(1)} %fusion.2), channel_id=1, source_target_pairs={{0,1},{1,0},{2,3},{3,2},{4,5},{5,4},{6,7},{7,6},{8,9},{9,8},{10,11... | collective-permute-start | bytes 638984 | tf_op jit(solution)/shard_map/ppermute | solution.py:144
  28.5 20.2 %collective-permute-start.6 = (bf16[128,2560]{1,0:T(8,128)(2,1)S(1)}, bf16[128,2560]{1,0:T(8,128)(2,1)S(1)}, u32[]{:S(2)}, u32[]{:S(2)}) collective-permute-start(bf16[128,2560]{1,0:T(8,128)(2,1)S(1)} %collective-permute-done.1), channel_id=1, source_target_pairs={{0,6},{1,7},{2,0},{3,1},{4,2},{5,3},{6,4},{7,5},{8,14},{9,15},{10,... | collective-permute-start | bytes 1966088 | tf_op jit(solution)/shard_map/ppermute | solution.py:141
  30.4 14.2 %collective-permute-start.5 = (bf16[80,2560]{1,0:T(8,128)(2,1)S(1)}, bf16[80,2560]{1,0:T(8,128)(2,1)S(1)}, u32[]{:S(2)}, u32[]{:S(2)}) collective-permute-start(bf16[80,2560]{1,0:T(8,128)(2,1)S(1)} %collective-permute-done), channel_id=1, source_target_pairs={{0,2},{1,3},{2,4},{3,5},{4,6},{5,7},{6,0},{7,1},{8,10},{9,11},{10,... | collective-permute-start | bytes 1228808 | tf_op jit(solution)/shard_map/ppermute | solution.py:141
  40.1 1.3 %copy-start.4 = (f32[1,2560,128]{2,1,0:T(8,128)S(1)}, f32[1,2560,128]{2,1,0:T(8,128)}, u32[]{:S(2)}) copy-start(f32[1,2560,128]{2,1,0:T(8,128)} %param.10) | copy-start | bytes 3932164
  49.5 4.0 %collective-permute-start.7 = (bf16[2560,128]{1,0:T(8,128)(2,1)S(1)}, bf16[2560,128]{1,0:T(8,128)(2,1)S(1)}, u32[]{:S(2)}, u32[]{:S(2)}) collective-permute-start(bf16[2560,128]{1,0:T(8,128)(2,1)S(1)} %add_convert_fusion), channel_id=1, source_target_pairs={{0,1},{1,0},{2,3},{3,2},{4,5},{5,4},{6,7},{7,6},{8,9},{9,8},{10,11... | collective-permute-start | bytes 1966088 | tf_op jit(solution)/shard_map/ppermute | solution.py:144
  51.8 1.7 %copy-start = (bf16[64,192]{1,0:T(8,128)(2,1)S(1)}, bf16[64,192]{1,0:T(8,128)(2,1)}, u32[]{:S(2)}) copy-start(bf16[64,192]{1,0:T(8,128)(2,1)} %constant.27.clone.forward) | copy-start | bytes 73732
  89.3 7.4 %copy-start.1 = (bf16[64,192]{1,0:T(8,128)(2,1)S(1)}, bf16[64,192]{1,0:T(8,128)(2,1)}, u32[]{:S(2)}) copy-start(bf16[64,192]{1,0:T(8,128)(2,1)} %constant.28.clone.backward) | copy-start | bytes 73732
  90.3 27.9 %all-to-all-start.1 = ((bf16[64,40,128]{2,1,0:T(8,128)(2,1)}), bf16[64,40,128]{2,1,0:T(8,128)(2,1)S(1)}, u32[]{:S(2)}, u32[]{:S(2)}) async-start(bf16[64,40,128]{2,1,0:T(8,128)(2,1)} %total.1), calls=%async_computation.1 | async-start | bytes 1310720 | tf_op jit(solution)/shard_map/all_to_all | solution.py:214
  96.7 21.4 %copy-start.2 = (bf16[64,128]{1,0:T(8,128)(2,1)S(1)}, bf16[64,128]{1,0:T(8,128)(2,1)}, u32[]{:S(2)}) copy-start(bf16[64,128]{1,0:T(8,128)(2,1)} %constant.29.clone.backward) | copy-start | bytes 49156

commit v7 on v6

--- a/solution.py
+++ b/solution.py
@@ -12,6 +12,8 @@
 BLK = 32
 SPAN = 64
 WIDE = 4
+ROW_GROUPS = 4
+OWN_COLS = 8
 
 
 def cosine_parts():
@@ -48,24 +50,54 @@
         ref[first : first + SPAN, :] = value[:, s * cols : (s + 1) * cols].astype(ref.dtype)
 
 
-def mask_kernel(ids, count, mask):
-    shape = (SPAN, mask.shape[1])
-    block = lax.shift_right_logical(lax.broadcasted_iota(jnp.int32, shape, 0), 1)
-    first = lax.broadcasted_iota(jnp.int32, shape, 1) < SPAN
-    most = ids.shape[0] * SPAN // (2 * mask.shape[0])
+def routes_kernel(ids, count, base, mask, picks, numbers):
+    cols = mask.shape[1]
+    spans = mask.shape[0] // SPAN
+    most = ids.shape[0] // (2 * spans)
+    each = spans // ROW_GROUPS
+
+    def number(a, b, k):
+        return jnp.where(k < count[0], ids[(2 * a + b) * most + k], -1)
+
+    block = lax.shift_right_logical(lax.broadcasted_iota(jnp.int32, (SPAN, cols), 0), 1)
+    first = lax.broadcasted_iota(jnp.int32, (SPAN, cols), 1) < SPAN
 
     def body(a, _):
-        hit = jnp.zeros(shape, jnp.bool_)
+        hit = jnp.zeros((SPAN, cols), jnp.bool_)
         for k in range(most):
-            active = k < count[0]
-            one = jnp.where(active, ids[2 * most * a + k], -1)
-            two = jnp.where(active, ids[2 * most * a + most + k], -1)
-            hit = hit | (jnp.where(first, one, two) == block)
+            hit = hit | (jnp.where(first, number(a, 0, k), number(a, 1, k)) == block)
         rows = pl.ds(pl.multiple_of(a * SPAN, SPAN), SPAN)
         mask[rows, :] = hit.astype(jnp.float32).astype(mask.dtype)
         return 0
 
-    lax.fori_loop(0, mask.shape[0] // SPAN, body, 0)
+    lax.fori_loop(0, spans, body, 0)
+
+    lane = lax.broadcasted_iota(jnp.int32, (SPAN, cols), 1)
+    square = (cols, cols)
+    column = lax.broadcasted_iota(jnp.int32, square, 1)
+    slot = lax.shift_right_logical(lax.broadcasted_iota(jnp.int32, square, 0), 1)
+    double = (column == slot).astype(jnp.float32).astype(jnp.bfloat16)
+    place = column.astype(jnp.float32)
+    for g in range(ROW_GROUPS):
+        halves = []
+        for b in range(2):
+            line = jnp.full((SPAN, cols), -1, jnp.int32)
+            for a in range(each):
+                for k in range(most):
+                    line = jnp.where(lane == a * most + k, number(g * each + a, b, k), line)
+            halves.append(line)
+        tile = jnp.concatenate(halves, axis=0).astype(jnp.float32)
+        numbers[g * cols : (g + 1) * cols, :] = tile.astype(numbers.dtype)
+        twice = jnp.dot(
+            double, tile.T.astype(jnp.bfloat16), preferred_element_type=jnp.float32
+        )
+        for b in range(2):
+            own = jnp.broadcast_to(twice[:, b * SPAN : b * SPAN + 1], square)
+            target = jnp.where(own < 0.0, -1.0, base[...] + 2.0 * own)
+            for i in range(picks.shape[1] // cols):
+                picks[(2 * g + b) * cols : (2 * g + b + 1) * cols, i * cols : (i + 1) * cols] = (
+                    (target == place + float(i * cols)).astype(jnp.float32).astype(picks.dtype)
+                )
 
 
 def chosen_rows(x, mask, forward, i):
@@ -74,7 +106,7 @@
     return product(forward, [high, low, high]) * keep
 
 
-def spectrum_kernel(part, other, mask, forward, advanced, sent):
+def spectrum_kernel(part, other, picks, numbers, forward, advanced, sent, rows):
     for i in range(part.shape[0] // (SPAN * WIDE)):
         x = beside(
             [
@@ -83,7 +115,24 @@
             ]
         )
         put(advanced, i, WIDE, x)
-        put(sent, i, WIDE, chosen_rows(x, mask, forward, i))
+        high, low = split(x)
+        put(rows, i, WIDE, product(forward, [high, low, high]))
+    cols = part.shape[1]
+    height = picks.shape[1]
+    first = lax.broadcasted_iota(jnp.int32, (cols, cols), 1) < SPAN
+    for g in range(ROW_GROUPS):
+        band = rows[g * height : (g + 1) * height, :]
+        one, two = (
+            jnp.dot(
+                picks[(2 * g + b) * cols : (2 * g + b + 1) * cols, :],
+                band,
+                preferred_element_type=jnp.float32,
+            )
+            for b in range(2)
+        )
+        message = slice(g * cols, (g + 1) * cols)
+        sent[message, :cols] = jnp.where(first, one, two).T.astype(sent.dtype)
+        sent[message, cols:] = numbers[message, :]
 
 
 def kept_kernel(advanced, mask, forward, backward, kept):
@@ -93,19 +142,61 @@
         put(kept, i, WIDE, x - product(backward, [high, low, high]))
 
 
-def total_kernel(pieces, totals):
-    total = pieces[0].astype(jnp.float32)
-    for r in range(1, pieces.shape[0]):
-        total = total + pieces[r].astype(jnp.float32)
-    total = total.astype(totals.dtype)
-    for r in range(totals.shape[0]):
-        totals[r] = total
-
-
-def inverse_kernel(summed, backward, update):
-    for i in range(update.shape[0] // (SPAN * WIDE)):
-        s = beside(spans_of(summed, i, WIDE))
-        put(update, i, WIDE, product(backward, [s, s]))
+def total_kernel(pieces, backward, totals, placed):
+    wide = pieces.shape[1] // 2
+    spans = totals.shape[1] // SPAN
+    lane = lax.broadcasted_iota(jnp.int32, (BLK, wide), 0).astype(jnp.float32)
+    for t in range(pieces.shape[0] // wide):
+        values = pieces[t * wide : (t + 1) * wide, :wide].astype(jnp.float32).T
+        numbers = pieces[t * wide : (t + 1) * wide, wide:].astype(jnp.float32).T
+        most = wide // (2 * spans)
+        for a in range(spans):
+            upper = jnp.zeros((BLK, wide), jnp.float32)
+            lower = upper
+            for k in range(most):
+                at = a * most + k
+                here = numbers[at : at + 1, :] == lane
+                upper = jnp.where(here, values[2 * at : 2 * at + 1, :], upper)
+                lower = jnp.where(here, values[2 * at + 1 : 2 * at + 2, :], lower)
+            both = jnp.concatenate([upper, lower], axis=0)
+            placed[a * SPAN : (a + 1) * SPAN, t * wide : (t + 1) * wide] = both.astype(placed.dtype)
+    shape = (2 * OWN_COLS, placed.shape[1])
+    column = lax.broadcasted_iota(jnp.int32, shape, 1) & (OWN_COLS - 1)
+    row = lax.broadcasted_iota(jnp.int32, shape, 0) & (OWN_COLS - 1)
+    total = lax.dot_general(
+        (column == row).astype(jnp.float32).astype(placed.dtype),
+        placed[...],
+        (((1,), (1,)), ((), ())),
+        preferred_element_type=jnp.float32,
+    )
+    pair = 2 * SPAN
+    for i in range(totals.shape[1] // pair):
+        high, low = split(total[:, i * pair : (i + 1) * pair])
+        done = jnp.dot(
+            jnp.concatenate([high, low, high], axis=1),
+            backward[...],
+            preferred_element_type=jnp.float32,
+        ).astype(totals.dtype)
+        for r in range(totals.shape[0] // shape[0]):
+            totals[r * shape[0] : (r + 1) * shape[0], i * pair : (i + 1) * pair] = done
+
+
+def turn_kernel(turned, update):
+    cols, height = update.shape[1], turned.shape[1]
+    square = (cols, cols)
+    same = lax.broadcasted_iota(jnp.int32, square, 0) == lax.broadcasted_iota(
+        jnp.int32, square, 1
+    )
+    same = same.astype(jnp.float32).astype(turned.dtype)
+    for g in range(ROW_GROUPS):
+        for i in range(height // cols):
+            rows = g * height + i * cols
+            update[rows : rows + cols, :] = lax.dot_general(
+                same,
+                turned[g * cols : (g + 1) * cols, i * cols : (i + 1) * cols],
+                (((1,), (1,)), ((), ())),
+                preferred_element_type=jnp.float32,
+            ).astype(update.dtype)
 
 
 def gram(a, k):
@@ -115,13 +206,14 @@
 VMEM, SMEM = (pl.BlockSpec(memory_space=space) for space in (pltpu.VMEM, pltpu.SMEM))
 
 
-def call(kernel, name, outs, *args, places=None):
+def call(kernel, name, outs, *args, places=None, scratch=()):
     moved = sum(x.size * x.dtype.itemsize for x in args + outs)
     return pl.pallas_call(
         kernel,
         out_shape=outs,
         in_specs=places or [VMEM] * len(args),
         out_specs=(VMEM,) * len(outs),
+        scratch_shapes=scratch,
         compiler_params=pltpu.CompilerParams(vmem_limit_bytes=10 << 20),
         cost_estimate=pl.CostEstimate(
             flops=6 * 2 * SPAN * outs[0].size, bytes_accessed=moved, transcendentals=0
@@ -178,13 +270,26 @@
 
     flat = jax.ShapeDtypeStruct((features, cols), jnp.float32)
     flat_half = jax.ShapeDtypeStruct((features, cols), jnp.bfloat16)
-    (mask,) = call(
-        mask_kernel, "mask", (flat_half,), block_ids.reshape(-1), counts, places=[SMEM, SMEM]
-    )
-
-    (own_near, their_near, own_far, their_far, mask, far_head, far_tail) = (
+    height = features // ROW_GROUPS
+    lines = np.arange(cols)
+    base = SPAN * (lines // (2 * block_ids.shape[3])) + lines % 2
+    mask, picks, numbers = call(
+        routes_kernel,
+        "routes",
+        (
+            flat_half,
+            jax.ShapeDtypeStruct((2 * ROW_GROUPS * cols, height), jnp.bfloat16),
+            jax.ShapeDtypeStruct((ROW_GROUPS * cols, cols), jnp.bfloat16),
+        ),
+        block_ids.reshape(-1),
+        counts,
+        jnp.asarray(np.repeat(base[:, None], cols, axis=1).astype(np.float32)),
+        places=[SMEM, SMEM, VMEM],
+    )
+
+    (own_near, their_near, own_far, their_far, mask, picks, numbers, far_head, far_tail) = (
         lax.optimization_barrier(
-            (own_near, their_near, own_far, their_far, mask, far_head, far_tail)
+            (own_near, their_near, own_far, their_far, mask, picks, numbers, far_head, far_tail)
         )
     )
     other = swap(whole(their_near, their_far).astype(jnp.bfloat16))
@@ -193,26 +298,39 @@
     high, low = cosine_parts()
     forward = jnp.asarray(np.concatenate([high, high, low], axis=1))
     backward = jnp.asarray(np.concatenate([high.T, high.T, low.T], axis=1))
-    backward_once = jnp.asarray(np.concatenate([high.T, low.T], axis=1))
-
+    order = np.concatenate([np.arange(0, SPAN, 2), np.arange(1, SPAN, 2)])
+    both_high, both_low = (np.kron(np.eye(2, dtype=p.dtype), p[order]) for p in (high, low))
+    backward_pair = jnp.asarray(np.concatenate([both_high, both_high, both_low], axis=0))
+
+    message = jax.ShapeDtypeStruct((ROW_GROUPS * cols, 2 * cols), jnp.bfloat16)
     advanced, sent = call(
         spectrum_kernel,
         "spectrum",
-        (flat, flat_half),
+        (flat, message),
         part,
         other,
-        mask,
+        picks,
+        numbers,
         forward,
-    )
-    pieces = lax.all_to_all(
-        sent.reshape(replicas, features // replicas, cols), "dp", 0, 0, tiled=True
-    )
+        scratch=(pltpu.VMEM((features, cols), jnp.bfloat16),),
+    )
+
+    def exchange(x):
+        return lax.all_to_all(
+            x.reshape(replicas, OWN_COLS, x.shape[1]), "dp", 0, 0, tiled=True
+        ).reshape(x.shape)
+
+    pieces = exchange(sent)
     (kept,) = call(kept_kernel, "kept", (flat,), advanced, mask, forward, backward)
     (totals,) = call(
-        total_kernel, "total", (jax.ShapeDtypeStruct(pieces.shape, jnp.bfloat16),), pieces
-    )
-    summed = lax.all_to_all(totals, "dp", 0, 0, tiled=True).reshape(features, cols)
-    (update,) = call(inverse_kernel, "inverse", (flat_half,), summed, backward_once)
+        total_kernel,
+        "total",
+        (jax.ShapeDtypeStruct((replicas * OWN_COLS, height), jnp.bfloat16),),
+        pieces,
+        backward_pair,
+        scratch=(pltpu.VMEM((height, replicas * OWN_COLS), jnp.bfloat16),),
+    )
+    (update,) = call(turn_kernel, "turn", (flat_half,), exchange(totals))
     return kept[None], update
 
 

time: 120 us -> 113 us (0.942)
  blocking collectives: 35.2 us -> 28.9 us
  Pallas kernels: 7.55 us -> 10 us
  starting transfers between devices: 32.8 us -> 31 us
    all_to_all x1, blocking collectives: 35.2 us -> 28.9 us  [exchange(): lax.all_to_all(x.reshape(replicas, OWN_COLS, x.shape[1]), 'dp', 0, 0, til...]
    pallas_call x5, Pallas kernels: 7.55 us -> 10 us  [call(): pl.pallas_call(kernel, out_shape=outs, in_specs=places or [VMEM] * len(ar...]
    all_to_all x1, starting transfers between devices: 6.4 us -> 4.64 us  [exchange(): lax.all_to_all(x.reshape(replicas, OWN_COLS, x.shape[1]), 'dp', 0, 0, til...]
  transfers between devices with their start and end apart: 9 -> 9, of which waited for: 6 -> 6; matrix products, arithmetic and copies ran while one was open for 6% -> 6% of each run, Pallas kernels for 4% -> 5%
where the time goes in v7:
time: 113 us
  starting transfers between devices  31 us (27%)
  waiting for transfers between devices  30.2 us (27%)
  blocking collectives  28.9 us (26%)
  Pallas kernels  10 us (9%)
  matrix products  6.52 us (6%)
  local copies, waits for them, and re-layouts  3.84 us (3%)
  between operations  1.6 us (1%)
    all_to_all x1, blocking collectives, exchange(): lax.all_to_all(x.reshape(replicas, OWN_COLS, x.shape[1]), 'dp', 0, 0, til...  28.9 us
    ppermute x6, starting transfers between devices, along(): lax.ppermute(x, 'tensor', [(i, (i + 2 * step) % group) for i in range(gro...  22.6 us
    all_to_all x1, waiting for transfers between devices, exchange(): lax.all_to_all(x.reshape(replicas, OWN_COLS, x.shape[1]), 'dp', 0, 0, til...  18.1 us
    ppermute x6, waiting for transfers between devices, along(): lax.ppermute(x, 'tensor', [(i, (i + 2 * step) % group) for i in range(gro...  10.8 us
    pallas_call x5, Pallas kernels, call(): pl.pallas_call(kernel, out_shape=outs, in_specs=places or [VMEM] * len(ar...  10 us
    dot_general x9, matrix products, gram(): lax.dot_general(a, k, (((0,), (0,)), ((), ())), preferred_element_type=jn...  6.52 us
    all_to_all x1, starting transfers between devices, exchange(): lax.all_to_all(x.reshape(replicas, OWN_COLS, x.shape[1]), 'dp', 0, 0, til...  4.64 us
    ppermute x2, starting transfers between devices, swap(): return lax.ppermute(x, 'tensor', [(i, i ^ 1) for i in range(group)])  3.84 us
  transfers between devices with their start and end apart: 9, of which 6 were waited for; matrix products, arithmetic and copies ran while one was open for 6% of the time, Pallas kernels for 5%

profile of v7, /device:TPU:6, one launch (start us, length us, event | category | flops | bytes accessed | tf_op | source)
XLA Modules:
  0.0 112.6 jit_solution(7032101577904181598)
XLA Ops:
  0.6 0.0 copy-start.3
  0.6 0.0 copy-start.4
  0.7 2.1 %slice.64 = bf16[128,2560]{1,0:T(8,128)(2,1)} slice(bf16[208,2560]{1,0:T(8,128)(2,1)} %param.9), slice={[80:208], [0:2560]} | slice | bytes 1310720 | tf_op jit(solution)/shard_map/slice | solution.py:239
  2.8 2.7 %collective-permute-start.1 = (bf16[128,2560]{1,0:T(8,128)(2,1)}, bf16[128,2560]{1,0:T(8,128)(2,1)S(1)}, u32[]{:S(2)}, u32[]{:S(2)}) collective-permute-start(bf16[128,2560]{1,0:T(8,128)(2,1)} %slice.64), channel_id=1, source_target_pairs={{0,6},{1,7},{2,0},{3,1},{4,2},{5,3},{6,4},{7,5},{8,14},{9,15},{10,... | collective-permute-start | bytes 1966088 | tf_op jit(solution)/shard_map/ppermute | solution.py:233
  5.5 0.8 slice.63
  6.3 6.9 %collective-permute-start = (bf16[80,2560]{1,0:T(8,128)(2,1)}, bf16[80,2560]{1,0:T(8,128)(2,1)S(1)}, u32[]{:S(2)}, u32[]{:S(2)}) collective-permute-start(bf16[80,2560]{1,0:T(8,128)(2,1)} %slice.63), channel_id=1, source_target_pairs={{0,2},{1,3},{2,4},{3,5},{4,6},{5,7},{6,0},{7,1},{8,10},{9,11},{10,... | collective-permute-start | bytes 1228808 | tf_op jit(solution)/shard_map/ppermute | solution.py:233
  13.2 3.9 %collective-permute-start.3 = (bf16[128,2560]{1,0:T(8,128)(2,1)}, bf16[128,2560]{1,0:T(8,128)(2,1)}, u32[]{:S(2)}, u32[]{:S(2)}) collective-permute-start(bf16[128,2560]{1,0:T(8,128)(2,1)} %slice.64), channel_id=1, source_target_pairs={{0,2},{1,3},{2,4},{3,5},{4,6},{5,7},{6,0},{7,1},{8,10},{9,11},{10,... | collective-permute-start | bytes 1966088 | tf_op jit(solution)/shard_map/ppermute | solution.py:233
  17.1 1.9 %collective-permute-start.4 = (bf16[80,2560]{1,0:T(8,128)(2,1)}, bf16[80,2560]{1,0:T(8,128)(2,1)}, u32[]{:S(2)}, u32[]{:S(2)}) collective-permute-start(bf16[80,2560]{1,0:T(8,128)(2,1)} %slice.63), channel_id=1, source_target_pairs={{0,6},{1,7},{2,0},{3,1},{4,2},{5,3},{6,4},{7,5},{8,14},{9,15},{10,... | collective-permute-start | bytes 1228808 | tf_op jit(solution)/shard_map/ppermute | solution.py:233
  19.1 0.1 copy.15
  19.2 0.1 reshape.29.ids
  20.0 2.6 %routes.1 = (bf16[2560,128]{1,0:T(8,128)(2,1)S(1)}, bf16[1024,640]{1,0:T(8,128)(2,1)S(1)}, bf16[512,128]{1,0:T(8,128)(2,1)S(1)}) custom-call(s32[480]{0:T(512)S(1)} %reshape.29.ids, s32[1]{0:T(128)S(6)} %copy.18.count, f32[128,128]{1,0:T(8,128)S(1)} %copy-done.3), custom_call_target="tpu_custom_call" | custom-call | flops 251658240 | bytes 2164612 | tf_op jit(solution)/shard_map/routes/pallas_call | solution.py:211
  22.7 0.8 collective-permute-done
  23.4 2.9 %collective-permute-done.1 = bf16[128,2560]{1,0:T(8,128)(2,1)S(1)} collective-permute-done((bf16[128,2560]{1,0:T(8,128)(2,1)}, bf16[128,2560]{1,0:T(8,128)(2,1)S(1)}, u32[]{:S(2)}, u32[]{:S(2)}) %collective-permute-start.1) | collective-permute-done | bytes 655392 | tf_op jit(solution)/shard_map/ppermute | solution.py:233
  26.4 0.1 fusion.2
  26.5 1.9 %collective-permute-start.2 = (bf16[4,208,128]{2,1,0:T(8,128)(2,1)S(1)}, bf16[4,208,128]{2,1,0:T(8,128)(2,1)S(1)}, u32[]{:S(2)}, u32[]{:S(2)}) collective-permute-start(bf16[4,208,128]{2,1,0:T(8,128)(2,1)S(1)} %fusion.2), channel_id=1, source_target_pairs={{0,1},{1,0},{2,3},{3,2},{4,5},{5,4},{6,7},{7,6},{8,9},{9,8},{10,11... | collective-permute-start | bytes 638984 | tf_op jit(solution)/shard_map/ppermute | solution.py:236
  28.4 0.1 fusion.3
  28.5 1.9 %collective-permute-start.6 = (bf16[128,2560]{1,0:T(8,128)(2,1)S(1)}, bf16[128,2560]{1,0:T(8,128)(2,1)S(1)}, u32[]{:S(2)}, u32[]{:S(2)}) collective-permute-start(bf16[128,2560]{1,0:T(8,128)(2,1)S(1)} %collective-permute-done.1), channel_id=1, source_target_pairs={{0,6},{1,7},{2,0},{3,1},{4,2},{5,3},{6,4},{7,5},{8,14},{9,15},{10,... | collective-permute-start | bytes 1966088 | tf_op jit(solution)/shard_map/ppermute | solution.py:233
  30.5 5.1 %collective-permute-start.5 = (bf16[80,2560]{1,0:T(8,128)(2,1)S(1)}, bf16[80,2560]{1,0:T(8,128)(2,1)S(1)}, u32[]{:S(2)}, u32[]{:S(2)}) collective-permute-start(bf16[80,2560]{1,0:T(8,128)(2,1)S(1)} %collective-permute-done), channel_id=1, source_target_pairs={{0,2},{1,3},{2,4},{3,5},{4,6},{5,7},{6,0},{7,1},{8,10},{9,11},{10,... | collective-permute-start | bytes 1228808 | tf_op jit(solution)/shard_map/ppermute | solution.py:233
  35.6 0.0 collective-permute-done.2
  35.6 0.1 pad_maximum_fusion
  35.7 0.5 fusion.4
  36.2 0.0 collective-permute-done.3
  36.2 1.6 %convolution_bitcast_fusion.1 = f32[2560,256]{1,0:T(8,128)S(1)} fusion(bf16[128,2560]{1,0:T(8,128)(2,1)} %collective-permute-done.3, bf16[4,208,256]{2,1,0:T(8,128)(2,1)S(1)} %pad_maximum_fusion), kind=kOutput, calls=%fused_computation.5 | convolution fusion | flops 167772160 | bytes 3342336 | tf_op jit(solution)/shard_map/dot_general | solution.py:203
  37.9 0.6 fusion.1
  38.5 0.0 collective-permute-done.4
  38.5 1.6 %convolution_bitcast_fusion = f32[2560,256]{1,0:T(8,128)S(1)} fusion(bf16[80,2560]{1,0:T(8,128)(2,1)} %collective-permute-done.4, bf16[4,208,256]{2,1,0:T(8,128)(2,1)S(1)} %pad_maximum_fusion), kind=kOutput, calls=%fused_computation.4 | convolution fusion | flops 104857600 | bytes 3072000 | tf_op jit(solution)/shard_map/dot_general | solution.py:203
  40.1 0.0 copy-start.5
  40.1 0.7 fusion
  40.7 0.6 copy-done.5
  41.4 0.2 fusion.17
  41.6 3.1 %collective-permute-done.5 = bf16[80,2560]{1,0:T(8,128)(2,1)S(1)} collective-permute-done((bf16[80,2560]{1,0:T(8,128)(2,1)S(1)}, bf16[80,2560]{1,0:T(8,128)(2,1)S(1)}, u32[]{:S(2)}, u32[]{:S(2)}) %collective-permute-start.5) | collective-permute-done | bytes 409632 | tf_op jit(solution)/shard_map/ppermute | solution.py:233
  44.7 4.1 %collective-permute-done.6 = bf16[128,2560]{1,0:T(8,128)(2,1)S(1)} collective-permute-done((bf16[128,2560]{1,0:T(8,128)(2,1)S(1)}, bf16[128,2560]{1,0:T(8,128)(2,1)S(1)}, u32[]{:S(2)}, u32[]{:S(2)}) %collective-permute-start.6) | collective-permute-done | bytes 655392 | tf_op jit(solution)/shard_map/ppermute | solution.py:233
  48.8 0.4 fusion.13
  49.1 0.4 add_convert_fusion
  49.6 1.9 %collective-permute-start.7 = (bf16[2560,128]{1,0:T(8,128)(2,1)S(1)}, bf16[2560,128]{1,0:T(8,128)(2,1)S(1)}, u32[]{:S(2)}, u32[]{:S(2)}) collective-permute-start(bf16[2560,128]{1,0:T(8,128)(2,1)S(1)} %add_convert_fusion), channel_id=1, source_target_pairs={{0,1},{1,0},{2,3},{3,2},{4,5},{5,4},{6,7},{7,6},{8,9},{9,8},{10,11... | collective-permute-start | bytes 1966088 | tf_op jit(solution)/shard_map/ppermute | solution.py:236
  51.5 0.4 fusion.15
  51.9 0.0 copy-start
  51.9 0.4 add_add_fusion.part
  52.3 0.0 copy-start.1
  52.3 1.3 %collective-permute-done.7.other = bf16[2560,128]{1,0:T(8,128)(2,1)S(1)} collective-permute-done((bf16[2560,128]{1,0:T(8,128)(2,1)S(1)}, bf16[2560,128]{1,0:T(8,128)(2,1)S(1)}, u32[]{:S(2)}, u32[]{:S(2)}) %collective-permute-start.7) | collective-permute-done | bytes 655392 | tf_op jit(solution)/shard_map/ppermute | solution.py:236
  53.5 1.0 spectrum.1
  54.5 0.0 copy-start.2
  54.6 28.9 %all_to_all.10 = bf16[64,8,256]{2,1,0:T(8,128)(2,1)S(1)} all-to-all(bf16[64,8,256]{2,1,0:T(8,128)(2,1)S(1)} %bitcast.46), channel_id=1, replica_groups=mesh['dp'=64,'tensor'=8] {'dp'}, dimensions={0} | all-to-all | bytes 524288 | tf_op jit(solution)/shard_map/all_to_all | solution.py:319
  83.5 1.9 %total.1 = bf16[512,640]{1,0:T(8,128)(2,1)} custom-call(bf16[512,256]{1,0:T(8,128)(2,1)S(1)} %bitcast.45, bf16[384,128]{1,0:T(8,128)(2,1)S(1)} %copy-done.1), custom_call_target="tpu_custom_call" | custom-call | flops 251658240 | bytes 1015808 | tf_op jit(solution)/shard_map/total/pallas_call | solution.py:211
  85.4 4.6 %all-to-all-start.1 = ((bf16[64,8,640]{2,1,0:T(8,128)(2,1)}), bf16[64,8,640]{2,1,0:T(8,128)(2,1)S(1)}, u32[]{:S(2)}, u32[]{:S(2)}) async-start(bf16[64,8,640]{2,1,0:T(8,128)(2,1)} %bitcast.16), calls=%async_computation.1 | async-start | bytes 1310720 | tf_op jit(solution)/shard_map/all_to_all | solution.py:319
  90.1 3.1 %kept.1 = f32[2560,128]{1,0:T(8,128)} custom-call(f32[2560,128]{1,0:T(8,128)S(1)} %get-tuple-element.37.advanced, bf16[2560,128]{1,0:T(8,128)(2,1)S(1)} %get-tuple-element.38.mask, bf16[64,192]{1,0:T(8,128)(2,1)S(1)} %copy-done, bf16[64,192]{1,0:T(8,128)(2,1)S(1)} %copy-done.2), custom_call_target="tpu_custom_call" | custom-call | flops 251658240 | bytes 3325952 | tf_op jit(solution)/shard_map/kept/pallas_call | solution.py:211
  93.1 18.1 %all-to-all-done.1 = bf16[64,8,640]{2,1,0:T(8,128)(2,1)S(1)} async-done(((bf16[64,8,640]{2,1,0:T(8,128)(2,1)}), bf16[64,8,640]{2,1,0:T(8,128)(2,1)S(1)}, u32[]{:S(2)}, u32[]{:S(2)}) %all-to-all-start.1) | async-done | bytes 655392 | tf_op jit(solution)/shard_map/all_to_all | solution.py:319
  111.2 1.4 %turn.1 = bf16[2560,128]{1,0:T(8,128)(2,1)} custom-call(bf16[512,640]{1,0:T(8,128)(2,1)S(1)} %bitcast.44), custom_call_target="tpu_custom_call" | custom-call | flops 251658240 | bytes 1310720 | tf_op jit(solution)/shard_map/turn/pallas_call | solution.py:211
  (12 shorter events, 0.1 us)
Async XLA Ops:
  0.6 19.4 %copy-start.3 = (f32[128,128]{1,0:T(8,128)S(1)}, f32[128,128]{1,0:T(8,128)}, u32[]{:S(2)}) copy-start(f32[128,128]{1,0:T(8,128)} %constant.29.clone.base) | copy-start | bytes 196612
  0.6 4.8 %copy-start.4 = (bf16[208,2560]{1,0:T(8,128)(2,1)S(1)}, bf16[208,2560]{1,0:T(8,128)(2,1)}, u32[]{:S(2)}) copy-start(bf16[208,2560]{1,0:T(8,128)(2,1)} %param.9) | copy-start | bytes 3194884
  0.7 18.4 %copy-start.7 = (s32[1,40,2,6]{1,2,3,0:T(2,128)S(1)}, s32[1,40,2,6]{1,2,3,0:T(2,128)}, u32[]{:S(2)}) copy-start(s32[1,40,2,6]{1,2,3,0:T(2,128)} %param.12) | copy-start | bytes 5764
  0.7 25.7 %copy-start.6 = (bf16[1664,128]{1,0:T(8,128)(2,1)S(1)}, bf16[1664,128]{1,0:T(8,128)(2,1)}, u32[]{:S(2)}) copy-start(bf16[1664,128]{1,0:T(8,128)(2,1)} %param.10) | copy-start | bytes 1277956
  2.8 23.6 %collective-permute-start.1 = (bf16[128,2560]{1,0:T(8,128)(2,1)}, bf16[128,2560]{1,0:T(8,128)(2,1)S(1)}, u32[]{:S(2)}, u32[]{:S(2)}) collective-permute-start(bf16[128,2560]{1,0:T(8,128)(2,1)} %slice.64), channel_id=1, source_target_pairs={{0,6},{1,7},{2,0},{3,1},{4,2},{5,3},{6,4},{7,5},{8,14},{9,15},{10,... | collective-permute-start | bytes 1966088 | tf_op jit(solution)/shard_map/ppermute | solution.py:233
  6.3 17.2 %collective-permute-start = (bf16[80,2560]{1,0:T(8,128)(2,1)}, bf16[80,2560]{1,0:T(8,128)(2,1)S(1)}, u32[]{:S(2)}, u32[]{:S(2)}) collective-permute-start(bf16[80,2560]{1,0:T(8,128)(2,1)} %slice.63), channel_id=1, source_target_pairs={{0,2},{1,3},{2,4},{3,5},{4,6},{5,7},{6,0},{7,1},{8,10},{9,11},{10,... | collective-permute-start | bytes 1228808 | tf_op jit(solution)/shard_map/ppermute | solution.py:233
  13.2 23.0 %collective-permute-start.3 = (bf16[128,2560]{1,0:T(8,128)(2,1)}, bf16[128,2560]{1,0:T(8,128)(2,1)}, u32[]{:S(2)}, u32[]{:S(2)}) collective-permute-start(bf16[128,2560]{1,0:T(8,128)(2,1)} %slice.64), channel_id=1, source_target_pairs={{0,2},{1,3},{2,4},{3,5},{4,6},{5,7},{6,0},{7,1},{8,10},{9,11},{10,... | collective-permute-start | bytes 1966088 | tf_op jit(solution)/shard_map/ppermute | solution.py:233
  17.1 21.4 %collective-permute-start.4 = (bf16[80,2560]{1,0:T(8,128)(2,1)}, bf16[80,2560]{1,0:T(8,128)(2,1)}, u32[]{:S(2)}, u32[]{:S(2)}) collective-permute-start(bf16[80,2560]{1,0:T(8,128)(2,1)} %slice.63), channel_id=1, source_target_pairs={{0,6},{1,7},{2,0},{3,1},{4,2},{5,3},{6,4},{7,5},{8,14},{9,15},{10,... | collective-permute-start | bytes 1228808 | tf_op jit(solution)/shard_map/ppermute | solution.py:233
  26.5 9.1 %collective-permute-start.2 = (bf16[4,208,128]{2,1,0:T(8,128)(2,1)S(1)}, bf16[4,208,128]{2,1,0:T(8,128)(2,1)S(1)}, u32[]{:S(2)}, u32[]{:S(2)}) collective-permute-start(bf16[4,208,128]{2,1,0:T(8,128)(2,1)S(1)} %fusion.2), channel_id=1, source_target_pairs={{0,1},{1,0},{2,3},{3,2},{4,5},{5,4},{6,7},{7,6},{8,9},{9,8},{10,11... | collective-permute-start | bytes 638984 | tf_op jit(solution)/shard_map/ppermute | solution.py:236
  28.5 20.2 %collective-permute-start.6 = (bf16[128,2560]{1,0:T(8,128)(2,1)S(1)}, bf16[128,2560]{1,0:T(8,128)(2,1)S(1)}, u32[]{:S(2)}, u32[]{:S(2)}) collective-permute-start(bf16[128,2560]{1,0:T(8,128)(2,1)S(1)} %collective-permute-done.1), channel_id=1, source_target_pairs={{0,6},{1,7},{2,0},{3,1},{4,2},{5,3},{6,4},{7,5},{8,14},{9,15},{10,... | collective-permute-start | bytes 1966088 | tf_op jit(solution)/shard_map/ppermute | solution.py:233
  30.5 14.2 %collective-permute-start.5 = (bf16[80,2560]{1,0:T(8,128)(2,1)S(1)}, bf16[80,2560]{1,0:T(8,128)(2,1)S(1)}, u32[]{:S(2)}, u32[]{:S(2)}) collective-permute-start(bf16[80,2560]{1,0:T(8,128)(2,1)S(1)} %collective-permute-done), channel_id=1, source_target_pairs={{0,2},{1,3},{2,4},{3,5},{4,6},{5,7},{6,0},{7,1},{8,10},{9,11},{10,... | collective-permute-start | bytes 1228808 | tf_op jit(solution)/shard_map/ppermute | solution.py:233
  40.1 1.3 %copy-start.5 = (f32[1,2560,128]{2,1,0:T(8,128)S(1)}, f32[1,2560,128]{2,1,0:T(8,128)}, u32[]{:S(2)}) copy-start(f32[1,2560,128]{2,1,0:T(8,128)} %param.11) | copy-start | bytes 3932164
  49.6 4.0 %collective-permute-start.7 = (bf16[2560,128]{1,0:T(8,128)(2,1)S(1)}, bf16[2560,128]{1,0:T(8,128)(2,1)S(1)}, u32[]{:S(2)}, u32[]{:S(2)}) collective-permute-start(bf16[2560,128]{1,0:T(8,128)(2,1)S(1)} %add_convert_fusion), channel_id=1, source_target_pairs={{0,1},{1,0},{2,3},{3,2},{4,5},{5,4},{6,7},{7,6},{8,9},{9,8},{10,11... | collective-permute-start | bytes 1966088 | tf_op jit(solution)/shard_map/ppermute | solution.py:236
  51.9 1.7 %copy-start = (bf16[64,192]{1,0:T(8,128)(2,1)S(1)}, bf16[64,192]{1,0:T(8,128)(2,1)}, u32[]{:S(2)}) copy-start(bf16[64,192]{1,0:T(8,128)(2,1)} %constant.30.clone.forward) | copy-start | bytes 73732
  52.3 31.2 %copy-start.1 = (bf16[384,128]{1,0:T(8,128)(2,1)S(1)}, bf16[384,128]{1,0:T(8,128)(2,1)}, u32[]{:S(2)}) copy-start(bf16[384,128]{1,0:T(8,128)(2,1)} %constant.32.clone.backward) | copy-start | bytes 294916
  54.5 35.5 %copy-start.2 = (bf16[64,192]{1,0:T(8,128)(2,1)S(1)}, bf16[64,192]{1,0:T(8,128)(2,1)}, u32[]{:S(2)}) copy-start(bf16[64,192]{1,0:T(8,128)(2,1)} %constant.31.clone.backward) | copy-start | bytes 73732
  85.4 25.8 %all-to-all-start.1 = ((bf16[64,8,640]{2,1,0:T(8,128)(2,1)}), bf16[64,8,640]{2,1,0:T(8,128)(2,1)S(1)}, u32[]{:S(2)}, u32[]{:S(2)}) async-start(bf16[64,8,640]{2,1,0:T(8,128)(2,1)} %bitcast.16), calls=%async_computation.1 | async-start | bytes 1310720 | tf_op jit(solution)/shard_map/all_to_all | solution.py:319

commit v8 on v7

--- a/solution.py
+++ b/solution.py
@@ -50,14 +50,24 @@
         ref[first : first + SPAN, :] = value[:, s * cols : (s + 1) * cols].astype(ref.dtype)
 
 
+def keys_kernel(chips, tokens, keys, own, partner):
+    spot = lax.axis_index("tensor")
+    chip, core = lax.shift_right_logical(spot, 1), lax.bitwise_and(spot, 1)
+    for step in range(chips):
+        pair = 2 * lax.bitwise_and(chip + step, chips - 1)
+        here = slice(step * tokens, (step + 1) * tokens)
+        own[here, :] = keys[pl.ds(pl.multiple_of((pair + core) * tokens, 16), tokens), :]
+        partner[here, :] = keys[pl.ds(pl.multiple_of((pair + 1 - core) * tokens, 16), tokens), :]
+
+
 def routes_kernel(ids, count, base, mask, picks, numbers):
     cols = mask.shape[1]
     spans = mask.shape[0] // SPAN
-    most = ids.shape[0] // (2 * spans)
+    most = ids.shape[0]
     each = spans // ROW_GROUPS
 
     def number(a, b, k):
-        return jnp.where(k < count[0], ids[(2 * a + b) * most + k], -1)
+        return jnp.where(k < count[0], ids[k, b, a], -1)
 
     block = lax.shift_right_logical(lax.broadcasted_iota(jnp.int32, (SPAN, cols), 0), 1)
     first = lax.broadcasted_iota(jnp.int32, (SPAN, cols), 1) < SPAN
@@ -207,7 +217,6 @@
 
 
 def call(kernel, name, outs, *args, places=None, scratch=()):
-    moved = sum(x.size * x.dtype.itemsize for x in args + outs)
     return pl.pallas_call(
         kernel,
         out_shape=outs,
@@ -215,9 +224,7 @@
         out_specs=(VMEM,) * len(outs),
         scratch_shapes=scratch,
         compiler_params=pltpu.CompilerParams(vmem_limit_bytes=10 << 20),
-        cost_estimate=pl.CostEstimate(
-            flops=6 * 2 * SPAN * outs[0].size, bytes_accessed=moved, transcendentals=0
-        ),
+        cost_estimate=pl.CostEstimate(flops=0, bytes_accessed=0, transcendentals=0),
         name=name,
     )(*args)
 
@@ -226,8 +233,6 @@
     tokens, features = activations.shape
     cols = key_grad.shape[1]
     chips = group // 2
-    spot = lax.axis_index("tensor")
-    chip, core = lax.shift_right_logical(spot, 1), lax.bitwise_and(spot, 1)
 
     def along(x, step):
         return lax.ppermute(x, "tensor", [(i, (i + 2 * step) % group) for i in range(group)])
@@ -238,20 +243,24 @@
     cut = tokens * 2 // 5 // 16 * 16
     head, tail = activations[:cut], activations[cut:]
     left_head, right_tail = along(head, 1), along(tail, -1)
+
+    rows = jax.ShapeDtypeStruct((chips * tokens, cols), jnp.bfloat16)
+    own_keys, sent_keys = call(
+        functools.partial(keys_kernel, chips, tokens), "keys", (rows, rows), key_grad
+    )
+
+    head, tail, own_keys, sent_keys, block_ids, counts = lax.optimization_barrier(
+        (head, tail, own_keys, sent_keys, block_ids, counts)
+    )
     left_tail, right_head = along(tail, 1), along(head, -1)
-
-    left_head, right_tail, block, key_grad, momentum = lax.optimization_barrier(
-        (left_head, right_tail, activations, key_grad, momentum)
+    their_keys = swap(sent_keys)
+
+    left_head, right_tail, block, own_keys, momentum = lax.optimization_barrier(
+        (left_head, right_tail, activations, own_keys, momentum)
     )
     far_head, far_tail = along(left_head, 1), along(right_tail, -1)
-
-    by_core = key_grad.reshape(chips, 2, tokens, cols)
-
-    def keys_for(which):
-        rows = lax.dynamic_index_in_dim(by_core, which, 1, keepdims=False)
-        return lax.dynamic_slice_in_dim(jnp.concatenate([rows, rows]), chip, chips, 0)
-
-    own_keys, their_keys = keys_for(core), swap(keys_for(1 - core))
+    own_keys = own_keys.reshape(chips, tokens, cols)
+    their_keys = their_keys.reshape(chips, tokens, cols)
     keys = lax.optimization_barrier(jnp.concatenate([own_keys, their_keys], axis=2))
     before, after = keys[chips - 1], keys[1]
     near = (
@@ -281,7 +290,7 @@
             jax.ShapeDtypeStruct((2 * ROW_GROUPS * cols, height), jnp.bfloat16),
             jax.ShapeDtypeStruct((ROW_GROUPS * cols, cols), jnp.bfloat16),
         ),
-        block_ids.reshape(-1),
+        jnp.transpose(block_ids[0], (2, 1, 0)),
         counts,
         jnp.asarray(np.repeat(base[:, None], cols, axis=1).astype(np.float32)),
         places=[SMEM, SMEM, VMEM],

time: 113 us -> 111 us (0.982)
  waiting for transfers between devices: 30.2 us -> 32.5 us
  matrix products: 6.52 us -> 4.46 us
  local copies, waits for them, and re-layouts: 3.84 us -> 1.8 us
    ppermute x6, waiting for transfers between devices: 10.8 us -> 13.1 us  [along(): lax.ppermute(x, 'tensor', [(i, (i + 2 * step) % group) for i in range(gro...]
    dot_general x9, matrix products: 6.52 us -> 4.46 us  [gram(): lax.dot_general(a, k, (((0,), (0,)), ((), ())), preferred_element_type=jn...]
    slice x2, local copies, waits for them, and re-layouts: 2.86 us -> 1.27 us  [shards(): head, tail = (activations[:cut], activations[cut:])]
    pallas_call x5 -> x6, Pallas kernels: 10 us -> 10.2 us  [call(): pl.pallas_call(kernel, out_shape=outs, in_specs=places or [VMEM] * len(ar...]
  transfers between devices with their start and end apart: 9 -> 9, of which waited for: 6 -> 5; matrix products, arithmetic and copies ran while one was open for 6% -> 4% of each run, Pallas kernels for 5% -> 5%
where the time goes in v8:
time: 111 us
  waiting for transfers between devices  32.5 us (29%)
  starting transfers between devices  31.1 us (28%)
  blocking collectives  29 us (26%)
  Pallas kernels  10.2 us (9%)
  matrix products  4.46 us (4%)
  local copies, waits for them, and re-layouts  1.8 us (2%)
  between operations  1.59 us (1%)
    all_to_all x1, blocking collectives, exchange(): lax.all_to_all(x.reshape(replicas, OWN_COLS, x.shape[1]), 'dp', 0, 0, til...  29 us
    ppermute x6, starting transfers between devices, along(): lax.ppermute(x, 'tensor', [(i, (i + 2 * step) % group) for i in range(gro...  22.6 us
    all_to_all x1, waiting for transfers between devices, exchange(): lax.all_to_all(x.reshape(replicas, OWN_COLS, x.shape[1]), 'dp', 0, 0, til...  18.1 us
    ppermute x6, waiting for transfers between devices, along(): lax.ppermute(x, 'tensor', [(i, (i + 2 * step) % group) for i in range(gro...  13.1 us
    pallas_call x6, Pallas kernels, call(): pl.pallas_call(kernel, out_shape=outs, in_specs=places or [VMEM] * len(ar...  10.2 us
    all_to_all x1, starting transfers between devices, exchange(): lax.all_to_all(x.reshape(replicas, OWN_COLS, x.shape[1]), 'dp', 0, 0, til...  4.64 us
    dot_general x9, matrix products, gram(): lax.dot_general(a, k, (((0,), (0,)), ((), ())), preferred_element_type=jn...  4.46 us
    ppermute x2, starting transfers between devices, swap(): return lax.ppermute(x, 'tensor', [(i, i ^ 1) for i in range(group)])  3.84 us
  transfers between devices with their start and end apart: 9, of which 5 were waited for; matrix products, arithmetic and copies ran while one was open for 4% of the time, Pallas kernels for 5%

profile of v8, /device:TPU:6, one launch (start us, length us, event | category | flops | bytes accessed | tf_op | source)
XLA Modules:
  0.0 110.9 jit_solution(5760661096952864473)
XLA Ops:
  0.6 0.0 copy-start.3
  0.6 0.0 copy-start.6
  0.7 0.0 copy-start
  0.7 0.0 copy-start.5
  0.7 1.2 %slice.66 = bf16[128,2560]{1,0:T(8,128)(2,1)S(1)} slice(bf16[208,2560]{1,0:T(8,128)(2,1)} %param.9), slice={[80:208], [0:2560]} | slice | bytes 1310720 | tf_op jit(solution)/shard_map/slice | solution.py:244
  1.9 2.7 %collective-permute-start.1 = (bf16[128,2560]{1,0:T(8,128)(2,1)S(1)}, bf16[128,2560]{1,0:T(8,128)(2,1)S(1)}, u32[]{:S(2)}, u32[]{:S(2)}) collective-permute-start(bf16[128,2560]{1,0:T(8,128)(2,1)S(1)} %slice.66), channel_id=1, source_target_pairs={{0,6},{1,7},{2,0},{3,1},{4,2},{5,3},{6,4},{7,5},{8,14},{9,15},{10,... | collective-permute-start | bytes 1966088 | tf_op jit(solution)/shard_map/ppermute | solution.py:238
  4.7 0.0 copy-done.6
  4.7 6.9 %collective-permute-start = (bf16[80,2560]{1,0:T(8,128)(2,1)S(1)}, bf16[80,2560]{1,0:T(8,128)(2,1)S(1)}, u32[]{:S(2)}, u32[]{:S(2)}) collective-permute-start(bf16[80,2560]{1,0:T(8,128)(2,1)S(1)} %slice.65), channel_id=1, source_target_pairs={{0,2},{1,3},{2,4},{3,5},{4,6},{5,7},{6,0},{7,1},{8,10},{9,11},{10,... | collective-permute-start | bytes 1228808 | tf_op jit(solution)/shard_map/ppermute | solution.py:238
  11.7 0.0 copy-done
  11.7 1.9 %collective-permute-start.2 = (bf16[832,128]{1,0:T(8,128)(2,1)S(1)}, bf16[832,128]{1,0:T(8,128)(2,1)S(1)}, u32[]{:S(2)}, u32[]{:S(2)}) collective-permute-start(bf16[832,128]{1,0:T(8,128)(2,1)S(1)} %get-tuple-element.34), channel_id=1, source_target_pairs={{0,1},{1,0},{2,3},{3,2},{4,5},{5,4},{6,7},{7,6},{8,9},{9,8},{10,11... | collective-permute-start | bytes 638984 | tf_op jit(solution)/shard_map/ppermute | solution.py:241
  13.7 1.9 %collective-permute-start.4 = (bf16[80,2560]{1,0:T(8,128)(2,1)S(1)}, bf16[80,2560]{1,0:T(8,128)(2,1)S(1)}, u32[]{:S(2)}, u32[]{:S(2)}) collective-permute-start(bf16[80,2560]{1,0:T(8,128)(2,1)S(1)} %slice.65), channel_id=1, source_target_pairs={{0,6},{1,7},{2,0},{3,1},{4,2},{5,3},{6,4},{7,5},{8,14},{9,15},{10,... | collective-permute-start | bytes 1228808 | tf_op jit(solution)/shard_map/ppermute | solution.py:238
  15.6 5.1 %collective-permute-start.3 = (bf16[128,2560]{1,0:T(8,128)(2,1)S(1)}, bf16[128,2560]{1,0:T(8,128)(2,1)S(1)}, u32[]{:S(2)}, u32[]{:S(2)}) collective-permute-start(bf16[128,2560]{1,0:T(8,128)(2,1)S(1)} %slice.66), channel_id=1, source_target_pairs={{0,2},{1,3},{2,4},{3,5},{4,6},{5,7},{6,0},{7,1},{8,10},{9,11},{10,... | collective-permute-start | bytes 1966088 | tf_op jit(solution)/shard_map/ppermute | solution.py:238
  21.4 0.0 copy-done.3
  21.4 0.0 copy-done.5
  21.4 2.7 %routes.1 = (bf16[2560,128]{1,0:T(8,128)(2,1)S(1)}, bf16[1024,640]{1,0:T(8,128)(2,1)S(1)}, bf16[512,128]{1,0:T(8,128)(2,1)S(1)}) custom-call(s32[6,2,40]{2,1,0:T(2,128)S(1)} %bitcast.40, s32[1]{0:T(128)S(6)} %copy.11.count, f32[128,128]{1,0:T(8,128)S(1)} %copy-done.3), custom_call_target="tpu_custom_call" | custom-call | tf_op jit(solution)/shard_map/routes/pallas_call | solution.py:220
  24.1 0.0 collective-permute-done.2
  24.2 0.0 collective-permute-done
  24.2 0.0 collective-permute-done.1
  24.2 2.7 %collective-permute-start.5 = (bf16[80,2560]{1,0:T(8,128)(2,1)S(1)}, bf16[80,2560]{1,0:T(8,128)(2,1)S(1)}, u32[]{:S(2)}, u32[]{:S(2)}) collective-permute-start(bf16[80,2560]{1,0:T(8,128)(2,1)S(1)} %collective-permute-done), channel_id=1, source_target_pairs={{0,2},{1,3},{2,4},{3,5},{4,6},{5,7},{6,0},{7,1},{8,10},{9,11},{10,... | collective-permute-start | bytes 1228808 | tf_op jit(solution)/shard_map/ppermute | solution.py:238
  27.0 0.5 fusion.6
  27.5 3.1 %collective-permute-start.6 = (bf16[128,2560]{1,0:T(8,128)(2,1)S(1)}, bf16[128,2560]{1,0:T(8,128)(2,1)S(1)}, u32[]{:S(2)}, u32[]{:S(2)}) collective-permute-start(bf16[128,2560]{1,0:T(8,128)(2,1)S(1)} %collective-permute-done.1), channel_id=1, source_target_pairs={{0,6},{1,7},{2,0},{3,1},{4,2},{5,3},{6,4},{7,5},{8,14},{9,15},{10,... | collective-permute-start | bytes 1966088 | tf_op jit(solution)/shard_map/ppermute | solution.py:238
  30.6 0.0 collective-permute-done.4
  30.6 0.5 fusion.5
  31.2 0.5 fusion.3
  31.7 4.1 %collective-permute-done.3 = bf16[128,2560]{1,0:T(8,128)(2,1)S(1)} collective-permute-done((bf16[128,2560]{1,0:T(8,128)(2,1)S(1)}, bf16[128,2560]{1,0:T(8,128)(2,1)S(1)}, u32[]{:S(2)}, u32[]{:S(2)}) %collective-permute-start.3) | collective-permute-done | bytes 655392 | tf_op jit(solution)/shard_map/ppermute | solution.py:238
  35.8 0.5 fusion.4
  36.3 0.0 copy-start.7
  36.3 0.8 fusion.2
  37.2 0.5 copy-done.7
  37.6 0.2 fusion.19
  37.9 6.0 %collective-permute-done.5 = bf16[80,2560]{1,0:T(8,128)(2,1)S(1)} collective-permute-done((bf16[80,2560]{1,0:T(8,128)(2,1)S(1)}, bf16[80,2560]{1,0:T(8,128)(2,1)S(1)}, u32[]{:S(2)}, u32[]{:S(2)}) %collective-permute-start.5) | collective-permute-done | bytes 409632 | tf_op jit(solution)/shard_map/ppermute | solution.py:238
  43.9 3.0 %collective-permute-done.6 = bf16[128,2560]{1,0:T(8,128)(2,1)S(1)} collective-permute-done((bf16[128,2560]{1,0:T(8,128)(2,1)S(1)}, bf16[128,2560]{1,0:T(8,128)(2,1)S(1)}, u32[]{:S(2)}, u32[]{:S(2)}) %collective-permute-start.6) | collective-permute-done | bytes 655392 | tf_op jit(solution)/shard_map/ppermute | solution.py:238
  46.9 0.4 fusion.15
  47.3 0.4 add_convert_fusion
  47.7 1.9 %collective-permute-start.7 = (bf16[2560,128]{1,0:T(8,128)(2,1)S(1)}, bf16[2560,128]{1,0:T(8,128)(2,1)S(1)}, u32[]{:S(2)}, u32[]{:S(2)}) collective-permute-start(bf16[2560,128]{1,0:T(8,128)(2,1)S(1)} %add_convert_fusion), channel_id=1, source_target_pairs={{0,1},{1,0},{2,3},{3,2},{4,5},{5,4},{6,7},{7,6},{8,9},{9,8},{10,11... | collective-permute-start | bytes 1966088 | tf_op jit(solution)/shard_map/ppermute | solution.py:241
  49.6 0.4 fusion.17
  50.0 0.0 copy-start.1
  50.0 0.4 add_add_fusion.part
  50.4 0.0 copy-start.2
  50.4 1.3 %collective-permute-done.7.other = bf16[2560,128]{1,0:T(8,128)(2,1)S(1)} collective-permute-done((bf16[2560,128]{1,0:T(8,128)(2,1)S(1)}, bf16[2560,128]{1,0:T(8,128)(2,1)S(1)}, u32[]{:S(2)}, u32[]{:S(2)}) %collective-permute-start.7) | collective-permute-done | bytes 655392 | tf_op jit(solution)/shard_map/ppermute | solution.py:241
  51.7 1.0 spectrum.1
  52.7 0.0 copy-start.4
  52.7 29.0 %all_to_all.10 = bf16[64,8,256]{2,1,0:T(8,128)(2,1)S(1)} all-to-all(bf16[64,8,256]{2,1,0:T(8,128)(2,1)S(1)} %bitcast.39), channel_id=1, replica_groups=mesh['dp'=64,'tensor'=8] {'dp'}, dimensions={0} | all-to-all | bytes 524288 | tf_op jit(solution)/shard_map/all_to_all | solution.py:328
  81.7 1.9 %total.1 = bf16[512,640]{1,0:T(8,128)(2,1)} custom-call(bf16[512,256]{1,0:T(8,128)(2,1)S(1)} %bitcast.37, bf16[384,128]{1,0:T(8,128)(2,1)S(1)} %copy-done.2), custom_call_target="tpu_custom_call" | custom-call | tf_op jit(solution)/shard_map/total/pallas_call | solution.py:220
  83.7 4.6 %all-to-all-start.1 = ((bf16[64,8,640]{2,1,0:T(8,128)(2,1)}), bf16[64,8,640]{2,1,0:T(8,128)(2,1)S(1)}, u32[]{:S(2)}, u32[]{:S(2)}) async-start(bf16[64,8,640]{2,1,0:T(8,128)(2,1)} %bitcast.13), calls=%async_computation.1 | async-start | bytes 1310720 | tf_op jit(solution)/shard_map/all_to_all | solution.py:328
  88.3 3.1 %kept.1 = f32[2560,128]{1,0:T(8,128)} custom-call(f32[2560,128]{1,0:T(8,128)S(1)} %get-tuple-element.53.advanced, bf16[2560,128]{1,0:T(8,128)(2,1)S(1)} %get-tuple-element.54.mask, bf16[64,192]{1,0:T(8,128)(2,1)S(1)} %copy-done.1, bf16[64,192]{1,0:T(8,128)(2,1)S(1)} %copy-done.4), custom_call_target="tpu_custom_call" | custom-call | tf_op jit(solution)/shard_map/kept/pallas_call | solution.py:220
  91.4 18.1 %all-to-all-done.1 = bf16[64,8,640]{2,1,0:T(8,128)(2,1)S(1)} async-done(((bf16[64,8,640]{2,1,0:T(8,128)(2,1)}), bf16[64,8,640]{2,1,0:T(8,128)(2,1)S(1)}, u32[]{:S(2)}, u32[]{:S(2)}) %all-to-all-start.1) | async-done | bytes 655392 | tf_op jit(solution)/shard_map/all_to_all | solution.py:328
  109.4 1.4 %turn.1 = bf16[2560,128]{1,0:T(8,128)(2,1)} custom-call(bf16[512,640]{1,0:T(8,128)(2,1)S(1)} %bitcast.36), custom_call_target="tpu_custom_call" | custom-call | tf_op jit(solution)/shard_map/turn/pallas_call | solution.py:220
  (8 shorter events, 0.1 us)
Async XLA Ops:
  0.6 20.7 %copy-start.3 = (f32[128,128]{1,0:T(8,128)S(1)}, f32[128,128]{1,0:T(8,128)}, u32[]{:S(2)}) copy-start(f32[128,128]{1,0:T(8,128)} %constant.10.clone.base) | copy-start | bytes 196612
  0.6 4.0 %copy-start.6 = (bf16[208,2560]{1,0:T(8,128)(2,1)S(1)}, bf16[208,2560]{1,0:T(8,128)(2,1)}, u32[]{:S(2)}) copy-start(bf16[208,2560]{1,0:T(8,128)(2,1)} %param.9) | copy-start | bytes 3194884
  0.7 11.0 %copy-start = (bf16[1664,128]{1,0:T(8,128)(2,1)S(1)}, bf16[1664,128]{1,0:T(8,128)(2,1)}, u32[]{:S(2)}) copy-start(bf16[1664,128]{1,0:T(8,128)(2,1)} %keys.3) | copy-start | bytes 1277956
  0.7 20.7 %copy-start.5 = (s32[1,40,2,6]{1,2,3,0:T(2,128)S(1)}, s32[1,40,2,6]{1,2,3,0:T(2,128)}, u32[]{:S(2)}) copy-start(s32[1,40,2,6]{1,2,3,0:T(2,128)} %param.12) | copy-start | bytes 5764
  1.9 22.2 %collective-permute-start.1 = (bf16[128,2560]{1,0:T(8,128)(2,1)S(1)}, bf16[128,2560]{1,0:T(8,128)(2,1)S(1)}, u32[]{:S(2)}, u32[]{:S(2)}) collective-permute-start(bf16[128,2560]{1,0:T(8,128)(2,1)S(1)} %slice.66), channel_id=1, source_target_pairs={{0,6},{1,7},{2,0},{3,1},{4,2},{5,3},{6,4},{7,5},{8,14},{9,15},{10,... | collective-permute-start | bytes 1966088 | tf_op jit(solution)/shard_map/ppermute | solution.py:238
  4.7 19.4 %collective-permute-start = (bf16[80,2560]{1,0:T(8,128)(2,1)S(1)}, bf16[80,2560]{1,0:T(8,128)(2,1)S(1)}, u32[]{:S(2)}, u32[]{:S(2)}) collective-permute-start(bf16[80,2560]{1,0:T(8,128)(2,1)S(1)} %slice.65), channel_id=1, source_target_pairs={{0,2},{1,3},{2,4},{3,5},{4,6},{5,7},{6,0},{7,1},{8,10},{9,11},{10,... | collective-permute-start | bytes 1228808 | tf_op jit(solution)/shard_map/ppermute | solution.py:238
  11.7 12.4 %collective-permute-start.2 = (bf16[832,128]{1,0:T(8,128)(2,1)S(1)}, bf16[832,128]{1,0:T(8,128)(2,1)S(1)}, u32[]{:S(2)}, u32[]{:S(2)}) collective-permute-start(bf16[832,128]{1,0:T(8,128)(2,1)S(1)} %get-tuple-element.34), channel_id=1, source_target_pairs={{0,1},{1,0},{2,3},{3,2},{4,5},{5,4},{6,7},{7,6},{8,9},{9,8},{10,11... | collective-permute-start | bytes 638984 | tf_op jit(solution)/shard_map/ppermute | solution.py:241
  13.7 17.0 %collective-permute-start.4 = (bf16[80,2560]{1,0:T(8,128)(2,1)S(1)}, bf16[80,2560]{1,0:T(8,128)(2,1)S(1)}, u32[]{:S(2)}, u32[]{:S(2)}) collective-permute-start(bf16[80,2560]{1,0:T(8,128)(2,1)S(1)} %slice.65), channel_id=1, source_target_pairs={{0,6},{1,7},{2,0},{3,1},{4,2},{5,3},{6,4},{7,5},{8,14},{9,15},{10,... | collective-permute-start | bytes 1228808 | tf_op jit(solution)/shard_map/ppermute | solution.py:238
  15.6 20.2 %collective-permute-start.3 = (bf16[128,2560]{1,0:T(8,128)(2,1)S(1)}, bf16[128,2560]{1,0:T(8,128)(2,1)S(1)}, u32[]{:S(2)}, u32[]{:S(2)}) collective-permute-start(bf16[128,2560]{1,0:T(8,128)(2,1)S(1)} %slice.66), channel_id=1, source_target_pairs={{0,2},{1,3},{2,4},{3,5},{4,6},{5,7},{6,0},{7,1},{8,10},{9,11},{10,... | collective-permute-start | bytes 1966088 | tf_op jit(solution)/shard_map/ppermute | solution.py:238
  24.2 19.6 %collective-permute-start.5 = (bf16[80,2560]{1,0:T(8,128)(2,1)S(1)}, bf16[80,2560]{1,0:T(8,128)(2,1)S(1)}, u32[]{:S(2)}, u32[]{:S(2)}) collective-permute-start(bf16[80,2560]{1,0:T(8,128)(2,1)S(1)} %collective-permute-done), channel_id=1, source_target_pairs={{0,2},{1,3},{2,4},{3,5},{4,6},{5,7},{6,0},{7,1},{8,10},{9,11},{10,... | collective-permute-start | bytes 1228808 | tf_op jit(solution)/shard_map/ppermute | solution.py:238
  27.5 19.4 %collective-permute-start.6 = (bf16[128,2560]{1,0:T(8,128)(2,1)S(1)}, bf16[128,2560]{1,0:T(8,128)(2,1)S(1)}, u32[]{:S(2)}, u32[]{:S(2)}) collective-permute-start(bf16[128,2560]{1,0:T(8,128)(2,1)S(1)} %collective-permute-done.1), channel_id=1, source_target_pairs={{0,6},{1,7},{2,0},{3,1},{4,2},{5,3},{6,4},{7,5},{8,14},{9,15},{10,... | collective-permute-start | bytes 1966088 | tf_op jit(solution)/shard_map/ppermute | solution.py:238
  36.3 1.3 %copy-start.7 = (f32[1,2560,128]{2,1,0:T(8,128)S(1)}, f32[1,2560,128]{2,1,0:T(8,128)}, u32[]{:S(2)}) copy-start(f32[1,2560,128]{2,1,0:T(8,128)} %param.11) | copy-start | bytes 3932164
  47.7 4.0 %collective-permute-start.7 = (bf16[2560,128]{1,0:T(8,128)(2,1)S(1)}, bf16[2560,128]{1,0:T(8,128)(2,1)S(1)}, u32[]{:S(2)}, u32[]{:S(2)}) collective-permute-start(bf16[2560,128]{1,0:T(8,128)(2,1)S(1)} %add_convert_fusion), channel_id=1, source_target_pairs={{0,1},{1,0},{2,3},{3,2},{4,5},{5,4},{6,7},{7,6},{8,9},{9,8},{10,11... | collective-permute-start | bytes 1966088 | tf_op jit(solution)/shard_map/ppermute | solution.py:241
  50.0 1.7 %copy-start.1 = (bf16[64,192]{1,0:T(8,128)(2,1)S(1)}, bf16[64,192]{1,0:T(8,128)(2,1)}, u32[]{:S(2)}) copy-start(bf16[64,192]{1,0:T(8,128)(2,1)} %constant.11.clone.forward) | copy-start | bytes 73732
  50.4 31.4 %copy-start.2 = (bf16[384,128]{1,0:T(8,128)(2,1)S(1)}, bf16[384,128]{1,0:T(8,128)(2,1)}, u32[]{:S(2)}) copy-start(bf16[384,128]{1,0:T(8,128)(2,1)} %constant.13.clone.backward) | copy-start | bytes 294916
  52.7 35.6 %copy-start.4 = (bf16[64,192]{1,0:T(8,128)(2,1)S(1)}, bf16[64,192]{1,0:T(8,128)(2,1)}, u32[]{:S(2)}) copy-start(bf16[64,192]{1,0:T(8,128)(2,1)} %constant.12.clone.backward) | copy-start | bytes 73732
  83.7 25.8 %all-to-all-start.1 = ((bf16[64,8,640]{2,1,0:T(8,128)(2,1)}), bf16[64,8,640]{2,1,0:T(8,128)(2,1)S(1)}, u32[]{:S(2)}, u32[]{:S(2)}) async-start(bf16[64,8,640]{2,1,0:T(8,128)(2,1)} %bitcast.13), calls=%async_computation.1 | async-start | bytes 1310720 | tf_op jit(solution)/shard_map/all_to_all | solution.py:328

commit v9 on v8

--- a/solution.py
+++ b/solution.py
@@ -240,33 +240,33 @@
     def swap(x):
         return lax.ppermute(x, "tensor", [(i, i ^ 1) for i in range(group)])
 
-    cut = tokens * 2 // 5 // 16 * 16
+    cut = tokens * 9 // 16 // 16 * 16
     head, tail = activations[:cut], activations[cut:]
-    left_head, right_tail = along(head, 1), along(tail, -1)
+    left, right_tail = along(activations, 1), along(tail, -1)
 
     rows = jax.ShapeDtypeStruct((chips * tokens, cols), jnp.bfloat16)
     own_keys, sent_keys = call(
         functools.partial(keys_kernel, chips, tokens), "keys", (rows, rows), key_grad
     )
 
-    head, tail, own_keys, sent_keys, block_ids, counts = lax.optimization_barrier(
-        (head, tail, own_keys, sent_keys, block_ids, counts)
-    )
-    left_tail, right_head = along(tail, 1), along(head, -1)
+    head, own_keys, sent_keys, block_ids, counts = lax.optimization_barrier(
+        (head, own_keys, sent_keys, block_ids, counts)
+    )
+    right_head = along(head, -1)
     their_keys = swap(sent_keys)
-
-    left_head, right_tail, block, own_keys, momentum = lax.optimization_barrier(
-        (left_head, right_tail, activations, own_keys, momentum)
-    )
-    far_head, far_tail = along(left_head, 1), along(right_tail, -1)
+    far_tail = along(right_tail, -1)
+
+    left, right_tail, block, own_keys, momentum = lax.optimization_barrier(
+        (left, right_tail, activations, own_keys, momentum)
+    )
+    far_head = along(left[:cut], 1)
     own_keys = own_keys.reshape(chips, tokens, cols)
     their_keys = their_keys.reshape(chips, tokens, cols)
     keys = lax.optimization_barrier(jnp.concatenate([own_keys, their_keys], axis=2))
     before, after = keys[chips - 1], keys[1]
     near = (
         gram(block, keys[0])
-        + gram(left_head, before[:cut])
-        + gram(left_tail, before[cut:])
+        + gram(left, before)
         + gram(right_tail, after[cut:])
         + gram(right_head, after[:cut])
     )
@@ -296,10 +296,8 @@
         places=[SMEM, SMEM, VMEM],
     )
 
-    (own_near, their_near, own_far, their_far, mask, picks, numbers, far_head, far_tail) = (
-        lax.optimization_barrier(
-            (own_near, their_near, own_far, their_far, mask, picks, numbers, far_head, far_tail)
-        )
+    own_near, their_near, own_far, their_far, picks, numbers = lax.optimization_barrier(
+        (own_near, their_near, own_far, their_far, picks, numbers)
     )
     other = swap(whole(their_near, their_far).astype(jnp.bfloat16))
     part = whole(own_near, own_far)

time: 111 us -> 113 us (1.018)
  the two profiles are of different devices: /device:TPU:6 before, /device:TPU:8 now
where the time goes in v9:
time: 113 us
  waiting for transfers between devices  36.5 us (32%)
  blocking collectives  31 us (27%)
  starting transfers between devices  26.6 us (24%)
  Pallas kernels  10.2 us (9%)
  matrix products  3.76 us (3%)
  local copies, waits for them, and re-layouts  2.94 us (3%)
  between operations  1.57 us (1%)
    all_to_all x1, blocking collectives, exchange(): lax.all_to_all(x.reshape(replicas, OWN_COLS, x.shape[1]), 'dp', 0, 0, til...  31 us
    all_to_all x1, waiting for transfers between devices, exchange(): lax.all_to_all(x.reshape(replicas, OWN_COLS, x.shape[1]), 'dp', 0, 0, til...  18.1 us
    ppermute x5, starting transfers between devices, along(): lax.ppermute(x, 'tensor', [(i, (i + 2 * step) % group) for i in range(gro...  17.7 us
    ppermute x5, waiting for transfers between devices, along(): lax.ppermute(x, 'tensor', [(i, (i + 2 * step) % group) for i in range(gro...  17.1 us
    pallas_call x6, Pallas kernels, call(): pl.pallas_call(kernel, out_shape=outs, in_specs=places or [VMEM] * len(ar...  10.2 us
    all_to_all x1, starting transfers between devices, exchange(): lax.all_to_all(x.reshape(replicas, OWN_COLS, x.shape[1]), 'dp', 0, 0, til...  5.12 us
    ppermute x2, starting transfers between devices, swap(): return lax.ppermute(x, 'tensor', [(i, i ^ 1) for i in range(group)])  3.84 us
    dot_general x8, matrix products, gram(): lax.dot_general(a, k, (((0,), (0,)), ((), ())), preferred_element_type=jn...  3.76 us
  transfers between devices with their start and end apart: 8, of which 6 were waited for; matrix products, arithmetic and copies ran while one was open for 5% of the time, Pallas kernels for 5%

profile of v9, /device:TPU:8, one launch (start us, length us, event | category | flops | bytes accessed | tf_op | source)
XLA Modules:
  0.0 112.8 jit_solution(2378188477185934391)
XLA Ops:
  0.6 0.0 copy-start.3
  0.6 0.0 copy-start
  0.7 0.0 copy-start.5
  0.7 3.5 %collective-permute-start = (bf16[208,2560]{1,0:T(8,128)(2,1)}, bf16[208,2560]{1,0:T(8,128)(2,1)S(1)}, u32[]{:S(2)}, u32[]{:S(2)}) collective-permute-start(bf16[208,2560]{1,0:T(8,128)(2,1)} %param.9), channel_id=1, source_target_pairs={{0,2},{1,3},{2,4},{3,5},{4,6},{5,7},{6,0},{7,1},{8,10},{9,11},{10,... | collective-permute-start | bytes 3194888 | tf_op jit(solution)/shard_map/ppermute | solution.py:238
  4.2 1.1 slice.56
  5.3 3.7 %collective-permute-start.1 = (bf16[96,2560]{1,0:T(8,128)(2,1)S(1)}, bf16[96,2560]{1,0:T(8,128)(2,1)S(1)}, u32[]{:S(2)}, u32[]{:S(2)}) collective-permute-start(bf16[96,2560]{1,0:T(8,128)(2,1)S(1)} %slice.56), channel_id=1, source_target_pairs={{0,6},{1,7},{2,0},{3,1},{4,2},{5,3},{6,4},{7,5},{8,14},{9,15},{10,... | collective-permute-start | bytes 1474568 | tf_op jit(solution)/shard_map/ppermute | solution.py:238
  8.9 1.1 slice.57
  10.0 0.0 copy-done
  10.1 1.9 %collective-permute-start.2 = (bf16[832,128]{1,0:T(8,128)(2,1)S(1)}, bf16[832,128]{1,0:T(8,128)(2,1)S(1)}, u32[]{:S(2)}, u32[]{:S(2)}) collective-permute-start(bf16[832,128]{1,0:T(8,128)(2,1)S(1)} %get-tuple-element.30), channel_id=1, source_target_pairs={{0,1},{1,0},{2,3},{3,2},{4,5},{5,4},{6,7},{7,6},{8,9},{9,8},{10,11... | collective-permute-start | bytes 638984 | tf_op jit(solution)/shard_map/ppermute | solution.py:241
  12.0 3.5 %collective-permute-start.3 = (bf16[112,2560]{1,0:T(8,128)(2,1)S(1)}, bf16[112,2560]{1,0:T(8,128)(2,1)S(1)}, u32[]{:S(2)}, u32[]{:S(2)}) collective-permute-start(bf16[112,2560]{1,0:T(8,128)(2,1)S(1)} %slice.57), channel_id=1, source_target_pairs={{0,6},{1,7},{2,0},{3,1},{4,2},{5,3},{6,4},{7,5},{8,14},{9,15},{10,... | collective-permute-start | bytes 1720328 | tf_op jit(solution)/shard_map/ppermute | solution.py:238
  16.1 0.0 copy-done.3
  16.2 0.0 copy-done.5
  16.2 2.7 %routes.1 = (bf16[2560,128]{1,0:T(8,128)(2,1)S(1)}, bf16[1024,640]{1,0:T(8,128)(2,1)S(1)}, bf16[512,128]{1,0:T(8,128)(2,1)S(1)}) custom-call(s32[6,2,40]{2,1,0:T(2,128)S(1)} %bitcast.46, s32[1]{0:T(128)S(6)} %copy.15.count, f32[128,128]{1,0:T(8,128)S(1)} %copy-done.3), custom_call_target="tpu_custom_call" | custom-call | tf_op jit(solution)/shard_map/routes/pallas_call | solution.py:220
  18.9 0.0 collective-permute-done.2
  18.9 2.4 %collective-permute-done.1 = bf16[96,2560]{1,0:T(8,128)(2,1)S(1)} collective-permute-done((bf16[96,2560]{1,0:T(8,128)(2,1)S(1)}, bf16[96,2560]{1,0:T(8,128)(2,1)S(1)}, u32[]{:S(2)}, u32[]{:S(2)}) %collective-permute-start.1) | collective-permute-done | bytes 491552 | tf_op jit(solution)/shard_map/ppermute | solution.py:238
  21.3 4.9 %collective-permute-start.5 = (bf16[96,2560]{1,0:T(8,128)(2,1)S(1)}, bf16[96,2560]{1,0:T(8,128)(2,1)S(1)}, u32[]{:S(2)}, u32[]{:S(2)}) collective-permute-start(bf16[96,2560]{1,0:T(8,128)(2,1)S(1)} %collective-permute-done.1), channel_id=1, source_target_pairs={{0,6},{1,7},{2,0},{3,1},{4,2},{5,3},{6,4},{7,5},{8,14},{9,15},{10,... | collective-permute-start | bytes 1474568 | tf_op jit(solution)/shard_map/ppermute | solution.py:238
  26.2 3.2 %collective-permute-done = bf16[208,2560]{1,0:T(8,128)(2,1)S(1)} collective-permute-done((bf16[208,2560]{1,0:T(8,128)(2,1)}, bf16[208,2560]{1,0:T(8,128)(2,1)S(1)}, u32[]{:S(2)}, u32[]{:S(2)}) %collective-permute-start) | collective-permute-done | bytes 1064992 | tf_op jit(solution)/shard_map/ppermute | solution.py:238
  29.5 2.2 %collective-permute-start.4 = (bf16[112,2560]{1,0:T(8,128)(2,1)S(1)}, bf16[112,2560]{1,0:T(8,128)(2,1)S(1)}, u32[]{:S(2)}, u32[]{:S(2)}) collective-permute-start(bf16[112,2560]{1,0:T(8,128)(2,1)S(1)} %slice.68), channel_id=1, source_target_pairs={{0,2},{1,3},{2,4},{3,5},{4,6},{5,7},{6,0},{7,1},{8,10},{9,11},{10,... | collective-permute-start | bytes 1720328 | tf_op jit(solution)/shard_map/ppermute | solution.py:238
  31.7 0.5 fusion.7
  32.2 0.6 fusion.5
  32.8 0.0 copy-start.6
  32.8 0.8 collective-permute-done.3
  33.6 0.5 fusion.6
  34.2 0.0 copy-done.6
  34.2 0.0 copy-start.7
  34.2 0.6 fusion.1
  34.8 0.7 copy-done.7
  35.5 0.2 fusion.14
  35.7 10.7 %collective-permute-done.4 = bf16[112,2560]{1,0:T(8,128)(2,1)S(1)} collective-permute-done((bf16[112,2560]{1,0:T(8,128)(2,1)S(1)}, bf16[112,2560]{1,0:T(8,128)(2,1)S(1)}, u32[]{:S(2)}, u32[]{:S(2)}) %collective-permute-start.4) | collective-permute-done | bytes 573472 | tf_op jit(solution)/shard_map/ppermute | solution.py:238
  46.4 0.4 fusion.8
  46.8 0.0 collective-permute-done.5
  46.8 0.4 fusion.4
  47.2 1.9 %collective-permute-start.6 = (bf16[2560,128]{1,0:T(8,128)(2,1)S(1)}, bf16[2560,128]{1,0:T(8,128)(2,1)S(1)}, u32[]{:S(2)}, u32[]{:S(2)}) collective-permute-start(bf16[2560,128]{1,0:T(8,128)(2,1)S(1)} %fusion.4), channel_id=1, source_target_pairs={{0,1},{1,0},{2,3},{3,2},{4,5},{5,4},{6,7},{7,6},{8,9},{9,8},{10,11... | collective-permute-start | bytes 1966088 | tf_op jit(solution)/shard_map/ppermute | solution.py:241
  49.1 0.4 fusion.10
  49.5 0.0 copy-start.1
  49.5 0.4 fusion.3.part
  49.9 0.0 copy-start.2
  49.9 1.3 %collective-permute-done.6.other = bf16[2560,128]{1,0:T(8,128)(2,1)S(1)} collective-permute-done((bf16[2560,128]{1,0:T(8,128)(2,1)S(1)}, bf16[2560,128]{1,0:T(8,128)(2,1)S(1)}, u32[]{:S(2)}, u32[]{:S(2)}) %collective-permute-start.6) | collective-permute-done | bytes 655392 | tf_op jit(solution)/shard_map/ppermute | solution.py:241
  51.2 0.0 copy-done.1
  51.2 1.0 spectrum.1
  52.2 0.0 copy-start.4
  52.2 31.0 %all_to_all.10 = bf16[64,8,256]{2,1,0:T(8,128)(2,1)S(1)} all-to-all(bf16[64,8,256]{2,1,0:T(8,128)(2,1)S(1)} %bitcast.45), channel_id=1, replica_groups=mesh['dp'=64,'tensor'=8] {'dp'}, dimensions={0} | all-to-all | bytes 524288 | tf_op jit(solution)/shard_map/all_to_all | solution.py:326
  83.2 1.9 %total.1 = bf16[512,640]{1,0:T(8,128)(2,1)} custom-call(bf16[512,256]{1,0:T(8,128)(2,1)S(1)} %bitcast.43, bf16[384,128]{1,0:T(8,128)(2,1)S(1)} %copy-done.2), custom_call_target="tpu_custom_call" | custom-call | tf_op jit(solution)/shard_map/total/pallas_call | solution.py:220
  85.1 5.1 %all-to-all-start.1 = ((bf16[64,8,640]{2,1,0:T(8,128)(2,1)}), bf16[64,8,640]{2,1,0:T(8,128)(2,1)S(1)}, u32[]{:S(2)}, u32[]{:S(2)}) async-start(bf16[64,8,640]{2,1,0:T(8,128)(2,1)} %bitcast.14), calls=%async_computation.1 | async-start | bytes 1310720 | tf_op jit(solution)/shard_map/all_to_all | solution.py:326
  90.2 0.0 copy-done.4
  90.3 3.1 %kept.1 = f32[2560,128]{1,0:T(8,128)} custom-call(f32[2560,128]{1,0:T(8,128)S(1)} %get-tuple-element.45.advanced, bf16[2560,128]{1,0:T(8,128)(2,1)S(1)} %get-tuple-element.46.mask, bf16[64,192]{1,0:T(8,128)(2,1)S(1)} %copy-done.1, bf16[64,192]{1,0:T(8,128)(2,1)S(1)} %copy-done.4), custom_call_target="tpu_custom_call" | custom-call | tf_op jit(solution)/shard_map/kept/pallas_call | solution.py:220
  93.3 18.1 %all-to-all-done.1 = bf16[64,8,640]{2,1,0:T(8,128)(2,1)S(1)} async-done(((bf16[64,8,640]{2,1,0:T(8,128)(2,1)}), bf16[64,8,640]{2,1,0:T(8,128)(2,1)S(1)}, u32[]{:S(2)}, u32[]{:S(2)}) %all-to-all-start.1) | async-done | bytes 655392 | tf_op jit(solution)/shard_map/all_to_all | solution.py:326
  111.4 1.4 %turn.1 = bf16[2560,128]{1,0:T(8,128)(2,1)} custom-call(bf16[512,640]{1,0:T(8,128)(2,1)S(1)} %bitcast.42), custom_call_target="tpu_custom_call" | custom-call | tf_op jit(solution)/shard_map/turn/pallas_call | solution.py:220
  (6 shorter events, 0.1 us)
Async XLA Ops:
  0.6 15.5 %copy-start.3 = (f32[128,128]{1,0:T(8,128)S(1)}, f32[128,128]{1,0:T(8,128)}, u32[]{:S(2)}) copy-start(f32[128,128]{1,0:T(8,128)} %constant.10.clone.base) | copy-start | bytes 196612
  0.6 9.4 %copy-start = (bf16[1664,128]{1,0:T(8,128)(2,1)S(1)}, bf16[1664,128]{1,0:T(8,128)(2,1)}, u32[]{:S(2)}) copy-start(bf16[1664,128]{1,0:T(8,128)(2,1)} %keys.3) | copy-start | bytes 1277956
  0.7 15.5 %copy-start.5 = (s32[1,40,2,6]{1,2,3,0:T(2,128)S(1)}, s32[1,40,2,6]{1,2,3,0:T(2,128)}, u32[]{:S(2)}) copy-start(s32[1,40,2,6]{1,2,3,0:T(2,128)} %param.12) | copy-start | bytes 5764
  0.7 28.7 %collective-permute-start = (bf16[208,2560]{1,0:T(8,128)(2,1)}, bf16[208,2560]{1,0:T(8,128)(2,1)S(1)}, u32[]{:S(2)}, u32[]{:S(2)}) collective-permute-start(bf16[208,2560]{1,0:T(8,128)(2,1)} %param.9), channel_id=1, source_target_pairs={{0,2},{1,3},{2,4},{3,5},{4,6},{5,7},{6,0},{7,1},{8,10},{9,11},{10,... | collective-permute-start | bytes 3194888 | tf_op jit(solution)/shard_map/ppermute | solution.py:238
  5.3 16.0 %collective-permute-start.1 = (bf16[96,2560]{1,0:T(8,128)(2,1)S(1)}, bf16[96,2560]{1,0:T(8,128)(2,1)S(1)}, u32[]{:S(2)}, u32[]{:S(2)}) collective-permute-start(bf16[96,2560]{1,0:T(8,128)(2,1)S(1)} %slice.56), channel_id=1, source_target_pairs={{0,6},{1,7},{2,0},{3,1},{4,2},{5,3},{6,4},{7,5},{8,14},{9,15},{10,... | collective-permute-start | bytes 1474568 | tf_op jit(solution)/shard_map/ppermute | solution.py:238
  10.1 8.8 %collective-permute-start.2 = (bf16[832,128]{1,0:T(8,128)(2,1)S(1)}, bf16[832,128]{1,0:T(8,128)(2,1)S(1)}, u32[]{:S(2)}, u32[]{:S(2)}) collective-permute-start(bf16[832,128]{1,0:T(8,128)(2,1)S(1)} %get-tuple-element.30), channel_id=1, source_target_pairs={{0,1},{1,0},{2,3},{3,2},{4,5},{5,4},{6,7},{7,6},{8,9},{9,8},{10,11... | collective-permute-start | bytes 638984 | tf_op jit(solution)/shard_map/ppermute | solution.py:241
  12.0 21.6 %collective-permute-start.3 = (bf16[112,2560]{1,0:T(8,128)(2,1)S(1)}, bf16[112,2560]{1,0:T(8,128)(2,1)S(1)}, u32[]{:S(2)}, u32[]{:S(2)}) collective-permute-start(bf16[112,2560]{1,0:T(8,128)(2,1)S(1)} %slice.57), channel_id=1, source_target_pairs={{0,6},{1,7},{2,0},{3,1},{4,2},{5,3},{6,4},{7,5},{8,14},{9,15},{10,... | collective-permute-start | bytes 1720328 | tf_op jit(solution)/shard_map/ppermute | solution.py:238
  21.3 25.5 %collective-permute-start.5 = (bf16[96,2560]{1,0:T(8,128)(2,1)S(1)}, bf16[96,2560]{1,0:T(8,128)(2,1)S(1)}, u32[]{:S(2)}, u32[]{:S(2)}) collective-permute-start(bf16[96,2560]{1,0:T(8,128)(2,1)S(1)} %collective-permute-done.1), channel_id=1, source_target_pairs={{0,6},{1,7},{2,0},{3,1},{4,2},{5,3},{6,4},{7,5},{8,14},{9,15},{10,... | collective-permute-start | bytes 1474568 | tf_op jit(solution)/shard_map/ppermute | solution.py:238
  29.5 16.9 %collective-permute-start.4 = (bf16[112,2560]{1,0:T(8,128)(2,1)S(1)}, bf16[112,2560]{1,0:T(8,128)(2,1)S(1)}, u32[]{:S(2)}, u32[]{:S(2)}) collective-permute-start(bf16[112,2560]{1,0:T(8,128)(2,1)S(1)} %slice.68), channel_id=1, source_target_pairs={{0,2},{1,3},{2,4},{3,5},{4,6},{5,7},{6,0},{7,1},{8,10},{9,11},{10,... | collective-permute-start | bytes 1720328 | tf_op jit(solution)/shard_map/ppermute | solution.py:238
  32.8 1.4 %copy-start.6 = (bf16[208,2560]{1,0:T(8,128)(2,1)S(1)}, bf16[208,2560]{1,0:T(8,128)(2,1)}, u32[]{:S(2)}) copy-start(bf16[208,2560]{1,0:T(8,128)(2,1)} %param.9) | copy-start | bytes 3194884
  34.2 1.3 %copy-start.7 = (f32[1,2560,128]{2,1,0:T(8,128)S(1)}, f32[1,2560,128]{2,1,0:T(8,128)}, u32[]{:S(2)}) copy-start(f32[1,2560,128]{2,1,0:T(8,128)} %param.11) | copy-start | bytes 3932164
  47.2 4.0 %collective-permute-start.6 = (bf16[2560,128]{1,0:T(8,128)(2,1)S(1)}, bf16[2560,128]{1,0:T(8,128)(2,1)S(1)}, u32[]{:S(2)}, u32[]{:S(2)}) collective-permute-start(bf16[2560,128]{1,0:T(8,128)(2,1)S(1)} %fusion.4), channel_id=1, source_target_pairs={{0,1},{1,0},{2,3},{3,2},{4,5},{5,4},{6,7},{7,6},{8,9},{9,8},{10,11... | collective-permute-start | bytes 1966088 | tf_op jit(solution)/shard_map/ppermute | solution.py:241
  49.5 1.7 %copy-start.1 = (bf16[64,192]{1,0:T(8,128)(2,1)S(1)}, bf16[64,192]{1,0:T(8,128)(2,1)}, u32[]{:S(2)}) copy-start(bf16[64,192]{1,0:T(8,128)(2,1)} %constant.11.clone.forward) | copy-start | bytes 73732
  49.9 33.3 %copy-start.2 = (bf16[384,128]{1,0:T(8,128)(2,1)S(1)}, bf16[384,128]{1,0:T(8,128)(2,1)}, u32[]{:S(2)}) copy-start(bf16[384,128]{1,0:T(8,128)(2,1)} %constant.13.clone.backward) | copy-start | bytes 294916
  52.2 38.1 %copy-start.4 = (bf16[64,192]{1,0:T(8,128)(2,1)S(1)}, bf16[64,192]{1,0:T(8,128)(2,1)}, u32[]{:S(2)}) copy-start(bf16[64,192]{1,0:T(8,128)(2,1)} %constant.12.clone.backward) | copy-start | bytes 73732
  85.1 26.3 %all-to-all-start.1 = ((bf16[64,8,640]{2,1,0:T(8,128)(2,1)}), bf16[64,8,640]{2,1,0:T(8,128)(2,1)S(1)}, u32[]{:S(2)}, u32[]{:S(2)}) async-start(bf16[64,8,640]{2,1,0:T(8,128)(2,1)} %bitcast.14), calls=%async_computation.1 | async-start | bytes 1310720 | tf_op jit(solution)/shard_map/all_to_all | solution.py:326

commit v10 on v9

--- a/solution.py
+++ b/solution.py
@@ -14,6 +14,8 @@
 WIDE = 4
 ROW_GROUPS = 4
 OWN_COLS = 8
+NEAR = (0, 1, 3)
+FAR = 2
 
 
 def cosine_parts():
@@ -50,14 +52,26 @@
         ref[first : first + SPAN, :] = value[:, s * cols : (s + 1) * cols].astype(ref.dtype)
 
 
-def keys_kernel(chips, tokens, keys, own, partner):
+def keys_kernel(chips, tokens, keys, ids, own, partner, far_own, far_partner):
     spot = lax.axis_index("tensor")
     chip, core = lax.shift_right_logical(spot, 1), lax.bitwise_and(spot, 1)
-    for step in range(chips):
-        pair = 2 * lax.bitwise_and(chip + step, chips - 1)
-        here = slice(step * tokens, (step + 1) * tokens)
-        own[here, :] = keys[pl.ds(pl.multiple_of((pair + core) * tokens, 16), tokens), :]
-        partner[here, :] = keys[pl.ds(pl.multiple_of((pair + 1 - core) * tokens, 16), tokens), :]
+
+    def block(step, which):
+        first = (2 * lax.bitwise_and(chip + step, chips - 1) + which) * tokens
+        return keys[pl.ds(pl.multiple_of(first, 16), tokens), :]
+
+    for place, step in enumerate(NEAR):
+        here = slice(place * tokens, (place + 1) * tokens)
+        own[here, :] = block(step, core)
+        partner[here, :] = block(step, 1 - core)
+    far_own[:tokens, :] = block(FAR, core)
+    far_partner[...] = block(FAR, 1 - core)
+    most, halves, spans = ids.shape
+    rows = [ids[k].astype(jnp.float32) for k in range(most)]
+    rows.append(jnp.zeros((16 - most * halves, spans), jnp.float32))
+    rows = jnp.concatenate(rows, axis=0)
+    rows = jnp.concatenate([rows, jnp.zeros((16, far_own.shape[1] - spans), jnp.float32)], axis=1)
+    far_own[tokens:, :] = rows.astype(far_own.dtype)
 
 
 def routes_kernel(ids, count, base, mask, picks, numbers):
@@ -116,7 +130,53 @@
     return product(forward, [high, low, high]) * keep
 
 
-def spectrum_kernel(part, other, picks, numbers, forward, advanced, sent, rows):
+def chosen(picks, rows, group, first):
+    cols = rows.shape[1]
+    height = picks.shape[1]
+    band = rows[group * height : (group + 1) * height, :]
+    one, two = (
+        jnp.dot(
+            picks[(2 * group + b) * cols : (2 * group + b + 1) * cols, :],
+            band,
+            preferred_element_type=jnp.float32,
+        )
+        for b in range(2)
+    )
+    return jnp.where(first, one, two)
+
+
+def left_half(cols):
+    return lax.broadcasted_iota(jnp.int32, (cols, cols), 1) < SPAN
+
+
+def far_kernel(
+    numbers, count, spans, slots, base, part, other, forward, whole, sent, picks, rows
+):
+    cols = part.shape[1]
+    height = picks.shape[1]
+    square = (cols, cols)
+    known = numbers[...].astype(jnp.float32)
+    known = jnp.concatenate(
+        [known, jnp.zeros((cols - known.shape[0], cols), jnp.float32)], axis=0
+    ).T.astype(jnp.bfloat16)
+    place = lax.broadcasted_iota(jnp.int32, square, 1).astype(jnp.float32)
+    ones = jnp.ones(square, jnp.bfloat16)
+    slot = slots[...]
+    active = slot < count[0].astype(jnp.float32)
+    for g in range(ROW_GROUPS):
+        by_span = jnp.dot(
+            spans[g * cols : (g + 1) * cols, :], known, preferred_element_type=jnp.float32
+        )
+        for b in range(2):
+            single = jnp.where(place == 2.0 * slot + float(b), by_span, 0.0)
+            own = jnp.dot(
+                single.astype(jnp.bfloat16), ones, preferred_element_type=jnp.float32
+            )
+            target = jnp.where(active, base[...] + 2.0 * own, -1.0)
+            for i in range(height // cols):
+                picks[(2 * g + b) * cols : (2 * g + b + 1) * cols, i * cols : (i + 1) * cols] = (
+                    (target == place + float(i * cols)).astype(jnp.float32).astype(picks.dtype)
+                )
     for i in range(part.shape[0] // (SPAN * WIDE)):
         x = beside(
             [
@@ -124,30 +184,42 @@
                 for p, o in zip(spans_of(part, i, WIDE), spans_of(other, i, WIDE))
             ]
         )
+        put(whole, i, WIDE, x)
+        high, low = split(x)
+        put(rows, i, WIDE, product(forward, [high, low, high]))
+    first = left_half(cols)
+    for g in range(ROW_GROUPS):
+        sent[g * cols : (g + 1) * cols, :] = chosen(picks, rows, g, first).astype(sent.dtype)
+
+
+def spectrum_kernel(part, other, far, picks, numbers, forward, advanced, sent, rows):
+    for i in range(part.shape[0] // (SPAN * WIDE)):
+        x = beside(
+            [
+                p + o.astype(jnp.float32)
+                for p, o in zip(spans_of(part, i, WIDE), spans_of(other, i, WIDE))
+            ]
+        )
         put(advanced, i, WIDE, x)
         high, low = split(x)
         put(rows, i, WIDE, product(forward, [high, low, high]))
     cols = part.shape[1]
-    height = picks.shape[1]
-    first = lax.broadcasted_iota(jnp.int32, (cols, cols), 1) < SPAN
+    first = left_half(cols)
     for g in range(ROW_GROUPS):
-        band = rows[g * height : (g + 1) * height, :]
-        one, two = (
-            jnp.dot(
-                picks[(2 * g + b) * cols : (2 * g + b + 1) * cols, :],
-                band,
-                preferred_element_type=jnp.float32,
-            )
-            for b in range(2)
-        )
         message = slice(g * cols, (g + 1) * cols)
-        sent[message, :cols] = jnp.where(first, one, two).T.astype(sent.dtype)
+        total = chosen(picks, rows, g, first) + far[message, :].astype(jnp.float32)
+        sent[message, :cols] = total.T.astype(sent.dtype)
         sent[message, cols:] = numbers[message, :]
 
 
-def kept_kernel(advanced, mask, forward, backward, kept):
+def kept_kernel(advanced, far, mask, forward, backward, kept):
     for i in range(kept.shape[0] // (SPAN * WIDE)):
-        x = beside(spans_of(advanced, i, WIDE))
+        x = beside(
+            [
+                n + f.astype(jnp.float32)
+                for n, f in zip(spans_of(advanced, i, WIDE), spans_of(far, i, WIDE))
+            ]
+        )
         high, low = split(chosen_rows(x, mask, forward, i))
         put(kept, i, WIDE, x - product(backward, [high, low, high]))
 
@@ -193,20 +265,11 @@
 
 def turn_kernel(turned, update):
     cols, height = update.shape[1], turned.shape[1]
-    square = (cols, cols)
-    same = lax.broadcasted_iota(jnp.int32, square, 0) == lax.broadcasted_iota(
-        jnp.int32, square, 1
-    )
-    same = same.astype(jnp.float32).astype(turned.dtype)
     for g in range(ROW_GROUPS):
         for i in range(height // cols):
             rows = g * height + i * cols
-            update[rows : rows + cols, :] = lax.dot_general(
-                same,
-                turned[g * cols : (g + 1) * cols, i * cols : (i + 1) * cols],
-                (((1,), (1,)), ((), ())),
-                preferred_element_type=jnp.float32,
-            ).astype(update.dtype)
+            block = turned[g * cols : (g + 1) * cols, i * cols : (i + 1) * cols]
+            update[rows : rows + cols, :] = block.astype(jnp.float32).T.astype(update.dtype)
 
 
 def gram(a, k):
@@ -234,77 +297,94 @@
     cols = key_grad.shape[1]
     chips = group // 2
 
-    def along(x, step):
-        return lax.ppermute(x, "tensor", [(i, (i + 2 * step) % group) for i in range(group)])
+    def along(x, step, across=False):
+        pairs = [(i, ((i + 2 * step) % group) ^ int(across)) for i in range(group)]
+        return lax.ppermute(x, "tensor", pairs)
 
     def swap(x):
         return lax.ppermute(x, "tensor", [(i, i ^ 1) for i in range(group)])
 
-    cut = tokens * 9 // 16 // 16 * 16
-    head, tail = activations[:cut], activations[cut:]
-    left, right_tail = along(activations, 1), along(tail, -1)
-
-    rows = jax.ShapeDtypeStruct((chips * tokens, cols), jnp.bfloat16)
-    own_keys, sent_keys = call(
-        functools.partial(keys_kernel, chips, tokens), "keys", (rows, rows), key_grad
-    )
-
-    head, own_keys, sent_keys, block_ids, counts = lax.optimization_barrier(
-        (head, own_keys, sent_keys, block_ids, counts)
-    )
-    right_head = along(head, -1)
-    their_keys = swap(sent_keys)
-    far_tail = along(right_tail, -1)
-
-    left, right_tail, block, own_keys, momentum = lax.optimization_barrier(
-        (left, right_tail, activations, own_keys, momentum)
-    )
-    far_head = along(left[:cut], 1)
-    own_keys = own_keys.reshape(chips, tokens, cols)
-    their_keys = their_keys.reshape(chips, tokens, cols)
-    keys = lax.optimization_barrier(jnp.concatenate([own_keys, their_keys], axis=2))
-    before, after = keys[chips - 1], keys[1]
-    near = (
-        gram(block, keys[0])
-        + gram(left, before)
-        + gram(right_tail, after[cut:])
-        + gram(right_head, after[:cut])
-    )
-    own_near = near[:, :cols] + 0.999 * momentum[0]
-    their_near = near[:, cols:]
-    own_far, their_far = own_keys[2], their_keys[2]
-
-    def whole(total, far):
-        return total + gram(far_head, far[:cut]) + gram(far_tail, far[cut:])
+    near_rows = jax.ShapeDtypeStruct((len(NEAR) * tokens, cols), jnp.bfloat16)
+    ids = jnp.transpose(block_ids[0], (2, 1, 0))
+    own_keys, partner_keys, far_own, far_partner = call(
+        functools.partial(keys_kernel, chips, tokens),
+        "keys",
+        (
+            near_rows,
+            near_rows,
+            jax.ShapeDtypeStruct((tokens + 16, cols), jnp.bfloat16),
+            jax.ShapeDtypeStruct((tokens, cols), jnp.bfloat16),
+        ),
+        key_grad,
+        ids,
+    )
+    far_own, far_partner = along(far_own, FAR), along(far_partner, FAR, across=True)
+    left, right = along(activations, 1), along(activations, -1)
+
+    far_other = swap(gram(activations, far_partner).astype(jnp.bfloat16))
+    far_part = gram(activations, far_own[:tokens])
+    their_keys = swap(partner_keys)
 
     flat = jax.ShapeDtypeStruct((features, cols), jnp.float32)
     flat_half = jax.ShapeDtypeStruct((features, cols), jnp.bfloat16)
+    high, low = cosine_parts()
+    forward = jnp.asarray(np.concatenate([high, high, low], axis=1))
+    backward = jnp.asarray(np.concatenate([high.T, high.T, low.T], axis=1))
     height = features // ROW_GROUPS
     lines = np.arange(cols)
     base = SPAN * (lines // (2 * block_ids.shape[3])) + lines % 2
+    base = jnp.asarray(np.repeat(base[:, None], cols, axis=1).astype(np.float32))
+    picks_shape = (2 * ROW_GROUPS * cols, height)
     mask, picks, numbers = call(
         routes_kernel,
         "routes",
         (
             flat_half,
-            jax.ShapeDtypeStruct((2 * ROW_GROUPS * cols, height), jnp.bfloat16),
+            jax.ShapeDtypeStruct(picks_shape, jnp.bfloat16),
             jax.ShapeDtypeStruct((ROW_GROUPS * cols, cols), jnp.bfloat16),
         ),
-        jnp.transpose(block_ids[0], (2, 1, 0)),
+        ids,
         counts,
-        jnp.asarray(np.repeat(base[:, None], cols, axis=1).astype(np.float32)),
+        base,
         places=[SMEM, SMEM, VMEM],
     )
 
-    own_near, their_near, own_far, their_far, picks, numbers = lax.optimization_barrier(
-        (own_near, their_near, own_far, their_far, picks, numbers)
-    )
-    other = swap(whole(their_near, their_far).astype(jnp.bfloat16))
-    part = whole(own_near, own_far)
-
-    high, low = cosine_parts()
-    forward = jnp.asarray(np.concatenate([high, high, low], axis=1))
-    backward = jnp.asarray(np.concatenate([high.T, high.T, low.T], axis=1))
+    most = block_ids.shape[3]
+    span = lines // (2 * most)
+    each = features // SPAN // ROW_GROUPS
+    span_table = np.concatenate(
+        [(span[:, None] + g * each == lines) & (span[:, None] < each) for g in range(ROW_GROUPS)]
+    )
+    slot_table = np.where(span < each, lines % (2 * most) // 2, most)
+    slot_table = np.repeat(slot_table[:, None], cols, axis=1)
+    far_whole, far_sent = call(
+        far_kernel,
+        "far",
+        (flat_half, jax.ShapeDtypeStruct((ROW_GROUPS * cols, cols), jnp.bfloat16)),
+        far_own[tokens:],
+        counts,
+        jnp.asarray(span_table.astype(np.float32).astype(ml_dtypes.bfloat16)),
+        jnp.asarray(slot_table.astype(np.float32)),
+        base,
+        far_part,
+        far_other,
+        forward,
+        places=[VMEM, SMEM] + [VMEM] * 6,
+        scratch=(
+            pltpu.VMEM(picks_shape, jnp.bfloat16),
+            pltpu.VMEM((features, cols), jnp.bfloat16),
+        ),
+    )
+    far_sent = along(far_sent, FAR)
+
+    keys = jnp.concatenate([own_keys, their_keys], axis=1)
+    keys = lax.optimization_barrier(keys.reshape(len(NEAR), tokens, 2 * cols))
+    left, right, far_whole = lax.optimization_barrier((left, right, far_whole))
+    far_whole = along(far_whole, FAR)
+    near = gram(activations, keys[0]) + gram(right, keys[1]) + gram(left, keys[2])
+    other = swap(near[:, cols:].astype(jnp.bfloat16))
+    part = near[:, :cols] + 0.999 * momentum[0]
+
     order = np.concatenate([np.arange(0, SPAN, 2), np.arange(1, SPAN, 2)])
     both_high, both_low = (np.kron(np.eye(2, dtype=p.dtype), p[order]) for p in (high, low))
     backward_pair = jnp.asarray(np.concatenate([both_high, both_high, both_low], axis=0))
@@ -316,6 +396,7 @@
         (flat, message),
         part,
         other,
+        far_sent,
         picks,
         numbers,
         forward,
@@ -328,7 +409,7 @@
         ).reshape(x.shape)
 
     pieces = exchange(sent)
-    (kept,) = call(kept_kernel, "kept", (flat,), advanced, mask, forward, backward)
+    (kept,) = call(kept_kernel, "kept", (flat,), advanced, far_whole, mask, forward, backward)
     (totals,) = call(
         total_kernel,
         "total",

time: 113 us -> 112 us (level)
  the two profiles are of different devices: /device:TPU:8 before, /device:TPU:6 now
where the time goes in v10:
time: 112 us; the launch traced here: 111 us
  starting transfers between devices  36.6 us (33%)
  blocking collectives  31.6 us (28%)
  waiting for transfers between devices  22 us (20%)
  Pallas kernels  11.7 us (10%)
  matrix products  4.32 us (4%)
  local copies, waits for them, and re-layouts  3.36 us (3%)
  between operations  1.56 us (1%)
    all_to_all x1, blocking collectives, exchange(): lax.all_to_all(x.reshape(replicas, OWN_COLS, x.shape[1]), 'dp', 0, 0, til...  31.6 us
    ppermute x6, starting transfers between devices, along(): return lax.ppermute(x, 'tensor', pairs)  22.4 us
    ppermute x6, waiting for transfers between devices, along(): return lax.ppermute(x, 'tensor', pairs)  21.6 us
    pallas_call x7, Pallas kernels, call(): pl.pallas_call(kernel, out_shape=outs, in_specs=places or [VMEM] * len(ar...  11.7 us
    ppermute x3, starting transfers between devices, swap(): return lax.ppermute(x, 'tensor', [(i, i ^ 1) for i in range(group)])  9.61 us
    all_to_all x1, starting transfers between devices, exchange(): lax.all_to_all(x.reshape(replicas, OWN_COLS, x.shape[1]), 'dp', 0, 0, til...  4.64 us
    dot_general x5, matrix products, gram(): lax.dot_general(a, k, (((0,), (0,)), ((), ())), preferred_element_type=jn...  4.32 us
    unnamed x24, local copies, waits for them, and re-layouts  3.27 us
  transfers between devices with their start and end apart: 10, of which 5 were waited for; matrix products, arithmetic and copies ran while one was open for 4% of the time, Pallas kernels for 7%

profile of v10, /device:TPU:6, one launch (start us, length us, event | category | flops | bytes accessed | tf_op | source)
XLA Modules:
  0.0 111.3 jit_solution(2544266374377195611)
XLA Ops:
  0.6 7.8 %collective-permute-start.1 = (bf16[208,2560]{1,0:T(8,128)(2,1)}, bf16[208,2560]{1,0:T(8,128)(2,1)S(1)}, u32[]{:S(2)}, u32[]{:S(2)}) collective-permute-start(bf16[208,2560]{1,0:T(8,128)(2,1)} %param.11), channel_id=1, source_target_pairs={{0,2},{1,3},{2,4},{3,5},{4,6},{5,7},{6,0},{7,1},{8,10},{9,11},{10,... | collective-permute-start | bytes 3194888 | tf_op jit(solution)/shard_map/ppermute | solution.py:302
  8.4 1.9 %collective-permute-start.2 = (bf16[208,2560]{1,0:T(8,128)(2,1)}, bf16[208,2560]{1,0:T(8,128)(2,1)S(1)}, u32[]{:S(2)}, u32[]{:S(2)}) collective-permute-start(bf16[208,2560]{1,0:T(8,128)(2,1)} %param.11), channel_id=1, source_target_pairs={{0,6},{1,7},{2,0},{3,1},{4,2},{5,3},{6,4},{7,5},{8,14},{9,15},{10,... | collective-permute-start | bytes 3194888 | tf_op jit(solution)/shard_map/ppermute | solution.py:302
  10.3 1.0 copy-done
  11.3 0.7 copy-done.8
  12.1 1.9 %collective-permute-start.4 = (bf16[208,128]{1,0:T(8,128)(2,1)S(1)}, bf16[208,128]{1,0:T(8,128)(2,1)S(1)}, u32[]{:S(2)}, u32[]{:S(2)}) collective-permute-start(bf16[208,128]{1,0:T(8,128)(2,1)S(1)} %get-tuple-element.19), channel_id=1, source_target_pairs={{0,5},{1,4},{2,7},{3,6},{4,1},{5,0},{6,3},{7,2},{8,13},{9,12},{10,... | collective-permute-start | bytes 159752 | tf_op jit(solution)/shard_map/ppermute | solution.py:302
  14.0 3.4 %collective-permute-start.3 = (bf16[224,128]{1,0:T(8,128)(2,1)S(1)}, bf16[224,128]{1,0:T(8,128)(2,1)S(1)}, u32[]{:S(2)}, u32[]{:S(2)}) collective-permute-start(bf16[224,128]{1,0:T(8,128)(2,1)S(1)} %get-tuple-element.18), channel_id=1, source_target_pairs={{0,4},{1,5},{2,6},{3,7},{4,0},{5,1},{6,2},{7,3},{8,12},{9,13},{10,... | collective-permute-start | bytes 172040 | tf_op jit(solution)/shard_map/ppermute | solution.py:302
  17.4 3.8 %collective-permute-start = (bf16[624,128]{1,0:T(8,128)(2,1)S(1)}, bf16[624,128]{1,0:T(8,128)(2,1)S(1)}, u32[]{:S(2)}, u32[]{:S(2)}) collective-permute-start(bf16[624,128]{1,0:T(8,128)(2,1)S(1)} %get-tuple-element.17), channel_id=1, source_target_pairs={{0,1},{1,0},{2,3},{3,2},{4,5},{5,4},{6,7},{7,6},{8,9},{9,8},{10,11... | collective-permute-start | bytes 479240 | tf_op jit(solution)/shard_map/ppermute | solution.py:305
  21.8 0.0 copy-start.2
  21.8 0.8 copy-done.2
  22.7 0.7 copy-done.9
  23.4 2.7 %routes.1 = (bf16[2560,128]{1,0:T(8,128)(2,1)S(1)}, bf16[1024,640]{1,0:T(8,128)(2,1)S(1)}, bf16[512,128]{1,0:T(8,128)(2,1)S(1)}) custom-call(s32[6,2,40]{2,1,0:T(2,128)S(1)} %bitcast.36, s32[1]{0:T(128)S(6)} %copy.19.count, f32[128,128]{1,0:T(8,128)S(1)} %copy-done.2), custom_call_target="tpu_custom_call" | custom-call | tf_op jit(solution)/shard_map/routes/pallas_call | solution.py:283
  26.1 4.8 %collective-permute-done.4 = bf16[208,128]{1,0:T(8,128)(2,1)S(1)} collective-permute-done((bf16[208,128]{1,0:T(8,128)(2,1)S(1)}, bf16[208,128]{1,0:T(8,128)(2,1)S(1)}, u32[]{:S(2)}, u32[]{:S(2)}) %collective-permute-start.4) | collective-permute-done | bytes 53280 | tf_op jit(solution)/shard_map/ppermute | solution.py:302
  30.9 1.9 %fusion.1 = bf16[2560,128]{1,0:T(8,128)(2,1)S(1)} fusion(bf16[208,128]{1,0:T(8,128)(2,1)S(1)} %collective-permute-done.4, bf16[208,2560]{1,0:T(8,128)(2,1)} %param.11), kind=kOutput, calls=%fused_computation.5 | convolution fusion | flops 136642560 | bytes 1773568 | tf_op jit(solution)/shard_map/dot_general | solution.py:276
  32.8 3.7 %collective-permute-start.5 = (bf16[2560,128]{1,0:T(8,128)(2,1)S(1)}, bf16[2560,128]{1,0:T(8,128)(2,1)S(1)}, u32[]{:S(2)}, u32[]{:S(2)}) collective-permute-start(bf16[2560,128]{1,0:T(8,128)(2,1)S(1)} %fusion.1), channel_id=1, source_target_pairs={{0,1},{1,0},{2,3},{3,2},{4,5},{5,4},{6,7},{7,6},{8,9},{9,8},{10,11... | collective-permute-start | bytes 1966088 | tf_op jit(solution)/shard_map/ppermute | solution.py:305
  36.5 0.0 collective-permute-done.3
  36.5 0.7 convolution_bitcast_fusion.1.part
  37.2 0.0 collective-permute-done
  37.3 0.0 copy-start.1
  37.3 0.0 copy-start.3
  37.3 0.0 copy-start.4
  37.3 0.0 copy-start.6
  37.3 0.7 convolution_bitcast_fusion
  38.0 0.2 collective-permute-done.5.other
  38.2 0.0 copy-done.3
  38.2 0.0 copy-done.4
  38.2 0.0 copy-done.6
  38.2 1.8 %far.1 = (bf16[2560,128]{1,0:T(8,128)(2,1)S(1)}, bf16[512,128]{1,0:T(8,128)(2,1)S(1)}) custom-call(bf16[16,128]{1,0:T(8,128)(2,1)S(1)} %slice.30.numbers, s32[1]{0:T(128)S(6)} %copy.19.count, bf16[512,128]{1,0:T(8,128)(2,1)S(1)} %copy-done.4, f32[128,128]{1,0:T(8,128)S(1)} %copy-done.6, f32[128,128]{1,0:T(8,128)S(1)} %copy-done.3, ...), custom_call_target="tpu_custom_call" | custom-call | tf_op jit(solution)/shard_map/far/pallas_call | solution.py:283
  40.1 4.0 %collective-permute-start.7 = (bf16[512,128]{1,0:T(8,128)(2,1)S(1)}, bf16[512,128]{1,0:T(8,128)(2,1)S(1)}, u32[]{:S(2)}, u32[]{:S(2)}) collective-permute-start(bf16[512,128]{1,0:T(8,128)(2,1)S(1)} %get-tuple-element.23), channel_id=1, source_target_pairs={{0,4},{1,5},{2,6},{3,7},{4,0},{5,1},{6,2},{7,3},{8,12},{9,13},{10,... | collective-permute-start | bytes 393224 | tf_op jit(solution)/shard_map/ppermute | solution.py:302
  44.0 0.0 collective-permute-done.1
  44.0 0.0 collective-permute-done.2
  44.0 0.6 fusion.2
  44.6 0.6 fusion
  45.2 0.0 copy-start.11
  45.2 0.1 slice.46
  45.3 2.1 %collective-permute-start.6 = (bf16[2560,128]{1,0:T(8,128)(2,1)S(1)}, bf16[2560,128]{1,0:T(8,128)(2,1)S(1)}, u32[]{:S(2)}, u32[]{:S(2)}) collective-permute-start(bf16[2560,128]{1,0:T(8,128)(2,1)S(1)} %slice.46), channel_id=1, source_target_pairs={{0,1},{1,0},{2,3},{3,2},{4,5},{5,4},{6,7},{7,6},{8,9},{9,8},{10,11... | collective-permute-start | bytes 1966088 | tf_op jit(solution)/shard_map/ppermute | solution.py:305
  47.4 0.2 slice_add_fusion.part
  47.6 1.6 %collective-permute-done.7.far = bf16[512,128]{1,0:T(8,128)(2,1)S(1)} collective-permute-done((bf16[512,128]{1,0:T(8,128)(2,1)S(1)}, bf16[512,128]{1,0:T(8,128)(2,1)S(1)}, u32[]{:S(2)}, u32[]{:S(2)}) %collective-permute-start.7) | collective-permute-done | bytes 131104 | tf_op jit(solution)/shard_map/ppermute | solution.py:302
  49.2 0.2 collective-permute-done.6.other
  49.4 1.0 spectrum.1
  50.4 0.0 copy-start.7
  50.4 31.6 %all_to_all.10 = bf16[64,8,256]{2,1,0:T(8,128)(2,1)S(1)} all-to-all(bf16[64,8,256]{2,1,0:T(8,128)(2,1)S(1)} %bitcast.34), channel_id=1, replica_groups=mesh['dp'=64,'tensor'=8] {'dp'}, dimensions={0} | all-to-all | bytes 524288 | tf_op jit(solution)/shard_map/all_to_all | solution.py:407
  82.1 1.9 %total.1 = bf16[512,640]{1,0:T(8,128)(2,1)} custom-call(bf16[512,256]{1,0:T(8,128)(2,1)S(1)} %bitcast.33, bf16[384,128]{1,0:T(8,128)(2,1)S(1)} %copy-done.5), custom_call_target="tpu_custom_call" | custom-call | tf_op jit(solution)/shard_map/total/pallas_call | solution.py:283
  84.0 4.6 %all-to-all-start.1 = ((bf16[64,8,640]{2,1,0:T(8,128)(2,1)}), bf16[64,8,640]{2,1,0:T(8,128)(2,1)S(1)}, u32[]{:S(2)}, u32[]{:S(2)}) async-start(bf16[64,8,640]{2,1,0:T(8,128)(2,1)} %bitcast.14), calls=%async_computation.1 | async-start | bytes 1310720 | tf_op jit(solution)/shard_map/all_to_all | solution.py:407
  88.6 3.4 %collective-permute-start.8 = (bf16[2560,128]{1,0:T(8,128)(2,1)S(1)}, bf16[2560,128]{1,0:T(8,128)(2,1)S(1)}, u32[]{:S(2)}, u32[]{:S(2)}) collective-permute-start(bf16[2560,128]{1,0:T(8,128)(2,1)S(1)} %get-tuple-element.27), channel_id=1, source_target_pairs={{0,4},{1,5},{2,6},{3,7},{4,0},{5,1},{6,2},{7,3},{8,12},{9,13},{10,... | collective-permute-start | bytes 1966088 | tf_op jit(solution)/shard_map/ppermute | solution.py:302
  92.1 15.1 %collective-permute-done.8.far = bf16[2560,128]{1,0:T(8,128)(2,1)S(1)} collective-permute-done((bf16[2560,128]{1,0:T(8,128)(2,1)S(1)}, bf16[2560,128]{1,0:T(8,128)(2,1)S(1)}, u32[]{:S(2)}, u32[]{:S(2)}) %collective-permute-start.8) | collective-permute-done | bytes 655392 | tf_op jit(solution)/shard_map/ppermute | solution.py:302
  107.2 3.1 %kept.1 = f32[2560,128]{1,0:T(8,128)} custom-call(f32[2560,128]{1,0:T(8,128)S(1)} %get-tuple-element.26.advanced, bf16[2560,128]{1,0:T(8,128)(2,1)S(1)} %collective-permute-done.8.far, bf16[2560,128]{1,0:T(8,128)(2,1)S(1)} %get-tuple-element.28.mask, bf16[64,192]{1,0:T(8,128)(2,1)S(1)} %copy-done.1, bf16[64,192]{1,0:T(8,128)(2,1)S(1)} %copy-done.7), custom_call_target="tpu_custom_call" | custom-call | tf_op jit(solution)/shard_map/kept/pallas_call | solution.py:283
  110.3 0.0 all-to-all-done.1
  110.3 1.1 turn.1
  (13 shorter events, 0.1 us)
Async XLA Ops:
  0.6 43.4 %collective-permute-start.1 = (bf16[208,2560]{1,0:T(8,128)(2,1)}, bf16[208,2560]{1,0:T(8,128)(2,1)S(1)}, u32[]{:S(2)}, u32[]{:S(2)}) collective-permute-start(bf16[208,2560]{1,0:T(8,128)(2,1)} %param.11), channel_id=1, source_target_pairs={{0,2},{1,3},{2,4},{3,5},{4,6},{5,7},{6,0},{7,1},{8,10},{9,11},{10,... | collective-permute-start | bytes 3194888 | tf_op jit(solution)/shard_map/ppermute | solution.py:302
  8.4 35.6 %collective-permute-start.2 = (bf16[208,2560]{1,0:T(8,128)(2,1)}, bf16[208,2560]{1,0:T(8,128)(2,1)S(1)}, u32[]{:S(2)}, u32[]{:S(2)}) collective-permute-start(bf16[208,2560]{1,0:T(8,128)(2,1)} %param.11), channel_id=1, source_target_pairs={{0,6},{1,7},{2,0},{3,1},{4,2},{5,3},{6,4},{7,5},{8,14},{9,15},{10,... | collective-permute-start | bytes 3194888 | tf_op jit(solution)/shard_map/ppermute | solution.py:302
  10.3 1.0 copy-start
  11.3 0.7 copy-start.8
  12.1 18.9 %collective-permute-start.4 = (bf16[208,128]{1,0:T(8,128)(2,1)S(1)}, bf16[208,128]{1,0:T(8,128)(2,1)S(1)}, u32[]{:S(2)}, u32[]{:S(2)}) collective-permute-start(bf16[208,128]{1,0:T(8,128)(2,1)S(1)} %get-tuple-element.19), channel_id=1, source_target_pairs={{0,5},{1,4},{2,7},{3,6},{4,1},{5,0},{6,3},{7,2},{8,13},{9,12},{10,... | collective-permute-start | bytes 159752 | tf_op jit(solution)/shard_map/ppermute | solution.py:302
  14.0 22.5 %collective-permute-start.3 = (bf16[224,128]{1,0:T(8,128)(2,1)S(1)}, bf16[224,128]{1,0:T(8,128)(2,1)S(1)}, u32[]{:S(2)}, u32[]{:S(2)}) collective-permute-start(bf16[224,128]{1,0:T(8,128)(2,1)S(1)} %get-tuple-element.18), channel_id=1, source_target_pairs={{0,4},{1,5},{2,6},{3,7},{4,0},{5,1},{6,2},{7,3},{8,12},{9,13},{10,... | collective-permute-start | bytes 172040 | tf_op jit(solution)/shard_map/ppermute | solution.py:302
  17.4 19.8 %collective-permute-start = (bf16[624,128]{1,0:T(8,128)(2,1)S(1)}, bf16[624,128]{1,0:T(8,128)(2,1)S(1)}, u32[]{:S(2)}, u32[]{:S(2)}) collective-permute-start(bf16[624,128]{1,0:T(8,128)(2,1)S(1)} %get-tuple-element.17), channel_id=1, source_target_pairs={{0,1},{1,0},{2,3},{3,2},{4,5},{5,4},{6,7},{7,6},{8,9},{9,8},{10,11... | collective-permute-start | bytes 479240 | tf_op jit(solution)/shard_map/ppermute | solution.py:305
  21.8 0.8 copy-start.2
  22.7 0.7 copy-start.9
  23.4 13.2 %copy-start.10 = (bf16[208,2560]{1,0:T(8,128)(2,1)S(1)}, bf16[208,2560]{1,0:T(8,128)(2,1)}, u32[]{:S(2)}) copy-start(bf16[208,2560]{1,0:T(8,128)(2,1)} %param.11) | copy-start | bytes 3194884
  32.8 5.4 %collective-permute-start.5 = (bf16[2560,128]{1,0:T(8,128)(2,1)S(1)}, bf16[2560,128]{1,0:T(8,128)(2,1)S(1)}, u32[]{:S(2)}, u32[]{:S(2)}) collective-permute-start(bf16[2560,128]{1,0:T(8,128)(2,1)S(1)} %fusion.1), channel_id=1, source_target_pairs={{0,1},{1,0},{2,3},{3,2},{4,5},{5,4},{6,7},{7,6},{8,9},{9,8},{10,11... | collective-permute-start | bytes 1966088 | tf_op jit(solution)/shard_map/ppermute | solution.py:305
  37.3 1.0 copy-start.1
  37.3 0.9 copy-start.3
  37.3 0.9 copy-start.4
  37.3 0.9 copy-start.6
  40.1 9.2 %collective-permute-start.7 = (bf16[512,128]{1,0:T(8,128)(2,1)S(1)}, bf16[512,128]{1,0:T(8,128)(2,1)S(1)}, u32[]{:S(2)}, u32[]{:S(2)}) collective-permute-start(bf16[512,128]{1,0:T(8,128)(2,1)S(1)} %get-tuple-element.23), channel_id=1, source_target_pairs={{0,4},{1,5},{2,6},{3,7},{4,0},{5,1},{6,2},{7,3},{8,12},{9,13},{10,... | collective-permute-start | bytes 393224 | tf_op jit(solution)/shard_map/ppermute | solution.py:302
  45.2 2.2 %copy-start.11 = (f32[1,2560,128]{2,1,0:T(8,128)S(1)}, f32[1,2560,128]{2,1,0:T(8,128)}, u32[]{:S(2)}) copy-start(f32[1,2560,128]{2,1,0:T(8,128)} %param.13) | copy-start | bytes 3932164
  45.3 4.1 %collective-permute-start.6 = (bf16[2560,128]{1,0:T(8,128)(2,1)S(1)}, bf16[2560,128]{1,0:T(8,128)(2,1)S(1)}, u32[]{:S(2)}, u32[]{:S(2)}) collective-permute-start(bf16[2560,128]{1,0:T(8,128)(2,1)S(1)} %slice.46), channel_id=1, source_target_pairs={{0,1},{1,0},{2,3},{3,2},{4,5},{5,4},{6,7},{7,6},{8,9},{9,8},{10,11... | collective-permute-start | bytes 1966088 | tf_op jit(solution)/shard_map/ppermute | solution.py:305
  49.4 32.6 %copy-start.5 = (bf16[384,128]{1,0:T(8,128)(2,1)S(1)}, bf16[384,128]{1,0:T(8,128)(2,1)}, u32[]{:S(2)}) copy-start(bf16[384,128]{1,0:T(8,128)(2,1)} %constant.19.clone.backward) | copy-start | bytes 294916
  50.4 56.7 %copy-start.7 = (bf16[64,192]{1,0:T(8,128)(2,1)S(1)}, bf16[64,192]{1,0:T(8,128)(2,1)}, u32[]{:S(2)}) copy-start(bf16[64,192]{1,0:T(8,128)(2,1)} %constant.15.clone.backward) | copy-start | bytes 73732
  84.0 26.3 %all-to-all-start.1 = ((bf16[64,8,640]{2,1,0:T(8,128)(2,1)}), bf16[64,8,640]{2,1,0:T(8,128)(2,1)S(1)}, u32[]{:S(2)}, u32[]{:S(2)}) async-start(bf16[64,8,640]{2,1,0:T(8,128)(2,1)} %bitcast.14), calls=%async_computation.1 | async-start | bytes 1310720 | tf_op jit(solution)/shard_map/all_to_all | solution.py:407
  88.6 18.6 %collective-permute-start.8 = (bf16[2560,128]{1,0:T(8,128)(2,1)S(1)}, bf16[2560,128]{1,0:T(8,128)(2,1)S(1)}, u32[]{:S(2)}, u32[]{:S(2)}) collective-permute-start(bf16[2560,128]{1,0:T(8,128)(2,1)S(1)} %get-tuple-element.27), channel_id=1, source_target_pairs={{0,4},{1,5},{2,6},{3,7},{4,0},{5,1},{6,2},{7,3},{8,12},{9,13},{10,... | collective-permute-start | bytes 1966088 | tf_op jit(solution)/shard_map/ppermute | solution.py:302

commit v11 on v10

--- a/solution.py
+++ b/solution.py
@@ -52,26 +52,32 @@
         ref[first : first + SPAN, :] = value[:, s * cols : (s + 1) * cols].astype(ref.dtype)
 
 
-def keys_kernel(chips, tokens, keys, ids, own, partner, far_own, far_partner):
+def keys_kernel(chips, tokens, keys, ids, own, partner, far):
     spot = lax.axis_index("tensor")
     chip, core = lax.shift_right_logical(spot, 1), lax.bitwise_and(spot, 1)
 
-    def block(step, which):
-        first = (2 * lax.bitwise_and(chip + step, chips - 1) + which) * tokens
-        return keys[pl.ds(pl.multiple_of(first, 16), tokens), :]
+    def first(step, which):
+        block = 2 * lax.bitwise_and(chip + step, chips - 1) + which
+        return pl.multiple_of(block * tokens, 16)
 
     for place, step in enumerate(NEAR):
         here = slice(place * tokens, (place + 1) * tokens)
-        own[here, :] = block(step, core)
-        partner[here, :] = block(step, 1 - core)
-    far_own[:tokens, :] = block(FAR, core)
-    far_partner[...] = block(FAR, 1 - core)
+        own[here, :] = keys[pl.ds(first(step, core), tokens), :]
+        partner[here, :] = keys[pl.ds(first(step, 1 - core), tokens), :]
+    far[: 2 * tokens, :] = keys[pl.ds(first(FAR, 0), 2 * tokens), :]
     most, halves, spans = ids.shape
+    wide = far.shape[1]
     rows = [ids[k].astype(jnp.float32) for k in range(most)]
     rows.append(jnp.zeros((16 - most * halves, spans), jnp.float32))
     rows = jnp.concatenate(rows, axis=0)
-    rows = jnp.concatenate([rows, jnp.zeros((16, far_own.shape[1] - spans), jnp.float32)], axis=1)
-    far_own[tokens:, :] = rows.astype(far_own.dtype)
+    rows = jnp.concatenate([rows, jnp.zeros((16, wide - spans), jnp.float32)], axis=1)
+    far[2 * tokens :, :] = rows.astype(far.dtype)
+
+
+def pair_kernel(tokens, far, mine, theirs):
+    core = lax.bitwise_and(lax.axis_index("tensor"), 1)
+    mine[...] = far[pl.ds(pl.multiple_of(core * tokens, 16), tokens), :]
+    theirs[...] = far[pl.ds(pl.multiple_of((1 - core) * tokens, 16), tokens), :]
 
 
 def routes_kernel(ids, count, base, mask, picks, numbers):
@@ -297,32 +303,35 @@
     cols = key_grad.shape[1]
     chips = group // 2
 
-    def along(x, step, across=False):
-        pairs = [(i, ((i + 2 * step) % group) ^ int(across)) for i in range(group)]
-        return lax.ppermute(x, "tensor", pairs)
+    def along(x, step):
+        return lax.ppermute(x, "tensor", [(i, (i + 2 * step) % group) for i in range(group)])
 
     def swap(x):
         return lax.ppermute(x, "tensor", [(i, i ^ 1) for i in range(group)])
 
     near_rows = jax.ShapeDtypeStruct((len(NEAR) * tokens, cols), jnp.bfloat16)
+    far_rows = jax.ShapeDtypeStruct((2 * tokens + 16, cols), jnp.bfloat16)
     ids = jnp.transpose(block_ids[0], (2, 1, 0))
-    own_keys, partner_keys, far_own, far_partner = call(
+    own_keys, partner_keys, far_keys = call(
         functools.partial(keys_kernel, chips, tokens),
         "keys",
-        (
-            near_rows,
-            near_rows,
-            jax.ShapeDtypeStruct((tokens + 16, cols), jnp.bfloat16),
-            jax.ShapeDtypeStruct((tokens, cols), jnp.bfloat16),
-        ),
+        (near_rows, near_rows, far_rows),
         key_grad,
         ids,
     )
-    far_own, far_partner = along(far_own, FAR), along(far_partner, FAR, across=True)
+    far_keys = along(far_keys, FAR)
+    activations, own_keys, partner_keys = lax.optimization_barrier(
+        (activations, own_keys, partner_keys)
+    )
     left, right = along(activations, 1), along(activations, -1)
 
-    far_other = swap(gram(activations, far_partner).astype(jnp.bfloat16))
-    far_part = gram(activations, far_own[:tokens])
+    block_rows = jax.ShapeDtypeStruct((tokens, cols), jnp.bfloat16)
+    far_own, far_theirs = call(
+        functools.partial(pair_kernel, tokens), "pair", (block_rows, block_rows), far_keys
+    )
+    far_theirs = swap(far_theirs)
+    far_other = swap(gram(activations, far_theirs).astype(jnp.bfloat16))
+    far_part = gram(activations, far_own)
     their_keys = swap(partner_keys)
 
     flat = jax.ShapeDtypeStruct((features, cols), jnp.float32)
@@ -361,7 +370,7 @@
         far_kernel,
         "far",
         (flat_half, jax.ShapeDtypeStruct((ROW_GROUPS * cols, cols), jnp.bfloat16)),
-        far_own[tokens:],
+        far_keys[2 * tokens :],
         counts,
         jnp.asarray(span_table.astype(np.float32).astype(ml_dtypes.bfloat16)),
         jnp.asarray(slot_table.astype(np.float32)),
@@ -408,7 +417,7 @@
             x.reshape(replicas, OWN_COLS, x.shape[1]), "dp", 0, 0, tiled=True
         ).reshape(x.shape)
 
-    pieces = exchange(sent)
+    pieces, far_whole = lax.optimization_barrier((exchange(sent), far_whole))
     (kept,) = call(kept_kernel, "kept", (flat,), advanced, far_whole, mask, forward, backward)
     (totals,) = call(
         total_kernel,

time: 112 us -> 111 us (level)
  the two profiles are of different devices: /device:TPU:6 before, /device:TPU:2 now
where the time goes in v11:
time: 111 us
  starting transfers between devices  54.5 us (49%)
  waiting for transfers between devices  34.2 us (31%)
  Pallas kernels  12.7 us (11%)
  matrix products  4.04 us (4%)
  local copies, waits for them, and re-layouts  3.36 us (3%)
  between operations  1.62 us (1%)
    all_to_all x2, waiting for transfers between devices, exchange(): lax.all_to_all(x.reshape(replicas, OWN_COLS, x.shape[1]), 'dp', 0, 0, til...  33.3 us
    all_to_all x2, starting transfers between devices, exchange(): lax.all_to_all(x.reshape(replicas, OWN_COLS, x.shape[1]), 'dp', 0, 0, til...  24.2 us
    ppermute x5, starting transfers between devices, along(): lax.ppermute(x, 'tensor', [(i, (i + 2 * step) % group) for i in range(gro...  22.1 us
    pallas_call x8, Pallas kernels, call(): pl.pallas_call(kernel, out_shape=outs, in_specs=places or [VMEM] * len(ar...  12.7 us
    ppermute x4, starting transfers between devices, swap(): return lax.ppermute(x, 'tensor', [(i, i ^ 1) for i in range(group)])  8.3 us
    dot_general x5, matrix products, gram(): lax.dot_general(a, k, (((0,), (0,)), ((), ())), preferred_element_type=jn...  4.04 us
    unnamed x24, local copies, waits for them, and re-layouts  3.27 us
  transfers between devices with their start and end apart: 11, of which 3 were waited for; matrix products, arithmetic and copies ran while one was open for 4% of the time, Pallas kernels for 9%

profile of v11, /device:TPU:2, one launch (start us, length us, event | category | flops | bytes accessed | tf_op | source)
XLA Modules:
  0.0 110.6 jit_solution(16938442015157928425)
XLA Ops:
  0.6 0.0 copy-start
  0.6 1.0 copy-done
  1.6 0.7 copy-done.8
  2.4 4.0 %collective-permute-start.3 = (bf16[432,128]{1,0:T(8,128)(2,1)S(1)}, bf16[432,128]{1,0:T(8,128)(2,1)S(1)}, u32[]{:S(2)}, u32[]{:S(2)}) collective-permute-start(bf16[432,128]{1,0:T(8,128)(2,1)S(1)} %get-tuple-element.27), channel_id=1, source_target_pairs={{0,4},{1,5},{2,6},{3,7},{4,0},{5,1},{6,2},{7,3},{8,12},{9,13},{10,... | collective-permute-start | bytes 331784 | tf_op jit(solution)/shard_map/ppermute | solution.py:307
  6.4 7.2 %collective-permute-start.1 = (bf16[208,2560]{1,0:T(8,128)(2,1)}, bf16[208,2560]{1,0:T(8,128)(2,1)S(1)}, u32[]{:S(2)}, u32[]{:S(2)}) collective-permute-start(bf16[208,2560]{1,0:T(8,128)(2,1)} %param.11), channel_id=1, source_target_pairs={{0,2},{1,3},{2,4},{3,5},{4,6},{5,7},{6,0},{7,1},{8,10},{9,11},{10,... | collective-permute-start | bytes 3194888 | tf_op jit(solution)/shard_map/ppermute | solution.py:307
  13.6 1.9 %collective-permute-start.2 = (bf16[208,2560]{1,0:T(8,128)(2,1)}, bf16[208,2560]{1,0:T(8,128)(2,1)S(1)}, u32[]{:S(2)}, u32[]{:S(2)}) collective-permute-start(bf16[208,2560]{1,0:T(8,128)(2,1)} %param.11), channel_id=1, source_target_pairs={{0,6},{1,7},{2,0},{3,1},{4,2},{5,3},{6,4},{7,5},{8,14},{9,15},{10,... | collective-permute-start | bytes 3194888 | tf_op jit(solution)/shard_map/ppermute | solution.py:307
  15.5 0.0 collective-permute-done.3.far
  15.5 1.9 %collective-permute-start.4 = (bf16[208,128]{1,0:T(8,128)(2,1)S(1)}, bf16[208,128]{1,0:T(8,128)(2,1)S(1)}, u32[]{:S(2)}, u32[]{:S(2)}) collective-permute-start(bf16[208,128]{1,0:T(8,128)(2,1)S(1)} %get-tuple-element.29), channel_id=1, source_target_pairs={{0,1},{1,0},{2,3},{3,2},{4,5},{5,4},{6,7},{7,6},{8,9},{9,8},{10,11... | collective-permute-start | bytes 159752 | tf_op jit(solution)/shard_map/ppermute | solution.py:310
  17.5 2.4 %collective-permute-start = (bf16[624,128]{1,0:T(8,128)(2,1)S(1)}, bf16[624,128]{1,0:T(8,128)(2,1)S(1)}, u32[]{:S(2)}, u32[]{:S(2)}) collective-permute-start(bf16[624,128]{1,0:T(8,128)(2,1)S(1)} %get-tuple-element.26), channel_id=1, source_target_pairs={{0,1},{1,0},{2,3},{3,2},{4,5},{5,4},{6,7},{7,6},{8,9},{9,8},{10,11... | collective-permute-start | bytes 479240 | tf_op jit(solution)/shard_map/ppermute | solution.py:310
  20.5 0.0 copy-start.2
  20.5 0.8 copy-done.2
  21.4 0.7 copy-done.9
  22.1 2.7 %routes.1 = (bf16[2560,128]{1,0:T(8,128)(2,1)S(1)}, bf16[1024,640]{1,0:T(8,128)(2,1)S(1)}, bf16[512,128]{1,0:T(8,128)(2,1)S(1)}) custom-call(s32[6,2,40]{2,1,0:T(2,128)S(1)} %bitcast.30, s32[1]{0:T(128)S(6)} %copy.13.count, f32[128,128]{1,0:T(8,128)S(1)} %copy-done.2), custom_call_target="tpu_custom_call" | custom-call | tf_op jit(solution)/shard_map/routes/pallas_call | solution.py:289
  24.8 0.0 collective-permute-done.4
  24.8 1.8 %convolution_convert_fusion = bf16[2560,128]{1,0:T(8,128)(2,1)S(1)} fusion(bf16[208,2560]{1,0:T(8,128)(2,1)} %param.11, bf16[208,128]{1,0:T(8,128)(2,1)S(1)} %collective-permute-done.4), kind=kOutput, calls=%fused_computation.2 | convolution fusion | flops 136642560 | bytes 1773568 | tf_op jit(solution)/shard_map/dot_general | solution.py:282
  26.6 1.9 %collective-permute-start.5 = (bf16[2560,128]{1,0:T(8,128)(2,1)S(1)}, bf16[2560,128]{1,0:T(8,128)(2,1)S(1)}, u32[]{:S(2)}, u32[]{:S(2)}) collective-permute-start(bf16[2560,128]{1,0:T(8,128)(2,1)S(1)} %convolution_convert_fusion), channel_id=1, source_target_pairs={{0,1},{1,0},{2,3},{3,2},{4,5},{5,4},{6,7},{7,6},{8,9},{9,8},{10,11... | collective-permute-start | bytes 1966088 | tf_op jit(solution)/shard_map/ppermute | solution.py:310
  28.6 0.6 fusion.1.part
  29.1 0.0 collective-permute-done
  29.2 0.0 copy-start.1
  29.2 0.0 copy-start.3
  29.2 0.0 copy-start.4
  29.2 0.0 copy-start.6
  29.2 0.6 fusion
  29.8 0.8 collective-permute-done.5.other
  30.6 0.0 copy-done.1
  30.6 2.1 %far.1 = (bf16[2560,128]{1,0:T(8,128)(2,1)}, bf16[512,128]{1,0:T(8,128)(2,1)S(1)}) custom-call(bf16[16,128]{1,0:T(8,128)(2,1)S(1)} %slice.26.numbers, s32[1]{0:T(128)S(6)} %copy.13.count, bf16[512,128]{1,0:T(8,128)(2,1)S(1)} %copy-done.4, f32[128,128]{1,0:T(8,128)S(1)} %copy-done.6, f32[128,128]{1,0:T(8,128)S(1)} %copy-done.3, f32[2560,128]{1,0:T(8,128)S(1)} %fusion.1.part, ...), custom_call_target="tpu_custom_call" | custom-call | tf_op jit(solution)/shard_map/far/pallas_call | solution.py:289
  32.8 3.4 %collective-permute-start.7 = (bf16[512,128]{1,0:T(8,128)(2,1)S(1)}, bf16[512,128]{1,0:T(8,128)(2,1)S(1)}, u32[]{:S(2)}, u32[]{:S(2)}) collective-permute-start(bf16[512,128]{1,0:T(8,128)(2,1)S(1)} %get-tuple-element.33), channel_id=1, source_target_pairs={{0,4},{1,5},{2,6},{3,7},{4,0},{5,1},{6,2},{7,3},{8,12},{9,13},{10,... | collective-permute-start | bytes 393224 | tf_op jit(solution)/shard_map/ppermute | solution.py:307
  36.1 0.0 collective-permute-done.1
  36.1 0.0 collective-permute-done.2
  36.2 0.6 convolution_add_fusion.1
  36.7 0.6 convolution_add_fusion
  37.3 0.0 copy-start.11
  37.3 0.1 slice.39
  37.4 2.1 %collective-permute-start.6 = (bf16[2560,128]{1,0:T(8,128)(2,1)S(1)}, bf16[2560,128]{1,0:T(8,128)(2,1)S(1)}, u32[]{:S(2)}, u32[]{:S(2)}) collective-permute-start(bf16[2560,128]{1,0:T(8,128)(2,1)S(1)} %slice.39), channel_id=1, source_target_pairs={{0,1},{1,0},{2,3},{3,2},{4,5},{5,4},{6,7},{7,6},{8,9},{9,8},{10,11... | collective-permute-start | bytes 1966088 | tf_op jit(solution)/shard_map/ppermute | solution.py:310
  39.5 5.6 %collective-permute-start.8 = (bf16[2560,128]{1,0:T(8,128)(2,1)}, bf16[2560,128]{1,0:T(8,128)(2,1)S(1)}, u32[]{:S(2)}, u32[]{:S(2)}) collective-permute-start(bf16[2560,128]{1,0:T(8,128)(2,1)} %get-tuple-element.38), channel_id=1, source_target_pairs={{0,4},{1,5},{2,6},{3,7},{4,0},{5,1},{6,2},{7,3},{8,12},{9,13},{10,... | collective-permute-start | bytes 1966088 | tf_op jit(solution)/shard_map/ppermute | solution.py:307
  45.1 0.2 slice_add_fusion.part
  45.2 0.0 collective-permute-done.7.far
  45.2 0.0 collective-permute-done.6.other
  45.3 0.0 copy-start.5
  45.3 1.7 %spectrum.1 = (f32[2560,128]{1,0:T(8,128)S(1)}, bf16[512,256]{1,0:T(8,128)(2,1)}) custom-call(f32[2560,128]{1,0:T(8,128)S(1)} %slice_add_fusion.part, bf16[2560,128]{1,0:T(8,128)(2,1)S(1)} %collective-permute-done.6.other, bf16[512,128]{1,0:T(8,128)(2,1)S(1)} %collective-permute-done.7.far, bf16[1024,640]{1,0:T(8,128)(2,1)S(1)} %get-tuple-element.34.picks, ...), custom_call_target="tpu_custom_call" | custom-call | tf_op jit(solution)/shard_map/spectrum/pallas_call | solution.py:289
  47.0 19.5 %all-to-all-start = ((bf16[64,8,256]{2,1,0:T(8,128)(2,1)}), bf16[64,8,256]{2,1,0:T(8,128)(2,1)S(1)}, u32[]{:S(2)}, u32[]{:S(2)}) async-start(bf16[64,8,256]{2,1,0:T(8,128)(2,1)} %bitcast.8), calls=%async_computation | async-start | bytes 524288 | tf_op jit(solution)/shard_map/all_to_all | solution.py:416
  66.5 0.0 collective-permute-done.8.far
  66.5 15.3 %all-to-all-done = bf16[64,8,256]{2,1,0:T(8,128)(2,1)S(1)} async-done(((bf16[64,8,256]{2,1,0:T(8,128)(2,1)}), bf16[64,8,256]{2,1,0:T(8,128)(2,1)S(1)}, u32[]{:S(2)}, u32[]{:S(2)}) %all-to-all-start) | async-done | bytes 262176 | tf_op jit(solution)/shard_map/all_to_all | solution.py:416
  81.9 1.9 %total.1 = bf16[512,640]{1,0:T(8,128)(2,1)} custom-call(bf16[512,256]{1,0:T(8,128)(2,1)S(1)} %bitcast.28, bf16[384,128]{1,0:T(8,128)(2,1)S(1)} %copy-done.5), custom_call_target="tpu_custom_call" | custom-call | tf_op jit(solution)/shard_map/total/pallas_call | solution.py:289
  83.8 4.6 %all-to-all-start.1 = ((bf16[64,8,640]{2,1,0:T(8,128)(2,1)}), bf16[64,8,640]{2,1,0:T(8,128)(2,1)S(1)}, u32[]{:S(2)}, u32[]{:S(2)}) async-start(bf16[64,8,640]{2,1,0:T(8,128)(2,1)} %bitcast.11), calls=%async_computation.1 | async-start | bytes 1310720 | tf_op jit(solution)/shard_map/all_to_all | solution.py:416
  88.4 3.1 %kept.1 = f32[2560,128]{1,0:T(8,128)} custom-call(f32[2560,128]{1,0:T(8,128)S(1)} %get-tuple-element.36.advanced, bf16[2560,128]{1,0:T(8,128)(2,1)S(1)} %collective-permute-done.8.far, bf16[2560,128]{1,0:T(8,128)(2,1)S(1)} %get-tuple-element.40.mask, bf16[64,192]{1,0:T(8,128)(2,1)S(1)} %copy-done.1, bf16[64,192]{1,0:T(8,128)(2,1)S(1)} %copy-done.7), custom_call_target="tpu_custom_call" | custom-call | tf_op jit(solution)/shard_map/kept/pallas_call | solution.py:289
  91.5 18.0 %all-to-all-done.1 = bf16[64,8,640]{2,1,0:T(8,128)(2,1)S(1)} async-done(((bf16[64,8,640]{2,1,0:T(8,128)(2,1)}), bf16[64,8,640]{2,1,0:T(8,128)(2,1)S(1)}, u32[]{:S(2)}, u32[]{:S(2)}) %all-to-all-start.1) | async-done | bytes 655392 | tf_op jit(solution)/shard_map/all_to_all | solution.py:416
  109.5 1.1 turn.1
  (15 shorter events, 0.1 us)
Async XLA Ops:
  0.6 1.0 copy-start
  1.6 0.7 copy-start.8
  2.4 13.1 %collective-permute-start.3 = (bf16[432,128]{1,0:T(8,128)(2,1)S(1)}, bf16[432,128]{1,0:T(8,128)(2,1)S(1)}, u32[]{:S(2)}, u32[]{:S(2)}) collective-permute-start(bf16[432,128]{1,0:T(8,128)(2,1)S(1)} %get-tuple-element.27), channel_id=1, source_target_pairs={{0,4},{1,5},{2,6},{3,7},{4,0},{5,1},{6,2},{7,3},{8,12},{9,13},{10,... | collective-permute-start | bytes 331784 | tf_op jit(solution)/shard_map/ppermute | solution.py:307
  6.4 29.7 %collective-permute-start.1 = (bf16[208,2560]{1,0:T(8,128)(2,1)}, bf16[208,2560]{1,0:T(8,128)(2,1)S(1)}, u32[]{:S(2)}, u32[]{:S(2)}) collective-permute-start(bf16[208,2560]{1,0:T(8,128)(2,1)} %param.11), channel_id=1, source_target_pairs={{0,2},{1,3},{2,4},{3,5},{4,6},{5,7},{6,0},{7,1},{8,10},{9,11},{10,... | collective-permute-start | bytes 3194888 | tf_op jit(solution)/shard_map/ppermute | solution.py:307
  13.6 22.6 %collective-permute-start.2 = (bf16[208,2560]{1,0:T(8,128)(2,1)}, bf16[208,2560]{1,0:T(8,128)(2,1)S(1)}, u32[]{:S(2)}, u32[]{:S(2)}) collective-permute-start(bf16[208,2560]{1,0:T(8,128)(2,1)} %param.11), channel_id=1, source_target_pairs={{0,6},{1,7},{2,0},{3,1},{4,2},{5,3},{6,4},{7,5},{8,14},{9,15},{10,... | collective-permute-start | bytes 3194888 | tf_op jit(solution)/shard_map/ppermute | solution.py:307
  15.5 9.3 %collective-permute-start.4 = (bf16[208,128]{1,0:T(8,128)(2,1)S(1)}, bf16[208,128]{1,0:T(8,128)(2,1)S(1)}, u32[]{:S(2)}, u32[]{:S(2)}) collective-permute-start(bf16[208,128]{1,0:T(8,128)(2,1)S(1)} %get-tuple-element.29), channel_id=1, source_target_pairs={{0,1},{1,0},{2,3},{3,2},{4,5},{5,4},{6,7},{7,6},{8,9},{9,8},{10,11... | collective-permute-start | bytes 159752 | tf_op jit(solution)/shard_map/ppermute | solution.py:310
  17.5 11.7 %collective-permute-start = (bf16[624,128]{1,0:T(8,128)(2,1)S(1)}, bf16[624,128]{1,0:T(8,128)(2,1)S(1)}, u32[]{:S(2)}, u32[]{:S(2)}) collective-permute-start(bf16[624,128]{1,0:T(8,128)(2,1)S(1)} %get-tuple-element.26), channel_id=1, source_target_pairs={{0,1},{1,0},{2,3},{3,2},{4,5},{5,4},{6,7},{7,6},{8,9},{9,8},{10,11... | collective-permute-start | bytes 479240 | tf_op jit(solution)/shard_map/ppermute | solution.py:310
  20.5 0.8 copy-start.2
  21.4 0.7 copy-start.9
  22.1 6.5 %copy-start.10 = (bf16[208,2560]{1,0:T(8,128)(2,1)S(1)}, bf16[208,2560]{1,0:T(8,128)(2,1)}, u32[]{:S(2)}) copy-start(bf16[208,2560]{1,0:T(8,128)(2,1)} %param.11) | copy-start | bytes 3194884
  26.6 4.0 %collective-permute-start.5 = (bf16[2560,128]{1,0:T(8,128)(2,1)S(1)}, bf16[2560,128]{1,0:T(8,128)(2,1)S(1)}, u32[]{:S(2)}, u32[]{:S(2)}) collective-permute-start(bf16[2560,128]{1,0:T(8,128)(2,1)S(1)} %convolution_convert_fusion), channel_id=1, source_target_pairs={{0,1},{1,0},{2,3},{3,2},{4,5},{5,4},{6,7},{7,6},{8,9},{9,8},{10,11... | collective-permute-start | bytes 1966088 | tf_op jit(solution)/shard_map/ppermute | solution.py:310
  29.2 1.4 %copy-start.1 = (bf16[64,192]{1,0:T(8,128)(2,1)S(1)}, bf16[64,192]{1,0:T(8,128)(2,1)}, u32[]{:S(2)}) copy-start(bf16[64,192]{1,0:T(8,128)(2,1)} %constant.14.clone.forward) | copy-start | bytes 73732
  29.2 1.4 %copy-start.3 = (f32[128,128]{1,0:T(8,128)S(1)}, f32[128,128]{1,0:T(8,128)}, u32[]{:S(2)}) copy-start(f32[128,128]{1,0:T(8,128)} %constant.16.clone.base) | copy-start | bytes 196612
  29.2 1.4 %copy-start.4 = (bf16[512,128]{1,0:T(8,128)(2,1)S(1)}, bf16[512,128]{1,0:T(8,128)(2,1)}, u32[]{:S(2)}) copy-start(bf16[512,128]{1,0:T(8,128)(2,1)} %constant.17.clone.spans) | copy-start | bytes 393220
  29.2 1.4 %copy-start.6 = (f32[128,128]{1,0:T(8,128)S(1)}, f32[128,128]{1,0:T(8,128)}, u32[]{:S(2)}) copy-start(f32[128,128]{1,0:T(8,128)} %constant.18.clone.slots) | copy-start | bytes 196612
  32.8 12.5 %collective-permute-start.7 = (bf16[512,128]{1,0:T(8,128)(2,1)S(1)}, bf16[512,128]{1,0:T(8,128)(2,1)S(1)}, u32[]{:S(2)}, u32[]{:S(2)}) collective-permute-start(bf16[512,128]{1,0:T(8,128)(2,1)S(1)} %get-tuple-element.33), channel_id=1, source_target_pairs={{0,4},{1,5},{2,6},{3,7},{4,0},{5,1},{6,2},{7,3},{8,12},{9,13},{10,... | collective-permute-start | bytes 393224 | tf_op jit(solution)/shard_map/ppermute | solution.py:307
  37.3 7.8 %copy-start.11 = (f32[1,2560,128]{2,1,0:T(8,128)S(1)}, f32[1,2560,128]{2,1,0:T(8,128)}, u32[]{:S(2)}) copy-start(f32[1,2560,128]{2,1,0:T(8,128)} %param.13) | copy-start | bytes 3932164
  37.4 7.8 %collective-permute-start.6 = (bf16[2560,128]{1,0:T(8,128)(2,1)S(1)}, bf16[2560,128]{1,0:T(8,128)(2,1)S(1)}, u32[]{:S(2)}, u32[]{:S(2)}) collective-permute-start(bf16[2560,128]{1,0:T(8,128)(2,1)S(1)} %slice.39), channel_id=1, source_target_pairs={{0,1},{1,0},{2,3},{3,2},{4,5},{5,4},{6,7},{7,6},{8,9},{9,8},{10,11... | collective-permute-start | bytes 1966088 | tf_op jit(solution)/shard_map/ppermute | solution.py:310
  39.5 27.1 %collective-permute-start.8 = (bf16[2560,128]{1,0:T(8,128)(2,1)}, bf16[2560,128]{1,0:T(8,128)(2,1)S(1)}, u32[]{:S(2)}, u32[]{:S(2)}) collective-permute-start(bf16[2560,128]{1,0:T(8,128)(2,1)} %get-tuple-element.38), channel_id=1, source_target_pairs={{0,4},{1,5},{2,6},{3,7},{4,0},{5,1},{6,2},{7,3},{8,12},{9,13},{10,... | collective-permute-start | bytes 1966088 | tf_op jit(solution)/shard_map/ppermute | solution.py:307
  45.3 36.6 %copy-start.5 = (bf16[384,128]{1,0:T(8,128)(2,1)S(1)}, bf16[384,128]{1,0:T(8,128)(2,1)}, u32[]{:S(2)}) copy-start(bf16[384,128]{1,0:T(8,128)(2,1)} %constant.19.clone.backward) | copy-start | bytes 294916
  47.0 41.4 %copy-start.7 = (bf16[64,192]{1,0:T(8,128)(2,1)S(1)}, bf16[64,192]{1,0:T(8,128)(2,1)}, u32[]{:S(2)}) copy-start(bf16[64,192]{1,0:T(8,128)(2,1)} %constant.15.clone.backward) | copy-start | bytes 73732
  47.0 34.9 %all-to-all-start = ((bf16[64,8,256]{2,1,0:T(8,128)(2,1)}), bf16[64,8,256]{2,1,0:T(8,128)(2,1)S(1)}, u32[]{:S(2)}, u32[]{:S(2)}) async-start(bf16[64,8,256]{2,1,0:T(8,128)(2,1)} %bitcast.8), calls=%async_computation | async-start | bytes 524288 | tf_op jit(solution)/shard_map/all_to_all | solution.py:416
  83.8 25.8 %all-to-all-start.1 = ((bf16[64,8,640]{2,1,0:T(8,128)(2,1)}), bf16[64,8,640]{2,1,0:T(8,128)(2,1)S(1)}, u32[]{:S(2)}, u32[]{:S(2)}) async-start(bf16[64,8,640]{2,1,0:T(8,128)(2,1)} %bitcast.11), calls=%async_computation.1 | async-start | bytes 1310720 | tf_op jit(solution)/shard_map/all_to_all | solution.py:416

commit v12 on v11

--- a/solution.py
+++ b/solution.py
@@ -72,6 +72,10 @@
     rows = jnp.concatenate(rows, axis=0)
     rows = jnp.concatenate([rows, jnp.zeros((16, wide - spans), jnp.float32)], axis=1)
     far[2 * tokens :, :] = rows.astype(far.dtype)
+
+
+def copy_kernel(x, y):
+    y[...] = x[...]
 
 
 def pair_kernel(tokens, far, mine, theirs):
@@ -320,6 +324,12 @@
         ids,
     )
     far_keys = along(far_keys, FAR)
+    (activations,) = call(
+        copy_kernel,
+        "copy",
+        (jax.ShapeDtypeStruct(activations.shape, activations.dtype),),
+        activations,
+    )
     activations, own_keys, partner_keys = lax.optimization_barrier(
         (activations, own_keys, partner_keys)
     )
@@ -388,10 +398,11 @@
 
     keys = jnp.concatenate([own_keys, their_keys], axis=1)
     keys = lax.optimization_barrier(keys.reshape(len(NEAR), tokens, 2 * cols))
-    left, right, far_whole = lax.optimization_barrier((left, right, far_whole))
-    far_whole = along(far_whole, FAR)
     near = gram(activations, keys[0]) + gram(right, keys[1]) + gram(left, keys[2])
-    other = swap(near[:, cols:].astype(jnp.bfloat16))
+    other, far_whole = lax.optimization_barrier(
+        (near[:, cols:].astype(jnp.bfloat16), far_whole)
+    )
+    other, far_whole = swap(other), along(far_whole, FAR)
     part = near[:, :cols] + 0.999 * momentum[0]
 
     order = np.concatenate([np.arange(0, SPAN, 2), np.arange(1, SPAN, 2)])
@@ -417,8 +428,7 @@
             x.reshape(replicas, OWN_COLS, x.shape[1]), "dp", 0, 0, tiled=True
         ).reshape(x.shape)
 
-    pieces, far_whole = lax.optimization_barrier((exchange(sent), far_whole))
-    (kept,) = call(kept_kernel, "kept", (flat,), advanced, far_whole, mask, forward, backward)
+    pieces = exchange(sent)
     (totals,) = call(
         total_kernel,
         "total",
@@ -427,6 +437,8 @@
         backward_pair,
         scratch=(pltpu.VMEM((height, replicas * OWN_COLS), jnp.bfloat16),),
     )
+    totals, far_whole = lax.optimization_barrier((totals, far_whole))
+    (kept,) = call(kept_kernel, "kept", (flat,), advanced, far_whole, mask, forward, backward)
     (update,) = call(turn_kernel, "turn", (flat_half,), exchange(totals))
     return kept[None], update
 

time: 111 us -> 113 us (1.018)
  the two profiles are of different devices: /device:TPU:2 before, /device:TPU:4 now
where the time goes in v12:
time: 113 us; the launch traced here: 112 us
  starting transfers between devices  38.6 us (34%)
  blocking collectives  27.5 us (24%)
  waiting for transfers between devices  26.8 us (24%)
  Pallas kernels  11.8 us (10%)
  local copies, waits for them, and re-layouts  3.06 us (3%)
  matrix products  2.81 us (2%)
  between operations  1.61 us (1%)
    all_to_all x1, blocking collectives, exchange(): lax.all_to_all(x.reshape(replicas, OWN_COLS, x.shape[1]), 'dp', 0, 0, til...  27.5 us
    ppermute x5, starting transfers between devices, along(): lax.ppermute(x, 'tensor', [(i, (i + 2 * step) % group) for i in range(gro...  25.7 us
    all_to_all x1, waiting for transfers between devices, exchange(): lax.all_to_all(x.reshape(replicas, OWN_COLS, x.shape[1]), 'dp', 0, 0, til...  18 us
    pallas_call x9, Pallas kernels, call(): pl.pallas_call(kernel, out_shape=outs, in_specs=places or [VMEM] * len(ar...  11.8 us
    ppermute x4, starting transfers between devices, swap(): return lax.ppermute(x, 'tensor', [(i, i ^ 1) for i in range(group)])  8.3 us
    ppermute x5, waiting for transfers between devices, along(): lax.ppermute(x, 'tensor', [(i, (i + 2 * step) % group) for i in range(gro...  8.17 us
    all_to_all x1, starting transfers between devices, exchange(): lax.all_to_all(x.reshape(replicas, OWN_COLS, x.shape[1]), 'dp', 0, 0, til...  4.64 us
    unnamed x22, local copies, waits for them, and re-layouts  2.97 us
  transfers between devices with their start and end apart: 10, of which 3 were waited for; matrix products, arithmetic and copies ran while one was open for 3% of the time, Pallas kernels for 10%

profile of v12, /device:TPU:4, one launch (start us, length us, event | category | flops | bytes accessed | tf_op | source)
XLA Modules:
  0.0 112.3 jit_solution(15161047748699193094)
XLA Ops:
  0.6 0.0 copy-start.1
  0.6 1.0 copy-done.1
  1.6 0.7 copy-done.8
  2.4 7.8 %collective-permute-start.3 = (bf16[432,128]{1,0:T(8,128)(2,1)S(1)}, bf16[432,128]{1,0:T(8,128)(2,1)S(1)}, u32[]{:S(2)}, u32[]{:S(2)}) collective-permute-start(bf16[432,128]{1,0:T(8,128)(2,1)S(1)} %get-tuple-element.26), channel_id=1, source_target_pairs={{0,4},{1,5},{2,6},{3,7},{4,0},{5,1},{6,2},{7,3},{8,12},{9,13},{10,... | collective-permute-start | bytes 331784 | tf_op jit(solution)/shard_map/ppermute | solution.py:311
  10.2 0.0 copy-start
  10.2 1.2 %copy-done = bf16[208,2560]{1,0:T(8,128)(2,1)S(1)} copy-done((bf16[208,2560]{1,0:T(8,128)(2,1)S(1)}, bf16[208,2560]{1,0:T(8,128)(2,1)}, u32[]{:S(2)}) %copy-start) | copy-done | bytes 1064984
  11.4 0.1 copy.15
  11.5 1.9 %collective-permute-start.1 = (bf16[208,2560]{1,0:T(8,128)(2,1)S(1)}, bf16[208,2560]{1,0:T(8,128)(2,1)S(1)}, u32[]{:S(2)}, u32[]{:S(2)}) collective-permute-start(bf16[208,2560]{1,0:T(8,128)(2,1)S(1)} %copy.15), channel_id=1, source_target_pairs={{0,6},{1,7},{2,0},{3,1},{4,2},{5,3},{6,4},{7,5},{8,14},{9,15},{10,... | collective-permute-start | bytes 3194888 | tf_op jit(solution)/shard_map/ppermute | solution.py:311
  13.4 0.0 collective-permute-done.3.far
  13.4 1.9 %collective-permute-start.4 = (bf16[208,128]{1,0:T(8,128)(2,1)S(1)}, bf16[208,128]{1,0:T(8,128)(2,1)S(1)}, u32[]{:S(2)}, u32[]{:S(2)}) collective-permute-start(bf16[208,128]{1,0:T(8,128)(2,1)S(1)} %get-tuple-element.28), channel_id=1, source_target_pairs={{0,1},{1,0},{2,3},{3,2},{4,5},{5,4},{6,7},{7,6},{8,9},{9,8},{10,11... | collective-permute-start | bytes 159752 | tf_op jit(solution)/shard_map/ppermute | solution.py:314
  15.4 3.9 %collective-permute-start.2 = (bf16[208,2560]{1,0:T(8,128)(2,1)S(1)}, bf16[208,2560]{1,0:T(8,128)(2,1)S(1)}, u32[]{:S(2)}, u32[]{:S(2)}) collective-permute-start(bf16[208,2560]{1,0:T(8,128)(2,1)S(1)} %copy.15), channel_id=1, source_target_pairs={{0,2},{1,3},{2,4},{3,5},{4,6},{5,7},{6,0},{7,1},{8,10},{9,11},{10,... | collective-permute-start | bytes 3194888 | tf_op jit(solution)/shard_map/ppermute | solution.py:311
  19.3 2.1 %collective-permute-start = (bf16[624,128]{1,0:T(8,128)(2,1)S(1)}, bf16[624,128]{1,0:T(8,128)(2,1)S(1)}, u32[]{:S(2)}, u32[]{:S(2)}) collective-permute-start(bf16[624,128]{1,0:T(8,128)(2,1)S(1)} %get-tuple-element.25), channel_id=1, source_target_pairs={{0,1},{1,0},{2,3},{3,2},{4,5},{5,4},{6,7},{7,6},{8,9},{9,8},{10,11... | collective-permute-start | bytes 479240 | tf_op jit(solution)/shard_map/ppermute | solution.py:314
  22.1 0.0 copy-done.3
  22.1 2.7 %routes.1 = (bf16[2560,128]{1,0:T(8,128)(2,1)S(1)}, bf16[1024,640]{1,0:T(8,128)(2,1)S(1)}, bf16[512,128]{1,0:T(8,128)(2,1)S(1)}) custom-call(s32[6,2,40]{2,1,0:T(2,128)S(1)} %bitcast.31, s32[1]{0:T(128)S(6)} %copy.14.count, f32[128,128]{1,0:T(8,128)S(1)} %copy-done.3), custom_call_target="tpu_custom_call" | custom-call | tf_op jit(solution)/shard_map/routes/pallas_call | solution.py:293
  24.9 0.0 collective-permute-done.4
  24.9 0.6 convolution_convert_fusion
  25.4 2.2 %collective-permute-start.5 = (bf16[2560,128]{1,0:T(8,128)(2,1)S(1)}, bf16[2560,128]{1,0:T(8,128)(2,1)S(1)}, u32[]{:S(2)}, u32[]{:S(2)}) collective-permute-start(bf16[2560,128]{1,0:T(8,128)(2,1)S(1)} %convolution_convert_fusion), channel_id=1, source_target_pairs={{0,1},{1,0},{2,3},{3,2},{4,5},{5,4},{6,7},{7,6},{8,9},{9,8},{10,11... | collective-permute-start | bytes 1966088 | tf_op jit(solution)/shard_map/ppermute | solution.py:314
  27.6 0.6 fusion.1.part
  28.2 0.0 collective-permute-done
  28.3 0.0 copy-start.2
  28.3 0.0 copy-start.4
  28.3 0.0 copy-start.6
  28.3 0.6 fusion
  28.9 0.6 collective-permute-done.5.other
  29.4 0.0 copy-done.4
  29.4 1.8 %far.1 = (bf16[2560,128]{1,0:T(8,128)(2,1)S(1)}, bf16[512,128]{1,0:T(8,128)(2,1)S(1)}) custom-call(bf16[16,128]{1,0:T(8,128)(2,1)S(1)} %slice.30.numbers, s32[1]{0:T(128)S(6)} %copy.14.count, bf16[512,128]{1,0:T(8,128)(2,1)S(1)} %copy-done.4, f32[128,128]{1,0:T(8,128)S(1)} %copy-done.6, f32[128,128]{1,0:T(8,128)S(1)} %copy-done.3, ...), custom_call_target="tpu_custom_call" | custom-call | tf_op jit(solution)/shard_map/far/pallas_call | solution.py:293
  31.3 3.2 %collective-permute-start.7 = (bf16[512,128]{1,0:T(8,128)(2,1)S(1)}, bf16[512,128]{1,0:T(8,128)(2,1)S(1)}, u32[]{:S(2)}, u32[]{:S(2)}) collective-permute-start(bf16[512,128]{1,0:T(8,128)(2,1)S(1)} %get-tuple-element.31), channel_id=1, source_target_pairs={{0,4},{1,5},{2,6},{3,7},{4,0},{5,1},{6,2},{7,3},{8,12},{9,13},{10,... | collective-permute-start | bytes 393224 | tf_op jit(solution)/shard_map/ppermute | solution.py:311
  34.4 0.0 collective-permute-done.1
  34.4 0.6 convolution_add_fusion.1
  35.0 8.2 %collective-permute-done.2 = bf16[208,2560]{1,0:T(8,128)(2,1)S(1)} collective-permute-done((bf16[208,2560]{1,0:T(8,128)(2,1)S(1)}, bf16[208,2560]{1,0:T(8,128)(2,1)S(1)}, u32[]{:S(2)}, u32[]{:S(2)}) %collective-permute-start.2) | collective-permute-done | bytes 1064992 | tf_op jit(solution)/shard_map/ppermute | solution.py:311
  43.2 0.6 convolution_add_fusion
  43.8 0.0 copy-start.10
  43.8 0.1 slice.39
  43.9 2.1 %collective-permute-start.6 = (bf16[2560,128]{1,0:T(8,128)(2,1)S(1)}, bf16[2560,128]{1,0:T(8,128)(2,1)S(1)}, u32[]{:S(2)}, u32[]{:S(2)}) collective-permute-start(bf16[2560,128]{1,0:T(8,128)(2,1)S(1)} %slice.39), channel_id=1, source_target_pairs={{0,1},{1,0},{2,3},{3,2},{4,5},{5,4},{6,7},{7,6},{8,9},{9,8},{10,11... | collective-permute-start | bytes 1966088 | tf_op jit(solution)/shard_map/ppermute | solution.py:314
  45.9 8.9 %collective-permute-start.8 = (bf16[2560,128]{1,0:T(8,128)(2,1)S(1)}, bf16[2560,128]{1,0:T(8,128)(2,1)S(1)}, u32[]{:S(2)}, u32[]{:S(2)}) collective-permute-start(bf16[2560,128]{1,0:T(8,128)(2,1)S(1)} %get-tuple-element.36), channel_id=1, source_target_pairs={{0,4},{1,5},{2,6},{3,7},{4,0},{5,1},{6,2},{7,3},{8,12},{9,13},{10,... | collective-permute-start | bytes 1966088 | tf_op jit(solution)/shard_map/ppermute | solution.py:311
  54.8 0.2 slice_add_fusion.part
  55.0 0.0 collective-permute-done.7.far
  55.0 0.0 collective-permute-done.6.other
  55.0 0.0 copy-start.5
  55.0 1.0 spectrum.1
  56.1 0.0 copy-start.7
  56.1 27.5 %all_to_all.10 = bf16[64,8,256]{2,1,0:T(8,128)(2,1)S(1)} all-to-all(bf16[64,8,256]{2,1,0:T(8,128)(2,1)S(1)} %bitcast.29), channel_id=1, replica_groups=mesh['dp'=64,'tensor'=8] {'dp'}, dimensions={0} | all-to-all | bytes 524288 | tf_op jit(solution)/shard_map/all_to_all | solution.py:427
  83.6 1.9 %total.1 = bf16[512,640]{1,0:T(8,128)(2,1)} custom-call(bf16[512,256]{1,0:T(8,128)(2,1)S(1)} %bitcast.28, bf16[384,128]{1,0:T(8,128)(2,1)S(1)} %copy-done.5), custom_call_target="tpu_custom_call" | custom-call | tf_op jit(solution)/shard_map/total/pallas_call | solution.py:293
  85.5 0.0 collective-permute-done.8.far
  85.5 4.6 %all-to-all-start.1 = ((bf16[64,8,640]{2,1,0:T(8,128)(2,1)}), bf16[64,8,640]{2,1,0:T(8,128)(2,1)S(1)}, u32[]{:S(2)}, u32[]{:S(2)}) async-start(bf16[64,8,640]{2,1,0:T(8,128)(2,1)} %bitcast.11), calls=%async_computation.1 | async-start | bytes 1310720 | tf_op jit(solution)/shard_map/all_to_all | solution.py:427
  90.2 3.1 %kept.1 = f32[2560,128]{1,0:T(8,128)} custom-call(f32[2560,128]{1,0:T(8,128)S(1)} %get-tuple-element.34.advanced, bf16[2560,128]{1,0:T(8,128)(2,1)S(1)} %collective-permute-done.8.far, bf16[2560,128]{1,0:T(8,128)(2,1)S(1)} %get-tuple-element.38.mask, bf16[64,192]{1,0:T(8,128)(2,1)S(1)} %copy-done.2, bf16[64,192]{1,0:T(8,128)(2,1)S(1)} %copy-done.7), custom_call_target="tpu_custom_call" | custom-call | tf_op jit(solution)/shard_map/kept/pallas_call | solution.py:293
  93.3 18.0 %all-to-all-done.1 = bf16[64,8,640]{2,1,0:T(8,128)(2,1)S(1)} async-done(((bf16[64,8,640]{2,1,0:T(8,128)(2,1)}), bf16[64,8,640]{2,1,0:T(8,128)(2,1)S(1)}, u32[]{:S(2)}, u32[]{:S(2)}) %all-to-all-start.1) | async-done | bytes 655392 | tf_op jit(solution)/shard_map/all_to_all | solution.py:427
  111.3 1.1 turn.1
  (13 shorter events, 0.1 us)
Async XLA Ops:
  0.6 1.0 copy-start.1
  1.6 0.7 copy-start.8
  2.3 19.8 %copy-start.3 = (f32[128,128]{1,0:T(8,128)S(1)}, f32[128,128]{1,0:T(8,128)}, u32[]{:S(2)}) copy-start(f32[128,128]{1,0:T(8,128)} %constant.16.clone.base) | copy-start | bytes 196612
  2.3 19.8 %copy-start.9 = (s32[1,40,2,6]{1,2,3,0:T(2,128)S(1)}, s32[1,40,2,6]{1,2,3,0:T(2,128)}, u32[]{:S(2)}) copy-start(s32[1,40,2,6]{1,2,3,0:T(2,128)} %param.14) | copy-start | bytes 5764
  2.4 11.0 %collective-permute-start.3 = (bf16[432,128]{1,0:T(8,128)(2,1)S(1)}, bf16[432,128]{1,0:T(8,128)(2,1)S(1)}, u32[]{:S(2)}, u32[]{:S(2)}) collective-permute-start(bf16[432,128]{1,0:T(8,128)(2,1)S(1)} %get-tuple-element.26), channel_id=1, source_target_pairs={{0,4},{1,5},{2,6},{3,7},{4,0},{5,1},{6,2},{7,3},{8,12},{9,13},{10,... | collective-permute-start | bytes 331784 | tf_op jit(solution)/shard_map/ppermute | solution.py:311
  10.2 1.2 %copy-start = (bf16[208,2560]{1,0:T(8,128)(2,1)S(1)}, bf16[208,2560]{1,0:T(8,128)(2,1)}, u32[]{:S(2)}) copy-start(bf16[208,2560]{1,0:T(8,128)(2,1)} %x.1) | copy-start | bytes 3194884
  11.5 23.0 %collective-permute-start.1 = (bf16[208,2560]{1,0:T(8,128)(2,1)S(1)}, bf16[208,2560]{1,0:T(8,128)(2,1)S(1)}, u32[]{:S(2)}, u32[]{:S(2)}) collective-permute-start(bf16[208,2560]{1,0:T(8,128)(2,1)S(1)} %copy.15), channel_id=1, source_target_pairs={{0,6},{1,7},{2,0},{3,1},{4,2},{5,3},{6,4},{7,5},{8,14},{9,15},{10,... | collective-permute-start | bytes 3194888 | tf_op jit(solution)/shard_map/ppermute | solution.py:311
  13.4 11.4 %collective-permute-start.4 = (bf16[208,128]{1,0:T(8,128)(2,1)S(1)}, bf16[208,128]{1,0:T(8,128)(2,1)S(1)}, u32[]{:S(2)}, u32[]{:S(2)}) collective-permute-start(bf16[208,128]{1,0:T(8,128)(2,1)S(1)} %get-tuple-element.28), channel_id=1, source_target_pairs={{0,1},{1,0},{2,3},{3,2},{4,5},{5,4},{6,7},{7,6},{8,9},{9,8},{10,11... | collective-permute-start | bytes 159752 | tf_op jit(solution)/shard_map/ppermute | solution.py:314
  15.4 27.8 %collective-permute-start.2 = (bf16[208,2560]{1,0:T(8,128)(2,1)S(1)}, bf16[208,2560]{1,0:T(8,128)(2,1)S(1)}, u32[]{:S(2)}, u32[]{:S(2)}) collective-permute-start(bf16[208,2560]{1,0:T(8,128)(2,1)S(1)} %copy.15), channel_id=1, source_target_pairs={{0,2},{1,3},{2,4},{3,5},{4,6},{5,7},{6,0},{7,1},{8,10},{9,11},{10,... | collective-permute-start | bytes 3194888 | tf_op jit(solution)/shard_map/ppermute | solution.py:311
  19.3 8.9 %collective-permute-start = (bf16[624,128]{1,0:T(8,128)(2,1)S(1)}, bf16[624,128]{1,0:T(8,128)(2,1)S(1)}, u32[]{:S(2)}, u32[]{:S(2)}) collective-permute-start(bf16[624,128]{1,0:T(8,128)(2,1)S(1)} %get-tuple-element.25), channel_id=1, source_target_pairs={{0,1},{1,0},{2,3},{3,2},{4,5},{5,4},{6,7},{7,6},{8,9},{9,8},{10,11... | collective-permute-start | bytes 479240 | tf_op jit(solution)/shard_map/ppermute | solution.py:314
  25.4 4.0 %collective-permute-start.5 = (bf16[2560,128]{1,0:T(8,128)(2,1)S(1)}, bf16[2560,128]{1,0:T(8,128)(2,1)S(1)}, u32[]{:S(2)}, u32[]{:S(2)}) collective-permute-start(bf16[2560,128]{1,0:T(8,128)(2,1)S(1)} %convolution_convert_fusion), channel_id=1, source_target_pairs={{0,1},{1,0},{2,3},{3,2},{4,5},{5,4},{6,7},{7,6},{8,9},{9,8},{10,11... | collective-permute-start | bytes 1966088 | tf_op jit(solution)/shard_map/ppermute | solution.py:314
  28.3 1.2 %copy-start.2 = (bf16[64,192]{1,0:T(8,128)(2,1)S(1)}, bf16[64,192]{1,0:T(8,128)(2,1)}, u32[]{:S(2)}) copy-start(bf16[64,192]{1,0:T(8,128)(2,1)} %constant.14.clone.forward) | copy-start | bytes 73732
  28.3 1.2 %copy-start.4 = (bf16[512,128]{1,0:T(8,128)(2,1)S(1)}, bf16[512,128]{1,0:T(8,128)(2,1)}, u32[]{:S(2)}) copy-start(bf16[512,128]{1,0:T(8,128)(2,1)} %constant.17.clone.spans) | copy-start | bytes 393220
  28.3 1.1 %copy-start.6 = (f32[128,128]{1,0:T(8,128)S(1)}, f32[128,128]{1,0:T(8,128)}, u32[]{:S(2)}) copy-start(f32[128,128]{1,0:T(8,128)} %constant.18.clone.slots) | copy-start | bytes 196612
  31.3 23.7 %collective-permute-start.7 = (bf16[512,128]{1,0:T(8,128)(2,1)S(1)}, bf16[512,128]{1,0:T(8,128)(2,1)S(1)}, u32[]{:S(2)}, u32[]{:S(2)}) collective-permute-start(bf16[512,128]{1,0:T(8,128)(2,1)S(1)} %get-tuple-element.31), channel_id=1, source_target_pairs={{0,4},{1,5},{2,6},{3,7},{4,0},{5,1},{6,2},{7,3},{8,12},{9,13},{10,... | collective-permute-start | bytes 393224 | tf_op jit(solution)/shard_map/ppermute | solution.py:311
  43.8 11.1 %copy-start.10 = (f32[1,2560,128]{2,1,0:T(8,128)S(1)}, f32[1,2560,128]{2,1,0:T(8,128)}, u32[]{:S(2)}) copy-start(f32[1,2560,128]{2,1,0:T(8,128)} %param.13) | copy-start | bytes 3932164
  43.9 11.2 %collective-permute-start.6 = (bf16[2560,128]{1,0:T(8,128)(2,1)S(1)}, bf16[2560,128]{1,0:T(8,128)(2,1)S(1)}, u32[]{:S(2)}, u32[]{:S(2)}) collective-permute-start(bf16[2560,128]{1,0:T(8,128)(2,1)S(1)} %slice.39), channel_id=1, source_target_pairs={{0,1},{1,0},{2,3},{3,2},{4,5},{5,4},{6,7},{7,6},{8,9},{9,8},{10,11... | collective-permute-start | bytes 1966088 | tf_op jit(solution)/shard_map/ppermute | solution.py:314
  45.9 39.6 %collective-permute-start.8 = (bf16[2560,128]{1,0:T(8,128)(2,1)S(1)}, bf16[2560,128]{1,0:T(8,128)(2,1)S(1)}, u32[]{:S(2)}, u32[]{:S(2)}) collective-permute-start(bf16[2560,128]{1,0:T(8,128)(2,1)S(1)} %get-tuple-element.36), channel_id=1, source_target_pairs={{0,4},{1,5},{2,6},{3,7},{4,0},{5,1},{6,2},{7,3},{8,12},{9,13},{10,... | collective-permute-start | bytes 1966088 | tf_op jit(solution)/shard_map/ppermute | solution.py:311
  55.0 28.6 %copy-start.5 = (bf16[384,128]{1,0:T(8,128)(2,1)S(1)}, bf16[384,128]{1,0:T(8,128)(2,1)}, u32[]{:S(2)}) copy-start(bf16[384,128]{1,0:T(8,128)(2,1)} %constant.19.clone.backward) | copy-start | bytes 294916
  56.1 34.1 %copy-start.7 = (bf16[64,192]{1,0:T(8,128)(2,1)S(1)}, bf16[64,192]{1,0:T(8,128)(2,1)}, u32[]{:S(2)}) copy-start(bf16[64,192]{1,0:T(8,128)(2,1)} %constant.15.clone.backward) | copy-start | bytes 73732
  85.5 25.8 %all-to-all-start.1 = ((bf16[64,8,640]{2,1,0:T(8,128)(2,1)}), bf16[64,8,640]{2,1,0:T(8,128)(2,1)S(1)}, u32[]{:S(2)}, u32[]{:S(2)}) async-start(bf16[64,8,640]{2,1,0:T(8,128)(2,1)} %bitcast.11), calls=%async_computation.1 | async-start | bytes 1310720 | tf_op jit(solution)/shard_map/all_to_all | solution.py:427

commit v13 on v12

--- a/solution.py
+++ b/solution.py
@@ -72,10 +72,6 @@
     rows = jnp.concatenate(rows, axis=0)
     rows = jnp.concatenate([rows, jnp.zeros((16, wide - spans), jnp.float32)], axis=1)
     far[2 * tokens :, :] = rows.astype(far.dtype)
-
-
-def copy_kernel(x, y):
-    y[...] = x[...]
 
 
 def pair_kernel(tokens, far, mine, theirs):
@@ -324,12 +320,6 @@
         ids,
     )
     far_keys = along(far_keys, FAR)
-    (activations,) = call(
-        copy_kernel,
-        "copy",
-        (jax.ShapeDtypeStruct(activations.shape, activations.dtype),),
-        activations,
-    )
     activations, own_keys, partner_keys = lax.optimization_barrier(
         (activations, own_keys, partner_keys)
     )
@@ -398,6 +388,7 @@
 
     keys = jnp.concatenate([own_keys, their_keys], axis=1)
     keys = lax.optimization_barrier(keys.reshape(len(NEAR), tokens, 2 * cols))
+    left, right = lax.optimization_barrier((left, right))
     near = gram(activations, keys[0]) + gram(right, keys[1]) + gram(left, keys[2])
     other, far_whole = lax.optimization_barrier(
         (near[:, cols:].astype(jnp.bfloat16), far_whole)

time: 113 us -> 110 us (0.973)
  the two profiles are of different devices: /device:TPU:4 before, /device:TPU:2 now
where the time goes in v13:
time: 110 us
  starting transfers between devices  35.3 us (32%)
  blocking collectives  34.5 us (31%)
  waiting for transfers between devices  18.9 us (17%)
  Pallas kernels  11.7 us (11%)
  matrix products  4.04 us (4%)
  local copies, waits for them, and re-layouts  3.36 us (3%)
  between operations  1.62 us (1%)
    all_to_all x1, blocking collectives, exchange(): lax.all_to_all(x.reshape(replicas, OWN_COLS, x.shape[1]), 'dp', 0, 0, til...  34.5 us
    ppermute x5, starting transfers between devices, along(): lax.ppermute(x, 'tensor', [(i, (i + 2 * step) % group) for i in range(gro...  22.4 us
    all_to_all x1, waiting for transfers between devices, exchange(): lax.all_to_all(x.reshape(replicas, OWN_COLS, x.shape[1]), 'dp', 0, 0, til...  18 us
    pallas_call x8, Pallas kernels, call(): pl.pallas_call(kernel, out_shape=outs, in_specs=places or [VMEM] * len(ar...  11.7 us
    ppermute x4, starting transfers between devices, swap(): return lax.ppermute(x, 'tensor', [(i, i ^ 1) for i in range(group)])  8.3 us
    all_to_all x1, starting transfers between devices, exchange(): lax.all_to_all(x.reshape(replicas, OWN_COLS, x.shape[1]), 'dp', 0, 0, til...  4.64 us
    dot_general x5, matrix products, gram(): lax.dot_general(a, k, (((0,), (0,)), ((), ())), preferred_element_type=jn...  4.04 us
    unnamed x24, local copies, waits for them, and re-layouts  3.27 us
  transfers between devices with their start and end apart: 10, of which 2 were waited for; matrix products, arithmetic and copies ran while one was open for 4% of the time, Pallas kernels for 10%

profile of v13, /device:TPU:2, one launch (start us, length us, event | category | flops | bytes accessed | tf_op | source)
XLA Modules:
  0.0 109.6 jit_solution(10305655502960246036)
XLA Ops:
  0.6 0.0 copy-start
  0.6 1.0 copy-done
  1.6 0.7 copy-done.8
  2.4 4.0 %collective-permute-start.3 = (bf16[432,128]{1,0:T(8,128)(2,1)S(1)}, bf16[432,128]{1,0:T(8,128)(2,1)S(1)}, u32[]{:S(2)}, u32[]{:S(2)}) collective-permute-start(bf16[432,128]{1,0:T(8,128)(2,1)S(1)} %get-tuple-element.30), channel_id=1, source_target_pairs={{0,4},{1,5},{2,6},{3,7},{4,0},{5,1},{6,2},{7,3},{8,12},{9,13},{10,... | collective-permute-start | bytes 331784 | tf_op jit(solution)/shard_map/ppermute | solution.py:307
  6.4 7.2 %collective-permute-start.1 = (bf16[208,2560]{1,0:T(8,128)(2,1)}, bf16[208,2560]{1,0:T(8,128)(2,1)S(1)}, u32[]{:S(2)}, u32[]{:S(2)}) collective-permute-start(bf16[208,2560]{1,0:T(8,128)(2,1)} %param.11), channel_id=1, source_target_pairs={{0,2},{1,3},{2,4},{3,5},{4,6},{5,7},{6,0},{7,1},{8,10},{9,11},{10,... | collective-permute-start | bytes 3194888 | tf_op jit(solution)/shard_map/ppermute | solution.py:307
  13.6 1.9 %collective-permute-start.2 = (bf16[208,2560]{1,0:T(8,128)(2,1)}, bf16[208,2560]{1,0:T(8,128)(2,1)S(1)}, u32[]{:S(2)}, u32[]{:S(2)}) collective-permute-start(bf16[208,2560]{1,0:T(8,128)(2,1)} %param.11), channel_id=1, source_target_pairs={{0,6},{1,7},{2,0},{3,1},{4,2},{5,3},{6,4},{7,5},{8,14},{9,15},{10,... | collective-permute-start | bytes 3194888 | tf_op jit(solution)/shard_map/ppermute | solution.py:307
  15.5 0.0 collective-permute-done.3.far
  15.5 1.9 %collective-permute-start.4 = (bf16[208,128]{1,0:T(8,128)(2,1)S(1)}, bf16[208,128]{1,0:T(8,128)(2,1)S(1)}, u32[]{:S(2)}, u32[]{:S(2)}) collective-permute-start(bf16[208,128]{1,0:T(8,128)(2,1)S(1)} %get-tuple-element.32), channel_id=1, source_target_pairs={{0,1},{1,0},{2,3},{3,2},{4,5},{5,4},{6,7},{7,6},{8,9},{9,8},{10,11... | collective-permute-start | bytes 159752 | tf_op jit(solution)/shard_map/ppermute | solution.py:310
  17.5 2.4 %collective-permute-start = (bf16[624,128]{1,0:T(8,128)(2,1)S(1)}, bf16[624,128]{1,0:T(8,128)(2,1)S(1)}, u32[]{:S(2)}, u32[]{:S(2)}) collective-permute-start(bf16[624,128]{1,0:T(8,128)(2,1)S(1)} %get-tuple-element.27), channel_id=1, source_target_pairs={{0,1},{1,0},{2,3},{3,2},{4,5},{5,4},{6,7},{7,6},{8,9},{9,8},{10,11... | collective-permute-start | bytes 479240 | tf_op jit(solution)/shard_map/ppermute | solution.py:310
  20.5 0.0 copy-start.2
  20.5 0.8 copy-done.2
  21.4 0.7 copy-done.9
  22.1 2.7 %routes.1 = (bf16[2560,128]{1,0:T(8,128)(2,1)S(1)}, bf16[1024,640]{1,0:T(8,128)(2,1)S(1)}, bf16[512,128]{1,0:T(8,128)(2,1)S(1)}) custom-call(s32[6,2,40]{2,1,0:T(2,128)S(1)} %bitcast.31, s32[1]{0:T(128)S(6)} %copy.13.count, f32[128,128]{1,0:T(8,128)S(1)} %copy-done.2), custom_call_target="tpu_custom_call" | custom-call | tf_op jit(solution)/shard_map/routes/pallas_call | solution.py:289
  24.8 0.0 collective-permute-done.4
  24.8 1.8 %convolution_convert_fusion = bf16[2560,128]{1,0:T(8,128)(2,1)S(1)} fusion(bf16[208,2560]{1,0:T(8,128)(2,1)} %param.11, bf16[208,128]{1,0:T(8,128)(2,1)S(1)} %collective-permute-done.4), kind=kOutput, calls=%fused_computation.2 | convolution fusion | flops 136642560 | bytes 1773568 | tf_op jit(solution)/shard_map/dot_general | solution.py:282
  26.6 1.9 %collective-permute-start.5 = (bf16[2560,128]{1,0:T(8,128)(2,1)S(1)}, bf16[2560,128]{1,0:T(8,128)(2,1)S(1)}, u32[]{:S(2)}, u32[]{:S(2)}) collective-permute-start(bf16[2560,128]{1,0:T(8,128)(2,1)S(1)} %convolution_convert_fusion), channel_id=1, source_target_pairs={{0,1},{1,0},{2,3},{3,2},{4,5},{5,4},{6,7},{7,6},{8,9},{9,8},{10,11... | collective-permute-start | bytes 1966088 | tf_op jit(solution)/shard_map/ppermute | solution.py:310
  28.6 0.6 fusion.1.part
  29.1 0.0 collective-permute-done
  29.2 0.0 copy-start.1
  29.2 0.0 copy-start.3
  29.2 0.0 copy-start.4
  29.2 0.0 copy-start.6
  29.2 0.6 fusion
  29.8 0.8 collective-permute-done.5.other
  30.6 0.0 copy-done.1
  30.6 1.8 %far.1 = (bf16[2560,128]{1,0:T(8,128)(2,1)S(1)}, bf16[512,128]{1,0:T(8,128)(2,1)S(1)}) custom-call(bf16[16,128]{1,0:T(8,128)(2,1)S(1)} %slice.30.numbers, s32[1]{0:T(128)S(6)} %copy.13.count, bf16[512,128]{1,0:T(8,128)(2,1)S(1)} %copy-done.4, f32[128,128]{1,0:T(8,128)S(1)} %copy-done.6, f32[128,128]{1,0:T(8,128)S(1)} %copy-done.3, ...), custom_call_target="tpu_custom_call" | custom-call | tf_op jit(solution)/shard_map/far/pallas_call | solution.py:289
  32.5 3.4 %collective-permute-start.7 = (bf16[512,128]{1,0:T(8,128)(2,1)S(1)}, bf16[512,128]{1,0:T(8,128)(2,1)S(1)}, u32[]{:S(2)}, u32[]{:S(2)}) collective-permute-start(bf16[512,128]{1,0:T(8,128)(2,1)S(1)} %get-tuple-element.35), channel_id=1, source_target_pairs={{0,4},{1,5},{2,6},{3,7},{4,0},{5,1},{6,2},{7,3},{8,12},{9,13},{10,... | collective-permute-start | bytes 393224 | tf_op jit(solution)/shard_map/ppermute | solution.py:307
  35.9 0.0 collective-permute-done.1
  35.9 0.0 collective-permute-done.2
  35.9 0.6 convolution_add_fusion.1
  36.4 0.6 convolution_add_fusion
  37.0 0.0 copy-start.11
  37.0 0.1 slice.39
  37.1 2.1 %collective-permute-start.6 = (bf16[2560,128]{1,0:T(8,128)(2,1)S(1)}, bf16[2560,128]{1,0:T(8,128)(2,1)S(1)}, u32[]{:S(2)}, u32[]{:S(2)}) collective-permute-start(bf16[2560,128]{1,0:T(8,128)(2,1)S(1)} %slice.39), channel_id=1, source_target_pairs={{0,1},{1,0},{2,3},{3,2},{4,5},{5,4},{6,7},{7,6},{8,9},{9,8},{10,11... | collective-permute-start | bytes 1966088 | tf_op jit(solution)/shard_map/ppermute | solution.py:310
  39.2 5.9 %collective-permute-start.8 = (bf16[2560,128]{1,0:T(8,128)(2,1)S(1)}, bf16[2560,128]{1,0:T(8,128)(2,1)S(1)}, u32[]{:S(2)}, u32[]{:S(2)}) collective-permute-start(bf16[2560,128]{1,0:T(8,128)(2,1)S(1)} %get-tuple-element.40), channel_id=1, source_target_pairs={{0,4},{1,5},{2,6},{3,7},{4,0},{5,1},{6,2},{7,3},{8,12},{9,13},{10,... | collective-permute-start | bytes 1966088 | tf_op jit(solution)/shard_map/ppermute | solution.py:307
  45.1 0.2 slice_add_fusion.part
  45.2 0.0 collective-permute-done.7.far
  45.2 0.0 collective-permute-done.6.other
  45.3 0.0 copy-start.5
  45.3 1.0 spectrum.1
  46.3 0.0 copy-start.7
  46.3 34.5 %all_to_all.10 = bf16[64,8,256]{2,1,0:T(8,128)(2,1)S(1)} all-to-all(bf16[64,8,256]{2,1,0:T(8,128)(2,1)S(1)} %bitcast.29), channel_id=1, replica_groups=mesh['dp'=64,'tensor'=8] {'dp'}, dimensions={0} | all-to-all | bytes 524288 | tf_op jit(solution)/shard_map/all_to_all | solution.py:418
  80.8 1.9 %total.1 = bf16[512,640]{1,0:T(8,128)(2,1)} custom-call(bf16[512,256]{1,0:T(8,128)(2,1)S(1)} %bitcast.28, bf16[384,128]{1,0:T(8,128)(2,1)S(1)} %copy-done.5), custom_call_target="tpu_custom_call" | custom-call | tf_op jit(solution)/shard_map/total/pallas_call | solution.py:289
  82.7 0.0 collective-permute-done.8.far
  82.7 4.6 %all-to-all-start.1 = ((bf16[64,8,640]{2,1,0:T(8,128)(2,1)}), bf16[64,8,640]{2,1,0:T(8,128)(2,1)S(1)}, u32[]{:S(2)}, u32[]{:S(2)}) async-start(bf16[64,8,640]{2,1,0:T(8,128)(2,1)} %bitcast.11), calls=%async_computation.1 | async-start | bytes 1310720 | tf_op jit(solution)/shard_map/all_to_all | solution.py:418
  87.4 3.1 %kept.1 = f32[2560,128]{1,0:T(8,128)} custom-call(f32[2560,128]{1,0:T(8,128)S(1)} %get-tuple-element.38.advanced, bf16[2560,128]{1,0:T(8,128)(2,1)S(1)} %collective-permute-done.8.far, bf16[2560,128]{1,0:T(8,128)(2,1)S(1)} %get-tuple-element.42.mask, bf16[64,192]{1,0:T(8,128)(2,1)S(1)} %copy-done.1, bf16[64,192]{1,0:T(8,128)(2,1)S(1)} %copy-done.7), custom_call_target="tpu_custom_call" | custom-call | tf_op jit(solution)/shard_map/kept/pallas_call | solution.py:289
  90.5 18.0 %all-to-all-done.1 = bf16[64,8,640]{2,1,0:T(8,128)(2,1)S(1)} async-done(((bf16[64,8,640]{2,1,0:T(8,128)(2,1)}), bf16[64,8,640]{2,1,0:T(8,128)(2,1)S(1)}, u32[]{:S(2)}, u32[]{:S(2)}) %all-to-all-start.1) | async-done | bytes 655392 | tf_op jit(solution)/shard_map/all_to_all | solution.py:418
  108.5 1.1 turn.1
  (14 shorter events, 0.1 us)
Async XLA Ops:
  0.6 1.0 copy-start
  1.6 0.7 copy-start.8
  2.4 13.1 %collective-permute-start.3 = (bf16[432,128]{1,0:T(8,128)(2,1)S(1)}, bf16[432,128]{1,0:T(8,128)(2,1)S(1)}, u32[]{:S(2)}, u32[]{:S(2)}) collective-permute-start(bf16[432,128]{1,0:T(8,128)(2,1)S(1)} %get-tuple-element.30), channel_id=1, source_target_pairs={{0,4},{1,5},{2,6},{3,7},{4,0},{5,1},{6,2},{7,3},{8,12},{9,13},{10,... | collective-permute-start | bytes 331784 | tf_op jit(solution)/shard_map/ppermute | solution.py:307
  6.4 29.4 %collective-permute-start.1 = (bf16[208,2560]{1,0:T(8,128)(2,1)}, bf16[208,2560]{1,0:T(8,128)(2,1)S(1)}, u32[]{:S(2)}, u32[]{:S(2)}) collective-permute-start(bf16[208,2560]{1,0:T(8,128)(2,1)} %param.11), channel_id=1, source_target_pairs={{0,2},{1,3},{2,4},{3,5},{4,6},{5,7},{6,0},{7,1},{8,10},{9,11},{10,... | collective-permute-start | bytes 3194888 | tf_op jit(solution)/shard_map/ppermute | solution.py:307
  13.6 22.3 %collective-permute-start.2 = (bf16[208,2560]{1,0:T(8,128)(2,1)}, bf16[208,2560]{1,0:T(8,128)(2,1)S(1)}, u32[]{:S(2)}, u32[]{:S(2)}) collective-permute-start(bf16[208,2560]{1,0:T(8,128)(2,1)} %param.11), channel_id=1, source_target_pairs={{0,6},{1,7},{2,0},{3,1},{4,2},{5,3},{6,4},{7,5},{8,14},{9,15},{10,... | collective-permute-start | bytes 3194888 | tf_op jit(solution)/shard_map/ppermute | solution.py:307
  15.5 9.3 %collective-permute-start.4 = (bf16[208,128]{1,0:T(8,128)(2,1)S(1)}, bf16[208,128]{1,0:T(8,128)(2,1)S(1)}, u32[]{:S(2)}, u32[]{:S(2)}) collective-permute-start(bf16[208,128]{1,0:T(8,128)(2,1)S(1)} %get-tuple-element.32), channel_id=1, source_target_pairs={{0,1},{1,0},{2,3},{3,2},{4,5},{5,4},{6,7},{7,6},{8,9},{9,8},{10,11... | collective-permute-start | bytes 159752 | tf_op jit(solution)/shard_map/ppermute | solution.py:310
  17.5 11.7 %collective-permute-start = (bf16[624,128]{1,0:T(8,128)(2,1)S(1)}, bf16[624,128]{1,0:T(8,128)(2,1)S(1)}, u32[]{:S(2)}, u32[]{:S(2)}) collective-permute-start(bf16[624,128]{1,0:T(8,128)(2,1)S(1)} %get-tuple-element.27), channel_id=1, source_target_pairs={{0,1},{1,0},{2,3},{3,2},{4,5},{5,4},{6,7},{7,6},{8,9},{9,8},{10,11... | collective-permute-start | bytes 479240 | tf_op jit(solution)/shard_map/ppermute | solution.py:310
  20.5 0.8 copy-start.2
  21.4 0.7 copy-start.9
  22.1 6.5 %copy-start.10 = (bf16[208,2560]{1,0:T(8,128)(2,1)S(1)}, bf16[208,2560]{1,0:T(8,128)(2,1)}, u32[]{:S(2)}) copy-start(bf16[208,2560]{1,0:T(8,128)(2,1)} %param.11) | copy-start | bytes 3194884
  26.6 4.0 %collective-permute-start.5 = (bf16[2560,128]{1,0:T(8,128)(2,1)S(1)}, bf16[2560,128]{1,0:T(8,128)(2,1)S(1)}, u32[]{:S(2)}, u32[]{:S(2)}) collective-permute-start(bf16[2560,128]{1,0:T(8,128)(2,1)S(1)} %convolution_convert_fusion), channel_id=1, source_target_pairs={{0,1},{1,0},{2,3},{3,2},{4,5},{5,4},{6,7},{7,6},{8,9},{9,8},{10,11... | collective-permute-start | bytes 1966088 | tf_op jit(solution)/shard_map/ppermute | solution.py:310
  29.2 1.4 %copy-start.1 = (bf16[64,192]{1,0:T(8,128)(2,1)S(1)}, bf16[64,192]{1,0:T(8,128)(2,1)}, u32[]{:S(2)}) copy-start(bf16[64,192]{1,0:T(8,128)(2,1)} %constant.14.clone.forward) | copy-start | bytes 73732
  29.2 1.4 %copy-start.3 = (f32[128,128]{1,0:T(8,128)S(1)}, f32[128,128]{1,0:T(8,128)}, u32[]{:S(2)}) copy-start(f32[128,128]{1,0:T(8,128)} %constant.16.clone.base) | copy-start | bytes 196612
  29.2 1.4 %copy-start.4 = (bf16[512,128]{1,0:T(8,128)(2,1)S(1)}, bf16[512,128]{1,0:T(8,128)(2,1)}, u32[]{:S(2)}) copy-start(bf16[512,128]{1,0:T(8,128)(2,1)} %constant.17.clone.spans) | copy-start | bytes 393220
  29.2 1.4 %copy-start.6 = (f32[128,128]{1,0:T(8,128)S(1)}, f32[128,128]{1,0:T(8,128)}, u32[]{:S(2)}) copy-start(f32[128,128]{1,0:T(8,128)} %constant.18.clone.slots) | copy-start | bytes 196612
  32.5 12.8 %collective-permute-start.7 = (bf16[512,128]{1,0:T(8,128)(2,1)S(1)}, bf16[512,128]{1,0:T(8,128)(2,1)S(1)}, u32[]{:S(2)}, u32[]{:S(2)}) collective-permute-start(bf16[512,128]{1,0:T(8,128)(2,1)S(1)} %get-tuple-element.35), channel_id=1, source_target_pairs={{0,4},{1,5},{2,6},{3,7},{4,0},{5,1},{6,2},{7,3},{8,12},{9,13},{10,... | collective-permute-start | bytes 393224 | tf_op jit(solution)/shard_map/ppermute | solution.py:307
  37.0 8.0 %copy-start.11 = (f32[1,2560,128]{2,1,0:T(8,128)S(1)}, f32[1,2560,128]{2,1,0:T(8,128)}, u32[]{:S(2)}) copy-start(f32[1,2560,128]{2,1,0:T(8,128)} %param.13) | copy-start | bytes 3932164
  37.1 8.1 %collective-permute-start.6 = (bf16[2560,128]{1,0:T(8,128)(2,1)S(1)}, bf16[2560,128]{1,0:T(8,128)(2,1)S(1)}, u32[]{:S(2)}, u32[]{:S(2)}) collective-permute-start(bf16[2560,128]{1,0:T(8,128)(2,1)S(1)} %slice.39), channel_id=1, source_target_pairs={{0,1},{1,0},{2,3},{3,2},{4,5},{5,4},{6,7},{7,6},{8,9},{9,8},{10,11... | collective-permute-start | bytes 1966088 | tf_op jit(solution)/shard_map/ppermute | solution.py:310
  39.2 43.6 %collective-permute-start.8 = (bf16[2560,128]{1,0:T(8,128)(2,1)S(1)}, bf16[2560,128]{1,0:T(8,128)(2,1)S(1)}, u32[]{:S(2)}, u32[]{:S(2)}) collective-permute-start(bf16[2560,128]{1,0:T(8,128)(2,1)S(1)} %get-tuple-element.40), channel_id=1, source_target_pairs={{0,4},{1,5},{2,6},{3,7},{4,0},{5,1},{6,2},{7,3},{8,12},{9,13},{10,... | collective-permute-start | bytes 1966088 | tf_op jit(solution)/shard_map/ppermute | solution.py:307
  45.3 35.6 %copy-start.5 = (bf16[384,128]{1,0:T(8,128)(2,1)S(1)}, bf16[384,128]{1,0:T(8,128)(2,1)}, u32[]{:S(2)}) copy-start(bf16[384,128]{1,0:T(8,128)(2,1)} %constant.19.clone.backward) | copy-start | bytes 294916
  46.3 41.1 %copy-start.7 = (bf16[64,192]{1,0:T(8,128)(2,1)S(1)}, bf16[64,192]{1,0:T(8,128)(2,1)}, u32[]{:S(2)}) copy-start(bf16[64,192]{1,0:T(8,128)(2,1)} %constant.15.clone.backward) | copy-start | bytes 73732
  82.7 25.8 %all-to-all-start.1 = ((bf16[64,8,640]{2,1,0:T(8,128)(2,1)}), bf16[64,8,640]{2,1,0:T(8,128)(2,1)S(1)}, u32[]{:S(2)}, u32[]{:S(2)}) async-start(bf16[64,8,640]{2,1,0:T(8,128)(2,1)} %bitcast.11), calls=%async_computation.1 | async-start | bytes 1310720 | tf_op jit(solution)/shard_map/all_to_all | solution.py:418

commit v14 on v13

--- a/solution.py
+++ b/solution.py
@@ -52,26 +52,39 @@
         ref[first : first + SPAN, :] = value[:, s * cols : (s + 1) * cols].astype(ref.dtype)
 
 
-def keys_kernel(chips, tokens, keys, ids, own, partner, far):
+def far_keys_kernel(chips, tokens, keys, ids, far, numbers, done):
+    chip = lax.shift_right_logical(lax.axis_index("tensor"), 1)
+    first = 2 * lax.bitwise_and(chip + FAR, chips - 1) * tokens
+    rows = pltpu.make_async_copy(
+        keys.at[pl.ds(pl.multiple_of(first, 16), 2 * tokens)],
+        far.at[pl.ds(0, 2 * tokens)],
+        done.at[0],
+    )
+    listed = pltpu.make_async_copy(ids, numbers, done.at[1])
+    rows.start()
+    listed.start()
+    listed.wait()
+    most, halves, spans = ids.shape
+    lines = [numbers[k].astype(jnp.float32) for k in range(most)]
+    lines.append(jnp.zeros((16 - most * halves, spans), jnp.float32))
+    lines = jnp.concatenate(lines, axis=0)
+    lines = jnp.concatenate([lines, jnp.zeros((16, far.shape[1] - spans), jnp.float32)], axis=1)
+    far[2 * tokens :, :] = lines.astype(far.dtype)
+    rows.wait()
+
+
+def keys_kernel(chips, tokens, keys, own, partner):
     spot = lax.axis_index("tensor")
     chip, core = lax.shift_right_logical(spot, 1), lax.bitwise_and(spot, 1)
 
-    def first(step, which):
-        block = 2 * lax.bitwise_and(chip + step, chips - 1) + which
-        return pl.multiple_of(block * tokens, 16)
+    def block(step, which):
+        first = (2 * lax.bitwise_and(chip + step, chips - 1) + which) * tokens
+        return keys[pl.ds(pl.multiple_of(first, 16), tokens), :]
 
     for place, step in enumerate(NEAR):
         here = slice(place * tokens, (place + 1) * tokens)
-        own[here, :] = keys[pl.ds(first(step, core), tokens), :]
-        partner[here, :] = keys[pl.ds(first(step, 1 - core), tokens), :]
-    far[: 2 * tokens, :] = keys[pl.ds(first(FAR, 0), 2 * tokens), :]
-    most, halves, spans = ids.shape
-    wide = far.shape[1]
-    rows = [ids[k].astype(jnp.float32) for k in range(most)]
-    rows.append(jnp.zeros((16 - most * halves, spans), jnp.float32))
-    rows = jnp.concatenate(rows, axis=0)
-    rows = jnp.concatenate([rows, jnp.zeros((16, wide - spans), jnp.float32)], axis=1)
-    far[2 * tokens :, :] = rows.astype(far.dtype)
+        own[here, :] = block(step, core)
+        partner[here, :] = block(step, 1 - core)
 
 
 def pair_kernel(tokens, far, mine, theirs):
@@ -282,7 +295,9 @@
     return lax.dot_general(a, k, (((0,), (0,)), ((), ())), preferred_element_type=jnp.float32)
 
 
-VMEM, SMEM = (pl.BlockSpec(memory_space=space) for space in (pltpu.VMEM, pltpu.SMEM))
+VMEM, SMEM, HBM = (
+    pl.BlockSpec(memory_space=space) for space in (pltpu.VMEM, pltpu.SMEM, pltpu.HBM)
+)
 
 
 def call(kernel, name, outs, *args, places=None, scratch=()):
@@ -312,17 +327,19 @@
     near_rows = jax.ShapeDtypeStruct((len(NEAR) * tokens, cols), jnp.bfloat16)
     far_rows = jax.ShapeDtypeStruct((2 * tokens + 16, cols), jnp.bfloat16)
     ids = jnp.transpose(block_ids[0], (2, 1, 0))
-    own_keys, partner_keys, far_keys = call(
-        functools.partial(keys_kernel, chips, tokens),
-        "keys",
-        (near_rows, near_rows, far_rows),
-        key_grad,
-        ids,
+    (far_keys,) = call(
+        functools.partial(far_keys_kernel, chips, tokens),
+        "far_keys",
+        (far_rows,),
+        pltpu.with_memory_space_constraint(key_grad, pltpu.HBM),
+        pltpu.with_memory_space_constraint(ids, pltpu.HBM),
+        places=[HBM, HBM],
+        scratch=(pltpu.VMEM(ids.shape, jnp.int32), pltpu.SemaphoreType.DMA((2,))),
+    )
+    activations, key_grad, far_keys = lax.optimization_barrier(
+        (activations, key_grad, far_keys)
     )
     far_keys = along(far_keys, FAR)
-    activations, own_keys, partner_keys = lax.optimization_barrier(
-        (activations, own_keys, partner_keys)
-    )
     left, right = along(activations, 1), along(activations, -1)
 
     block_rows = jax.ShapeDtypeStruct((tokens, cols), jnp.bfloat16)
@@ -332,6 +349,9 @@
     far_theirs = swap(far_theirs)
     far_other = swap(gram(activations, far_theirs).astype(jnp.bfloat16))
     far_part = gram(activations, far_own)
+    own_keys, partner_keys = call(
+        functools.partial(keys_kernel, chips, tokens), "keys", (near_rows, near_rows), key_grad
+    )
     their_keys = swap(partner_keys)
 
     flat = jax.ShapeDtypeStruct((features, cols), jnp.float32)

time: 110 us -> 109 us (level)
    pallas_call x8 -> x9, Pallas kernels: 11.7 us -> 12.6 us  [call(): pl.pallas_call(kernel, out_shape=outs, in_specs=places or [VMEM] * len(ar...]
    unnamed x24 -> x22, local copies, waits for them, and re-layouts: 3.27 us -> 2.58 us
where the time goes in v14:
time: 109 us
  blocking collectives  34.5 us (32%)
  starting transfers between devices  34.3 us (31%)
  waiting for transfers between devices  18.9 us (17%)
  Pallas kernels  12.6 us (12%)
  matrix products  4.04 us (4%)
  local copies, waits for them, and re-layouts  2.67 us (2%)
  between operations  1.62 us (1%)
    all_to_all x1, blocking collectives, exchange(): lax.all_to_all(x.reshape(replicas, OWN_COLS, x.shape[1]), 'dp', 0, 0, til...  34.5 us
    ppermute x5, starting transfers between devices, along(): lax.ppermute(x, 'tensor', [(i, (i + 2 * step) % group) for i in range(gro...  21.3 us
    all_to_all x1, waiting for transfers between devices, exchange(): lax.all_to_all(x.reshape(replicas, OWN_COLS, x.shape[1]), 'dp', 0, 0, til...  18 us
    pallas_call x9, Pallas kernels, call(): pl.pallas_call(kernel, out_shape=outs, in_specs=places or [VMEM] * len(ar...  12.6 us
    ppermute x4, starting transfers between devices, swap(): return lax.ppermute(x, 'tensor', [(i, i ^ 1) for i in range(group)])  8.3 us
    all_to_all x1, starting transfers between devices, exchange(): lax.all_to_all(x.reshape(replicas, OWN_COLS, x.shape[1]), 'dp', 0, 0, til...  4.64 us
    dot_general x5, matrix products, gram(): lax.dot_general(a, k, (((0,), (0,)), ((), ())), preferred_element_type=jn...  4.04 us
    unnamed x22, local copies, waits for them, and re-layouts  2.58 us
  transfers between devices with their start and end apart: 10, of which 2 were waited for; matrix products, arithmetic and copies ran while one was open for 4% of the time, Pallas kernels for 10%

profile of v14, /device:TPU:2, one launch (start us, length us, event | category | flops | bytes accessed | tf_op | source)
XLA Modules:
  0.0 108.8 jit_solution(1801854026792025776)
XLA Ops:
  0.6 0.9 far_keys.1
  1.6 4.0 %collective-permute-start.3 = (bf16[432,128]{1,0:T(8,128)(2,1)S(1)}, bf16[432,128]{1,0:T(8,128)(2,1)S(1)}, u32[]{:S(2)}, u32[]{:S(2)}) collective-permute-start(bf16[432,128]{1,0:T(8,128)(2,1)S(1)} %far_keys.1), channel_id=1, source_target_pairs={{0,4},{1,5},{2,6},{3,7},{4,0},{5,1},{6,2},{7,3},{8,12},{9,13},{10,... | collective-permute-start | bytes 331784 | tf_op jit(solution)/shard_map/ppermute | solution.py:322
  5.6 7.2 %collective-permute-start.1 = (bf16[208,2560]{1,0:T(8,128)(2,1)}, bf16[208,2560]{1,0:T(8,128)(2,1)S(1)}, u32[]{:S(2)}, u32[]{:S(2)}) collective-permute-start(bf16[208,2560]{1,0:T(8,128)(2,1)} %param.11), channel_id=1, source_target_pairs={{0,2},{1,3},{2,4},{3,5},{4,6},{5,7},{6,0},{7,1},{8,10},{9,11},{10,... | collective-permute-start | bytes 3194888 | tf_op jit(solution)/shard_map/ppermute | solution.py:322
  12.8 1.9 %collective-permute-start.2 = (bf16[208,2560]{1,0:T(8,128)(2,1)}, bf16[208,2560]{1,0:T(8,128)(2,1)S(1)}, u32[]{:S(2)}, u32[]{:S(2)}) collective-permute-start(bf16[208,2560]{1,0:T(8,128)(2,1)} %param.11), channel_id=1, source_target_pairs={{0,6},{1,7},{2,0},{3,1},{4,2},{5,3},{6,4},{7,5},{8,14},{9,15},{10,... | collective-permute-start | bytes 3194888 | tf_op jit(solution)/shard_map/ppermute | solution.py:322
  14.7 0.0 collective-permute-done.3.far
  14.7 1.9 %collective-permute-start.4 = (bf16[208,128]{1,0:T(8,128)(2,1)S(1)}, bf16[208,128]{1,0:T(8,128)(2,1)S(1)}, u32[]{:S(2)}, u32[]{:S(2)}) collective-permute-start(bf16[208,128]{1,0:T(8,128)(2,1)S(1)} %get-tuple-element.30), channel_id=1, source_target_pairs={{0,1},{1,0},{2,3},{3,2},{4,5},{5,4},{6,7},{7,6},{8,9},{9,8},{10,11... | collective-permute-start | bytes 159752 | tf_op jit(solution)/shard_map/ppermute | solution.py:325
  16.7 0.0 copy-start
  16.7 1.0 copy-done
  17.7 2.4 %collective-permute-start = (bf16[624,128]{1,0:T(8,128)(2,1)S(1)}, bf16[624,128]{1,0:T(8,128)(2,1)S(1)}, u32[]{:S(2)}, u32[]{:S(2)}) collective-permute-start(bf16[624,128]{1,0:T(8,128)(2,1)S(1)} %get-tuple-element.25), channel_id=1, source_target_pairs={{0,1},{1,0},{2,3},{3,2},{4,5},{5,4},{6,7},{7,6},{8,9},{9,8},{10,11... | collective-permute-start | bytes 479240 | tf_op jit(solution)/shard_map/ppermute | solution.py:325
  20.8 0.0 copy-start.2
  20.8 0.8 copy-done.2
  21.6 0.7 copy-done.8
  22.3 2.7 %routes.1 = (bf16[2560,128]{1,0:T(8,128)(2,1)S(1)}, bf16[1024,640]{1,0:T(8,128)(2,1)S(1)}, bf16[512,128]{1,0:T(8,128)(2,1)S(1)}) custom-call(s32[6,2,40]{2,1,0:T(2,128)S(1)} %bitcast.31, s32[1]{0:T(128)S(6)} %copy.13.count, f32[128,128]{1,0:T(8,128)S(1)} %copy-done.2), custom_call_target="tpu_custom_call" | custom-call | tf_op jit(solution)/shard_map/routes/pallas_call | solution.py:304
  25.0 0.0 collective-permute-done.4
  25.1 1.8 %convolution_convert_fusion = bf16[2560,128]{1,0:T(8,128)(2,1)S(1)} fusion(bf16[208,2560]{1,0:T(8,128)(2,1)} %param.11, bf16[208,128]{1,0:T(8,128)(2,1)S(1)} %collective-permute-done.4), kind=kOutput, calls=%fused_computation.2 | convolution fusion | flops 136642560 | bytes 1773568 | tf_op jit(solution)/shard_map/dot_general | solution.py:295
  26.9 1.9 %collective-permute-start.5 = (bf16[2560,128]{1,0:T(8,128)(2,1)S(1)}, bf16[2560,128]{1,0:T(8,128)(2,1)S(1)}, u32[]{:S(2)}, u32[]{:S(2)}) collective-permute-start(bf16[2560,128]{1,0:T(8,128)(2,1)S(1)} %convolution_convert_fusion), channel_id=1, source_target_pairs={{0,1},{1,0},{2,3},{3,2},{4,5},{5,4},{6,7},{7,6},{8,9},{9,8},{10,11... | collective-permute-start | bytes 1966088 | tf_op jit(solution)/shard_map/ppermute | solution.py:325
  28.8 0.0 copy-done.9
  28.8 0.6 fusion.1.part
  29.4 0.0 collective-permute-done
  29.4 0.0 copy-start.1
  29.4 0.0 copy-start.3
  29.4 0.0 copy-start.4
  29.5 0.0 copy-start.6
  29.5 0.6 fusion
  30.0 0.8 collective-permute-done.5.other
  30.9 1.8 %far.1 = (bf16[2560,128]{1,0:T(8,128)(2,1)S(1)}, bf16[512,128]{1,0:T(8,128)(2,1)S(1)}) custom-call(bf16[16,128]{1,0:T(8,128)(2,1)S(1)} %slice.30.numbers, s32[1]{0:T(128)S(6)} %copy.13.count, bf16[512,128]{1,0:T(8,128)(2,1)S(1)} %copy-done.4, f32[128,128]{1,0:T(8,128)S(1)} %copy-done.6, f32[128,128]{1,0:T(8,128)S(1)} %copy-done.3, ...), custom_call_target="tpu_custom_call" | custom-call | tf_op jit(solution)/shard_map/far/pallas_call | solution.py:304
  32.7 3.4 %collective-permute-start.7 = (bf16[512,128]{1,0:T(8,128)(2,1)S(1)}, bf16[512,128]{1,0:T(8,128)(2,1)S(1)}, u32[]{:S(2)}, u32[]{:S(2)}) collective-permute-start(bf16[512,128]{1,0:T(8,128)(2,1)S(1)} %get-tuple-element.33), channel_id=1, source_target_pairs={{0,4},{1,5},{2,6},{3,7},{4,0},{5,1},{6,2},{7,3},{8,12},{9,13},{10,... | collective-permute-start | bytes 393224 | tf_op jit(solution)/shard_map/ppermute | solution.py:322
  36.1 0.0 collective-permute-done.1
  36.1 0.0 collective-permute-done.2
  36.1 0.6 convolution_add_fusion.1
  36.7 0.6 convolution_add_fusion
  37.2 0.0 copy-start.10
  37.3 0.1 slice.39
  37.4 2.1 %collective-permute-start.6 = (bf16[2560,128]{1,0:T(8,128)(2,1)S(1)}, bf16[2560,128]{1,0:T(8,128)(2,1)S(1)}, u32[]{:S(2)}, u32[]{:S(2)}) collective-permute-start(bf16[2560,128]{1,0:T(8,128)(2,1)S(1)} %slice.39), channel_id=1, source_target_pairs={{0,1},{1,0},{2,3},{3,2},{4,5},{5,4},{6,7},{7,6},{8,9},{9,8},{10,11... | collective-permute-start | bytes 1966088 | tf_op jit(solution)/shard_map/ppermute | solution.py:325
  39.4 4.8 %collective-permute-start.8 = (bf16[2560,128]{1,0:T(8,128)(2,1)S(1)}, bf16[2560,128]{1,0:T(8,128)(2,1)S(1)}, u32[]{:S(2)}, u32[]{:S(2)}) collective-permute-start(bf16[2560,128]{1,0:T(8,128)(2,1)S(1)} %get-tuple-element.38), channel_id=1, source_target_pairs={{0,4},{1,5},{2,6},{3,7},{4,0},{5,1},{6,2},{7,3},{8,12},{9,13},{10,... | collective-permute-start | bytes 1966088 | tf_op jit(solution)/shard_map/ppermute | solution.py:322
  44.3 0.2 slice_add_fusion.part
  44.4 0.0 collective-permute-done.7.far
  44.4 0.0 collective-permute-done.6.other
  44.5 0.0 copy-start.5
  44.5 1.0 spectrum.1
  45.5 0.0 copy-start.7
  45.5 34.5 %all_to_all.10 = bf16[64,8,256]{2,1,0:T(8,128)(2,1)S(1)} all-to-all(bf16[64,8,256]{2,1,0:T(8,128)(2,1)S(1)} %bitcast.29), channel_id=1, replica_groups=mesh['dp'=64,'tensor'=8] {'dp'}, dimensions={0} | all-to-all | bytes 524288 | tf_op jit(solution)/shard_map/all_to_all | solution.py:438
  80.0 1.9 %total.1 = bf16[512,640]{1,0:T(8,128)(2,1)} custom-call(bf16[512,256]{1,0:T(8,128)(2,1)S(1)} %bitcast.28, bf16[384,128]{1,0:T(8,128)(2,1)S(1)} %copy-done.5), custom_call_target="tpu_custom_call" | custom-call | tf_op jit(solution)/shard_map/total/pallas_call | solution.py:304
  81.9 0.0 collective-permute-done.8.far
  81.9 4.6 %all-to-all-start.1 = ((bf16[64,8,640]{2,1,0:T(8,128)(2,1)}), bf16[64,8,640]{2,1,0:T(8,128)(2,1)S(1)}, u32[]{:S(2)}, u32[]{:S(2)}) async-start(bf16[64,8,640]{2,1,0:T(8,128)(2,1)} %bitcast.11), calls=%async_computation.1 | async-start | bytes 1310720 | tf_op jit(solution)/shard_map/all_to_all | solution.py:438
  86.6 3.1 %kept.1 = f32[2560,128]{1,0:T(8,128)} custom-call(f32[2560,128]{1,0:T(8,128)S(1)} %get-tuple-element.36.advanced, bf16[2560,128]{1,0:T(8,128)(2,1)S(1)} %collective-permute-done.8.far, bf16[2560,128]{1,0:T(8,128)(2,1)S(1)} %get-tuple-element.40.mask, bf16[64,192]{1,0:T(8,128)(2,1)S(1)} %copy-done.1, bf16[64,192]{1,0:T(8,128)(2,1)S(1)} %copy-done.7), custom_call_target="tpu_custom_call" | custom-call | tf_op jit(solution)/shard_map/kept/pallas_call | solution.py:304
  89.7 18.0 %all-to-all-done.1 = bf16[64,8,640]{2,1,0:T(8,128)(2,1)S(1)} async-done(((bf16[64,8,640]{2,1,0:T(8,128)(2,1)}), bf16[64,8,640]{2,1,0:T(8,128)(2,1)S(1)}, u32[]{:S(2)}, u32[]{:S(2)}) %all-to-all-start.1) | async-done | bytes 655392 | tf_op jit(solution)/shard_map/all_to_all | solution.py:438
  107.7 1.1 turn.1
  (13 shorter events, 0.1 us)
Async XLA Ops:
  1.6 13.1 %collective-permute-start.3 = (bf16[432,128]{1,0:T(8,128)(2,1)S(1)}, bf16[432,128]{1,0:T(8,128)(2,1)S(1)}, u32[]{:S(2)}, u32[]{:S(2)}) collective-permute-start(bf16[432,128]{1,0:T(8,128)(2,1)S(1)} %far_keys.1), channel_id=1, source_target_pairs={{0,4},{1,5},{2,6},{3,7},{4,0},{5,1},{6,2},{7,3},{8,12},{9,13},{10,... | collective-permute-start | bytes 331784 | tf_op jit(solution)/shard_map/ppermute | solution.py:322
  5.6 30.5 %collective-permute-start.1 = (bf16[208,2560]{1,0:T(8,128)(2,1)}, bf16[208,2560]{1,0:T(8,128)(2,1)S(1)}, u32[]{:S(2)}, u32[]{:S(2)}) collective-permute-start(bf16[208,2560]{1,0:T(8,128)(2,1)} %param.11), channel_id=1, source_target_pairs={{0,2},{1,3},{2,4},{3,5},{4,6},{5,7},{6,0},{7,1},{8,10},{9,11},{10,... | collective-permute-start | bytes 3194888 | tf_op jit(solution)/shard_map/ppermute | solution.py:322
  12.8 23.3 %collective-permute-start.2 = (bf16[208,2560]{1,0:T(8,128)(2,1)}, bf16[208,2560]{1,0:T(8,128)(2,1)S(1)}, u32[]{:S(2)}, u32[]{:S(2)}) collective-permute-start(bf16[208,2560]{1,0:T(8,128)(2,1)} %param.11), channel_id=1, source_target_pairs={{0,6},{1,7},{2,0},{3,1},{4,2},{5,3},{6,4},{7,5},{8,14},{9,15},{10,... | collective-permute-start | bytes 3194888 | tf_op jit(solution)/shard_map/ppermute | solution.py:322
  14.7 10.3 %collective-permute-start.4 = (bf16[208,128]{1,0:T(8,128)(2,1)S(1)}, bf16[208,128]{1,0:T(8,128)(2,1)S(1)}, u32[]{:S(2)}, u32[]{:S(2)}) collective-permute-start(bf16[208,128]{1,0:T(8,128)(2,1)S(1)} %get-tuple-element.30), channel_id=1, source_target_pairs={{0,1},{1,0},{2,3},{3,2},{4,5},{5,4},{6,7},{7,6},{8,9},{9,8},{10,11... | collective-permute-start | bytes 159752 | tf_op jit(solution)/shard_map/ppermute | solution.py:325
  16.7 1.0 copy-start
  17.7 11.7 %collective-permute-start = (bf16[624,128]{1,0:T(8,128)(2,1)S(1)}, bf16[624,128]{1,0:T(8,128)(2,1)S(1)}, u32[]{:S(2)}, u32[]{:S(2)}) collective-permute-start(bf16[624,128]{1,0:T(8,128)(2,1)S(1)} %get-tuple-element.25), channel_id=1, source_target_pairs={{0,1},{1,0},{2,3},{3,2},{4,5},{5,4},{6,7},{7,6},{8,9},{9,8},{10,11... | collective-permute-start | bytes 479240 | tf_op jit(solution)/shard_map/ppermute | solution.py:325
  20.8 0.8 copy-start.2
  21.6 0.7 copy-start.8
  22.3 6.5 %copy-start.9 = (bf16[208,2560]{1,0:T(8,128)(2,1)S(1)}, bf16[208,2560]{1,0:T(8,128)(2,1)}, u32[]{:S(2)}) copy-start(bf16[208,2560]{1,0:T(8,128)(2,1)} %param.11) | copy-start | bytes 3194884
  26.9 4.0 %collective-permute-start.5 = (bf16[2560,128]{1,0:T(8,128)(2,1)S(1)}, bf16[2560,128]{1,0:T(8,128)(2,1)S(1)}, u32[]{:S(2)}, u32[]{:S(2)}) collective-permute-start(bf16[2560,128]{1,0:T(8,128)(2,1)S(1)} %convolution_convert_fusion), channel_id=1, source_target_pairs={{0,1},{1,0},{2,3},{3,2},{4,5},{5,4},{6,7},{7,6},{8,9},{9,8},{10,11... | collective-permute-start | bytes 1966088 | tf_op jit(solution)/shard_map/ppermute | solution.py:325
  29.4 1.4 %copy-start.1 = (bf16[64,192]{1,0:T(8,128)(2,1)S(1)}, bf16[64,192]{1,0:T(8,128)(2,1)}, u32[]{:S(2)}) copy-start(bf16[64,192]{1,0:T(8,128)(2,1)} %constant.14.clone.forward) | copy-start | bytes 73732
  29.4 1.4 %copy-start.3 = (f32[128,128]{1,0:T(8,128)S(1)}, f32[128,128]{1,0:T(8,128)}, u32[]{:S(2)}) copy-start(f32[128,128]{1,0:T(8,128)} %constant.16.clone.base) | copy-start | bytes 196612
  29.4 1.4 %copy-start.4 = (bf16[512,128]{1,0:T(8,128)(2,1)S(1)}, bf16[512,128]{1,0:T(8,128)(2,1)}, u32[]{:S(2)}) copy-start(bf16[512,128]{1,0:T(8,128)(2,1)} %constant.17.clone.spans) | copy-start | bytes 393220
  29.5 1.4 %copy-start.6 = (f32[128,128]{1,0:T(8,128)S(1)}, f32[128,128]{1,0:T(8,128)}, u32[]{:S(2)}) copy-start(f32[128,128]{1,0:T(8,128)} %constant.18.clone.slots) | copy-start | bytes 196612
  32.7 11.7 %collective-permute-start.7 = (bf16[512,128]{1,0:T(8,128)(2,1)S(1)}, bf16[512,128]{1,0:T(8,128)(2,1)S(1)}, u32[]{:S(2)}, u32[]{:S(2)}) collective-permute-start(bf16[512,128]{1,0:T(8,128)(2,1)S(1)} %get-tuple-element.33), channel_id=1, source_target_pairs={{0,4},{1,5},{2,6},{3,7},{4,0},{5,1},{6,2},{7,3},{8,12},{9,13},{10,... | collective-permute-start | bytes 393224 | tf_op jit(solution)/shard_map/ppermute | solution.py:322
  37.2 7.0 %copy-start.10 = (f32[1,2560,128]{2,1,0:T(8,128)S(1)}, f32[1,2560,128]{2,1,0:T(8,128)}, u32[]{:S(2)}) copy-start(f32[1,2560,128]{2,1,0:T(8,128)} %param.13) | copy-start | bytes 3932164
  37.4 7.1 %collective-permute-start.6 = (bf16[2560,128]{1,0:T(8,128)(2,1)S(1)}, bf16[2560,128]{1,0:T(8,128)(2,1)S(1)}, u32[]{:S(2)}, u32[]{:S(2)}) collective-permute-start(bf16[2560,128]{1,0:T(8,128)(2,1)S(1)} %slice.39), channel_id=1, source_target_pairs={{0,1},{1,0},{2,3},{3,2},{4,5},{5,4},{6,7},{7,6},{8,9},{9,8},{10,11... | collective-permute-start | bytes 1966088 | tf_op jit(solution)/shard_map/ppermute | solution.py:325
  39.4 42.5 %collective-permute-start.8 = (bf16[2560,128]{1,0:T(8,128)(2,1)S(1)}, bf16[2560,128]{1,0:T(8,128)(2,1)S(1)}, u32[]{:S(2)}, u32[]{:S(2)}) collective-permute-start(bf16[2560,128]{1,0:T(8,128)(2,1)S(1)} %get-tuple-element.38), channel_id=1, source_target_pairs={{0,4},{1,5},{2,6},{3,7},{4,0},{5,1},{6,2},{7,3},{8,12},{9,13},{10,... | collective-permute-start | bytes 1966088 | tf_op jit(solution)/shard_map/ppermute | solution.py:322
  44.5 35.6 %copy-start.5 = (bf16[384,128]{1,0:T(8,128)(2,1)S(1)}, bf16[384,128]{1,0:T(8,128)(2,1)}, u32[]{:S(2)}) copy-start(bf16[384,128]{1,0:T(8,128)(2,1)} %constant.19.clone.backward) | copy-start | bytes 294916
  45.5 41.1 %copy-start.7 = (bf16[64,192]{1,0:T(8,128)(2,1)S(1)}, bf16[64,192]{1,0:T(8,128)(2,1)}, u32[]{:S(2)}) copy-start(bf16[64,192]{1,0:T(8,128)(2,1)} %constant.15.clone.backward) | copy-start | bytes 73732
  81.9 25.8 %all-to-all-start.1 = ((bf16[64,8,640]{2,1,0:T(8,128)(2,1)}), bf16[64,8,640]{2,1,0:T(8,128)(2,1)S(1)}, u32[]{:S(2)}, u32[]{:S(2)}) async-start(bf16[64,8,640]{2,1,0:T(8,128)(2,1)} %bitcast.11), calls=%async_computation.1 | async-start | bytes 1310720 | tf_op jit(solution)/shard_map/all_to_all | solution.py:438

commit v15 on v14

--- a/solution.py
+++ b/solution.py
@@ -121,6 +121,10 @@
     slot = lax.shift_right_logical(lax.broadcasted_iota(jnp.int32, square, 0), 1)
     double = (column == slot).astype(jnp.float32).astype(jnp.bfloat16)
     place = column.astype(jnp.float32)
+    row = lax.broadcasted_iota(jnp.int32, square, 0)
+    spread = lax.shift_right_logical(column, 3) == (row & (OWN_COLS - 1))
+    gather = (column == (row & (OWN_COLS - 1)) + cols - OWN_COLS).astype(jnp.float32)
+    gather = gather.astype(jnp.bfloat16)
     for g in range(ROW_GROUPS):
         halves = []
         for b in range(2):
@@ -130,7 +134,12 @@
                     line = jnp.where(lane == a * most + k, number(g * each + a, b, k), line)
             halves.append(line)
         tile = jnp.concatenate(halves, axis=0).astype(jnp.float32)
-        numbers[g * cols : (g + 1) * cols, :] = tile.astype(numbers.dtype)
+        packed = jnp.dot(
+            jnp.where(spread, tile, 0.0).astype(jnp.bfloat16),
+            gather,
+            preferred_element_type=jnp.float32,
+        )
+        numbers[g * cols : (g + 1) * cols, :] = packed.astype(numbers.dtype)
         twice = jnp.dot(
             double, tile.T.astype(jnp.bfloat16), preferred_element_type=jnp.float32
         )
@@ -227,8 +236,7 @@
     for g in range(ROW_GROUPS):
         message = slice(g * cols, (g + 1) * cols)
         total = chosen(picks, rows, g, first) + far[message, :].astype(jnp.float32)
-        sent[message, :cols] = total.T.astype(sent.dtype)
-        sent[message, cols:] = numbers[message, :]
+        sent[message, :] = (total.T + numbers[message, :].astype(jnp.float32)).astype(sent.dtype)
 
 
 def kept_kernel(advanced, far, mask, forward, backward, kept):
@@ -243,20 +251,25 @@
         put(kept, i, WIDE, x - product(backward, [high, low, high]))
 
 
-def total_kernel(pieces, backward, totals, placed):
-    wide = pieces.shape[1] // 2
+def total_kernel(pieces, unpack, backward, totals, placed):
+    wide = pieces.shape[1]
     spans = totals.shape[1] // SPAN
     lane = lax.broadcasted_iota(jnp.int32, (BLK, wide), 0).astype(jnp.float32)
     for t in range(pieces.shape[0] // wide):
-        values = pieces[t * wide : (t + 1) * wide, :wide].astype(jnp.float32).T
-        numbers = pieces[t * wide : (t + 1) * wide, wide:].astype(jnp.float32).T
+        values = pieces[t * wide : (t + 1) * wide, :].astype(jnp.float32).T
+        numbers = jnp.dot(
+            values[wide - OWN_COLS :, :].astype(jnp.bfloat16),
+            unpack[...],
+            preferred_element_type=jnp.float32,
+        )
         most = wide // (2 * spans)
         for a in range(spans):
             upper = jnp.zeros((BLK, wide), jnp.float32)
             lower = upper
             for k in range(most):
                 at = a * most + k
-                here = numbers[at : at + 1, :] == lane
+                down, across = at % OWN_COLS, at // OWN_COLS * wide
+                here = numbers[down : down + 1, across : across + wide] == lane
                 upper = jnp.where(here, values[2 * at : 2 * at + 1, :], upper)
                 lower = jnp.where(here, values[2 * at + 1 : 2 * at + 2, :], lower)
             both = jnp.concatenate([upper, lower], axis=0)
@@ -420,7 +433,7 @@
     both_high, both_low = (np.kron(np.eye(2, dtype=p.dtype), p[order]) for p in (high, low))
     backward_pair = jnp.asarray(np.concatenate([both_high, both_high, both_low], axis=0))
 
-    message = jax.ShapeDtypeStruct((ROW_GROUPS * cols, 2 * cols), jnp.bfloat16)
+    message = jax.ShapeDtypeStruct((ROW_GROUPS * cols, cols), jnp.bfloat16)
     advanced, sent = call(
         spectrum_kernel,
         "spectrum",
@@ -440,11 +453,19 @@
         ).reshape(x.shape)
 
     pieces = exchange(sent)
+    unpack = np.concatenate(
+        [
+            np.kron(np.eye(cols // OWN_COLS), np.outer(np.eye(OWN_COLS)[c], np.ones(OWN_COLS)))
+            for c in range(OWN_COLS)
+        ],
+        axis=1,
+    )
     (totals,) = call(
         total_kernel,
         "total",
         (jax.ShapeDtypeStruct((replicas * OWN_COLS, height), jnp.bfloat16),),
         pieces,
+        jnp.asarray(unpack.astype(ml_dtypes.bfloat16)),
         backward_pair,
         scratch=(pltpu.VMEM((height, replicas * OWN_COLS), jnp.bfloat16),),
     )

time: 109 us -> 107 us (0.982)
  blocking collectives: 34.5 us -> 32.2 us
    all_to_all x1, blocking collectives: 34.5 us -> 32.2 us  [exchange(): lax.all_to_all(x.reshape(replicas, OWN_COLS, x.shape[1]), 'dp', 0, 0, til...]
    unnamed x22 -> x24, local copies, waits for them, and re-layouts: 2.58 us -> 2.59 us
where the time goes in v15:
time: 107 us
  starting transfers between devices  34.2 us (32%)
  blocking collectives  32.2 us (30%)
  waiting for transfers between devices  18.9 us (18%)
  Pallas kernels  12.7 us (12%)
  matrix products  4.04 us (4%)
  local copies, waits for them, and re-layouts  2.68 us (3%)
  between operations  1.63 us (2%)
    all_to_all x1, blocking collectives, exchange(): lax.all_to_all(x.reshape(replicas, OWN_COLS, x.shape[1]), 'dp', 0, 0, til...  32.2 us
    ppermute x5, starting transfers between devices, along(): lax.ppermute(x, 'tensor', [(i, (i + 2 * step) % group) for i in range(gro...  21.3 us
    all_to_all x1, waiting for transfers between devices, exchange(): lax.all_to_all(x.reshape(replicas, OWN_COLS, x.shape[1]), 'dp', 0, 0, til...  18.1 us
    pallas_call x9, Pallas kernels, call(): pl.pallas_call(kernel, out_shape=outs, in_specs=places or [VMEM] * len(ar...  12.7 us
    ppermute x4, starting transfers between devices, swap(): return lax.ppermute(x, 'tensor', [(i, i ^ 1) for i in range(group)])  8.3 us
    all_to_all x1, starting transfers between devices, exchange(): lax.all_to_all(x.reshape(replicas, OWN_COLS, x.shape[1]), 'dp', 0, 0, til...  4.64 us
    dot_general x5, matrix products, gram(): lax.dot_general(a, k, (((0,), (0,)), ((), ())), preferred_element_type=jn...  4.04 us
    unnamed x24, local copies, waits for them, and re-layouts  2.59 us
  transfers between devices with their start and end apart: 10, of which 2 were waited for; matrix products, arithmetic and copies ran while one was open for 4% of the time, Pallas kernels for 10%

profile of v15, /device:TPU:2, one launch (start us, length us, event | category | flops | bytes accessed | tf_op | source)
XLA Modules:
  0.0 106.5 jit_solution(4614816360807342688)
XLA Ops:
  0.6 0.9 far_keys.1
  1.6 4.0 %collective-permute-start.3 = (bf16[432,128]{1,0:T(8,128)(2,1)S(1)}, bf16[432,128]{1,0:T(8,128)(2,1)S(1)}, u32[]{:S(2)}, u32[]{:S(2)}) collective-permute-start(bf16[432,128]{1,0:T(8,128)(2,1)S(1)} %far_keys.1), channel_id=1, source_target_pairs={{0,4},{1,5},{2,6},{3,7},{4,0},{5,1},{6,2},{7,3},{8,12},{9,13},{10,... | collective-permute-start | bytes 331784 | tf_op jit(solution)/shard_map/ppermute | solution.py:335
  5.6 7.2 %collective-permute-start.1 = (bf16[208,2560]{1,0:T(8,128)(2,1)}, bf16[208,2560]{1,0:T(8,128)(2,1)S(1)}, u32[]{:S(2)}, u32[]{:S(2)}) collective-permute-start(bf16[208,2560]{1,0:T(8,128)(2,1)} %param.12), channel_id=1, source_target_pairs={{0,2},{1,3},{2,4},{3,5},{4,6},{5,7},{6,0},{7,1},{8,10},{9,11},{10,... | collective-permute-start | bytes 3194888 | tf_op jit(solution)/shard_map/ppermute | solution.py:335
  12.8 1.9 %collective-permute-start.2 = (bf16[208,2560]{1,0:T(8,128)(2,1)}, bf16[208,2560]{1,0:T(8,128)(2,1)S(1)}, u32[]{:S(2)}, u32[]{:S(2)}) collective-permute-start(bf16[208,2560]{1,0:T(8,128)(2,1)} %param.12), channel_id=1, source_target_pairs={{0,6},{1,7},{2,0},{3,1},{4,2},{5,3},{6,4},{7,5},{8,14},{9,15},{10,... | collective-permute-start | bytes 3194888 | tf_op jit(solution)/shard_map/ppermute | solution.py:335
  14.7 0.0 collective-permute-done.3.far
  14.7 1.9 %collective-permute-start.4 = (bf16[208,128]{1,0:T(8,128)(2,1)S(1)}, bf16[208,128]{1,0:T(8,128)(2,1)S(1)}, u32[]{:S(2)}, u32[]{:S(2)}) collective-permute-start(bf16[208,128]{1,0:T(8,128)(2,1)S(1)} %get-tuple-element.30), channel_id=1, source_target_pairs={{0,1},{1,0},{2,3},{3,2},{4,5},{5,4},{6,7},{7,6},{8,9},{9,8},{10,11... | collective-permute-start | bytes 159752 | tf_op jit(solution)/shard_map/ppermute | solution.py:338
  16.7 0.0 copy-start
  16.7 1.0 copy-done
  17.7 2.4 %collective-permute-start = (bf16[624,128]{1,0:T(8,128)(2,1)S(1)}, bf16[624,128]{1,0:T(8,128)(2,1)S(1)}, u32[]{:S(2)}, u32[]{:S(2)}) collective-permute-start(bf16[624,128]{1,0:T(8,128)(2,1)S(1)} %get-tuple-element.25), channel_id=1, source_target_pairs={{0,1},{1,0},{2,3},{3,2},{4,5},{5,4},{6,7},{7,6},{8,9},{9,8},{10,11... | collective-permute-start | bytes 479240 | tf_op jit(solution)/shard_map/ppermute | solution.py:338
  20.8 0.0 copy-start.2
  20.8 0.8 copy-done.2
  21.6 0.7 copy-done.9
  22.3 2.8 %routes.1 = (bf16[2560,128]{1,0:T(8,128)(2,1)S(1)}, bf16[1024,640]{1,0:T(8,128)(2,1)S(1)}, bf16[512,128]{1,0:T(8,128)(2,1)S(1)}) custom-call(s32[6,2,40]{2,1,0:T(2,128)S(1)} %bitcast.31, s32[1]{0:T(128)S(6)} %copy.14.count, f32[128,128]{1,0:T(8,128)S(1)} %copy-done.2), custom_call_target="tpu_custom_call" | custom-call | tf_op jit(solution)/shard_map/routes/pallas_call | solution.py:317
  25.1 0.0 collective-permute-done.4
  25.1 1.8 %convolution_convert_fusion = bf16[2560,128]{1,0:T(8,128)(2,1)S(1)} fusion(bf16[208,2560]{1,0:T(8,128)(2,1)} %param.12, bf16[208,128]{1,0:T(8,128)(2,1)S(1)} %collective-permute-done.4), kind=kOutput, calls=%fused_computation.2 | convolution fusion | flops 136642560 | bytes 1773568 | tf_op jit(solution)/shard_map/dot_general | solution.py:308
  26.9 1.9 %collective-permute-start.5 = (bf16[2560,128]{1,0:T(8,128)(2,1)S(1)}, bf16[2560,128]{1,0:T(8,128)(2,1)S(1)}, u32[]{:S(2)}, u32[]{:S(2)}) collective-permute-start(bf16[2560,128]{1,0:T(8,128)(2,1)S(1)} %convolution_convert_fusion), channel_id=1, source_target_pairs={{0,1},{1,0},{2,3},{3,2},{4,5},{5,4},{6,7},{7,6},{8,9},{9,8},{10,11... | collective-permute-start | bytes 1966088 | tf_op jit(solution)/shard_map/ppermute | solution.py:338
  28.9 0.6 fusion.1.part
  29.4 0.0 collective-permute-done
  29.5 0.0 copy-start.1
  29.5 0.0 copy-start.3
  29.5 0.0 copy-start.5
  29.5 0.0 copy-start.7
  29.5 0.6 fusion
  30.1 0.8 collective-permute-done.5.other
  30.9 1.8 %far.1 = (bf16[2560,128]{1,0:T(8,128)(2,1)S(1)}, bf16[512,128]{1,0:T(8,128)(2,1)S(1)}) custom-call(bf16[16,128]{1,0:T(8,128)(2,1)S(1)} %slice.30.numbers, s32[1]{0:T(128)S(6)} %copy.14.count, bf16[512,128]{1,0:T(8,128)(2,1)S(1)} %copy-done.5, f32[128,128]{1,0:T(8,128)S(1)} %copy-done.7, f32[128,128]{1,0:T(8,128)S(1)} %copy-done.3, ...), custom_call_target="tpu_custom_call" | custom-call | tf_op jit(solution)/shard_map/far/pallas_call | solution.py:317
  32.8 3.4 %collective-permute-start.7 = (bf16[512,128]{1,0:T(8,128)(2,1)S(1)}, bf16[512,128]{1,0:T(8,128)(2,1)S(1)}, u32[]{:S(2)}, u32[]{:S(2)}) collective-permute-start(bf16[512,128]{1,0:T(8,128)(2,1)S(1)} %get-tuple-element.33), channel_id=1, source_target_pairs={{0,4},{1,5},{2,6},{3,7},{4,0},{5,1},{6,2},{7,3},{8,12},{9,13},{10,... | collective-permute-start | bytes 393224 | tf_op jit(solution)/shard_map/ppermute | solution.py:335
  36.1 0.0 collective-permute-done.1
  36.2 0.0 collective-permute-done.2
  36.2 0.6 convolution_add_fusion.1
  36.7 0.6 convolution_add_fusion
  37.3 0.0 copy-start.11
  37.3 0.1 slice.39
  37.4 2.1 %collective-permute-start.6 = (bf16[2560,128]{1,0:T(8,128)(2,1)S(1)}, bf16[2560,128]{1,0:T(8,128)(2,1)S(1)}, u32[]{:S(2)}, u32[]{:S(2)}) collective-permute-start(bf16[2560,128]{1,0:T(8,128)(2,1)S(1)} %slice.39), channel_id=1, source_target_pairs={{0,1},{1,0},{2,3},{3,2},{4,5},{5,4},{6,7},{7,6},{8,9},{9,8},{10,11... | collective-permute-start | bytes 1966088 | tf_op jit(solution)/shard_map/ppermute | solution.py:338
  39.5 4.8 %collective-permute-start.8 = (bf16[2560,128]{1,0:T(8,128)(2,1)S(1)}, bf16[2560,128]{1,0:T(8,128)(2,1)S(1)}, u32[]{:S(2)}, u32[]{:S(2)}) collective-permute-start(bf16[2560,128]{1,0:T(8,128)(2,1)S(1)} %get-tuple-element.38), channel_id=1, source_target_pairs={{0,4},{1,5},{2,6},{3,7},{4,0},{5,1},{6,2},{7,3},{8,12},{9,13},{10,... | collective-permute-start | bytes 1966088 | tf_op jit(solution)/shard_map/ppermute | solution.py:335
  44.3 0.2 slice_add_fusion.part
  44.4 0.0 collective-permute-done.7.far
  44.4 0.0 collective-permute-done.6.other
  44.5 0.0 copy-start.4
  44.5 0.0 copy-start.6
  44.5 1.0 spectrum.1
  45.5 0.0 copy-start.8
  45.5 32.2 %all_to_all.10 = bf16[64,8,128]{2,1,0:T(8,128)(2,1)S(1)} all-to-all(bf16[64,8,128]{2,1,0:T(8,128)(2,1)S(1)} %bitcast.29), channel_id=1, replica_groups=mesh['dp'=64,'tensor'=8] {'dp'}, dimensions={0} | all-to-all | bytes 262144 | tf_op jit(solution)/shard_map/all_to_all | solution.py:451
  77.7 1.9 %total.1 = bf16[512,640]{1,0:T(8,128)(2,1)} custom-call(bf16[512,128]{1,0:T(8,128)(2,1)S(1)} %bitcast.28, bf16[128,1024]{1,0:T(8,128)(2,1)S(1)} %copy-done.4, bf16[384,128]{1,0:T(8,128)(2,1)S(1)} %copy-done.6), custom_call_target="tpu_custom_call" | custom-call | tf_op jit(solution)/shard_map/total/pallas_call | solution.py:317
  79.6 0.0 collective-permute-done.8.far
  79.6 4.6 %all-to-all-start.1 = ((bf16[64,8,640]{2,1,0:T(8,128)(2,1)}), bf16[64,8,640]{2,1,0:T(8,128)(2,1)S(1)}, u32[]{:S(2)}, u32[]{:S(2)}) async-start(bf16[64,8,640]{2,1,0:T(8,128)(2,1)} %bitcast.11), calls=%async_computation.1 | async-start | bytes 1310720 | tf_op jit(solution)/shard_map/all_to_all | solution.py:451
  84.3 3.1 %kept.1 = f32[2560,128]{1,0:T(8,128)} custom-call(f32[2560,128]{1,0:T(8,128)S(1)} %get-tuple-element.36.advanced, bf16[2560,128]{1,0:T(8,128)(2,1)S(1)} %collective-permute-done.8.far, bf16[2560,128]{1,0:T(8,128)(2,1)S(1)} %get-tuple-element.40.mask, bf16[64,192]{1,0:T(8,128)(2,1)S(1)} %copy-done.1, bf16[64,192]{1,0:T(8,128)(2,1)S(1)} %copy-done.8), custom_call_target="tpu_custom_call" | custom-call | tf_op jit(solution)/shard_map/kept/pallas_call | solution.py:317
  87.3 18.1 %all-to-all-done.1 = bf16[64,8,640]{2,1,0:T(8,128)(2,1)S(1)} async-done(((bf16[64,8,640]{2,1,0:T(8,128)(2,1)}), bf16[64,8,640]{2,1,0:T(8,128)(2,1)S(1)}, u32[]{:S(2)}, u32[]{:S(2)}) %all-to-all-start.1) | async-done | bytes 655392 | tf_op jit(solution)/shard_map/all_to_all | solution.py:451
  105.4 1.1 %turn.1 = bf16[2560,128]{1,0:T(8,128)(2,1)} custom-call(bf16[512,640]{1,0:T(8,128)(2,1)S(1)} %bitcast.27), custom_call_target="tpu_custom_call" | custom-call | tf_op jit(solution)/shard_map/turn/pallas_call | solution.py:317
  (15 shorter events, 0.1 us)
Async XLA Ops:
  1.6 13.1 %collective-permute-start.3 = (bf16[432,128]{1,0:T(8,128)(2,1)S(1)}, bf16[432,128]{1,0:T(8,128)(2,1)S(1)}, u32[]{:S(2)}, u32[]{:S(2)}) collective-permute-start(bf16[432,128]{1,0:T(8,128)(2,1)S(1)} %far_keys.1), channel_id=1, source_target_pairs={{0,4},{1,5},{2,6},{3,7},{4,0},{5,1},{6,2},{7,3},{8,12},{9,13},{10,... | collective-permute-start | bytes 331784 | tf_op jit(solution)/shard_map/ppermute | solution.py:335
  5.6 30.5 %collective-permute-start.1 = (bf16[208,2560]{1,0:T(8,128)(2,1)}, bf16[208,2560]{1,0:T(8,128)(2,1)S(1)}, u32[]{:S(2)}, u32[]{:S(2)}) collective-permute-start(bf16[208,2560]{1,0:T(8,128)(2,1)} %param.12), channel_id=1, source_target_pairs={{0,2},{1,3},{2,4},{3,5},{4,6},{5,7},{6,0},{7,1},{8,10},{9,11},{10,... | collective-permute-start | bytes 3194888 | tf_op jit(solution)/shard_map/ppermute | solution.py:335
  12.8 23.4 %collective-permute-start.2 = (bf16[208,2560]{1,0:T(8,128)(2,1)}, bf16[208,2560]{1,0:T(8,128)(2,1)S(1)}, u32[]{:S(2)}, u32[]{:S(2)}) collective-permute-start(bf16[208,2560]{1,0:T(8,128)(2,1)} %param.12), channel_id=1, source_target_pairs={{0,6},{1,7},{2,0},{3,1},{4,2},{5,3},{6,4},{7,5},{8,14},{9,15},{10,... | collective-permute-start | bytes 3194888 | tf_op jit(solution)/shard_map/ppermute | solution.py:335
  14.7 10.4 %collective-permute-start.4 = (bf16[208,128]{1,0:T(8,128)(2,1)S(1)}, bf16[208,128]{1,0:T(8,128)(2,1)S(1)}, u32[]{:S(2)}, u32[]{:S(2)}) collective-permute-start(bf16[208,128]{1,0:T(8,128)(2,1)S(1)} %get-tuple-element.30), channel_id=1, source_target_pairs={{0,1},{1,0},{2,3},{3,2},{4,5},{5,4},{6,7},{7,6},{8,9},{9,8},{10,11... | collective-permute-start | bytes 159752 | tf_op jit(solution)/shard_map/ppermute | solution.py:338
  16.7 1.0 copy-start
  17.7 11.7 %collective-permute-start = (bf16[624,128]{1,0:T(8,128)(2,1)S(1)}, bf16[624,128]{1,0:T(8,128)(2,1)S(1)}, u32[]{:S(2)}, u32[]{:S(2)}) collective-permute-start(bf16[624,128]{1,0:T(8,128)(2,1)S(1)} %get-tuple-element.25), channel_id=1, source_target_pairs={{0,1},{1,0},{2,3},{3,2},{4,5},{5,4},{6,7},{7,6},{8,9},{9,8},{10,11... | collective-permute-start | bytes 479240 | tf_op jit(solution)/shard_map/ppermute | solution.py:338
  20.8 0.8 copy-start.2
  21.6 0.7 copy-start.9
  22.3 6.6 %copy-start.10 = (bf16[208,2560]{1,0:T(8,128)(2,1)S(1)}, bf16[208,2560]{1,0:T(8,128)(2,1)}, u32[]{:S(2)}) copy-start(bf16[208,2560]{1,0:T(8,128)(2,1)} %param.12) | copy-start | bytes 3194884
  26.9 4.0 %collective-permute-start.5 = (bf16[2560,128]{1,0:T(8,128)(2,1)S(1)}, bf16[2560,128]{1,0:T(8,128)(2,1)S(1)}, u32[]{:S(2)}, u32[]{:S(2)}) collective-permute-start(bf16[2560,128]{1,0:T(8,128)(2,1)S(1)} %convolution_convert_fusion), channel_id=1, source_target_pairs={{0,1},{1,0},{2,3},{3,2},{4,5},{5,4},{6,7},{7,6},{8,9},{9,8},{10,11... | collective-permute-start | bytes 1966088 | tf_op jit(solution)/shard_map/ppermute | solution.py:338
  29.5 1.4 %copy-start.1 = (bf16[64,192]{1,0:T(8,128)(2,1)S(1)}, bf16[64,192]{1,0:T(8,128)(2,1)}, u32[]{:S(2)}) copy-start(bf16[64,192]{1,0:T(8,128)(2,1)} %constant.16.clone.forward) | copy-start | bytes 73732
  29.5 1.4 %copy-start.3 = (f32[128,128]{1,0:T(8,128)S(1)}, f32[128,128]{1,0:T(8,128)}, u32[]{:S(2)}) copy-start(f32[128,128]{1,0:T(8,128)} %constant.18.clone.base) | copy-start | bytes 196612
  29.5 1.4 %copy-start.5 = (bf16[512,128]{1,0:T(8,128)(2,1)S(1)}, bf16[512,128]{1,0:T(8,128)(2,1)}, u32[]{:S(2)}) copy-start(bf16[512,128]{1,0:T(8,128)(2,1)} %constant.19.clone.spans) | copy-start | bytes 393220
  29.5 1.4 %copy-start.7 = (f32[128,128]{1,0:T(8,128)S(1)}, f32[128,128]{1,0:T(8,128)}, u32[]{:S(2)}) copy-start(f32[128,128]{1,0:T(8,128)} %constant.20.clone.slots) | copy-start | bytes 196612
  32.8 11.7 %collective-permute-start.7 = (bf16[512,128]{1,0:T(8,128)(2,1)S(1)}, bf16[512,128]{1,0:T(8,128)(2,1)S(1)}, u32[]{:S(2)}, u32[]{:S(2)}) collective-permute-start(bf16[512,128]{1,0:T(8,128)(2,1)S(1)} %get-tuple-element.33), channel_id=1, source_target_pairs={{0,4},{1,5},{2,6},{3,7},{4,0},{5,1},{6,2},{7,3},{8,12},{9,13},{10,... | collective-permute-start | bytes 393224 | tf_op jit(solution)/shard_map/ppermute | solution.py:335
  37.3 6.9 %copy-start.11 = (f32[1,2560,128]{2,1,0:T(8,128)S(1)}, f32[1,2560,128]{2,1,0:T(8,128)}, u32[]{:S(2)}) copy-start(f32[1,2560,128]{2,1,0:T(8,128)} %param.14) | copy-start | bytes 3932164
  37.4 7.0 %collective-permute-start.6 = (bf16[2560,128]{1,0:T(8,128)(2,1)S(1)}, bf16[2560,128]{1,0:T(8,128)(2,1)S(1)}, u32[]{:S(2)}, u32[]{:S(2)}) collective-permute-start(bf16[2560,128]{1,0:T(8,128)(2,1)S(1)} %slice.39), channel_id=1, source_target_pairs={{0,1},{1,0},{2,3},{3,2},{4,5},{5,4},{6,7},{7,6},{8,9},{9,8},{10,11... | collective-permute-start | bytes 1966088 | tf_op jit(solution)/shard_map/ppermute | solution.py:338
  39.5 40.1 %collective-permute-start.8 = (bf16[2560,128]{1,0:T(8,128)(2,1)S(1)}, bf16[2560,128]{1,0:T(8,128)(2,1)S(1)}, u32[]{:S(2)}, u32[]{:S(2)}) collective-permute-start(bf16[2560,128]{1,0:T(8,128)(2,1)S(1)} %get-tuple-element.38), channel_id=1, source_target_pairs={{0,4},{1,5},{2,6},{3,7},{4,0},{5,1},{6,2},{7,3},{8,12},{9,13},{10,... | collective-permute-start | bytes 1966088 | tf_op jit(solution)/shard_map/ppermute | solution.py:335
  44.5 33.2 %copy-start.4 = (bf16[128,1024]{1,0:T(8,128)(2,1)S(1)}, bf16[128,1024]{1,0:T(8,128)(2,1)}, u32[]{:S(2)}) copy-start(bf16[128,1024]{1,0:T(8,128)(2,1)} %constant.22.clone.unpack) | copy-start | bytes 786436
  44.5 33.2 %copy-start.6 = (bf16[384,128]{1,0:T(8,128)(2,1)S(1)}, bf16[384,128]{1,0:T(8,128)(2,1)}, u32[]{:S(2)}) copy-start(bf16[384,128]{1,0:T(8,128)(2,1)} %constant.21.clone.backward) | copy-start | bytes 294916
  45.5 38.8 %copy-start.8 = (bf16[64,192]{1,0:T(8,128)(2,1)S(1)}, bf16[64,192]{1,0:T(8,128)(2,1)}, u32[]{:S(2)}) copy-start(bf16[64,192]{1,0:T(8,128)(2,1)} %constant.17.clone.backward) | copy-start | bytes 73732
  79.6 25.8 %all-to-all-start.1 = ((bf16[64,8,640]{2,1,0:T(8,128)(2,1)}), bf16[64,8,640]{2,1,0:T(8,128)(2,1)S(1)}, u32[]{:S(2)}, u32[]{:S(2)}) async-start(bf16[64,8,640]{2,1,0:T(8,128)(2,1)} %bitcast.11), calls=%async_computation.1 | async-start | bytes 1310720 | tf_op jit(solution)/shard_map/all_to_all | solution.py:451

commit v16 on v15

--- a/solution.py
+++ b/solution.py
@@ -52,9 +52,9 @@
         ref[first : first + SPAN, :] = value[:, s * cols : (s + 1) * cols].astype(ref.dtype)
 
 
-def far_keys_kernel(chips, tokens, keys, ids, far, numbers, done):
+def far_keys_kernel(tokens, keys, ids, far, numbers, done):
     chip = lax.shift_right_logical(lax.axis_index("tensor"), 1)
-    first = 2 * lax.bitwise_and(chip + FAR, chips - 1) * tokens
+    first = 2 * lax.bitwise_xor(chip, FAR) * tokens
     rows = pltpu.make_async_copy(
         keys.at[pl.ds(pl.multiple_of(first, 16), 2 * tokens)],
         far.at[pl.ds(0, 2 * tokens)],
@@ -73,12 +73,12 @@
     rows.wait()
 
 
-def keys_kernel(chips, tokens, keys, own, partner):
+def keys_kernel(tokens, keys, own, partner):
     spot = lax.axis_index("tensor")
     chip, core = lax.shift_right_logical(spot, 1), lax.bitwise_and(spot, 1)
 
     def block(step, which):
-        first = (2 * lax.bitwise_and(chip + step, chips - 1) + which) * tokens
+        first = (2 * lax.bitwise_xor(chip, step) + which) * tokens
         return keys[pl.ds(pl.multiple_of(first, 16), tokens), :]
 
     for place, step in enumerate(NEAR):
@@ -329,10 +329,9 @@
 def shards(activations, key_grad, momentum, block_ids, counts, *, replicas, group):
     tokens, features = activations.shape
     cols = key_grad.shape[1]
-    chips = group // 2
 
     def along(x, step):
-        return lax.ppermute(x, "tensor", [(i, (i + 2 * step) % group) for i in range(group)])
+        return lax.ppermute(x, "tensor", [(i, i ^ (2 * step)) for i in range(group)])
 
     def swap(x):
         return lax.ppermute(x, "tensor", [(i, i ^ 1) for i in range(group)])
@@ -341,7 +340,7 @@
     far_rows = jax.ShapeDtypeStruct((2 * tokens + 16, cols), jnp.bfloat16)
     ids = jnp.transpose(block_ids[0], (2, 1, 0))
     (far_keys,) = call(
-        functools.partial(far_keys_kernel, chips, tokens),
+        functools.partial(far_keys_kernel, tokens),
         "far_keys",
         (far_rows,),
         pltpu.with_memory_space_constraint(key_grad, pltpu.HBM),
@@ -353,7 +352,7 @@
         (activations, key_grad, far_keys)
     )
     far_keys = along(far_keys, FAR)
-    left, right = along(activations, 1), along(activations, -1)
+    first, second = (along(activations, step) for step in NEAR[1:])
 
     block_rows = jax.ShapeDtypeStruct((tokens, cols), jnp.bfloat16)
     far_own, far_theirs = call(
@@ -363,7 +362,7 @@
     far_other = swap(gram(activations, far_theirs).astype(jnp.bfloat16))
     far_part = gram(activations, far_own)
     own_keys, partner_keys = call(
-        functools.partial(keys_kernel, chips, tokens), "keys", (near_rows, near_rows), key_grad
+        functools.partial(keys_kernel, tokens), "keys", (near_rows, near_rows), key_grad
     )
     their_keys = swap(partner_keys)
 
@@ -421,8 +420,8 @@
 
     keys = jnp.concatenate([own_keys, their_keys], axis=1)
     keys = lax.optimization_barrier(keys.reshape(len(NEAR), tokens, 2 * cols))
-    left, right = lax.optimization_barrier((left, right))
-    near = gram(activations, keys[0]) + gram(right, keys[1]) + gram(left, keys[2])
+    first, second = lax.optimization_barrier((first, second))
+    near = gram(activations, keys[0]) + gram(first, keys[1]) + gram(second, keys[2])
     other, far_whole = lax.optimization_barrier(
         (near[:, cols:].astype(jnp.bfloat16), far_whole)
     )

time: 107 us -> 106 us (level)
  the two profiles are of different devices: /device:TPU:2 before, /device:TPU:6 now
where the time goes in v16:
time: 106 us; the launch traced here: 105 us
  starting transfers between devices  32.7 us (31%)
  blocking collectives  31.7 us (30%)
  waiting for transfers between devices  18.9 us (18%)
  Pallas kernels  12.7 us (12%)
  matrix products  4.04 us (4%)
  local copies, waits for them, and re-layouts  2.68 us (3%)
  between operations  1.63 us (2%)
    all_to_all x1, blocking collectives, exchange(): lax.all_to_all(x.reshape(replicas, OWN_COLS, x.shape[1]), 'dp', 0, 0, til...  31.7 us
    ppermute x5, starting transfers between devices, along(): return lax.ppermute(x, 'tensor', [(i, i ^ 2 * step) for i in range(group)])  19.8 us
    all_to_all x1, waiting for transfers between devices, exchange(): lax.all_to_all(x.reshape(replicas, OWN_COLS, x.shape[1]), 'dp', 0, 0, til...  18.1 us
    pallas_call x9, Pallas kernels, call(): pl.pallas_call(kernel, out_shape=outs, in_specs=places or [VMEM] * len(ar...  12.7 us
    ppermute x4, starting transfers between devices, swap(): return lax.ppermute(x, 'tensor', [(i, i ^ 1) for i in range(group)])  8.3 us
    all_to_all x1, starting transfers between devices, exchange(): lax.all_to_all(x.reshape(replicas, OWN_COLS, x.shape[1]), 'dp', 0, 0, til...  4.64 us
    dot_general x5, matrix products, gram(): lax.dot_general(a, k, (((0,), (0,)), ((), ())), preferred_element_type=jn...  4.04 us
    unnamed x24, local copies, waits for them, and re-layouts  2.59 us
  transfers between devices with their start and end apart: 10, of which 2 were waited for; matrix products, arithmetic and copies ran while one was open for 4% of the time, Pallas kernels for 10%

profile of v16, /device:TPU:6, one launch (start us, length us, event | category | flops | bytes accessed | tf_op | source)
XLA Modules:
  0.0 104.6 jit_solution(16995854268024464674)
XLA Ops:
  0.6 0.9 far_keys.1
  1.6 3.3 %collective-permute-start.3 = (bf16[432,128]{1,0:T(8,128)(2,1)S(1)}, bf16[432,128]{1,0:T(8,128)(2,1)S(1)}, u32[]{:S(2)}, u32[]{:S(2)}) collective-permute-start(bf16[432,128]{1,0:T(8,128)(2,1)S(1)} %far_keys.1), channel_id=1, source_target_pairs={{0,4},{1,5},{2,6},{3,7},{4,0},{5,1},{6,2},{7,3},{8,12},{9,13},{10,... | collective-permute-start | bytes 331784 | tf_op jit(solution)/shard_map/ppermute | solution.py:334
  4.9 7.2 %collective-permute-start.1 = (bf16[208,2560]{1,0:T(8,128)(2,1)}, bf16[208,2560]{1,0:T(8,128)(2,1)S(1)}, u32[]{:S(2)}, u32[]{:S(2)}) collective-permute-start(bf16[208,2560]{1,0:T(8,128)(2,1)} %param.12), channel_id=1, source_target_pairs={{0,2},{1,3},{2,0},{3,1},{4,6},{5,7},{6,4},{7,5},{8,10},{9,11},{10,... | collective-permute-start | bytes 3194888 | tf_op jit(solution)/shard_map/ppermute | solution.py:334
  12.1 1.9 %collective-permute-start.2 = (bf16[208,2560]{1,0:T(8,128)(2,1)}, bf16[208,2560]{1,0:T(8,128)(2,1)S(1)}, u32[]{:S(2)}, u32[]{:S(2)}) collective-permute-start(bf16[208,2560]{1,0:T(8,128)(2,1)} %param.12), channel_id=1, source_target_pairs={{0,6},{1,7},{2,4},{3,5},{4,2},{5,3},{6,0},{7,1},{8,14},{9,15},{10,... | collective-permute-start | bytes 3194888 | tf_op jit(solution)/shard_map/ppermute | solution.py:334
  14.0 0.0 collective-permute-done.3.far
  14.1 1.9 %collective-permute-start.4 = (bf16[208,128]{1,0:T(8,128)(2,1)S(1)}, bf16[208,128]{1,0:T(8,128)(2,1)S(1)}, u32[]{:S(2)}, u32[]{:S(2)}) collective-permute-start(bf16[208,128]{1,0:T(8,128)(2,1)S(1)} %get-tuple-element.30), channel_id=1, source_target_pairs={{0,1},{1,0},{2,3},{3,2},{4,5},{5,4},{6,7},{7,6},{8,9},{9,8},{10,11... | collective-permute-start | bytes 159752 | tf_op jit(solution)/shard_map/ppermute | solution.py:337
  16.0 0.0 copy-start
  16.0 1.0 copy-done
  17.0 2.4 %collective-permute-start = (bf16[624,128]{1,0:T(8,128)(2,1)S(1)}, bf16[624,128]{1,0:T(8,128)(2,1)S(1)}, u32[]{:S(2)}, u32[]{:S(2)}) collective-permute-start(bf16[624,128]{1,0:T(8,128)(2,1)S(1)} %get-tuple-element.25), channel_id=1, source_target_pairs={{0,1},{1,0},{2,3},{3,2},{4,5},{5,4},{6,7},{7,6},{8,9},{9,8},{10,11... | collective-permute-start | bytes 479240 | tf_op jit(solution)/shard_map/ppermute | solution.py:337
  20.1 0.0 copy-start.2
  20.1 0.8 copy-done.2
  20.9 0.7 copy-done.9
  21.6 2.8 %routes.1 = (bf16[2560,128]{1,0:T(8,128)(2,1)S(1)}, bf16[1024,640]{1,0:T(8,128)(2,1)S(1)}, bf16[512,128]{1,0:T(8,128)(2,1)S(1)}) custom-call(s32[6,2,40]{2,1,0:T(2,128)S(1)} %bitcast.31, s32[1]{0:T(128)S(6)} %copy.14.count, f32[128,128]{1,0:T(8,128)S(1)} %copy-done.2), custom_call_target="tpu_custom_call" | custom-call | tf_op jit(solution)/shard_map/routes/pallas_call | solution.py:317
  24.4 0.0 collective-permute-done.4
  24.5 1.8 %convolution_convert_fusion = bf16[2560,128]{1,0:T(8,128)(2,1)S(1)} fusion(bf16[208,2560]{1,0:T(8,128)(2,1)} %param.12, bf16[208,128]{1,0:T(8,128)(2,1)S(1)} %collective-permute-done.4), kind=kOutput, calls=%fused_computation.2 | convolution fusion | flops 136642560 | bytes 1773568 | tf_op jit(solution)/shard_map/dot_general | solution.py:308
  26.3 1.9 %collective-permute-start.5 = (bf16[2560,128]{1,0:T(8,128)(2,1)S(1)}, bf16[2560,128]{1,0:T(8,128)(2,1)S(1)}, u32[]{:S(2)}, u32[]{:S(2)}) collective-permute-start(bf16[2560,128]{1,0:T(8,128)(2,1)S(1)} %convolution_convert_fusion), channel_id=1, source_target_pairs={{0,1},{1,0},{2,3},{3,2},{4,5},{5,4},{6,7},{7,6},{8,9},{9,8},{10,11... | collective-permute-start | bytes 1966088 | tf_op jit(solution)/shard_map/ppermute | solution.py:337
  28.2 0.6 fusion.1.part
  28.8 0.0 collective-permute-done
  28.8 0.0 copy-start.1
  28.8 0.0 copy-start.3
  28.8 0.0 copy-start.5
  28.9 0.0 copy-start.7
  28.9 0.6 fusion
  29.4 0.8 collective-permute-done.5.other
  30.3 1.8 %far.1 = (bf16[2560,128]{1,0:T(8,128)(2,1)S(1)}, bf16[512,128]{1,0:T(8,128)(2,1)S(1)}) custom-call(bf16[16,128]{1,0:T(8,128)(2,1)S(1)} %slice.30.numbers, s32[1]{0:T(128)S(6)} %copy.14.count, bf16[512,128]{1,0:T(8,128)(2,1)S(1)} %copy-done.5, f32[128,128]{1,0:T(8,128)S(1)} %copy-done.7, f32[128,128]{1,0:T(8,128)S(1)} %copy-done.3, ...), custom_call_target="tpu_custom_call" | custom-call | tf_op jit(solution)/shard_map/far/pallas_call | solution.py:317
  32.1 4.0 %collective-permute-start.7 = (bf16[512,128]{1,0:T(8,128)(2,1)S(1)}, bf16[512,128]{1,0:T(8,128)(2,1)S(1)}, u32[]{:S(2)}, u32[]{:S(2)}) collective-permute-start(bf16[512,128]{1,0:T(8,128)(2,1)S(1)} %get-tuple-element.33), channel_id=1, source_target_pairs={{0,4},{1,5},{2,6},{3,7},{4,0},{5,1},{6,2},{7,3},{8,12},{9,13},{10,... | collective-permute-start | bytes 393224 | tf_op jit(solution)/shard_map/ppermute | solution.py:334
  36.1 0.0 collective-permute-done.1
  36.1 0.0 collective-permute-done.2
  36.1 0.6 convolution_add_fusion.1
  36.7 0.6 convolution_add_fusion
  37.3 0.0 copy-start.11
  37.3 0.1 slice.39
  37.4 2.1 %collective-permute-start.6 = (bf16[2560,128]{1,0:T(8,128)(2,1)S(1)}, bf16[2560,128]{1,0:T(8,128)(2,1)S(1)}, u32[]{:S(2)}, u32[]{:S(2)}) collective-permute-start(bf16[2560,128]{1,0:T(8,128)(2,1)S(1)} %slice.39), channel_id=1, source_target_pairs={{0,1},{1,0},{2,3},{3,2},{4,5},{5,4},{6,7},{7,6},{8,9},{9,8},{10,11... | collective-permute-start | bytes 1966088 | tf_op jit(solution)/shard_map/ppermute | solution.py:337
  39.4 3.4 %collective-permute-start.8 = (bf16[2560,128]{1,0:T(8,128)(2,1)S(1)}, bf16[2560,128]{1,0:T(8,128)(2,1)S(1)}, u32[]{:S(2)}, u32[]{:S(2)}) collective-permute-start(bf16[2560,128]{1,0:T(8,128)(2,1)S(1)} %get-tuple-element.38), channel_id=1, source_target_pairs={{0,4},{1,5},{2,6},{3,7},{4,0},{5,1},{6,2},{7,3},{8,12},{9,13},{10,... | collective-permute-start | bytes 1966088 | tf_op jit(solution)/shard_map/ppermute | solution.py:334
  42.8 0.2 slice_add_fusion.part
  43.0 0.0 collective-permute-done.7.far
  43.0 0.0 collective-permute-done.6.other
  43.0 0.0 copy-start.4
  43.0 0.0 copy-start.6
  43.0 1.0 spectrum.1
  44.0 0.0 copy-start.8
  44.0 31.7 %all_to_all.10 = bf16[64,8,128]{2,1,0:T(8,128)(2,1)S(1)} all-to-all(bf16[64,8,128]{2,1,0:T(8,128)(2,1)S(1)} %bitcast.29), channel_id=1, replica_groups=mesh['dp'=64,'tensor'=8] {'dp'}, dimensions={0} | all-to-all | bytes 262144 | tf_op jit(solution)/shard_map/all_to_all | solution.py:450
  75.8 1.9 %total.1 = bf16[512,640]{1,0:T(8,128)(2,1)} custom-call(bf16[512,128]{1,0:T(8,128)(2,1)S(1)} %bitcast.28, bf16[128,1024]{1,0:T(8,128)(2,1)S(1)} %copy-done.4, bf16[384,128]{1,0:T(8,128)(2,1)S(1)} %copy-done.6), custom_call_target="tpu_custom_call" | custom-call | tf_op jit(solution)/shard_map/total/pallas_call | solution.py:317
  77.7 0.0 collective-permute-done.8.far
  77.7 4.6 %all-to-all-start.1 = ((bf16[64,8,640]{2,1,0:T(8,128)(2,1)}), bf16[64,8,640]{2,1,0:T(8,128)(2,1)S(1)}, u32[]{:S(2)}, u32[]{:S(2)}) async-start(bf16[64,8,640]{2,1,0:T(8,128)(2,1)} %bitcast.11), calls=%async_computation.1 | async-start | bytes 1310720 | tf_op jit(solution)/shard_map/all_to_all | solution.py:450
  82.4 3.1 %kept.1 = f32[2560,128]{1,0:T(8,128)} custom-call(f32[2560,128]{1,0:T(8,128)S(1)} %get-tuple-element.36.advanced, bf16[2560,128]{1,0:T(8,128)(2,1)S(1)} %collective-permute-done.8.far, bf16[2560,128]{1,0:T(8,128)(2,1)S(1)} %get-tuple-element.40.mask, bf16[64,192]{1,0:T(8,128)(2,1)S(1)} %copy-done.1, bf16[64,192]{1,0:T(8,128)(2,1)S(1)} %copy-done.8), custom_call_target="tpu_custom_call" | custom-call | tf_op jit(solution)/shard_map/kept/pallas_call | solution.py:317
  85.5 18.1 %all-to-all-done.1 = bf16[64,8,640]{2,1,0:T(8,128)(2,1)S(1)} async-done(((bf16[64,8,640]{2,1,0:T(8,128)(2,1)}), bf16[64,8,640]{2,1,0:T(8,128)(2,1)S(1)}, u32[]{:S(2)}, u32[]{:S(2)}) %all-to-all-start.1) | async-done | bytes 655392 | tf_op jit(solution)/shard_map/all_to_all | solution.py:450
  103.6 1.1 %turn.1 = bf16[2560,128]{1,0:T(8,128)(2,1)} custom-call(bf16[512,640]{1,0:T(8,128)(2,1)S(1)} %bitcast.27), custom_call_target="tpu_custom_call" | custom-call | tf_op jit(solution)/shard_map/turn/pallas_call | solution.py:317
  (15 shorter events, 0.1 us)
Async XLA Ops:
  1.6 12.5 %collective-permute-start.3 = (bf16[432,128]{1,0:T(8,128)(2,1)S(1)}, bf16[432,128]{1,0:T(8,128)(2,1)S(1)}, u32[]{:S(2)}, u32[]{:S(2)}) collective-permute-start(bf16[432,128]{1,0:T(8,128)(2,1)S(1)} %far_keys.1), channel_id=1, source_target_pairs={{0,4},{1,5},{2,6},{3,7},{4,0},{5,1},{6,2},{7,3},{8,12},{9,13},{10,... | collective-permute-start | bytes 331784 | tf_op jit(solution)/shard_map/ppermute | solution.py:334
  4.9 31.2 %collective-permute-start.1 = (bf16[208,2560]{1,0:T(8,128)(2,1)}, bf16[208,2560]{1,0:T(8,128)(2,1)S(1)}, u32[]{:S(2)}, u32[]{:S(2)}) collective-permute-start(bf16[208,2560]{1,0:T(8,128)(2,1)} %param.12), channel_id=1, source_target_pairs={{0,2},{1,3},{2,0},{3,1},{4,6},{5,7},{6,4},{7,5},{8,10},{9,11},{10,... | collective-permute-start | bytes 3194888 | tf_op jit(solution)/shard_map/ppermute | solution.py:334
  12.1 24.0 %collective-permute-start.2 = (bf16[208,2560]{1,0:T(8,128)(2,1)}, bf16[208,2560]{1,0:T(8,128)(2,1)S(1)}, u32[]{:S(2)}, u32[]{:S(2)}) collective-permute-start(bf16[208,2560]{1,0:T(8,128)(2,1)} %param.12), channel_id=1, source_target_pairs={{0,6},{1,7},{2,4},{3,5},{4,2},{5,3},{6,0},{7,1},{8,14},{9,15},{10,... | collective-permute-start | bytes 3194888 | tf_op jit(solution)/shard_map/ppermute | solution.py:334
  14.1 10.4 %collective-permute-start.4 = (bf16[208,128]{1,0:T(8,128)(2,1)S(1)}, bf16[208,128]{1,0:T(8,128)(2,1)S(1)}, u32[]{:S(2)}, u32[]{:S(2)}) collective-permute-start(bf16[208,128]{1,0:T(8,128)(2,1)S(1)} %get-tuple-element.30), channel_id=1, source_target_pairs={{0,1},{1,0},{2,3},{3,2},{4,5},{5,4},{6,7},{7,6},{8,9},{9,8},{10,11... | collective-permute-start | bytes 159752 | tf_op jit(solution)/shard_map/ppermute | solution.py:337
  16.0 1.0 copy-start
  17.0 11.7 %collective-permute-start = (bf16[624,128]{1,0:T(8,128)(2,1)S(1)}, bf16[624,128]{1,0:T(8,128)(2,1)S(1)}, u32[]{:S(2)}, u32[]{:S(2)}) collective-permute-start(bf16[624,128]{1,0:T(8,128)(2,1)S(1)} %get-tuple-element.25), channel_id=1, source_target_pairs={{0,1},{1,0},{2,3},{3,2},{4,5},{5,4},{6,7},{7,6},{8,9},{9,8},{10,11... | collective-permute-start | bytes 479240 | tf_op jit(solution)/shard_map/ppermute | solution.py:337
  20.1 0.8 copy-start.2
  20.9 0.7 copy-start.9
  21.6 6.6 %copy-start.10 = (bf16[208,2560]{1,0:T(8,128)(2,1)S(1)}, bf16[208,2560]{1,0:T(8,128)(2,1)}, u32[]{:S(2)}) copy-start(bf16[208,2560]{1,0:T(8,128)(2,1)} %param.12) | copy-start | bytes 3194884
  26.3 4.0 %collective-permute-start.5 = (bf16[2560,128]{1,0:T(8,128)(2,1)S(1)}, bf16[2560,128]{1,0:T(8,128)(2,1)S(1)}, u32[]{:S(2)}, u32[]{:S(2)}) collective-permute-start(bf16[2560,128]{1,0:T(8,128)(2,1)S(1)} %convolution_convert_fusion), channel_id=1, source_target_pairs={{0,1},{1,0},{2,3},{3,2},{4,5},{5,4},{6,7},{7,6},{8,9},{9,8},{10,11... | collective-permute-start | bytes 1966088 | tf_op jit(solution)/shard_map/ppermute | solution.py:337
  28.8 1.4 %copy-start.1 = (bf16[64,192]{1,0:T(8,128)(2,1)S(1)}, bf16[64,192]{1,0:T(8,128)(2,1)}, u32[]{:S(2)}) copy-start(bf16[64,192]{1,0:T(8,128)(2,1)} %constant.16.clone.forward) | copy-start | bytes 73732
  28.8 1.4 %copy-start.3 = (f32[128,128]{1,0:T(8,128)S(1)}, f32[128,128]{1,0:T(8,128)}, u32[]{:S(2)}) copy-start(f32[128,128]{1,0:T(8,128)} %constant.18.clone.base) | copy-start | bytes 196612
  28.8 1.4 %copy-start.5 = (bf16[512,128]{1,0:T(8,128)(2,1)S(1)}, bf16[512,128]{1,0:T(8,128)(2,1)}, u32[]{:S(2)}) copy-start(bf16[512,128]{1,0:T(8,128)(2,1)} %constant.19.clone.spans) | copy-start | bytes 393220
  28.9 1.4 %copy-start.7 = (f32[128,128]{1,0:T(8,128)S(1)}, f32[128,128]{1,0:T(8,128)}, u32[]{:S(2)}) copy-start(f32[128,128]{1,0:T(8,128)} %constant.20.clone.slots) | copy-start | bytes 196612
  32.1 10.9 %collective-permute-start.7 = (bf16[512,128]{1,0:T(8,128)(2,1)S(1)}, bf16[512,128]{1,0:T(8,128)(2,1)S(1)}, u32[]{:S(2)}, u32[]{:S(2)}) collective-permute-start(bf16[512,128]{1,0:T(8,128)(2,1)S(1)} %get-tuple-element.33), channel_id=1, source_target_pairs={{0,4},{1,5},{2,6},{3,7},{4,0},{5,1},{6,2},{7,3},{8,12},{9,13},{10,... | collective-permute-start | bytes 393224 | tf_op jit(solution)/shard_map/ppermute | solution.py:334
  37.3 5.5 %copy-start.11 = (f32[1,2560,128]{2,1,0:T(8,128)S(1)}, f32[1,2560,128]{2,1,0:T(8,128)}, u32[]{:S(2)}) copy-start(f32[1,2560,128]{2,1,0:T(8,128)} %param.14) | copy-start | bytes 3932164
  37.4 5.6 %collective-permute-start.6 = (bf16[2560,128]{1,0:T(8,128)(2,1)S(1)}, bf16[2560,128]{1,0:T(8,128)(2,1)S(1)}, u32[]{:S(2)}, u32[]{:S(2)}) collective-permute-start(bf16[2560,128]{1,0:T(8,128)(2,1)S(1)} %slice.39), channel_id=1, source_target_pairs={{0,1},{1,0},{2,3},{3,2},{4,5},{5,4},{6,7},{7,6},{8,9},{9,8},{10,11... | collective-permute-start | bytes 1966088 | tf_op jit(solution)/shard_map/ppermute | solution.py:337
  39.4 38.3 %collective-permute-start.8 = (bf16[2560,128]{1,0:T(8,128)(2,1)S(1)}, bf16[2560,128]{1,0:T(8,128)(2,1)S(1)}, u32[]{:S(2)}, u32[]{:S(2)}) collective-permute-start(bf16[2560,128]{1,0:T(8,128)(2,1)S(1)} %get-tuple-element.38), channel_id=1, source_target_pairs={{0,4},{1,5},{2,6},{3,7},{4,0},{5,1},{6,2},{7,3},{8,12},{9,13},{10,... | collective-permute-start | bytes 1966088 | tf_op jit(solution)/shard_map/ppermute | solution.py:334
  43.0 32.8 %copy-start.4 = (bf16[128,1024]{1,0:T(8,128)(2,1)S(1)}, bf16[128,1024]{1,0:T(8,128)(2,1)}, u32[]{:S(2)}) copy-start(bf16[128,1024]{1,0:T(8,128)(2,1)} %constant.22.clone.unpack) | copy-start | bytes 786436
  43.0 32.8 %copy-start.6 = (bf16[384,128]{1,0:T(8,128)(2,1)S(1)}, bf16[384,128]{1,0:T(8,128)(2,1)}, u32[]{:S(2)}) copy-start(bf16[384,128]{1,0:T(8,128)(2,1)} %constant.21.clone.backward) | copy-start | bytes 294916
  44.0 38.4 %copy-start.8 = (bf16[64,192]{1,0:T(8,128)(2,1)S(1)}, bf16[64,192]{1,0:T(8,128)(2,1)}, u32[]{:S(2)}) copy-start(bf16[64,192]{1,0:T(8,128)(2,1)} %constant.17.clone.backward) | copy-start | bytes 73732
  77.7 25.8 %all-to-all-start.1 = ((bf16[64,8,640]{2,1,0:T(8,128)(2,1)}), bf16[64,8,640]{2,1,0:T(8,128)(2,1)S(1)}, u32[]{:S(2)}, u32[]{:S(2)}) async-start(bf16[64,8,640]{2,1,0:T(8,128)(2,1)} %bitcast.11), calls=%async_computation.1 | async-start | bytes 1310720 | tf_op jit(solution)/shard_map/all_to_all | solution.py:450

commit v17 on v16

--- a/solution.py
+++ b/solution.py
@@ -14,7 +14,7 @@
 WIDE = 4
 ROW_GROUPS = 4
 OWN_COLS = 8
-NEAR = (0, 1, 3)
+NEAR = (0, 3, 1)
 FAR = 2
 
 

time: 106 us -> 105 us (level)
  the two profiles are of different devices: /device:TPU:6 before, /device:TPU:2 now
where the time goes in v17:
time: 105 us; the launch traced here: 104 us
  starting transfers between devices  33.4 us (32%)
  blocking collectives  30.3 us (29%)
  waiting for transfers between devices  18.9 us (18%)
  Pallas kernels  12.7 us (12%)
  matrix products  4.04 us (4%)
  local copies, waits for them, and re-layouts  2.68 us (3%)
  between operations  1.63 us (2%)
    all_to_all x1, blocking collectives, exchange(): lax.all_to_all(x.reshape(replicas, OWN_COLS, x.shape[1]), 'dp', 0, 0, til...  30.3 us
    ppermute x5, starting transfers between devices, along(): return lax.ppermute(x, 'tensor', [(i, i ^ 2 * step) for i in range(group)])  20.5 us
    all_to_all x1, waiting for transfers between devices, exchange(): lax.all_to_all(x.reshape(replicas, OWN_COLS, x.shape[1]), 'dp', 0, 0, til...  18.1 us
    pallas_call x9, Pallas kernels, call(): pl.pallas_call(kernel, out_shape=outs, in_specs=places or [VMEM] * len(ar...  12.7 us
    ppermute x4, starting transfers between devices, swap(): return lax.ppermute(x, 'tensor', [(i, i ^ 1) for i in range(group)])  8.3 us
    all_to_all x1, starting transfers between devices, exchange(): lax.all_to_all(x.reshape(replicas, OWN_COLS, x.shape[1]), 'dp', 0, 0, til...  4.64 us
    dot_general x5, matrix products, gram(): lax.dot_general(a, k, (((0,), (0,)), ((), ())), preferred_element_type=jn...  4.04 us
    unnamed x24, local copies, waits for them, and re-layouts  2.59 us
  transfers between devices with their start and end apart: 10, of which 2 were waited for; matrix products, arithmetic and copies ran while one was open for 4% of the time, Pallas kernels for 10%

profile of v17, /device:TPU:2, one launch (start us, length us, event | category | flops | bytes accessed | tf_op | source)
XLA Modules:
  0.0 103.9 jit_solution(16199656118217147165)
XLA Ops:
  0.6 0.9 far_keys.1
  1.6 4.0 %collective-permute-start.3 = (bf16[432,128]{1,0:T(8,128)(2,1)S(1)}, bf16[432,128]{1,0:T(8,128)(2,1)S(1)}, u32[]{:S(2)}, u32[]{:S(2)}) collective-permute-start(bf16[432,128]{1,0:T(8,128)(2,1)S(1)} %far_keys.1), channel_id=1, source_target_pairs={{0,4},{1,5},{2,6},{3,7},{4,0},{5,1},{6,2},{7,3},{8,12},{9,13},{10,... | collective-permute-start | bytes 331784 | tf_op jit(solution)/shard_map/ppermute | solution.py:334
  5.6 7.2 %collective-permute-start.1 = (bf16[208,2560]{1,0:T(8,128)(2,1)}, bf16[208,2560]{1,0:T(8,128)(2,1)S(1)}, u32[]{:S(2)}, u32[]{:S(2)}) collective-permute-start(bf16[208,2560]{1,0:T(8,128)(2,1)} %param.12), channel_id=1, source_target_pairs={{0,6},{1,7},{2,4},{3,5},{4,2},{5,3},{6,0},{7,1},{8,14},{9,15},{10,... | collective-permute-start | bytes 3194888 | tf_op jit(solution)/shard_map/ppermute | solution.py:334
  12.8 1.9 %collective-permute-start.2 = (bf16[208,2560]{1,0:T(8,128)(2,1)}, bf16[208,2560]{1,0:T(8,128)(2,1)S(1)}, u32[]{:S(2)}, u32[]{:S(2)}) collective-permute-start(bf16[208,2560]{1,0:T(8,128)(2,1)} %param.12), channel_id=1, source_target_pairs={{0,2},{1,3},{2,0},{3,1},{4,6},{5,7},{6,4},{7,5},{8,10},{9,11},{10,... | collective-permute-start | bytes 3194888 | tf_op jit(solution)/shard_map/ppermute | solution.py:334
  14.7 0.0 collective-permute-done.3.far
  14.7 1.9 %collective-permute-start.4 = (bf16[208,128]{1,0:T(8,128)(2,1)S(1)}, bf16[208,128]{1,0:T(8,128)(2,1)S(1)}, u32[]{:S(2)}, u32[]{:S(2)}) collective-permute-start(bf16[208,128]{1,0:T(8,128)(2,1)S(1)} %get-tuple-element.30), channel_id=1, source_target_pairs={{0,1},{1,0},{2,3},{3,2},{4,5},{5,4},{6,7},{7,6},{8,9},{9,8},{10,11... | collective-permute-start | bytes 159752 | tf_op jit(solution)/shard_map/ppermute | solution.py:337
  16.7 0.0 copy-start
  16.7 1.0 copy-done
  17.7 2.4 %collective-permute-start = (bf16[624,128]{1,0:T(8,128)(2,1)S(1)}, bf16[624,128]{1,0:T(8,128)(2,1)S(1)}, u32[]{:S(2)}, u32[]{:S(2)}) collective-permute-start(bf16[624,128]{1,0:T(8,128)(2,1)S(1)} %get-tuple-element.25), channel_id=1, source_target_pairs={{0,1},{1,0},{2,3},{3,2},{4,5},{5,4},{6,7},{7,6},{8,9},{9,8},{10,11... | collective-permute-start | bytes 479240 | tf_op jit(solution)/shard_map/ppermute | solution.py:337
  20.8 0.0 copy-start.2
  20.8 0.8 copy-done.2
  21.6 0.7 copy-done.9
  22.3 2.8 %routes.1 = (bf16[2560,128]{1,0:T(8,128)(2,1)S(1)}, bf16[1024,640]{1,0:T(8,128)(2,1)S(1)}, bf16[512,128]{1,0:T(8,128)(2,1)S(1)}) custom-call(s32[6,2,40]{2,1,0:T(2,128)S(1)} %bitcast.31, s32[1]{0:T(128)S(6)} %copy.14.count, f32[128,128]{1,0:T(8,128)S(1)} %copy-done.2), custom_call_target="tpu_custom_call" | custom-call | tf_op jit(solution)/shard_map/routes/pallas_call | solution.py:317
  25.1 0.0 collective-permute-done.4
  25.1 1.8 %convolution_convert_fusion = bf16[2560,128]{1,0:T(8,128)(2,1)S(1)} fusion(bf16[208,2560]{1,0:T(8,128)(2,1)} %param.12, bf16[208,128]{1,0:T(8,128)(2,1)S(1)} %collective-permute-done.4), kind=kOutput, calls=%fused_computation.2 | convolution fusion | flops 136642560 | bytes 1773568 | tf_op jit(solution)/shard_map/dot_general | solution.py:308
  26.9 1.9 %collective-permute-start.5 = (bf16[2560,128]{1,0:T(8,128)(2,1)S(1)}, bf16[2560,128]{1,0:T(8,128)(2,1)S(1)}, u32[]{:S(2)}, u32[]{:S(2)}) collective-permute-start(bf16[2560,128]{1,0:T(8,128)(2,1)S(1)} %convolution_convert_fusion), channel_id=1, source_target_pairs={{0,1},{1,0},{2,3},{3,2},{4,5},{5,4},{6,7},{7,6},{8,9},{9,8},{10,11... | collective-permute-start | bytes 1966088 | tf_op jit(solution)/shard_map/ppermute | solution.py:337
  28.9 0.6 fusion.1.part
  29.4 0.0 collective-permute-done
  29.5 0.0 copy-start.1
  29.5 0.0 copy-start.3
  29.5 0.0 copy-start.5
  29.5 0.0 copy-start.7
  29.5 0.6 fusion
  30.1 0.8 collective-permute-done.5.other
  30.9 1.8 %far.1 = (bf16[2560,128]{1,0:T(8,128)(2,1)S(1)}, bf16[512,128]{1,0:T(8,128)(2,1)S(1)}) custom-call(bf16[16,128]{1,0:T(8,128)(2,1)S(1)} %slice.30.numbers, s32[1]{0:T(128)S(6)} %copy.14.count, bf16[512,128]{1,0:T(8,128)(2,1)S(1)} %copy-done.5, f32[128,128]{1,0:T(8,128)S(1)} %copy-done.7, f32[128,128]{1,0:T(8,128)S(1)} %copy-done.3, ...), custom_call_target="tpu_custom_call" | custom-call | tf_op jit(solution)/shard_map/far/pallas_call | solution.py:317
  32.8 3.4 %collective-permute-start.7 = (bf16[512,128]{1,0:T(8,128)(2,1)S(1)}, bf16[512,128]{1,0:T(8,128)(2,1)S(1)}, u32[]{:S(2)}, u32[]{:S(2)}) collective-permute-start(bf16[512,128]{1,0:T(8,128)(2,1)S(1)} %get-tuple-element.33), channel_id=1, source_target_pairs={{0,4},{1,5},{2,6},{3,7},{4,0},{5,1},{6,2},{7,3},{8,12},{9,13},{10,... | collective-permute-start | bytes 393224 | tf_op jit(solution)/shard_map/ppermute | solution.py:334
  36.1 0.0 collective-permute-done.1
  36.2 0.0 collective-permute-done.2
  36.2 0.6 convolution_add_fusion.1
  36.7 0.6 convolution_add_fusion
  37.3 0.0 copy-start.11
  37.3 0.1 slice.39
  37.4 2.1 %collective-permute-start.6 = (bf16[2560,128]{1,0:T(8,128)(2,1)S(1)}, bf16[2560,128]{1,0:T(8,128)(2,1)S(1)}, u32[]{:S(2)}, u32[]{:S(2)}) collective-permute-start(bf16[2560,128]{1,0:T(8,128)(2,1)S(1)} %slice.39), channel_id=1, source_target_pairs={{0,1},{1,0},{2,3},{3,2},{4,5},{5,4},{6,7},{7,6},{8,9},{9,8},{10,11... | collective-permute-start | bytes 1966088 | tf_op jit(solution)/shard_map/ppermute | solution.py:337
  39.5 4.0 %collective-permute-start.8 = (bf16[2560,128]{1,0:T(8,128)(2,1)S(1)}, bf16[2560,128]{1,0:T(8,128)(2,1)S(1)}, u32[]{:S(2)}, u32[]{:S(2)}) collective-permute-start(bf16[2560,128]{1,0:T(8,128)(2,1)S(1)} %get-tuple-element.38), channel_id=1, source_target_pairs={{0,4},{1,5},{2,6},{3,7},{4,0},{5,1},{6,2},{7,3},{8,12},{9,13},{10,... | collective-permute-start | bytes 1966088 | tf_op jit(solution)/shard_map/ppermute | solution.py:334
  43.5 0.2 slice_add_fusion.part
  43.6 0.0 collective-permute-done.7.far
  43.6 0.0 collective-permute-done.6.other
  43.7 0.0 copy-start.4
  43.7 0.0 copy-start.6
  43.7 1.0 spectrum.1
  44.7 0.0 copy-start.8
  44.7 30.3 %all_to_all.10 = bf16[64,8,128]{2,1,0:T(8,128)(2,1)S(1)} all-to-all(bf16[64,8,128]{2,1,0:T(8,128)(2,1)S(1)} %bitcast.29), channel_id=1, replica_groups=mesh['dp'=64,'tensor'=8] {'dp'}, dimensions={0} | all-to-all | bytes 262144 | tf_op jit(solution)/shard_map/all_to_all | solution.py:450
  75.0 1.9 %total.1 = bf16[512,640]{1,0:T(8,128)(2,1)} custom-call(bf16[512,128]{1,0:T(8,128)(2,1)S(1)} %bitcast.28, bf16[128,1024]{1,0:T(8,128)(2,1)S(1)} %copy-done.4, bf16[384,128]{1,0:T(8,128)(2,1)S(1)} %copy-done.6), custom_call_target="tpu_custom_call" | custom-call | tf_op jit(solution)/shard_map/total/pallas_call | solution.py:317
  77.0 0.0 collective-permute-done.8.far
  77.0 4.6 %all-to-all-start.1 = ((bf16[64,8,640]{2,1,0:T(8,128)(2,1)}), bf16[64,8,640]{2,1,0:T(8,128)(2,1)S(1)}, u32[]{:S(2)}, u32[]{:S(2)}) async-start(bf16[64,8,640]{2,1,0:T(8,128)(2,1)} %bitcast.11), calls=%async_computation.1 | async-start | bytes 1310720 | tf_op jit(solution)/shard_map/all_to_all | solution.py:450
  81.6 3.1 %kept.1 = f32[2560,128]{1,0:T(8,128)} custom-call(f32[2560,128]{1,0:T(8,128)S(1)} %get-tuple-element.36.advanced, bf16[2560,128]{1,0:T(8,128)(2,1)S(1)} %collective-permute-done.8.far, bf16[2560,128]{1,0:T(8,128)(2,1)S(1)} %get-tuple-element.40.mask, bf16[64,192]{1,0:T(8,128)(2,1)S(1)} %copy-done.1, bf16[64,192]{1,0:T(8,128)(2,1)S(1)} %copy-done.8), custom_call_target="tpu_custom_call" | custom-call | tf_op jit(solution)/shard_map/kept/pallas_call | solution.py:317
  84.7 18.1 %all-to-all-done.1 = bf16[64,8,640]{2,1,0:T(8,128)(2,1)S(1)} async-done(((bf16[64,8,640]{2,1,0:T(8,128)(2,1)}), bf16[64,8,640]{2,1,0:T(8,128)(2,1)S(1)}, u32[]{:S(2)}, u32[]{:S(2)}) %all-to-all-start.1) | async-done | bytes 655392 | tf_op jit(solution)/shard_map/all_to_all | solution.py:450
  102.8 1.1 %turn.1 = bf16[2560,128]{1,0:T(8,128)(2,1)} custom-call(bf16[512,640]{1,0:T(8,128)(2,1)S(1)} %bitcast.27), custom_call_target="tpu_custom_call" | custom-call | tf_op jit(solution)/shard_map/turn/pallas_call | solution.py:317
  (15 shorter events, 0.1 us)
Async XLA Ops:
  1.6 13.1 %collective-permute-start.3 = (bf16[432,128]{1,0:T(8,128)(2,1)S(1)}, bf16[432,128]{1,0:T(8,128)(2,1)S(1)}, u32[]{:S(2)}, u32[]{:S(2)}) collective-permute-start(bf16[432,128]{1,0:T(8,128)(2,1)S(1)} %far_keys.1), channel_id=1, source_target_pairs={{0,4},{1,5},{2,6},{3,7},{4,0},{5,1},{6,2},{7,3},{8,12},{9,13},{10,... | collective-permute-start | bytes 331784 | tf_op jit(solution)/shard_map/ppermute | solution.py:334
  5.6 30.5 %collective-permute-start.1 = (bf16[208,2560]{1,0:T(8,128)(2,1)}, bf16[208,2560]{1,0:T(8,128)(2,1)S(1)}, u32[]{:S(2)}, u32[]{:S(2)}) collective-permute-start(bf16[208,2560]{1,0:T(8,128)(2,1)} %param.12), channel_id=1, source_target_pairs={{0,6},{1,7},{2,4},{3,5},{4,2},{5,3},{6,0},{7,1},{8,14},{9,15},{10,... | collective-permute-start | bytes 3194888 | tf_op jit(solution)/shard_map/ppermute | solution.py:334
  12.8 23.4 %collective-permute-start.2 = (bf16[208,2560]{1,0:T(8,128)(2,1)}, bf16[208,2560]{1,0:T(8,128)(2,1)S(1)}, u32[]{:S(2)}, u32[]{:S(2)}) collective-permute-start(bf16[208,2560]{1,0:T(8,128)(2,1)} %param.12), channel_id=1, source_target_pairs={{0,2},{1,3},{2,0},{3,1},{4,6},{5,7},{6,4},{7,5},{8,10},{9,11},{10,... | collective-permute-start | bytes 3194888 | tf_op jit(solution)/shard_map/ppermute | solution.py:334
  14.7 10.4 %collective-permute-start.4 = (bf16[208,128]{1,0:T(8,128)(2,1)S(1)}, bf16[208,128]{1,0:T(8,128)(2,1)S(1)}, u32[]{:S(2)}, u32[]{:S(2)}) collective-permute-start(bf16[208,128]{1,0:T(8,128)(2,1)S(1)} %get-tuple-element.30), channel_id=1, source_target_pairs={{0,1},{1,0},{2,3},{3,2},{4,5},{5,4},{6,7},{7,6},{8,9},{9,8},{10,11... | collective-permute-start | bytes 159752 | tf_op jit(solution)/shard_map/ppermute | solution.py:337
  16.7 1.0 copy-start
  17.7 11.7 %collective-permute-start = (bf16[624,128]{1,0:T(8,128)(2,1)S(1)}, bf16[624,128]{1,0:T(8,128)(2,1)S(1)}, u32[]{:S(2)}, u32[]{:S(2)}) collective-permute-start(bf16[624,128]{1,0:T(8,128)(2,1)S(1)} %get-tuple-element.25), channel_id=1, source_target_pairs={{0,1},{1,0},{2,3},{3,2},{4,5},{5,4},{6,7},{7,6},{8,9},{9,8},{10,11... | collective-permute-start | bytes 479240 | tf_op jit(solution)/shard_map/ppermute | solution.py:337
  20.8 0.8 copy-start.2
  21.6 0.7 copy-start.9
  22.3 6.6 %copy-start.10 = (bf16[208,2560]{1,0:T(8,128)(2,1)S(1)}, bf16[208,2560]{1,0:T(8,128)(2,1)}, u32[]{:S(2)}) copy-start(bf16[208,2560]{1,0:T(8,128)(2,1)} %param.12) | copy-start | bytes 3194884
  26.9 4.0 %collective-permute-start.5 = (bf16[2560,128]{1,0:T(8,128)(2,1)S(1)}, bf16[2560,128]{1,0:T(8,128)(2,1)S(1)}, u32[]{:S(2)}, u32[]{:S(2)}) collective-permute-start(bf16[2560,128]{1,0:T(8,128)(2,1)S(1)} %convolution_convert_fusion), channel_id=1, source_target_pairs={{0,1},{1,0},{2,3},{3,2},{4,5},{5,4},{6,7},{7,6},{8,9},{9,8},{10,11... | collective-permute-start | bytes 1966088 | tf_op jit(solution)/shard_map/ppermute | solution.py:337
  29.5 1.4 %copy-start.1 = (bf16[64,192]{1,0:T(8,128)(2,1)S(1)}, bf16[64,192]{1,0:T(8,128)(2,1)}, u32[]{:S(2)}) copy-start(bf16[64,192]{1,0:T(8,128)(2,1)} %constant.16.clone.forward) | copy-start | bytes 73732
  29.5 1.4 %copy-start.3 = (f32[128,128]{1,0:T(8,128)S(1)}, f32[128,128]{1,0:T(8,128)}, u32[]{:S(2)}) copy-start(f32[128,128]{1,0:T(8,128)} %constant.18.clone.base) | copy-start | bytes 196612
  29.5 1.4 %copy-start.5 = (bf16[512,128]{1,0:T(8,128)(2,1)S(1)}, bf16[512,128]{1,0:T(8,128)(2,1)}, u32[]{:S(2)}) copy-start(bf16[512,128]{1,0:T(8,128)(2,1)} %constant.19.clone.spans) | copy-start | bytes 393220
  29.5 1.4 %copy-start.7 = (f32[128,128]{1,0:T(8,128)S(1)}, f32[128,128]{1,0:T(8,128)}, u32[]{:S(2)}) copy-start(f32[128,128]{1,0:T(8,128)} %constant.20.clone.slots) | copy-start | bytes 196612
  32.8 10.9 %collective-permute-start.7 = (bf16[512,128]{1,0:T(8,128)(2,1)S(1)}, bf16[512,128]{1,0:T(8,128)(2,1)S(1)}, u32[]{:S(2)}, u32[]{:S(2)}) collective-permute-start(bf16[512,128]{1,0:T(8,128)(2,1)S(1)} %get-tuple-element.33), channel_id=1, source_target_pairs={{0,4},{1,5},{2,6},{3,7},{4,0},{5,1},{6,2},{7,3},{8,12},{9,13},{10,... | collective-permute-start | bytes 393224 | tf_op jit(solution)/shard_map/ppermute | solution.py:334
  37.3 6.2 %copy-start.11 = (f32[1,2560,128]{2,1,0:T(8,128)S(1)}, f32[1,2560,128]{2,1,0:T(8,128)}, u32[]{:S(2)}) copy-start(f32[1,2560,128]{2,1,0:T(8,128)} %param.14) | copy-start | bytes 3932164
  37.4 6.2 %collective-permute-start.6 = (bf16[2560,128]{1,0:T(8,128)(2,1)S(1)}, bf16[2560,128]{1,0:T(8,128)(2,1)S(1)}, u32[]{:S(2)}, u32[]{:S(2)}) collective-permute-start(bf16[2560,128]{1,0:T(8,128)(2,1)S(1)} %slice.39), channel_id=1, source_target_pairs={{0,1},{1,0},{2,3},{3,2},{4,5},{5,4},{6,7},{7,6},{8,9},{9,8},{10,11... | collective-permute-start | bytes 1966088 | tf_op jit(solution)/shard_map/ppermute | solution.py:337
  39.5 37.5 %collective-permute-start.8 = (bf16[2560,128]{1,0:T(8,128)(2,1)S(1)}, bf16[2560,128]{1,0:T(8,128)(2,1)S(1)}, u32[]{:S(2)}, u32[]{:S(2)}) collective-permute-start(bf16[2560,128]{1,0:T(8,128)(2,1)S(1)} %get-tuple-element.38), channel_id=1, source_target_pairs={{0,4},{1,5},{2,6},{3,7},{4,0},{5,1},{6,2},{7,3},{8,12},{9,13},{10,... | collective-permute-start | bytes 1966088 | tf_op jit(solution)/shard_map/ppermute | solution.py:334
  43.7 31.4 %copy-start.4 = (bf16[128,1024]{1,0:T(8,128)(2,1)S(1)}, bf16[128,1024]{1,0:T(8,128)(2,1)}, u32[]{:S(2)}) copy-start(bf16[128,1024]{1,0:T(8,128)(2,1)} %constant.22.clone.unpack) | copy-start | bytes 786436
  43.7 31.4 %copy-start.6 = (bf16[384,128]{1,0:T(8,128)(2,1)S(1)}, bf16[384,128]{1,0:T(8,128)(2,1)}, u32[]{:S(2)}) copy-start(bf16[384,128]{1,0:T(8,128)(2,1)} %constant.21.clone.backward) | copy-start | bytes 294916
  44.7 36.9 %copy-start.8 = (bf16[64,192]{1,0:T(8,128)(2,1)S(1)}, bf16[64,192]{1,0:T(8,128)(2,1)}, u32[]{:S(2)}) copy-start(bf16[64,192]{1,0:T(8,128)(2,1)} %constant.17.clone.backward) | copy-start | bytes 73732
  77.0 25.8 %all-to-all-start.1 = ((bf16[64,8,640]{2,1,0:T(8,128)(2,1)}), bf16[64,8,640]{2,1,0:T(8,128)(2,1)S(1)}, u32[]{:S(2)}, u32[]{:S(2)}) async-start(bf16[64,8,640]{2,1,0:T(8,128)(2,1)} %bitcast.11), calls=%async_computation.1 | async-start | bytes 1310720 | tf_op jit(solution)/shard_map/all_to_all | solution.py:450

commit v18 on v17

--- a/solution.py
+++ b/solution.py
@@ -255,16 +255,17 @@
     wide = pieces.shape[1]
     spans = totals.shape[1] // SPAN
     lane = lax.broadcasted_iota(jnp.int32, (BLK, wide), 0).astype(jnp.float32)
+    lane = lane.astype(placed.dtype)
     for t in range(pieces.shape[0] // wide):
-        values = pieces[t * wide : (t + 1) * wide, :].astype(jnp.float32).T
+        values = pieces[t * wide : (t + 1) * wide, :].astype(jnp.float32).T.astype(placed.dtype)
         numbers = jnp.dot(
-            values[wide - OWN_COLS :, :].astype(jnp.bfloat16),
+            values[wide - OWN_COLS :, :],
             unpack[...],
             preferred_element_type=jnp.float32,
-        )
+        ).astype(placed.dtype)
         most = wide // (2 * spans)
         for a in range(spans):
-            upper = jnp.zeros((BLK, wide), jnp.float32)
+            upper = jnp.zeros((BLK, wide), placed.dtype)
             lower = upper
             for k in range(most):
                 at = a * most + k
@@ -272,8 +273,9 @@
                 here = numbers[down : down + 1, across : across + wide] == lane
                 upper = jnp.where(here, values[2 * at : 2 * at + 1, :], upper)
                 lower = jnp.where(here, values[2 * at + 1 : 2 * at + 2, :], lower)
-            both = jnp.concatenate([upper, lower], axis=0)
-            placed[a * SPAN : (a + 1) * SPAN, t * wide : (t + 1) * wide] = both.astype(placed.dtype)
+            across = slice(t * wide, (t + 1) * wide)
+            placed[a * SPAN : a * SPAN + BLK, across] = upper
+            placed[a * SPAN + BLK : (a + 1) * SPAN, across] = lower
     shape = (2 * OWN_COLS, placed.shape[1])
     column = lax.broadcasted_iota(jnp.int32, shape, 1) & (OWN_COLS - 1)
     row = lax.broadcasted_iota(jnp.int32, shape, 0) & (OWN_COLS - 1)

time: 105 us -> 105 us (level)
  no operation moved by 1% of the time
where the time goes in v18:
time: 105 us; the launch traced here: 104 us
  starting transfers between devices  33.4 us (32%)
  blocking collectives  30.3 us (29%)
  waiting for transfers between devices  18.9 us (18%)
  Pallas kernels  12.6 us (12%)
  matrix products  4.04 us (4%)
  local copies, waits for them, and re-layouts  2.68 us (3%)
  between operations  1.63 us (2%)
    all_to_all x1, blocking collectives, exchange(): lax.all_to_all(x.reshape(replicas, OWN_COLS, x.shape[1]), 'dp', 0, 0, til...  30.3 us
    ppermute x5, starting transfers between devices, along(): return lax.ppermute(x, 'tensor', [(i, i ^ 2 * step) for i in range(group)])  20.5 us
    all_to_all x1, waiting for transfers between devices, exchange(): lax.all_to_all(x.reshape(replicas, OWN_COLS, x.shape[1]), 'dp', 0, 0, til...  18.1 us
    pallas_call x9, Pallas kernels, call(): pl.pallas_call(kernel, out_shape=outs, in_specs=places or [VMEM] * len(ar...  12.6 us
    ppermute x4, starting transfers between devices, swap(): return lax.ppermute(x, 'tensor', [(i, i ^ 1) for i in range(group)])  8.3 us
    all_to_all x1, starting transfers between devices, exchange(): lax.all_to_all(x.reshape(replicas, OWN_COLS, x.shape[1]), 'dp', 0, 0, til...  4.64 us
    dot_general x5, matrix products, gram(): lax.dot_general(a, k, (((0,), (0,)), ((), ())), preferred_element_type=jn...  4.04 us
    unnamed x24, local copies, waits for them, and re-layouts  2.59 us
  transfers between devices with their start and end apart: 10, of which 2 were waited for; matrix products, arithmetic and copies ran while one was open for 4% of the time, Pallas kernels for 10%

profile of v18, /device:TPU:2, one launch (start us, length us, event | category | flops | bytes accessed | tf_op | source)
XLA Modules:
  0.0 103.8 jit_solution(3000195935535455979)
XLA Ops:
  0.6 0.9 far_keys.1
  1.6 4.0 %collective-permute-start.3 = (bf16[432,128]{1,0:T(8,128)(2,1)S(1)}, bf16[432,128]{1,0:T(8,128)(2,1)S(1)}, u32[]{:S(2)}, u32[]{:S(2)}) collective-permute-start(bf16[432,128]{1,0:T(8,128)(2,1)S(1)} %far_keys.1), channel_id=1, source_target_pairs={{0,4},{1,5},{2,6},{3,7},{4,0},{5,1},{6,2},{7,3},{8,12},{9,13},{10,... | collective-permute-start | bytes 331784 | tf_op jit(solution)/shard_map/ppermute | solution.py:336
  5.6 7.2 %collective-permute-start.1 = (bf16[208,2560]{1,0:T(8,128)(2,1)}, bf16[208,2560]{1,0:T(8,128)(2,1)S(1)}, u32[]{:S(2)}, u32[]{:S(2)}) collective-permute-start(bf16[208,2560]{1,0:T(8,128)(2,1)} %param.12), channel_id=1, source_target_pairs={{0,6},{1,7},{2,4},{3,5},{4,2},{5,3},{6,0},{7,1},{8,14},{9,15},{10,... | collective-permute-start | bytes 3194888 | tf_op jit(solution)/shard_map/ppermute | solution.py:336
  12.8 1.9 %collective-permute-start.2 = (bf16[208,2560]{1,0:T(8,128)(2,1)}, bf16[208,2560]{1,0:T(8,128)(2,1)S(1)}, u32[]{:S(2)}, u32[]{:S(2)}) collective-permute-start(bf16[208,2560]{1,0:T(8,128)(2,1)} %param.12), channel_id=1, source_target_pairs={{0,2},{1,3},{2,0},{3,1},{4,6},{5,7},{6,4},{7,5},{8,10},{9,11},{10,... | collective-permute-start | bytes 3194888 | tf_op jit(solution)/shard_map/ppermute | solution.py:336
  14.7 0.0 collective-permute-done.3.far
  14.7 1.9 %collective-permute-start.4 = (bf16[208,128]{1,0:T(8,128)(2,1)S(1)}, bf16[208,128]{1,0:T(8,128)(2,1)S(1)}, u32[]{:S(2)}, u32[]{:S(2)}) collective-permute-start(bf16[208,128]{1,0:T(8,128)(2,1)S(1)} %get-tuple-element.30), channel_id=1, source_target_pairs={{0,1},{1,0},{2,3},{3,2},{4,5},{5,4},{6,7},{7,6},{8,9},{9,8},{10,11... | collective-permute-start | bytes 159752 | tf_op jit(solution)/shard_map/ppermute | solution.py:339
  16.7 0.0 copy-start
  16.7 1.0 copy-done
  17.7 2.4 %collective-permute-start = (bf16[624,128]{1,0:T(8,128)(2,1)S(1)}, bf16[624,128]{1,0:T(8,128)(2,1)S(1)}, u32[]{:S(2)}, u32[]{:S(2)}) collective-permute-start(bf16[624,128]{1,0:T(8,128)(2,1)S(1)} %get-tuple-element.25), channel_id=1, source_target_pairs={{0,1},{1,0},{2,3},{3,2},{4,5},{5,4},{6,7},{7,6},{8,9},{9,8},{10,11... | collective-permute-start | bytes 479240 | tf_op jit(solution)/shard_map/ppermute | solution.py:339
  20.8 0.0 copy-start.2
  20.8 0.8 copy-done.2
  21.6 0.7 copy-done.9
  22.3 2.8 %routes.1 = (bf16[2560,128]{1,0:T(8,128)(2,1)S(1)}, bf16[1024,640]{1,0:T(8,128)(2,1)S(1)}, bf16[512,128]{1,0:T(8,128)(2,1)S(1)}) custom-call(s32[6,2,40]{2,1,0:T(2,128)S(1)} %bitcast.31, s32[1]{0:T(128)S(6)} %copy.14.count, f32[128,128]{1,0:T(8,128)S(1)} %copy-done.2), custom_call_target="tpu_custom_call" | custom-call | tf_op jit(solution)/shard_map/routes/pallas_call | solution.py:319
  25.1 0.0 collective-permute-done.4
  25.1 1.8 %convolution_convert_fusion = bf16[2560,128]{1,0:T(8,128)(2,1)S(1)} fusion(bf16[208,2560]{1,0:T(8,128)(2,1)} %param.12, bf16[208,128]{1,0:T(8,128)(2,1)S(1)} %collective-permute-done.4), kind=kOutput, calls=%fused_computation.2 | convolution fusion | flops 136642560 | bytes 1773568 | tf_op jit(solution)/shard_map/dot_general | solution.py:310
  26.9 1.9 %collective-permute-start.5 = (bf16[2560,128]{1,0:T(8,128)(2,1)S(1)}, bf16[2560,128]{1,0:T(8,128)(2,1)S(1)}, u32[]{:S(2)}, u32[]{:S(2)}) collective-permute-start(bf16[2560,128]{1,0:T(8,128)(2,1)S(1)} %convolution_convert_fusion), channel_id=1, source_target_pairs={{0,1},{1,0},{2,3},{3,2},{4,5},{5,4},{6,7},{7,6},{8,9},{9,8},{10,11... | collective-permute-start | bytes 1966088 | tf_op jit(solution)/shard_map/ppermute | solution.py:339
  28.9 0.6 fusion.1.part
  29.4 0.0 collective-permute-done
  29.5 0.0 copy-start.1
  29.5 0.0 copy-start.3
  29.5 0.0 copy-start.5
  29.5 0.0 copy-start.7
  29.5 0.6 fusion
  30.1 0.8 collective-permute-done.5.other
  30.9 1.8 %far.1 = (bf16[2560,128]{1,0:T(8,128)(2,1)S(1)}, bf16[512,128]{1,0:T(8,128)(2,1)S(1)}) custom-call(bf16[16,128]{1,0:T(8,128)(2,1)S(1)} %slice.30.numbers, s32[1]{0:T(128)S(6)} %copy.14.count, bf16[512,128]{1,0:T(8,128)(2,1)S(1)} %copy-done.5, f32[128,128]{1,0:T(8,128)S(1)} %copy-done.7, f32[128,128]{1,0:T(8,128)S(1)} %copy-done.3, ...), custom_call_target="tpu_custom_call" | custom-call | tf_op jit(solution)/shard_map/far/pallas_call | solution.py:319
  32.8 3.4 %collective-permute-start.7 = (bf16[512,128]{1,0:T(8,128)(2,1)S(1)}, bf16[512,128]{1,0:T(8,128)(2,1)S(1)}, u32[]{:S(2)}, u32[]{:S(2)}) collective-permute-start(bf16[512,128]{1,0:T(8,128)(2,1)S(1)} %get-tuple-element.33), channel_id=1, source_target_pairs={{0,4},{1,5},{2,6},{3,7},{4,0},{5,1},{6,2},{7,3},{8,12},{9,13},{10,... | collective-permute-start | bytes 393224 | tf_op jit(solution)/shard_map/ppermute | solution.py:336
  36.1 0.0 collective-permute-done.1
  36.2 0.0 collective-permute-done.2
  36.2 0.6 convolution_add_fusion.1
  36.7 0.6 convolution_add_fusion
  37.3 0.0 copy-start.11
  37.3 0.1 slice.39
  37.4 2.1 %collective-permute-start.6 = (bf16[2560,128]{1,0:T(8,128)(2,1)S(1)}, bf16[2560,128]{1,0:T(8,128)(2,1)S(1)}, u32[]{:S(2)}, u32[]{:S(2)}) collective-permute-start(bf16[2560,128]{1,0:T(8,128)(2,1)S(1)} %slice.39), channel_id=1, source_target_pairs={{0,1},{1,0},{2,3},{3,2},{4,5},{5,4},{6,7},{7,6},{8,9},{9,8},{10,11... | collective-permute-start | bytes 1966088 | tf_op jit(solution)/shard_map/ppermute | solution.py:339
  39.5 4.0 %collective-permute-start.8 = (bf16[2560,128]{1,0:T(8,128)(2,1)S(1)}, bf16[2560,128]{1,0:T(8,128)(2,1)S(1)}, u32[]{:S(2)}, u32[]{:S(2)}) collective-permute-start(bf16[2560,128]{1,0:T(8,128)(2,1)S(1)} %get-tuple-element.38), channel_id=1, source_target_pairs={{0,4},{1,5},{2,6},{3,7},{4,0},{5,1},{6,2},{7,3},{8,12},{9,13},{10,... | collective-permute-start | bytes 1966088 | tf_op jit(solution)/shard_map/ppermute | solution.py:336
  43.5 0.2 slice_add_fusion.part
  43.6 0.0 collective-permute-done.7.far
  43.6 0.0 collective-permute-done.6.other
  43.7 0.0 copy-start.4
  43.7 0.0 copy-start.6
  43.7 1.0 spectrum.1
  44.7 0.0 copy-start.8
  44.7 30.3 %all_to_all.10 = bf16[64,8,128]{2,1,0:T(8,128)(2,1)S(1)} all-to-all(bf16[64,8,128]{2,1,0:T(8,128)(2,1)S(1)} %bitcast.29), channel_id=1, replica_groups=mesh['dp'=64,'tensor'=8] {'dp'}, dimensions={0} | all-to-all | bytes 262144 | tf_op jit(solution)/shard_map/all_to_all | solution.py:452
  75.0 1.9 %total.1 = bf16[512,640]{1,0:T(8,128)(2,1)} custom-call(bf16[512,128]{1,0:T(8,128)(2,1)S(1)} %bitcast.28, bf16[128,1024]{1,0:T(8,128)(2,1)S(1)} %copy-done.4, bf16[384,128]{1,0:T(8,128)(2,1)S(1)} %copy-done.6), custom_call_target="tpu_custom_call" | custom-call | tf_op jit(solution)/shard_map/total/pallas_call | solution.py:319
  76.9 0.0 collective-permute-done.8.far
  76.9 4.6 %all-to-all-start.1 = ((bf16[64,8,640]{2,1,0:T(8,128)(2,1)}), bf16[64,8,640]{2,1,0:T(8,128)(2,1)S(1)}, u32[]{:S(2)}, u32[]{:S(2)}) async-start(bf16[64,8,640]{2,1,0:T(8,128)(2,1)} %bitcast.11), calls=%async_computation.1 | async-start | bytes 1310720 | tf_op jit(solution)/shard_map/all_to_all | solution.py:452
  81.6 3.1 %kept.1 = f32[2560,128]{1,0:T(8,128)} custom-call(f32[2560,128]{1,0:T(8,128)S(1)} %get-tuple-element.36.advanced, bf16[2560,128]{1,0:T(8,128)(2,1)S(1)} %collective-permute-done.8.far, bf16[2560,128]{1,0:T(8,128)(2,1)S(1)} %get-tuple-element.40.mask, bf16[64,192]{1,0:T(8,128)(2,1)S(1)} %copy-done.1, bf16[64,192]{1,0:T(8,128)(2,1)S(1)} %copy-done.8), custom_call_target="tpu_custom_call" | custom-call | tf_op jit(solution)/shard_map/kept/pallas_call | solution.py:319
  84.6 18.1 %all-to-all-done.1 = bf16[64,8,640]{2,1,0:T(8,128)(2,1)S(1)} async-done(((bf16[64,8,640]{2,1,0:T(8,128)(2,1)}), bf16[64,8,640]{2,1,0:T(8,128)(2,1)S(1)}, u32[]{:S(2)}, u32[]{:S(2)}) %all-to-all-start.1) | async-done | bytes 655392 | tf_op jit(solution)/shard_map/all_to_all | solution.py:452
  102.7 1.1 %turn.1 = bf16[2560,128]{1,0:T(8,128)(2,1)} custom-call(bf16[512,640]{1,0:T(8,128)(2,1)S(1)} %bitcast.27), custom_call_target="tpu_custom_call" | custom-call | tf_op jit(solution)/shard_map/turn/pallas_call | solution.py:319
  (15 shorter events, 0.1 us)
Async XLA Ops:
  1.6 13.1 %collective-permute-start.3 = (bf16[432,128]{1,0:T(8,128)(2,1)S(1)}, bf16[432,128]{1,0:T(8,128)(2,1)S(1)}, u32[]{:S(2)}, u32[]{:S(2)}) collective-permute-start(bf16[432,128]{1,0:T(8,128)(2,1)S(1)} %far_keys.1), channel_id=1, source_target_pairs={{0,4},{1,5},{2,6},{3,7},{4,0},{5,1},{6,2},{7,3},{8,12},{9,13},{10,... | collective-permute-start | bytes 331784 | tf_op jit(solution)/shard_map/ppermute | solution.py:336
  5.6 30.5 %collective-permute-start.1 = (bf16[208,2560]{1,0:T(8,128)(2,1)}, bf16[208,2560]{1,0:T(8,128)(2,1)S(1)}, u32[]{:S(2)}, u32[]{:S(2)}) collective-permute-start(bf16[208,2560]{1,0:T(8,128)(2,1)} %param.12), channel_id=1, source_target_pairs={{0,6},{1,7},{2,4},{3,5},{4,2},{5,3},{6,0},{7,1},{8,14},{9,15},{10,... | collective-permute-start | bytes 3194888 | tf_op jit(solution)/shard_map/ppermute | solution.py:336
  12.8 23.4 %collective-permute-start.2 = (bf16[208,2560]{1,0:T(8,128)(2,1)}, bf16[208,2560]{1,0:T(8,128)(2,1)S(1)}, u32[]{:S(2)}, u32[]{:S(2)}) collective-permute-start(bf16[208,2560]{1,0:T(8,128)(2,1)} %param.12), channel_id=1, source_target_pairs={{0,2},{1,3},{2,0},{3,1},{4,6},{5,7},{6,4},{7,5},{8,10},{9,11},{10,... | collective-permute-start | bytes 3194888 | tf_op jit(solution)/shard_map/ppermute | solution.py:336
  14.7 10.4 %collective-permute-start.4 = (bf16[208,128]{1,0:T(8,128)(2,1)S(1)}, bf16[208,128]{1,0:T(8,128)(2,1)S(1)}, u32[]{:S(2)}, u32[]{:S(2)}) collective-permute-start(bf16[208,128]{1,0:T(8,128)(2,1)S(1)} %get-tuple-element.30), channel_id=1, source_target_pairs={{0,1},{1,0},{2,3},{3,2},{4,5},{5,4},{6,7},{7,6},{8,9},{9,8},{10,11... | collective-permute-start | bytes 159752 | tf_op jit(solution)/shard_map/ppermute | solution.py:339
  16.7 1.0 copy-start
  17.7 11.7 %collective-permute-start = (bf16[624,128]{1,0:T(8,128)(2,1)S(1)}, bf16[624,128]{1,0:T(8,128)(2,1)S(1)}, u32[]{:S(2)}, u32[]{:S(2)}) collective-permute-start(bf16[624,128]{1,0:T(8,128)(2,1)S(1)} %get-tuple-element.25), channel_id=1, source_target_pairs={{0,1},{1,0},{2,3},{3,2},{4,5},{5,4},{6,7},{7,6},{8,9},{9,8},{10,11... | collective-permute-start | bytes 479240 | tf_op jit(solution)/shard_map/ppermute | solution.py:339
  20.8 0.8 copy-start.2
  21.6 0.7 copy-start.9
  22.3 6.6 %copy-start.10 = (bf16[208,2560]{1,0:T(8,128)(2,1)S(1)}, bf16[208,2560]{1,0:T(8,128)(2,1)}, u32[]{:S(2)}) copy-start(bf16[208,2560]{1,0:T(8,128)(2,1)} %param.12) | copy-start | bytes 3194884
  26.9 4.0 %collective-permute-start.5 = (bf16[2560,128]{1,0:T(8,128)(2,1)S(1)}, bf16[2560,128]{1,0:T(8,128)(2,1)S(1)}, u32[]{:S(2)}, u32[]{:S(2)}) collective-permute-start(bf16[2560,128]{1,0:T(8,128)(2,1)S(1)} %convolution_convert_fusion), channel_id=1, source_target_pairs={{0,1},{1,0},{2,3},{3,2},{4,5},{5,4},{6,7},{7,6},{8,9},{9,8},{10,11... | collective-permute-start | bytes 1966088 | tf_op jit(solution)/shard_map/ppermute | solution.py:339
  29.5 1.4 %copy-start.1 = (bf16[64,192]{1,0:T(8,128)(2,1)S(1)}, bf16[64,192]{1,0:T(8,128)(2,1)}, u32[]{:S(2)}) copy-start(bf16[64,192]{1,0:T(8,128)(2,1)} %constant.16.clone.forward) | copy-start | bytes 73732
  29.5 1.4 %copy-start.3 = (f32[128,128]{1,0:T(8,128)S(1)}, f32[128,128]{1,0:T(8,128)}, u32[]{:S(2)}) copy-start(f32[128,128]{1,0:T(8,128)} %constant.18.clone.base) | copy-start | bytes 196612
  29.5 1.4 %copy-start.5 = (bf16[512,128]{1,0:T(8,128)(2,1)S(1)}, bf16[512,128]{1,0:T(8,128)(2,1)}, u32[]{:S(2)}) copy-start(bf16[512,128]{1,0:T(8,128)(2,1)} %constant.19.clone.spans) | copy-start | bytes 393220
  29.5 1.4 %copy-start.7 = (f32[128,128]{1,0:T(8,128)S(1)}, f32[128,128]{1,0:T(8,128)}, u32[]{:S(2)}) copy-start(f32[128,128]{1,0:T(8,128)} %constant.20.clone.slots) | copy-start | bytes 196612
  32.8 10.9 %collective-permute-start.7 = (bf16[512,128]{1,0:T(8,128)(2,1)S(1)}, bf16[512,128]{1,0:T(8,128)(2,1)S(1)}, u32[]{:S(2)}, u32[]{:S(2)}) collective-permute-start(bf16[512,128]{1,0:T(8,128)(2,1)S(1)} %get-tuple-element.33), channel_id=1, source_target_pairs={{0,4},{1,5},{2,6},{3,7},{4,0},{5,1},{6,2},{7,3},{8,12},{9,13},{10,... | collective-permute-start | bytes 393224 | tf_op jit(solution)/shard_map/ppermute | solution.py:336
  37.3 6.2 %copy-start.11 = (f32[1,2560,128]{2,1,0:T(8,128)S(1)}, f32[1,2560,128]{2,1,0:T(8,128)}, u32[]{:S(2)}) copy-start(f32[1,2560,128]{2,1,0:T(8,128)} %param.14) | copy-start | bytes 3932164
  37.4 6.2 %collective-permute-start.6 = (bf16[2560,128]{1,0:T(8,128)(2,1)S(1)}, bf16[2560,128]{1,0:T(8,128)(2,1)S(1)}, u32[]{:S(2)}, u32[]{:S(2)}) collective-permute-start(bf16[2560,128]{1,0:T(8,128)(2,1)S(1)} %slice.39), channel_id=1, source_target_pairs={{0,1},{1,0},{2,3},{3,2},{4,5},{5,4},{6,7},{7,6},{8,9},{9,8},{10,11... | collective-permute-start | bytes 1966088 | tf_op jit(solution)/shard_map/ppermute | solution.py:339
  39.5 37.4 %collective-permute-start.8 = (bf16[2560,128]{1,0:T(8,128)(2,1)S(1)}, bf16[2560,128]{1,0:T(8,128)(2,1)S(1)}, u32[]{:S(2)}, u32[]{:S(2)}) collective-permute-start(bf16[2560,128]{1,0:T(8,128)(2,1)S(1)} %get-tuple-element.38), channel_id=1, source_target_pairs={{0,4},{1,5},{2,6},{3,7},{4,0},{5,1},{6,2},{7,3},{8,12},{9,13},{10,... | collective-permute-start | bytes 1966088 | tf_op jit(solution)/shard_map/ppermute | solution.py:336
  43.7 31.4 %copy-start.4 = (bf16[128,1024]{1,0:T(8,128)(2,1)S(1)}, bf16[128,1024]{1,0:T(8,128)(2,1)}, u32[]{:S(2)}) copy-start(bf16[128,1024]{1,0:T(8,128)(2,1)} %constant.22.clone.unpack) | copy-start | bytes 786436
  43.7 31.4 %copy-start.6 = (bf16[384,128]{1,0:T(8,128)(2,1)S(1)}, bf16[384,128]{1,0:T(8,128)(2,1)}, u32[]{:S(2)}) copy-start(bf16[384,128]{1,0:T(8,128)(2,1)} %constant.21.clone.backward) | copy-start | bytes 294916
  44.7 36.8 %copy-start.8 = (bf16[64,192]{1,0:T(8,128)(2,1)S(1)}, bf16[64,192]{1,0:T(8,128)(2,1)}, u32[]{:S(2)}) copy-start(bf16[64,192]{1,0:T(8,128)(2,1)} %constant.17.clone.backward) | copy-start | bytes 73732
  76.9 25.8 %all-to-all-start.1 = ((bf16[64,8,640]{2,1,0:T(8,128)(2,1)}), bf16[64,8,640]{2,1,0:T(8,128)(2,1)S(1)}, u32[]{:S(2)}, u32[]{:S(2)}) async-start(bf16[64,8,640]{2,1,0:T(8,128)(2,1)} %bitcast.11), calls=%async_computation.1 | async-start | bytes 1310720 | tf_op jit(solution)/shard_map/all_to_all | solution.py:452

commit v19 on v18

--- a/solution.py
+++ b/solution.py
@@ -424,10 +424,7 @@
     keys = lax.optimization_barrier(keys.reshape(len(NEAR), tokens, 2 * cols))
     first, second = lax.optimization_barrier((first, second))
     near = gram(activations, keys[0]) + gram(first, keys[1]) + gram(second, keys[2])
-    other, far_whole = lax.optimization_barrier(
-        (near[:, cols:].astype(jnp.bfloat16), far_whole)
-    )
-    other, far_whole = swap(other), along(far_whole, FAR)
+    other = swap(near[:, cols:].astype(jnp.bfloat16))
     part = near[:, :cols] + 0.999 * momentum[0]
 
     order = np.concatenate([np.arange(0, SPAN, 2), np.arange(1, SPAN, 2)])
@@ -453,7 +450,8 @@
             x.reshape(replicas, OWN_COLS, x.shape[1]), "dp", 0, 0, tiled=True
         ).reshape(x.shape)
 
-    pieces = exchange(sent)
+    sent, far_whole = lax.optimization_barrier((sent, far_whole))
+    pieces, far_whole = exchange(sent), along(far_whole, FAR)
     unpack = np.concatenate(
         [
             np.kron(np.eye(cols // OWN_COLS), np.outer(np.eye(OWN_COLS)[c], np.ones(OWN_COLS)))

time: 105 us -> 106 us (level)
  waiting for transfers between devices: 18.9 us -> 20.8 us
    ppermute x5, waiting for transfers between devices: 0.01 us -> 2.06 us  [along(): return lax.ppermute(x, 'tensor', [(i, i ^ 2 * step) for i in range(group)])]
  transfers between devices with their start and end apart: 10 -> 10, of which waited for: 2 -> 3; matrix products, arithmetic and copies ran while one was open for 4% -> 4% of each run, Pallas kernels for 10% -> 9%
where the time goes in v19:
time: 106 us; the launch traced here: 105 us
  starting transfers between devices  33.2 us (31%)
  blocking collectives  30.1 us (28%)
  waiting for transfers between devices  20.8 us (20%)
  Pallas kernels  12.6 us (12%)
  matrix products  4.04 us (4%)
  local copies, waits for them, and re-layouts  2.67 us (3%)
  between operations  1.6 us (2%)
    all_to_all x1, blocking collectives, exchange(): lax.all_to_all(x.reshape(replicas, OWN_COLS, x.shape[1]), 'dp', 0, 0, til...  30.1 us
    ppermute x5, starting transfers between devices, along(): return lax.ppermute(x, 'tensor', [(i, i ^ 2 * step) for i in range(group)])  20.3 us
    all_to_all x1, waiting for transfers between devices, exchange(): lax.all_to_all(x.reshape(replicas, OWN_COLS, x.shape[1]), 'dp', 0, 0, til...  18 us
    pallas_call x9, Pallas kernels, call(): pl.pallas_call(kernel, out_shape=outs, in_specs=places or [VMEM] * len(ar...  12.6 us
    ppermute x4, starting transfers between devices, swap(): return lax.ppermute(x, 'tensor', [(i, i ^ 1) for i in range(group)])  8.3 us
    all_to_all x1, starting transfers between devices, exchange(): lax.all_to_all(x.reshape(replicas, OWN_COLS, x.shape[1]), 'dp', 0, 0, til...  4.64 us
    dot_general x5, matrix products, gram(): lax.dot_general(a, k, (((0,), (0,)), ((), ())), preferred_element_type=jn...  4.04 us
    unnamed x24, local copies, waits for them, and re-layouts  2.58 us
  transfers between devices with their start and end apart: 10, of which 3 were waited for; matrix products, arithmetic and copies ran while one was open for 4% of the time, Pallas kernels for 9%

profile of v19, /device:TPU:2, one launch (start us, length us, event | category | flops | bytes accessed | tf_op | source)
XLA Modules:
  0.0 105.3 jit_solution(12741740720516247966)
XLA Ops:
  0.6 0.9 far_keys.1
  1.6 4.0 %collective-permute-start.4 = (bf16[432,128]{1,0:T(8,128)(2,1)S(1)}, bf16[432,128]{1,0:T(8,128)(2,1)S(1)}, u32[]{:S(2)}, u32[]{:S(2)}) collective-permute-start(bf16[432,128]{1,0:T(8,128)(2,1)S(1)} %far_keys.1), channel_id=1, source_target_pairs={{0,4},{1,5},{2,6},{3,7},{4,0},{5,1},{6,2},{7,3},{8,12},{9,13},{10,... | collective-permute-start | bytes 331784 | tf_op jit(solution)/shard_map/ppermute | solution.py:336
  5.6 7.2 %collective-permute-start.1 = (bf16[208,2560]{1,0:T(8,128)(2,1)}, bf16[208,2560]{1,0:T(8,128)(2,1)S(1)}, u32[]{:S(2)}, u32[]{:S(2)}) collective-permute-start(bf16[208,2560]{1,0:T(8,128)(2,1)} %param.12), channel_id=1, source_target_pairs={{0,6},{1,7},{2,4},{3,5},{4,2},{5,3},{6,0},{7,1},{8,14},{9,15},{10,... | collective-permute-start | bytes 3194888 | tf_op jit(solution)/shard_map/ppermute | solution.py:336
  12.8 1.9 %collective-permute-start.2 = (bf16[208,2560]{1,0:T(8,128)(2,1)}, bf16[208,2560]{1,0:T(8,128)(2,1)S(1)}, u32[]{:S(2)}, u32[]{:S(2)}) collective-permute-start(bf16[208,2560]{1,0:T(8,128)(2,1)} %param.12), channel_id=1, source_target_pairs={{0,2},{1,3},{2,0},{3,1},{4,6},{5,7},{6,4},{7,5},{8,10},{9,11},{10,... | collective-permute-start | bytes 3194888 | tf_op jit(solution)/shard_map/ppermute | solution.py:336
  14.7 0.0 collective-permute-done.4.far
  14.7 1.9 %collective-permute-start.5 = (bf16[208,128]{1,0:T(8,128)(2,1)S(1)}, bf16[208,128]{1,0:T(8,128)(2,1)S(1)}, u32[]{:S(2)}, u32[]{:S(2)}) collective-permute-start(bf16[208,128]{1,0:T(8,128)(2,1)S(1)} %get-tuple-element.30), channel_id=1, source_target_pairs={{0,1},{1,0},{2,3},{3,2},{4,5},{5,4},{6,7},{7,6},{8,9},{9,8},{10,11... | collective-permute-start | bytes 159752 | tf_op jit(solution)/shard_map/ppermute | solution.py:339
  16.7 0.0 copy-start
  16.7 1.0 copy-done
  17.7 2.4 %collective-permute-start = (bf16[624,128]{1,0:T(8,128)(2,1)S(1)}, bf16[624,128]{1,0:T(8,128)(2,1)S(1)}, u32[]{:S(2)}, u32[]{:S(2)}) collective-permute-start(bf16[624,128]{1,0:T(8,128)(2,1)S(1)} %get-tuple-element.25), channel_id=1, source_target_pairs={{0,1},{1,0},{2,3},{3,2},{4,5},{5,4},{6,7},{7,6},{8,9},{9,8},{10,11... | collective-permute-start | bytes 479240 | tf_op jit(solution)/shard_map/ppermute | solution.py:339
  20.8 0.0 copy-start.2
  20.8 0.8 copy-done.2
  21.6 0.7 copy-done.9
  22.3 2.8 %routes.1 = (bf16[2560,128]{1,0:T(8,128)(2,1)S(1)}, bf16[1024,640]{1,0:T(8,128)(2,1)S(1)}, bf16[512,128]{1,0:T(8,128)(2,1)S(1)}) custom-call(s32[6,2,40]{2,1,0:T(2,128)S(1)} %bitcast.31, s32[1]{0:T(128)S(6)} %copy.14.count, f32[128,128]{1,0:T(8,128)S(1)} %copy-done.2), custom_call_target="tpu_custom_call" | custom-call | tf_op jit(solution)/shard_map/routes/pallas_call | solution.py:319
  25.1 0.0 collective-permute-done.5
  25.1 1.8 %convolution_convert_fusion = bf16[2560,128]{1,0:T(8,128)(2,1)S(1)} fusion(bf16[208,2560]{1,0:T(8,128)(2,1)} %param.12, bf16[208,128]{1,0:T(8,128)(2,1)S(1)} %collective-permute-done.5), kind=kOutput, calls=%fused_computation.2 | convolution fusion | flops 136642560 | bytes 1773568 | tf_op jit(solution)/shard_map/dot_general | solution.py:310
  26.9 1.9 %collective-permute-start.6 = (bf16[2560,128]{1,0:T(8,128)(2,1)S(1)}, bf16[2560,128]{1,0:T(8,128)(2,1)S(1)}, u32[]{:S(2)}, u32[]{:S(2)}) collective-permute-start(bf16[2560,128]{1,0:T(8,128)(2,1)S(1)} %convolution_convert_fusion), channel_id=1, source_target_pairs={{0,1},{1,0},{2,3},{3,2},{4,5},{5,4},{6,7},{7,6},{8,9},{9,8},{10,11... | collective-permute-start | bytes 1966088 | tf_op jit(solution)/shard_map/ppermute | solution.py:339
  28.9 0.0 copy-done.10
  28.9 0.6 fusion.1.part
  29.4 0.0 collective-permute-done
  29.4 0.1 pad_maximum_fusion
  29.5 0.0 copy-start.1
  29.5 0.0 copy-start.3
  29.5 0.0 copy-start.5
  29.5 0.0 copy-start.7
  29.5 0.6 fusion
  30.1 0.8 collective-permute-done.6.other
  30.9 1.8 %far.1 = (bf16[2560,128]{1,0:T(8,128)(2,1)S(1)}, bf16[512,128]{1,0:T(8,128)(2,1)S(1)}) custom-call(bf16[16,128]{1,0:T(8,128)(2,1)S(1)} %slice.30.numbers, s32[1]{0:T(128)S(6)} %copy.14.count, bf16[512,128]{1,0:T(8,128)(2,1)S(1)} %copy-done.5, f32[128,128]{1,0:T(8,128)S(1)} %copy-done.7, f32[128,128]{1,0:T(8,128)S(1)} %copy-done.3, ...), custom_call_target="tpu_custom_call" | custom-call | tf_op jit(solution)/shard_map/far/pallas_call | solution.py:319
  32.8 3.4 %collective-permute-start.7 = (bf16[512,128]{1,0:T(8,128)(2,1)S(1)}, bf16[512,128]{1,0:T(8,128)(2,1)S(1)}, u32[]{:S(2)}, u32[]{:S(2)}) collective-permute-start(bf16[512,128]{1,0:T(8,128)(2,1)S(1)} %get-tuple-element.31), channel_id=1, source_target_pairs={{0,4},{1,5},{2,6},{3,7},{4,0},{5,1},{6,2},{7,3},{8,12},{9,13},{10,... | collective-permute-start | bytes 393224 | tf_op jit(solution)/shard_map/ppermute | solution.py:336
  36.1 0.0 collective-permute-done.1
  36.2 0.0 collective-permute-done.2
  36.2 0.6 convolution_add_fusion.1
  36.7 0.6 convolution_add_fusion
  37.3 0.0 copy-start.11
  37.3 0.1 slice.39
  37.4 2.1 %collective-permute-start.3 = (bf16[2560,128]{1,0:T(8,128)(2,1)S(1)}, bf16[2560,128]{1,0:T(8,128)(2,1)S(1)}, u32[]{:S(2)}, u32[]{:S(2)}) collective-permute-start(bf16[2560,128]{1,0:T(8,128)(2,1)S(1)} %slice.39), channel_id=1, source_target_pairs={{0,1},{1,0},{2,3},{3,2},{4,5},{5,4},{6,7},{7,6},{8,9},{9,8},{10,11... | collective-permute-start | bytes 1966088 | tf_op jit(solution)/shard_map/ppermute | solution.py:339
  39.5 0.2 slice_add_fusion.part
  39.7 2.0 %collective-permute-done.7.far = bf16[512,128]{1,0:T(8,128)(2,1)S(1)} collective-permute-done((bf16[512,128]{1,0:T(8,128)(2,1)S(1)}, bf16[512,128]{1,0:T(8,128)(2,1)S(1)}, u32[]{:S(2)}, u32[]{:S(2)}) %collective-permute-start.7) | collective-permute-done | bytes 131104 | tf_op jit(solution)/shard_map/ppermute | solution.py:336
  41.7 0.0 collective-permute-done.3.other
  41.7 1.0 spectrum.1
  42.7 3.8 %collective-permute-start.8 = (bf16[2560,128]{1,0:T(8,128)(2,1)S(1)}, bf16[2560,128]{1,0:T(8,128)(2,1)S(1)}, u32[]{:S(2)}, u32[]{:S(2)}) collective-permute-start(bf16[2560,128]{1,0:T(8,128)(2,1)S(1)} %get-tuple-element.38), channel_id=1, source_target_pairs={{0,4},{1,5},{2,6},{3,7},{4,0},{5,1},{6,2},{7,3},{8,12},{9,13},{10,... | collective-permute-start | bytes 1966088 | tf_op jit(solution)/shard_map/ppermute | solution.py:336
  46.5 0.0 copy-start.8
  46.6 30.1 %all_to_all.10 = bf16[64,8,128]{2,1,0:T(8,128)(2,1)S(1)} all-to-all(bf16[64,8,128]{2,1,0:T(8,128)(2,1)S(1)} %bitcast.29), channel_id=1, replica_groups=mesh['dp'=64,'tensor'=8] {'dp'}, dimensions={0} | all-to-all | bytes 262144 | tf_op jit(solution)/shard_map/all_to_all | solution.py:449
  76.6 1.9 %total.1 = bf16[512,640]{1,0:T(8,128)(2,1)} custom-call(bf16[512,128]{1,0:T(8,128)(2,1)S(1)} %bitcast.28, bf16[128,1024]{1,0:T(8,128)(2,1)S(1)} %copy-done.4, bf16[384,128]{1,0:T(8,128)(2,1)S(1)} %copy-done.6), custom_call_target="tpu_custom_call" | custom-call | tf_op jit(solution)/shard_map/total/pallas_call | solution.py:319
  78.5 0.0 collective-permute-done.8.far
  78.5 4.6 %all-to-all-start.1 = ((bf16[64,8,640]{2,1,0:T(8,128)(2,1)}), bf16[64,8,640]{2,1,0:T(8,128)(2,1)S(1)}, u32[]{:S(2)}, u32[]{:S(2)}) async-start(bf16[64,8,640]{2,1,0:T(8,128)(2,1)} %bitcast.11), calls=%async_computation.1 | async-start | bytes 1310720 | tf_op jit(solution)/shard_map/all_to_all | solution.py:449
  83.2 3.1 %kept.1 = f32[2560,128]{1,0:T(8,128)} custom-call(f32[2560,128]{1,0:T(8,128)S(1)} %get-tuple-element.34.advanced, bf16[2560,128]{1,0:T(8,128)(2,1)S(1)} %collective-permute-done.8.far, bf16[2560,128]{1,0:T(8,128)(2,1)S(1)} %get-tuple-element.40.mask, bf16[64,192]{1,0:T(8,128)(2,1)S(1)} %copy-done.1, bf16[64,192]{1,0:T(8,128)(2,1)S(1)} %copy-done.8), custom_call_target="tpu_custom_call" | custom-call | tf_op jit(solution)/shard_map/kept/pallas_call | solution.py:319
  86.2 18.0 %all-to-all-done.1 = bf16[64,8,640]{2,1,0:T(8,128)(2,1)S(1)} async-done(((bf16[64,8,640]{2,1,0:T(8,128)(2,1)}), bf16[64,8,640]{2,1,0:T(8,128)(2,1)S(1)}, u32[]{:S(2)}, u32[]{:S(2)}) %all-to-all-start.1) | async-done | bytes 655392 | tf_op jit(solution)/shard_map/all_to_all | solution.py:449
  104.2 1.1 %turn.1 = bf16[2560,128]{1,0:T(8,128)(2,1)} custom-call(bf16[512,640]{1,0:T(8,128)(2,1)S(1)} %bitcast.27), custom_call_target="tpu_custom_call" | custom-call | tf_op jit(solution)/shard_map/turn/pallas_call | solution.py:319
  (15 shorter events, 0.1 us)
Async XLA Ops:
  1.6 13.1 %collective-permute-start.4 = (bf16[432,128]{1,0:T(8,128)(2,1)S(1)}, bf16[432,128]{1,0:T(8,128)(2,1)S(1)}, u32[]{:S(2)}, u32[]{:S(2)}) collective-permute-start(bf16[432,128]{1,0:T(8,128)(2,1)S(1)} %far_keys.1), channel_id=1, source_target_pairs={{0,4},{1,5},{2,6},{3,7},{4,0},{5,1},{6,2},{7,3},{8,12},{9,13},{10,... | collective-permute-start | bytes 331784 | tf_op jit(solution)/shard_map/ppermute | solution.py:336
  5.6 30.5 %collective-permute-start.1 = (bf16[208,2560]{1,0:T(8,128)(2,1)}, bf16[208,2560]{1,0:T(8,128)(2,1)S(1)}, u32[]{:S(2)}, u32[]{:S(2)}) collective-permute-start(bf16[208,2560]{1,0:T(8,128)(2,1)} %param.12), channel_id=1, source_target_pairs={{0,6},{1,7},{2,4},{3,5},{4,2},{5,3},{6,0},{7,1},{8,14},{9,15},{10,... | collective-permute-start | bytes 3194888 | tf_op jit(solution)/shard_map/ppermute | solution.py:336
  12.8 23.4 %collective-permute-start.2 = (bf16[208,2560]{1,0:T(8,128)(2,1)}, bf16[208,2560]{1,0:T(8,128)(2,1)S(1)}, u32[]{:S(2)}, u32[]{:S(2)}) collective-permute-start(bf16[208,2560]{1,0:T(8,128)(2,1)} %param.12), channel_id=1, source_target_pairs={{0,2},{1,3},{2,0},{3,1},{4,6},{5,7},{6,4},{7,5},{8,10},{9,11},{10,... | collective-permute-start | bytes 3194888 | tf_op jit(solution)/shard_map/ppermute | solution.py:336
  14.7 10.4 %collective-permute-start.5 = (bf16[208,128]{1,0:T(8,128)(2,1)S(1)}, bf16[208,128]{1,0:T(8,128)(2,1)S(1)}, u32[]{:S(2)}, u32[]{:S(2)}) collective-permute-start(bf16[208,128]{1,0:T(8,128)(2,1)S(1)} %get-tuple-element.30), channel_id=1, source_target_pairs={{0,1},{1,0},{2,3},{3,2},{4,5},{5,4},{6,7},{7,6},{8,9},{9,8},{10,11... | collective-permute-start | bytes 159752 | tf_op jit(solution)/shard_map/ppermute | solution.py:339
  16.7 1.0 copy-start
  17.7 11.7 %collective-permute-start = (bf16[624,128]{1,0:T(8,128)(2,1)S(1)}, bf16[624,128]{1,0:T(8,128)(2,1)S(1)}, u32[]{:S(2)}, u32[]{:S(2)}) collective-permute-start(bf16[624,128]{1,0:T(8,128)(2,1)S(1)} %get-tuple-element.25), channel_id=1, source_target_pairs={{0,1},{1,0},{2,3},{3,2},{4,5},{5,4},{6,7},{7,6},{8,9},{9,8},{10,11... | collective-permute-start | bytes 479240 | tf_op jit(solution)/shard_map/ppermute | solution.py:339
  20.8 0.8 copy-start.2
  21.6 0.7 copy-start.9
  22.3 6.6 %copy-start.10 = (bf16[208,2560]{1,0:T(8,128)(2,1)S(1)}, bf16[208,2560]{1,0:T(8,128)(2,1)}, u32[]{:S(2)}) copy-start(bf16[208,2560]{1,0:T(8,128)(2,1)} %param.12) | copy-start | bytes 3194884
  26.9 4.0 %collective-permute-start.6 = (bf16[2560,128]{1,0:T(8,128)(2,1)S(1)}, bf16[2560,128]{1,0:T(8,128)(2,1)S(1)}, u32[]{:S(2)}, u32[]{:S(2)}) collective-permute-start(bf16[2560,128]{1,0:T(8,128)(2,1)S(1)} %convolution_convert_fusion), channel_id=1, source_target_pairs={{0,1},{1,0},{2,3},{3,2},{4,5},{5,4},{6,7},{7,6},{8,9},{9,8},{10,11... | collective-permute-start | bytes 1966088 | tf_op jit(solution)/shard_map/ppermute | solution.py:339
  29.5 1.4 %copy-start.1 = (bf16[64,192]{1,0:T(8,128)(2,1)S(1)}, bf16[64,192]{1,0:T(8,128)(2,1)}, u32[]{:S(2)}) copy-start(bf16[64,192]{1,0:T(8,128)(2,1)} %constant.16.clone.forward) | copy-start | bytes 73732
  29.5 1.4 %copy-start.3 = (f32[128,128]{1,0:T(8,128)S(1)}, f32[128,128]{1,0:T(8,128)}, u32[]{:S(2)}) copy-start(f32[128,128]{1,0:T(8,128)} %constant.18.clone.base) | copy-start | bytes 196612
  29.5 1.4 %copy-start.5 = (bf16[512,128]{1,0:T(8,128)(2,1)S(1)}, bf16[512,128]{1,0:T(8,128)(2,1)}, u32[]{:S(2)}) copy-start(bf16[512,128]{1,0:T(8,128)(2,1)} %constant.19.clone.spans) | copy-start | bytes 393220
  29.5 1.4 %copy-start.7 = (f32[128,128]{1,0:T(8,128)S(1)}, f32[128,128]{1,0:T(8,128)}, u32[]{:S(2)}) copy-start(f32[128,128]{1,0:T(8,128)} %constant.20.clone.slots) | copy-start | bytes 196612
  32.8 8.9 %collective-permute-start.7 = (bf16[512,128]{1,0:T(8,128)(2,1)S(1)}, bf16[512,128]{1,0:T(8,128)(2,1)S(1)}, u32[]{:S(2)}, u32[]{:S(2)}) collective-permute-start(bf16[512,128]{1,0:T(8,128)(2,1)S(1)} %get-tuple-element.31), channel_id=1, source_target_pairs={{0,4},{1,5},{2,6},{3,7},{4,0},{5,1},{6,2},{7,3},{8,12},{9,13},{10,... | collective-permute-start | bytes 393224 | tf_op jit(solution)/shard_map/ppermute | solution.py:336
  37.3 2.2 %copy-start.11 = (f32[1,2560,128]{2,1,0:T(8,128)S(1)}, f32[1,2560,128]{2,1,0:T(8,128)}, u32[]{:S(2)}) copy-start(f32[1,2560,128]{2,1,0:T(8,128)} %param.14) | copy-start | bytes 3932164
  37.4 4.3 %collective-permute-start.3 = (bf16[2560,128]{1,0:T(8,128)(2,1)S(1)}, bf16[2560,128]{1,0:T(8,128)(2,1)S(1)}, u32[]{:S(2)}, u32[]{:S(2)}) collective-permute-start(bf16[2560,128]{1,0:T(8,128)(2,1)S(1)} %slice.39), channel_id=1, source_target_pairs={{0,1},{1,0},{2,3},{3,2},{4,5},{5,4},{6,7},{7,6},{8,9},{9,8},{10,11... | collective-permute-start | bytes 1966088 | tf_op jit(solution)/shard_map/ppermute | solution.py:339
  41.7 34.9 %copy-start.4 = (bf16[128,1024]{1,0:T(8,128)(2,1)S(1)}, bf16[128,1024]{1,0:T(8,128)(2,1)}, u32[]{:S(2)}) copy-start(bf16[128,1024]{1,0:T(8,128)(2,1)} %constant.22.clone.unpack) | copy-start | bytes 786436
  41.7 34.9 %copy-start.6 = (bf16[384,128]{1,0:T(8,128)(2,1)S(1)}, bf16[384,128]{1,0:T(8,128)(2,1)}, u32[]{:S(2)}) copy-start(bf16[384,128]{1,0:T(8,128)(2,1)} %constant.21.clone.backward) | copy-start | bytes 294916
  42.7 35.8 %collective-permute-start.8 = (bf16[2560,128]{1,0:T(8,128)(2,1)S(1)}, bf16[2560,128]{1,0:T(8,128)(2,1)S(1)}, u32[]{:S(2)}, u32[]{:S(2)}) collective-permute-start(bf16[2560,128]{1,0:T(8,128)(2,1)S(1)} %get-tuple-element.38), channel_id=1, source_target_pairs={{0,4},{1,5},{2,6},{3,7},{4,0},{5,1},{6,2},{7,3},{8,12},{9,13},{10,... | collective-permute-start | bytes 1966088 | tf_op jit(solution)/shard_map/ppermute | solution.py:336
  46.5 36.6 %copy-start.8 = (bf16[64,192]{1,0:T(8,128)(2,1)S(1)}, bf16[64,192]{1,0:T(8,128)(2,1)}, u32[]{:S(2)}) copy-start(bf16[64,192]{1,0:T(8,128)(2,1)} %constant.17.clone.backward) | copy-start | bytes 73732
  78.5 25.7 %all-to-all-start.1 = ((bf16[64,8,640]{2,1,0:T(8,128)(2,1)}), bf16[64,8,640]{2,1,0:T(8,128)(2,1)S(1)}, u32[]{:S(2)}, u32[]{:S(2)}) async-start(bf16[64,8,640]{2,1,0:T(8,128)(2,1)} %bitcast.11), calls=%async_computation.1 | async-start | bytes 1310720 | tf_op jit(solution)/shard_map/all_to_all | solution.py:449

commit v20 on v18

--- a/solution.py
+++ b/solution.py
@@ -303,7 +303,7 @@
         for i in range(height // cols):
             rows = g * height + i * cols
             block = turned[g * cols : (g + 1) * cols, i * cols : (i + 1) * cols]
-            update[rows : rows + cols, :] = block.astype(jnp.float32).T.astype(update.dtype)
+            update[rows : rows + cols, :] = block.T
 
 
 def gram(a, k):

time: 105 us -> 104 us (level)
  no operation moved by 1% of the time
where the time goes in v20:
time: 104 us
  starting transfers between devices  33.4 us (32%)
  blocking collectives  30.3 us (29%)
  waiting for transfers between devices  18.9 us (18%)
  Pallas kernels  12.6 us (12%)
  matrix products  4.04 us (4%)
  local copies, waits for them, and re-layouts  2.68 us (3%)
  between operations  1.63 us (2%)
    all_to_all x1, blocking collectives, exchange(): lax.all_to_all(x.reshape(replicas, OWN_COLS, x.shape[1]), 'dp', 0, 0, til...  30.3 us
    ppermute x5, starting transfers between devices, along(): return lax.ppermute(x, 'tensor', [(i, i ^ 2 * step) for i in range(group)])  20.5 us
    all_to_all x1, waiting for transfers between devices, exchange(): lax.all_to_all(x.reshape(replicas, OWN_COLS, x.shape[1]), 'dp', 0, 0, til...  18.1 us
    pallas_call x9, Pallas kernels, call(): pl.pallas_call(kernel, out_shape=outs, in_specs=places or [VMEM] * len(ar...  12.6 us
    ppermute x4, starting transfers between devices, swap(): return lax.ppermute(x, 'tensor', [(i, i ^ 1) for i in range(group)])  8.3 us
    all_to_all x1, starting transfers between devices, exchange(): lax.all_to_all(x.reshape(replicas, OWN_COLS, x.shape[1]), 'dp', 0, 0, til...  4.64 us
    dot_general x5, matrix products, gram(): lax.dot_general(a, k, (((0,), (0,)), ((), ())), preferred_element_type=jn...  4.04 us
    unnamed x24, local copies, waits for them, and re-layouts  2.59 us
  transfers between devices with their start and end apart: 10, of which 2 were waited for; matrix products, arithmetic and copies ran while one was open for 4% of the time, Pallas kernels for 10%

profile of v20, /device:TPU:2, one launch (start us, length us, event | category | flops | bytes accessed | tf_op | source)
XLA Modules:
  0.0 103.8 jit_solution(18313471465026327247)
XLA Ops:
  0.6 0.9 far_keys.1
  1.6 4.0 %collective-permute-start.3 = (bf16[432,128]{1,0:T(8,128)(2,1)S(1)}, bf16[432,128]{1,0:T(8,128)(2,1)S(1)}, u32[]{:S(2)}, u32[]{:S(2)}) collective-permute-start(bf16[432,128]{1,0:T(8,128)(2,1)S(1)} %far_keys.1), channel_id=1, source_target_pairs={{0,4},{1,5},{2,6},{3,7},{4,0},{5,1},{6,2},{7,3},{8,12},{9,13},{10,... | collective-permute-start | bytes 331784 | tf_op jit(solution)/shard_map/ppermute | solution.py:336
  5.6 7.2 %collective-permute-start.1 = (bf16[208,2560]{1,0:T(8,128)(2,1)}, bf16[208,2560]{1,0:T(8,128)(2,1)S(1)}, u32[]{:S(2)}, u32[]{:S(2)}) collective-permute-start(bf16[208,2560]{1,0:T(8,128)(2,1)} %param.12), channel_id=1, source_target_pairs={{0,6},{1,7},{2,4},{3,5},{4,2},{5,3},{6,0},{7,1},{8,14},{9,15},{10,... | collective-permute-start | bytes 3194888 | tf_op jit(solution)/shard_map/ppermute | solution.py:336
  12.8 1.9 %collective-permute-start.2 = (bf16[208,2560]{1,0:T(8,128)(2,1)}, bf16[208,2560]{1,0:T(8,128)(2,1)S(1)}, u32[]{:S(2)}, u32[]{:S(2)}) collective-permute-start(bf16[208,2560]{1,0:T(8,128)(2,1)} %param.12), channel_id=1, source_target_pairs={{0,2},{1,3},{2,0},{3,1},{4,6},{5,7},{6,4},{7,5},{8,10},{9,11},{10,... | collective-permute-start | bytes 3194888 | tf_op jit(solution)/shard_map/ppermute | solution.py:336
  14.7 0.0 collective-permute-done.3.far
  14.7 1.9 %collective-permute-start.4 = (bf16[208,128]{1,0:T(8,128)(2,1)S(1)}, bf16[208,128]{1,0:T(8,128)(2,1)S(1)}, u32[]{:S(2)}, u32[]{:S(2)}) collective-permute-start(bf16[208,128]{1,0:T(8,128)(2,1)S(1)} %get-tuple-element.30), channel_id=1, source_target_pairs={{0,1},{1,0},{2,3},{3,2},{4,5},{5,4},{6,7},{7,6},{8,9},{9,8},{10,11... | collective-permute-start | bytes 159752 | tf_op jit(solution)/shard_map/ppermute | solution.py:339
  16.7 0.0 copy-start
  16.7 1.0 copy-done
  17.7 2.4 %collective-permute-start = (bf16[624,128]{1,0:T(8,128)(2,1)S(1)}, bf16[624,128]{1,0:T(8,128)(2,1)S(1)}, u32[]{:S(2)}, u32[]{:S(2)}) collective-permute-start(bf16[624,128]{1,0:T(8,128)(2,1)S(1)} %get-tuple-element.25), channel_id=1, source_target_pairs={{0,1},{1,0},{2,3},{3,2},{4,5},{5,4},{6,7},{7,6},{8,9},{9,8},{10,11... | collective-permute-start | bytes 479240 | tf_op jit(solution)/shard_map/ppermute | solution.py:339
  20.8 0.0 copy-start.2
  20.8 0.8 copy-done.2
  21.6 0.7 copy-done.9
  22.3 2.8 %routes.1 = (bf16[2560,128]{1,0:T(8,128)(2,1)S(1)}, bf16[1024,640]{1,0:T(8,128)(2,1)S(1)}, bf16[512,128]{1,0:T(8,128)(2,1)S(1)}) custom-call(s32[6,2,40]{2,1,0:T(2,128)S(1)} %bitcast.31, s32[1]{0:T(128)S(6)} %copy.14.count, f32[128,128]{1,0:T(8,128)S(1)} %copy-done.2), custom_call_target="tpu_custom_call" | custom-call | tf_op jit(solution)/shard_map/routes/pallas_call | solution.py:319
  25.1 0.0 collective-permute-done.4
  25.1 1.8 %convolution_convert_fusion = bf16[2560,128]{1,0:T(8,128)(2,1)S(1)} fusion(bf16[208,2560]{1,0:T(8,128)(2,1)} %param.12, bf16[208,128]{1,0:T(8,128)(2,1)S(1)} %collective-permute-done.4), kind=kOutput, calls=%fused_computation.2 | convolution fusion | flops 136642560 | bytes 1773568 | tf_op jit(solution)/shard_map/dot_general | solution.py:310
  26.9 1.9 %collective-permute-start.5 = (bf16[2560,128]{1,0:T(8,128)(2,1)S(1)}, bf16[2560,128]{1,0:T(8,128)(2,1)S(1)}, u32[]{:S(2)}, u32[]{:S(2)}) collective-permute-start(bf16[2560,128]{1,0:T(8,128)(2,1)S(1)} %convolution_convert_fusion), channel_id=1, source_target_pairs={{0,1},{1,0},{2,3},{3,2},{4,5},{5,4},{6,7},{7,6},{8,9},{9,8},{10,11... | collective-permute-start | bytes 1966088 | tf_op jit(solution)/shard_map/ppermute | solution.py:339
  28.9 0.6 fusion.1.part
  29.4 0.0 collective-permute-done
  29.5 0.0 copy-start.1
  29.5 0.0 copy-start.3
  29.5 0.0 copy-start.5
  29.5 0.0 copy-start.7
  29.5 0.6 fusion
  30.1 0.8 collective-permute-done.5.other
  30.9 1.8 %far.1 = (bf16[2560,128]{1,0:T(8,128)(2,1)S(1)}, bf16[512,128]{1,0:T(8,128)(2,1)S(1)}) custom-call(bf16[16,128]{1,0:T(8,128)(2,1)S(1)} %slice.30.numbers, s32[1]{0:T(128)S(6)} %copy.14.count, bf16[512,128]{1,0:T(8,128)(2,1)S(1)} %copy-done.5, f32[128,128]{1,0:T(8,128)S(1)} %copy-done.7, f32[128,128]{1,0:T(8,128)S(1)} %copy-done.3, ...), custom_call_target="tpu_custom_call" | custom-call | tf_op jit(solution)/shard_map/far/pallas_call | solution.py:319
  32.8 3.4 %collective-permute-start.7 = (bf16[512,128]{1,0:T(8,128)(2,1)S(1)}, bf16[512,128]{1,0:T(8,128)(2,1)S(1)}, u32[]{:S(2)}, u32[]{:S(2)}) collective-permute-start(bf16[512,128]{1,0:T(8,128)(2,1)S(1)} %get-tuple-element.33), channel_id=1, source_target_pairs={{0,4},{1,5},{2,6},{3,7},{4,0},{5,1},{6,2},{7,3},{8,12},{9,13},{10,... | collective-permute-start | bytes 393224 | tf_op jit(solution)/shard_map/ppermute | solution.py:336
  36.1 0.0 collective-permute-done.1
  36.2 0.0 collective-permute-done.2
  36.2 0.6 convolution_add_fusion.1
  36.7 0.6 convolution_add_fusion
  37.3 0.0 copy-start.11
  37.3 0.1 slice.39
  37.4 2.1 %collective-permute-start.6 = (bf16[2560,128]{1,0:T(8,128)(2,1)S(1)}, bf16[2560,128]{1,0:T(8,128)(2,1)S(1)}, u32[]{:S(2)}, u32[]{:S(2)}) collective-permute-start(bf16[2560,128]{1,0:T(8,128)(2,1)S(1)} %slice.39), channel_id=1, source_target_pairs={{0,1},{1,0},{2,3},{3,2},{4,5},{5,4},{6,7},{7,6},{8,9},{9,8},{10,11... | collective-permute-start | bytes 1966088 | tf_op jit(solution)/shard_map/ppermute | solution.py:339
  39.5 4.0 %collective-permute-start.8 = (bf16[2560,128]{1,0:T(8,128)(2,1)S(1)}, bf16[2560,128]{1,0:T(8,128)(2,1)S(1)}, u32[]{:S(2)}, u32[]{:S(2)}) collective-permute-start(bf16[2560,128]{1,0:T(8,128)(2,1)S(1)} %get-tuple-element.38), channel_id=1, source_target_pairs={{0,4},{1,5},{2,6},{3,7},{4,0},{5,1},{6,2},{7,3},{8,12},{9,13},{10,... | collective-permute-start | bytes 1966088 | tf_op jit(solution)/shard_map/ppermute | solution.py:336
  43.5 0.2 slice_add_fusion.part
  43.6 0.0 collective-permute-done.7.far
  43.6 0.0 collective-permute-done.6.other
  43.7 0.0 copy-start.4
  43.7 0.0 copy-start.6
  43.7 1.0 spectrum.1
  44.7 0.0 copy-start.8
  44.7 30.3 %all_to_all.10 = bf16[64,8,128]{2,1,0:T(8,128)(2,1)S(1)} all-to-all(bf16[64,8,128]{2,1,0:T(8,128)(2,1)S(1)} %bitcast.29), channel_id=1, replica_groups=mesh['dp'=64,'tensor'=8] {'dp'}, dimensions={0} | all-to-all | bytes 262144 | tf_op jit(solution)/shard_map/all_to_all | solution.py:452
  75.0 1.9 %total.1 = bf16[512,640]{1,0:T(8,128)(2,1)} custom-call(bf16[512,128]{1,0:T(8,128)(2,1)S(1)} %bitcast.28, bf16[128,1024]{1,0:T(8,128)(2,1)S(1)} %copy-done.4, bf16[384,128]{1,0:T(8,128)(2,1)S(1)} %copy-done.6), custom_call_target="tpu_custom_call" | custom-call | tf_op jit(solution)/shard_map/total/pallas_call | solution.py:319
  76.9 0.0 collective-permute-done.8.far
  76.9 4.6 %all-to-all-start.1 = ((bf16[64,8,640]{2,1,0:T(8,128)(2,1)}), bf16[64,8,640]{2,1,0:T(8,128)(2,1)S(1)}, u32[]{:S(2)}, u32[]{:S(2)}) async-start(bf16[64,8,640]{2,1,0:T(8,128)(2,1)} %bitcast.11), calls=%async_computation.1 | async-start | bytes 1310720 | tf_op jit(solution)/shard_map/all_to_all | solution.py:452
  81.6 3.1 %kept.1 = f32[2560,128]{1,0:T(8,128)} custom-call(f32[2560,128]{1,0:T(8,128)S(1)} %get-tuple-element.36.advanced, bf16[2560,128]{1,0:T(8,128)(2,1)S(1)} %collective-permute-done.8.far, bf16[2560,128]{1,0:T(8,128)(2,1)S(1)} %get-tuple-element.40.mask, bf16[64,192]{1,0:T(8,128)(2,1)S(1)} %copy-done.1, bf16[64,192]{1,0:T(8,128)(2,1)S(1)} %copy-done.8), custom_call_target="tpu_custom_call" | custom-call | tf_op jit(solution)/shard_map/kept/pallas_call | solution.py:319
  84.6 18.1 %all-to-all-done.1 = bf16[64,8,640]{2,1,0:T(8,128)(2,1)S(1)} async-done(((bf16[64,8,640]{2,1,0:T(8,128)(2,1)}), bf16[64,8,640]{2,1,0:T(8,128)(2,1)S(1)}, u32[]{:S(2)}, u32[]{:S(2)}) %all-to-all-start.1) | async-done | bytes 655392 | tf_op jit(solution)/shard_map/all_to_all | solution.py:452
  102.7 1.1 %turn.1 = bf16[2560,128]{1,0:T(8,128)(2,1)} custom-call(bf16[512,640]{1,0:T(8,128)(2,1)S(1)} %bitcast.27), custom_call_target="tpu_custom_call" | custom-call | tf_op jit(solution)/shard_map/turn/pallas_call | solution.py:319
  (15 shorter events, 0.1 us)
Async XLA Ops:
  1.6 13.1 %collective-permute-start.3 = (bf16[432,128]{1,0:T(8,128)(2,1)S(1)}, bf16[432,128]{1,0:T(8,128)(2,1)S(1)}, u32[]{:S(2)}, u32[]{:S(2)}) collective-permute-start(bf16[432,128]{1,0:T(8,128)(2,1)S(1)} %far_keys.1), channel_id=1, source_target_pairs={{0,4},{1,5},{2,6},{3,7},{4,0},{5,1},{6,2},{7,3},{8,12},{9,13},{10,... | collective-permute-start | bytes 331784 | tf_op jit(solution)/shard_map/ppermute | solution.py:336
  5.6 30.5 %collective-permute-start.1 = (bf16[208,2560]{1,0:T(8,128)(2,1)}, bf16[208,2560]{1,0:T(8,128)(2,1)S(1)}, u32[]{:S(2)}, u32[]{:S(2)}) collective-permute-start(bf16[208,2560]{1,0:T(8,128)(2,1)} %param.12), channel_id=1, source_target_pairs={{0,6},{1,7},{2,4},{3,5},{4,2},{5,3},{6,0},{7,1},{8,14},{9,15},{10,... | collective-permute-start | bytes 3194888 | tf_op jit(solution)/shard_map/ppermute | solution.py:336
  12.8 23.4 %collective-permute-start.2 = (bf16[208,2560]{1,0:T(8,128)(2,1)}, bf16[208,2560]{1,0:T(8,128)(2,1)S(1)}, u32[]{:S(2)}, u32[]{:S(2)}) collective-permute-start(bf16[208,2560]{1,0:T(8,128)(2,1)} %param.12), channel_id=1, source_target_pairs={{0,2},{1,3},{2,0},{3,1},{4,6},{5,7},{6,4},{7,5},{8,10},{9,11},{10,... | collective-permute-start | bytes 3194888 | tf_op jit(solution)/shard_map/ppermute | solution.py:336
  14.7 10.4 %collective-permute-start.4 = (bf16[208,128]{1,0:T(8,128)(2,1)S(1)}, bf16[208,128]{1,0:T(8,128)(2,1)S(1)}, u32[]{:S(2)}, u32[]{:S(2)}) collective-permute-start(bf16[208,128]{1,0:T(8,128)(2,1)S(1)} %get-tuple-element.30), channel_id=1, source_target_pairs={{0,1},{1,0},{2,3},{3,2},{4,5},{5,4},{6,7},{7,6},{8,9},{9,8},{10,11... | collective-permute-start | bytes 159752 | tf_op jit(solution)/shard_map/ppermute | solution.py:339
  16.7 1.0 copy-start
  17.7 11.7 %collective-permute-start = (bf16[624,128]{1,0:T(8,128)(2,1)S(1)}, bf16[624,128]{1,0:T(8,128)(2,1)S(1)}, u32[]{:S(2)}, u32[]{:S(2)}) collective-permute-start(bf16[624,128]{1,0:T(8,128)(2,1)S(1)} %get-tuple-element.25), channel_id=1, source_target_pairs={{0,1},{1,0},{2,3},{3,2},{4,5},{5,4},{6,7},{7,6},{8,9},{9,8},{10,11... | collective-permute-start | bytes 479240 | tf_op jit(solution)/shard_map/ppermute | solution.py:339
  20.8 0.8 copy-start.2
  21.6 0.7 copy-start.9
  22.3 6.6 %copy-start.10 = (bf16[208,2560]{1,0:T(8,128)(2,1)S(1)}, bf16[208,2560]{1,0:T(8,128)(2,1)}, u32[]{:S(2)}) copy-start(bf16[208,2560]{1,0:T(8,128)(2,1)} %param.12) | copy-start | bytes 3194884
  26.9 4.0 %collective-permute-start.5 = (bf16[2560,128]{1,0:T(8,128)(2,1)S(1)}, bf16[2560,128]{1,0:T(8,128)(2,1)S(1)}, u32[]{:S(2)}, u32[]{:S(2)}) collective-permute-start(bf16[2560,128]{1,0:T(8,128)(2,1)S(1)} %convolution_convert_fusion), channel_id=1, source_target_pairs={{0,1},{1,0},{2,3},{3,2},{4,5},{5,4},{6,7},{7,6},{8,9},{9,8},{10,11... | collective-permute-start | bytes 1966088 | tf_op jit(solution)/shard_map/ppermute | solution.py:339
  29.5 1.4 %copy-start.1 = (bf16[64,192]{1,0:T(8,128)(2,1)S(1)}, bf16[64,192]{1,0:T(8,128)(2,1)}, u32[]{:S(2)}) copy-start(bf16[64,192]{1,0:T(8,128)(2,1)} %constant.16.clone.forward) | copy-start | bytes 73732
  29.5 1.4 %copy-start.3 = (f32[128,128]{1,0:T(8,128)S(1)}, f32[128,128]{1,0:T(8,128)}, u32[]{:S(2)}) copy-start(f32[128,128]{1,0:T(8,128)} %constant.18.clone.base) | copy-start | bytes 196612
  29.5 1.4 %copy-start.5 = (bf16[512,128]{1,0:T(8,128)(2,1)S(1)}, bf16[512,128]{1,0:T(8,128)(2,1)}, u32[]{:S(2)}) copy-start(bf16[512,128]{1,0:T(8,128)(2,1)} %constant.19.clone.spans) | copy-start | bytes 393220
  29.5 1.4 %copy-start.7 = (f32[128,128]{1,0:T(8,128)S(1)}, f32[128,128]{1,0:T(8,128)}, u32[]{:S(2)}) copy-start(f32[128,128]{1,0:T(8,128)} %constant.20.clone.slots) | copy-start | bytes 196612
  32.8 10.9 %collective-permute-start.7 = (bf16[512,128]{1,0:T(8,128)(2,1)S(1)}, bf16[512,128]{1,0:T(8,128)(2,1)S(1)}, u32[]{:S(2)}, u32[]{:S(2)}) collective-permute-start(bf16[512,128]{1,0:T(8,128)(2,1)S(1)} %get-tuple-element.33), channel_id=1, source_target_pairs={{0,4},{1,5},{2,6},{3,7},{4,0},{5,1},{6,2},{7,3},{8,12},{9,13},{10,... | collective-permute-start | bytes 393224 | tf_op jit(solution)/shard_map/ppermute | solution.py:336
  37.3 6.2 %copy-start.11 = (f32[1,2560,128]{2,1,0:T(8,128)S(1)}, f32[1,2560,128]{2,1,0:T(8,128)}, u32[]{:S(2)}) copy-start(f32[1,2560,128]{2,1,0:T(8,128)} %param.14) | copy-start | bytes 3932164
  37.4 6.2 %collective-permute-start.6 = (bf16[2560,128]{1,0:T(8,128)(2,1)S(1)}, bf16[2560,128]{1,0:T(8,128)(2,1)S(1)}, u32[]{:S(2)}, u32[]{:S(2)}) collective-permute-start(bf16[2560,128]{1,0:T(8,128)(2,1)S(1)} %slice.39), channel_id=1, source_target_pairs={{0,1},{1,0},{2,3},{3,2},{4,5},{5,4},{6,7},{7,6},{8,9},{9,8},{10,11... | collective-permute-start | bytes 1966088 | tf_op jit(solution)/shard_map/ppermute | solution.py:339
  39.5 37.4 %collective-permute-start.8 = (bf16[2560,128]{1,0:T(8,128)(2,1)S(1)}, bf16[2560,128]{1,0:T(8,128)(2,1)S(1)}, u32[]{:S(2)}, u32[]{:S(2)}) collective-permute-start(bf16[2560,128]{1,0:T(8,128)(2,1)S(1)} %get-tuple-element.38), channel_id=1, source_target_pairs={{0,4},{1,5},{2,6},{3,7},{4,0},{5,1},{6,2},{7,3},{8,12},{9,13},{10,... | collective-permute-start | bytes 1966088 | tf_op jit(solution)/shard_map/ppermute | solution.py:336
  43.7 31.4 %copy-start.4 = (bf16[128,1024]{1,0:T(8,128)(2,1)S(1)}, bf16[128,1024]{1,0:T(8,128)(2,1)}, u32[]{:S(2)}) copy-start(bf16[128,1024]{1,0:T(8,128)(2,1)} %constant.22.clone.unpack) | copy-start | bytes 786436
  43.7 31.4 %copy-start.6 = (bf16[384,128]{1,0:T(8,128)(2,1)S(1)}, bf16[384,128]{1,0:T(8,128)(2,1)}, u32[]{:S(2)}) copy-start(bf16[384,128]{1,0:T(8,128)(2,1)} %constant.21.clone.backward) | copy-start | bytes 294916
  44.7 36.8 %copy-start.8 = (bf16[64,192]{1,0:T(8,128)(2,1)S(1)}, bf16[64,192]{1,0:T(8,128)(2,1)}, u32[]{:S(2)}) copy-start(bf16[64,192]{1,0:T(8,128)(2,1)} %constant.17.clone.backward) | copy-start | bytes 73732
  76.9 25.8 %all-to-all-start.1 = ((bf16[64,8,640]{2,1,0:T(8,128)(2,1)}), bf16[64,8,640]{2,1,0:T(8,128)(2,1)S(1)}, u32[]{:S(2)}, u32[]{:S(2)}) async-start(bf16[64,8,640]{2,1,0:T(8,128)(2,1)} %bitcast.11), calls=%async_computation.1 | async-start | bytes 1310720 | tf_op jit(solution)/shard_map/all_to_all | solution.py:452
